TPU v7x, 512 devices: a whole 4x4x16 slice. The times are simulated.
512 devices in a mesh: mp: 64 (over y_hi, z, core), dp: 8 (over x, y_lo).
Axes of the slice: x: 4, y: 4 (y_hi: 2, y_lo: 2; y = y_hi * 2 + y_lo), z: 16, core: 2. Of those that a mesh axis runs over, the one named last changes fastest.
Arguments:
- table: bfloat16 [384, 8192], P('mp', 'dp'), may hold values from -6 to 6
- ids: int32 [384], replicated, may hold values from 0 to 383, each once
- gate_weight: bfloat16 [8192, 16384], P('dp', 'mp'), may hold values from -0.0625 to 0.0625
- up_weight: bfloat16 [8192, 16384], P('dp', 'mp'), may hold values from -0.0625 to 0.0625
- down_weight: bfloat16 [16384, 8192], P('mp', 'dp'), may hold values from -0.046875 to 0.046875
- gate_probe: bfloat16 [8192, 16384], P('dp', 'mp'), may hold values from -0.0625 to 0.0625
- up_probe: bfloat16 [8192, 16384], P('dp', 'mp'), may hold values from -0.0625 to 0.0625
- down_probe: bfloat16 [16384, 8192], P('mp', 'dp'), may hold values from -0.046875 to 0.046875
Outputs:
- tangent_out: bfloat16 [384, 8192], P('mp', 'dp')
- ggn_gate: bfloat16 [8192, 16384], P('dp', 'mp')
- ggn_up: bfloat16 [8192, 16384], P('dp', 'mp')
- ggn_down: bfloat16 [16384, 8192], P('mp', 'dp')
Inputs may be any that keep to these rules, and one draw needn't show every extreme that they name: ids holds every row of table exactly once.
All inputs are finite; a program needn't handle non-finite values.
Results may differ from a plain program's by a relative error of at most 0.009.
Values may be sent and summed in bfloat16 or wider, within the bound.
No kernel may reach another device: no remote copies, remote signals or barrier semaphores. Data moves between devices by JAX's collectives and lax.ppermute only.
A program may use at most 64 MiB of HBM per device.

v0:
```python
import jax
import jax.numpy as jnp
from jax import lax
from jax.sharding import PartitionSpec as P


def product(left, right):
    return jnp.dot(left, right, preferred_element_type=jnp.float32)


def over_rows(left, right):
    return lax.dot_general(
        left, right, (((0,), (0,)), ((), ())), preferred_element_type=jnp.float32
    )


def over_width(left, right):
    return lax.dot_general(
        left, right, (((1,), (1,)), ((), ())), preferred_element_type=jnp.float32
    )


def pointwise(gate, up_value, tan_gate, tan_up):
    sigmoid_gate = jax.nn.sigmoid(gate)
    activated = gate * sigmoid_gate
    slope = sigmoid_gate * (1.0 + gate * (1.0 - sigmoid_gate))
    hidden = (activated * up_value).astype(jnp.bfloat16)
    tan_hidden = (slope * tan_gate * up_value + activated * tan_up).astype(jnp.bfloat16)
    return (hidden, tan_hidden, activated, slope)


def local(table, ids, gate_weight, up_weight, down_weight, gate_probe, up_probe, down_probe):
    scale = float(ids.shape[0]) ** (-0.5)
    own_count = table.shape[0]
    full_table = lax.all_gather(table, "mp", axis=0, tiled=True)
    inputs = jnp.take(full_table, ids, axis=0)
    partials = (
        product(inputs, gate_weight),
        product(inputs, up_weight),
        product(inputs, gate_probe),
        product(inputs, up_probe),
    )
    gate, up_value, tan_gate, tan_up = lax.psum(
        (partials[0], partials[1], partials[2], partials[3]), "dp"
    )
    hidden, tan_hidden, activated, slope = pointwise(gate, up_value, tan_gate, tan_up)
    partial_out = product(tan_hidden, down_weight) + product(hidden, down_probe)
    tan_out = lax.psum(partial_out, "mp")
    own_rows = lax.dynamic_slice_in_dim(tan_out, lax.axis_index("mp") * own_count, own_count, 0)
    tangent_out = own_rows.astype(jnp.bfloat16)
    cotangent = (tan_out * scale).astype(jnp.bfloat16)
    ggn_down = over_rows(hidden, cotangent)
    cot_hidden = over_width(cotangent, down_weight)
    summed = lax.psum(cot_hidden, "dp")
    cot_gate = (summed * up_value * slope).astype(jnp.bfloat16)
    cot_up = (summed * activated).astype(jnp.bfloat16)
    ggn_gate = over_rows(inputs, cot_gate)
    ggn_up = over_rows(inputs, cot_up)
    return (
        tangent_out,
        ggn_gate.astype(jnp.bfloat16),
        ggn_up.astype(jnp.bfloat16),
        ggn_down.astype(jnp.bfloat16),
    )


def solution(mesh):
    in_specs = (
        P("mp", "dp"),
        P(),
        P("dp", "mp"),
        P("dp", "mp"),
        P("mp", "dp"),
        P("dp", "mp"),
        P("dp", "mp"),
        P("mp", "dp"),
    )
    out_specs = (P("mp", "dp"), P("dp", "mp"), P("dp", "mp"), P("mp", "dp"))
    return jax.shard_map(local, mesh=mesh, in_specs=in_specs, out_specs=out_specs, check_vma=False)
```

profile of v0, /device:TPU:1, one launch (start us, length us, event | category | flops | bytes accessed | tf_op | source)
XLA Modules:
  0.0 817.1 jit_solution(154190890492234432)
XLA Ops:
  7.2 0.0 copy-start
  7.2 0.0 all-reduce.9.cloned.1.call-start
  7.2 0.7 compare_select_fusion
  8.0 0.7 compare_and_fusion
  8.6 87.8 %all-gather = bf16[64,6,1024]{2,1,0:T(8,128)(2,1)S(1)} all-gather(bf16[1,6,1024]{2,1,0:T(8,128)(2,1)} %bitcast.10), channel_id=1, replica_groups=mesh['mp'=64,'dp'=8] {'mp'}, dimensions={0}, use_global_device_ids=true | all-gather | bytes 798720 | tf_op jit(solution)/shard_map/all_gather | solution.py:35
  96.4 0.3 reshape.23
  96.7 0.0 copy-start.7
  96.7 2.1 gather_fusion
  98.8 0.0 copy-start.8
  98.8 1.2 fusion.7
  100.0 0.2 copy-done.8
  100.1 1.2 fusion.8
  101.3 0.0 copy-done.9
  101.3 1.2 fusion.9
  102.5 1.2 fusion.10
  103.6 0.0 all-reduce.9.cloned.1.call-update
  103.7 0.0 all-reduce.5.cloned.1.call-start
  103.7 91.3 %all-reduce.9.cloned.1.call-done = (f32[384,256]{1,0:T(8,128)}, f32[384,256]{1,0:T(8,128)}, f32[384,256]{1,0:T(8,128)}, f32[384,256]{1,0:T(8,128)}) async-done(((f32[384,256]{1,0:T(8,128)}, f32[384,256]{1,0:T(8,128)}, f32[384,256]{1,0:T(8,128)}, f32[384,256]{1,0:T(8,128)}), (f32[384,256]{1,0:T(8,128)}, f32[384,256]{1,0:T(8,128)}, f32[384,256]{1,0:T(8,128)}, ...) | async-done | bytes 1572880 | tf_op jit(solution)/shard_map/psum | solution.py:43
  195.1 1.2 multiply_convert_fusion.3
  196.3 0.0 copy-start.6
  196.3 1.9 fusion.2
  198.2 1.5 convolution_add_fusion
  199.7 0.0 all-reduce.5.cloned.1.call-update
  199.8 0.0 all-reduce.7.cloned.1.call-start
  199.8 525.1 %all-reduce.5.cloned.1.call-done = f32[384,1024]{1,0:T(8,128)} async-done(((f32[384,1024]{1,0:T(8,128)}), f32[384,1024]{1,0:T(8,128)}) %all-reduce.5.cloned.1.call-update) | async-done | bytes 1572880 | tf_op jit(solution)/shard_map/psum | solution.py:48
  724.9 2.7 fusion.1
  727.6 0.0 all-reduce.7.cloned.1.call-update
  727.6 0.6 dynamic-slice_convert_fusion
  728.2 1.3 convolution_convert_fusion
  729.5 77.0 %all-reduce.7.cloned.1.call-done = f32[384,256]{1,0:T(8,128)} async-done(((f32[384,256]{1,0:T(8,128)}), f32[384,256]{1,0:T(8,128)}) %all-reduce.7.cloned.1.call-update) | async-done | bytes 393232 | tf_op jit(solution)/shard_map/psum | solution.py:54
  806.5 2.7 convolution_convert_fusion.2
  809.2 1.4 convolution_convert_fusion.1
  (19 shorter events, 0.0 us)
Async XLA Ops:
  7.2 189.1 %copy-start = (bf16[256,1024]{1,0:T(8,128)(2,1)S(1)}, bf16[256,1024]{1,0:T(8,128)(2,1)}, u32[]{:S(2)}) copy-start(bf16[256,1024]{1,0:T(8,128)(2,1)} %param.12) | copy-start | bytes 1572868
  7.2 187.9 %all-reduce.9.cloned.1.call-start = ((), (), s32[]{:S(2)}) async-start(), calls=%async_computation.2 | async-start | bytes 3145728 | tf_op jit(solution)/shard_map/psum | solution.py:43
  96.7 2.1 copy-start.7
  98.8 3.7 copy-start.4
  98.8 1.3 copy-start.8
  100.1 1.2 copy-start.9
  101.3 1.2 copy-start.10
  103.7 621.2 %all-reduce.5.cloned.1.call-start = ((), (), s32[]{:S(2)}) async-start(), calls=%async_computation | async-start | bytes 3145728 | tf_op jit(solution)/shard_map/psum | solution.py:48
  196.3 1.9 copy-start.6
  199.8 606.7 %all-reduce.7.cloned.1.call-start = ((), (), s32[]{:S(2)}) async-start(), calls=%async_computation.1 | async-start | bytes 786432 | tf_op jit(solution)/shard_map/psum | solution.py:54
  724.9 2.7 copy-start.1
  727.6 78.9 %copy-start.2 = (f32[384,256]{1,0:T(8,128)S(1)}, f32[384,256]{1,0:T(8,128)}, u32[]{:S(2)}) copy-start(f32[384,256]{1,0:T(8,128)} %get-tuple-element.7) | copy-start | bytes 1179652
  727.6 78.9 %copy-start.3 = (f32[384,256]{1,0:T(8,128)S(1)}, f32[384,256]{1,0:T(8,128)}, u32[]{:S(2)}) copy-start(f32[384,256]{1,0:T(8,128)} %get-tuple-element.5) | copy-start | bytes 1179652
  729.5 79.7 %copy-start.5 = (bf16[384,1024]{1,0:T(8,128)(2,1)S(1)}, bf16[384,1024]{1,0:T(8,128)(2,1)}, u32[]{:S(2)}) copy-start(bf16[384,1024]{1,0:T(8,128)(2,1)} %copy-done.4) | copy-start | bytes 2359300
  806.5 2.7 copy-start.11
Sparse Core Ops, SparseCore 0:
  103.8 91.2 all-reduce.8
  199.9 524.9 all-reduce.4
  728.6 77.7 all-reduce.6
where the time goes:
time: 821 us; the launch traced here: 817 us
  waiting for transfers between devices  693 us (84%)
  blocking collectives  87.8 us (11%)
  matrix products  16.1 us (2%)
  between operations  13.9 us (2%)
    psum x1, waiting for transfers between devices, local(): tan_out = lax.psum(partial_out, 'mp')  525 us
    psum x1, waiting for transfers between devices, local(): lax.psum((partials[0], partials[1], partials[2], partials[3]), 'dp')  91.3 us
    all_gather x1, blocking collectives, local(): full_table = lax.all_gather(table, 'mp', axis=0, tiled=True)  87.8 us
    psum x1, waiting for transfers between devices, local(): summed = lax.psum(cot_hidden, 'dp')  77 us
  transfers between devices with their start and end apart: 3, of which 3 were waited for; matrix products, arithmetic and copies ran while one was open for 0% of the time, Pallas kernels for 0%

commit v1 on v0

v1 whole, which is shorter than its diff:
```python
import jax
import jax.numpy as jnp
from jax import lax
from jax.sharding import Mesh, PartitionSpec as P

YH, Z, CORE, X, YL = "yh", "z", "core", "x", "yl"
MP = (YH, Z, CORE)
DP = (X, YL)
bf16 = jnp.bfloat16
f32 = jnp.float32


def product(left, right):
    return jnp.dot(left, right, preferred_element_type=f32)


def over_rows(left, right):
    return lax.dot_general(left, right, (((0,), (0,)), ((), ())), preferred_element_type=f32)


def over_width(left, right):
    return lax.dot_general(left, right, (((1,), (1,)), ((), ())), preferred_element_type=f32)


def swap(value, axis):
    return lax.ppermute(value, axis, [(0, 1), (1, 0)])


def spread(value, axes, count):
    return lax.all_to_all(jnp.broadcast_to(value[None], (count,) + value.shape), axes, 0, 0)


def join(own, other, position, axis):
    return jnp.where(
        position == 0,
        jnp.concatenate([own, other], axis=axis),
        jnp.concatenate([other, own], axis=axis),
    )


def local(table, ids, gate_weight, up_weight, down_weight, gate_probe, up_probe, down_probe):
    tokens = ids.shape[0]
    own_count, width = table.shape
    units = gate_weight.shape[1]
    scale = float(tokens) ** (-0.5)
    nz, ndp = lax.axis_size(Z), lax.axis_size(X) * lax.axis_size(YL)
    core, yh = lax.axis_index(CORE), lax.axis_index(YH)

    rows = spread(table, Z, nz)
    rows = join(rows[None], swap(rows, YH)[None], yh, 0)
    rows = rows[:, :, None]
    rows = join(rows, swap(rows, CORE), core, 2)
    inputs = jnp.take(rows.reshape(tokens, width), ids, axis=0)

    partials = jnp.concatenate(
        [product(inputs, w).astype(bf16) for w in (gate_weight, up_weight, gate_probe, up_probe)], axis=1
    )
    own = tokens // ndp
    parts = lax.all_to_all(partials.reshape(ndp, own, 4 * units), DP, 0, 0)
    sums = jnp.sum(parts.astype(f32), axis=0)
    gate, up_value, tan_gate, tan_up = (sums[:, i * units : (i + 1) * units] for i in range(4))
    sigmoid_gate = jax.nn.sigmoid(gate)
    activated = gate * sigmoid_gate
    slope = sigmoid_gate * (1.0 + gate * (1.0 - sigmoid_gate))
    both = jnp.concatenate(
        [
            (activated * up_value).astype(bf16),
            (slope * tan_gate * up_value + activated * tan_up).astype(bf16),
        ],
        axis=1,
    )
    both = spread(both, DP, ndp).reshape(tokens, 2 * units)
    hidden, tan_hidden = both[:, :units], both[:, units:]

    partial_out = product(tan_hidden, down_weight) + product(hidden, down_probe)
    half, quarter = width // 2, width // 4
    left, right = partial_out[:, :half], partial_out[:, half:]
    kept = jnp.where(core == 0, left, right)
    sent = jnp.where(core == 0, right, left).astype(bf16)
    kept = kept + swap(sent, CORE).astype(f32)
    left, right = kept[:, :quarter], kept[:, quarter:]
    kept = jnp.where(yh == 0, left, right)
    sent = jnp.where(yh == 0, right, left).astype(bf16)
    kept = kept + swap(sent, YH).astype(f32)
    parts = lax.all_to_all(kept.astype(bf16).reshape(nz, tokens // nz, quarter), Z, 0, 0)
    block = jnp.sum(parts.astype(f32), axis=0).astype(bf16)

    out = spread(block, Z, nz).reshape(tokens, quarter)
    out = join(out, swap(out, YH), yh, 1)
    out = join(out, swap(out, CORE), core, 1)
    tangent_out = lax.dynamic_slice_in_dim(out, lax.axis_index(MP) * own_count, own_count, 0)

    ggn_down = (over_rows(hidden, out) * scale).astype(bf16)
    cot_hidden = over_width(out, down_weight).astype(bf16)
    parts = lax.all_to_all(cot_hidden.reshape(ndp, own, units), DP, 0, 0)
    summed = jnp.sum(parts.astype(f32), axis=0) * scale
    both = jnp.concatenate(
        [(summed * up_value * slope).astype(bf16), (summed * activated).astype(bf16)], axis=1
    )
    both = spread(both, DP, ndp).reshape(tokens, 2 * units)
    ggn = over_rows(inputs, both).astype(bf16)
    return tangent_out, ggn[:, :units], ggn[:, units:], ggn_down


def solution(mesh):
    devices = mesh.devices.reshape(2, 16, 2, 4, 2)
    fine = Mesh(devices, (YH, Z, CORE, X, YL))
    in_specs = (
        P(MP, DP),
        P(),
        P(DP, MP),
        P(DP, MP),
        P(MP, DP),
        P(DP, MP),
        P(DP, MP),
        P(MP, DP),
    )
    out_specs = (P(MP, DP), P(DP, MP), P(DP, MP), P(MP, DP))
    return jax.shard_map(local, mesh=fine, in_specs=in_specs, out_specs=out_specs, check_vma=False)
```

time: 821 us -> 181 us (0.22)
  waiting for transfers between devices: 693 us -> 26.4 us
  starting transfers between devices: 0.12 us -> 42.6 us
  between operations: 13.9 us -> 1.01 us
  matrix products: 16.1 us -> 6.1 us
    psum x3 -> x0, waiting for transfers between devices: 693 us -> none  [the longest x1 525 us: local(): tan_out = lax.psum(partial_out, 'mp')]
    all_to_all x0 -> x5, blocking collectives: none -> 95.5 us  [the longest x3 60 us: spread(): lax.all_to_all(jnp.broadcast_to(value[None], (count,) + value.shape), axe...]
    all_gather x1 -> x0, blocking collectives: 87.8 us -> none  [local(): full_table = lax.all_gather(table, 'mp', axis=0, tiled=True)]
    ppermute x0 -> x6, starting transfers between devices: none -> 35.7 us  [swap(): return lax.ppermute(value, axis, [(0, 1), (1, 0)])]
    ppermute x0 -> x6, waiting for transfers between devices: none -> 16.3 us  [swap(): return lax.ppermute(value, axis, [(0, 1), (1, 0)])]
    all_to_all x0 -> x2, waiting for transfers between devices: none -> 10.1 us  [the longest x1 5.71 us: local(): parts = lax.all_to_all(cot_hidden.reshape(ndp, own, units), DP, 0, 0)]
  transfers between devices with their start and end apart: 3 -> 8, of which waited for: 3 -> 8; matrix products, arithmetic and copies ran while one was open for 0% -> 1% of each run, Pallas kernels for 0% -> 0%
where the time goes in v1:
time: 181 us; the launch traced here: 180 us
  blocking collectives  95.5 us (53%)
  starting transfers between devices  42.6 us (24%)
  waiting for transfers between devices  26.4 us (15%)
  local copies, waits for them, and re-layouts  6.41 us (4%)
  matrix products  6.1 us (3%)
    all_to_all x3, blocking collectives, spread(): lax.all_to_all(jnp.broadcast_to(value[None], (count,) + value.shape), axe...  60 us
    ppermute x6, starting transfers between devices, swap(): return lax.ppermute(value, axis, [(0, 1), (1, 0)])  35.7 us
    all_to_all x1, blocking collectives, local(): lax.all_to_all(kept.astype(bf16).reshape(nz, tokens // nz, quarter), Z, 0...  19.3 us
    all_to_all x1, blocking collectives, local(): parts = lax.all_to_all(partials.reshape(ndp, own, 4 * units), DP, 0, 0)  16.3 us
    ppermute x6, waiting for transfers between devices, swap(): return lax.ppermute(value, axis, [(0, 1), (1, 0)])  16.3 us
    all_to_all x1, waiting for transfers between devices, local(): parts = lax.all_to_all(cot_hidden.reshape(ndp, own, units), DP, 0, 0)  5.71 us
    all_to_all x1, waiting for transfers between devices, spread(): lax.all_to_all(jnp.broadcast_to(value[None], (count,) + value.shape), axe...  4.42 us
  transfers between devices with their start and end apart: 8, of which 8 were waited for; matrix products, arithmetic and copies ran while one was open for 1% of the time, Pallas kernels for 0%

profile of v1, /device:TPU:1, one launch (start us, length us, event | category | flops | bytes accessed | tf_op | source)
XLA Modules:
  0.0 179.5 jit_solution(13704686392600161942)
XLA Ops:
  0.7 0.8 broadcast_in_dim.21
  1.5 28.7 %all_to_all.35 = bf16[16,6,1024]{2,1,0:T(8,128)(2,1)S(1)} all-to-all(bf16[16,6,1024]{2,1,0:T(8,128)(2,1)S(1)} %broadcast_in_dim.21), channel_id=1, replica_groups=mesh['yh'=2,'z'=16,'core'=2,'x'=4,'yl'=2] {'z'}, dimensions={0} | all-to-all | bytes 393216 | tf_op jit(solution)/shard_map/all_to_all | solution.py:30
  30.1 4.8 %collective-permute-start = (bf16[16,6,1024]{2,1,0:T(8,128)(2,1)S(1)}, bf16[16,6,1024]{2,1,0:T(8,128)(2,1)S(1)}, u32[]{:S(2)}, u32[]{:S(2)}) collective-permute-start(bf16[16,6,1024]{2,1,0:T(8,128)(2,1)S(1)} %all_to_all.35), channel_id=1, source_target_pairs={{0,256},{256,0},{1,257},{257,1},{2,258},{258,2},{3,259},{259,3},{4... | collective-permute-start | bytes 589832 | tf_op jit(solution)/shard_map/ppermute | solution.py:26
  35.0 3.8 %collective-permute-done = bf16[16,6,1024]{2,1,0:T(8,128)(2,1)S(1)} collective-permute-done((bf16[16,6,1024]{2,1,0:T(8,128)(2,1)S(1)}, bf16[16,6,1024]{2,1,0:T(8,128)(2,1)S(1)}, u32[]{:S(2)}, u32[]{:S(2)}) %collective-permute-start) | collective-permute-done | bytes 196640 | tf_op jit(solution)/shard_map/ppermute | solution.py:26
  38.9 9.2 %collective-permute-start.1 = (bf16[2,16,1,6,1024]{4,3,2,1,0:T(8,128)(2,1)S(1)}, bf16[2,16,1,6,1024]{4,3,2,1,0:T(8,128)(2,1)S(1)}, u32[]{:S(2)}, u32[]{:S(2)}) collective-permute-start(bf16[2,16,1,6,1024]{4,3,2,1,0:T(8,128)(2,1)S(1)} %maximum_select_fusion.2), channel_id=1, source_target_pairs={{0,8},{8,0},{1,9},{9,1},{2,10},{10,2},{3,11},{11,3},{4,12},{12,4},... | collective-permute-start | bytes 1179656 | tf_op jit(solution)/shard_map/ppermute | solution.py:26
  48.2 1.5 collective-permute-done.1
  50.3 2.1 %gather_fusion = bf16[384,1024]{1,0:T(8,128)(2,1)S(1)} fusion(bf16[384,1024]{1,0:T(8,128)(2,1)S(1)} %select_n.88, s32[1024]{0:T(1024)S(1)} %pad_clamp_fusion), kind=kCustom, calls=%fused_computation | custom fusion | bytes 1574400 | tf_op jit(solution)/shard_map/jit(_take)/gather | solution.py:53
  52.4 0.6 convolution_convert_fusion.4
  54.0 0.6 convolution_convert_fusion.2
  54.6 0.5 convolution_convert_fusion.5
  55.5 16.3 %all_to_all.36 = bf16[8,48,1024]{2,1,0:T(8,128)(2,1)S(1)} all-to-all(bf16[8,48,1024]{2,1,0:T(8,128)(2,1)S(1)} %bitcast.18), channel_id=1, replica_groups=mesh['yh'=2,'z'=16,'core'=2,'x'=4,'yl'=2] {'x','yl'}, dimensions={0} | all-to-all | bytes 1572864 | tf_op jit(solution)/shard_map/all_to_all | solution.py:59
  72.0 10.5 %all_to_all.37 = bf16[8,48,512]{2,1,0:T(8,128)(2,1)S(1)} all-to-all(bf16[8,48,512]{2,1,0:T(8,128)(2,1)S(1)} %broadcast_in_dim.24), channel_id=1, replica_groups=mesh['yh'=2,'z'=16,'core'=2,'x'=4,'yl'=2] {'x','yl'}, dimensions={0} | all-to-all | bytes 786432 | tf_op jit(solution)/shard_map/all_to_all | solution.py:30
  83.4 4.5 %collective-permute-start.2 = (bf16[384,512]{1,0:T(8,128)(2,1)S(1)}, bf16[384,512]{1,0:T(8,128)(2,1)S(1)}, u32[]{:S(2)}, u32[]{:S(2)}) collective-permute-start(bf16[384,512]{1,0:T(8,128)(2,1)S(1)} %select_convert_fusion), channel_id=1, source_target_pairs={{0,8},{8,0},{1,9},{9,1},{2,10},{10,2},{3,11},{11,3},{4,12},{12,4},... | collective-permute-start | bytes 1179656 | tf_op jit(solution)/shard_map/ppermute | solution.py:26
  87.8 1.3 collective-permute-done.2
  89.4 4.5 %collective-permute-start.3 = (bf16[384,256]{1,0:T(8,128)(2,1)S(1)}, bf16[384,256]{1,0:T(8,128)(2,1)S(1)}, u32[]{:S(2)}, u32[]{:S(2)}) collective-permute-start(bf16[384,256]{1,0:T(8,128)(2,1)S(1)} %select_convert_fusion.1), channel_id=1, source_target_pairs={{0,256},{256,0},{1,257},{257,1},{2,258},{258,2},{3,259},{259,3},{4... | collective-permute-start | bytes 589832 | tf_op jit(solution)/shard_map/ppermute | solution.py:26
  94.0 5.0 %collective-permute-done.3 = bf16[384,256]{1,0:T(8,128)(2,1)S(1)} collective-permute-done((bf16[384,256]{1,0:T(8,128)(2,1)S(1)}, bf16[384,256]{1,0:T(8,128)(2,1)S(1)}, u32[]{:S(2)}, u32[]{:S(2)}) %collective-permute-start.3) | collective-permute-done | bytes 196640 | tf_op jit(solution)/shard_map/ppermute | solution.py:26
  99.0 19.3 %all_to_all.38 = bf16[16,24,256]{2,1,0:T(8,128)(2,1)S(1)} all-to-all(bf16[16,24,256]{2,1,0:T(8,128)(2,1)S(1)} %bitcast.25), channel_id=1, replica_groups=mesh['yh'=2,'z'=16,'core'=2,'x'=4,'yl'=2] {'z'}, dimensions={0} | all-to-all | bytes 393216 | tf_op jit(solution)/shard_map/all_to_all | solution.py:85
  118.3 20.8 %all_to_all.39 = bf16[16,24,256]{2,1,0:T(8,128)(2,1)S(1)} all-to-all(bf16[16,24,256]{2,1,0:T(8,128)(2,1)S(1)} %broadcast_in_dim.44), channel_id=1, replica_groups=mesh['yh'=2,'z'=16,'core'=2,'x'=4,'yl'=2] {'z'}, dimensions={0} | all-to-all | bytes 393216 | tf_op jit(solution)/shard_map/all_to_all | solution.py:30
  139.1 4.5 %collective-permute-start.4 = (bf16[384,256]{1,0:T(8,128)(2,1)S(1)}, bf16[384,256]{1,0:T(8,128)(2,1)S(1)}, u32[]{:S(2)}, u32[]{:S(2)}) collective-permute-start(bf16[384,256]{1,0:T(8,128)(2,1)S(1)} %bitcast.23), channel_id=1, source_target_pairs={{0,256},{256,0},{1,257},{257,1},{2,258},{258,2},{3,259},{259,3},{4... | collective-permute-start | bytes 589832 | tf_op jit(solution)/shard_map/ppermute | solution.py:26
  143.6 3.4 %collective-permute-done.4 = bf16[384,256]{1,0:T(8,128)(2,1)S(1)} collective-permute-done((bf16[384,256]{1,0:T(8,128)(2,1)S(1)}, bf16[384,256]{1,0:T(8,128)(2,1)S(1)}, u32[]{:S(2)}, u32[]{:S(2)}) %collective-permute-start.4) | collective-permute-done | bytes 196640 | tf_op jit(solution)/shard_map/ppermute | solution.py:26
  147.1 8.2 %collective-permute-start.5 = (bf16[384,512]{1,0:T(8,128)(2,1)S(1)}, bf16[384,512]{1,0:T(8,128)(2,1)S(1)}, u32[]{:S(2)}, u32[]{:S(2)}) collective-permute-start(bf16[384,512]{1,0:T(8,128)(2,1)S(1)} %maximum_select_fusion.3), channel_id=1, source_target_pairs={{0,8},{8,0},{1,9},{9,1},{2,10},{10,2},{3,11},{11,3},{4,12},{12,4},... | collective-permute-start | bytes 1179656 | tf_op jit(solution)/shard_map/ppermute | solution.py:26
  155.3 1.3 collective-permute-done.5
  156.8 1.1 convolution_convert_fusion.1
  157.9 3.4 %all-to-all-start.5 = ((bf16[8,48,256]{2,1,0:T(8,128)(2,1)}), bf16[8,48,256]{2,1,0:T(8,128)(2,1)S(1)}, u32[]{:S(2)}, u32[]{:S(2)}) async-start(bf16[8,48,256]{2,1,0:T(8,128)(2,1)} %bitcast.6), calls=%async_computation.5 | async-start | bytes 393216 | tf_op jit(solution)/shard_map/all_to_all | solution.py:95
  161.3 5.7 %all-to-all-done.5 = bf16[8,48,256]{2,1,0:T(8,128)(2,1)S(1)} async-done(((bf16[8,48,256]{2,1,0:T(8,128)(2,1)}), bf16[8,48,256]{2,1,0:T(8,128)(2,1)S(1)}, u32[]{:S(2)}, u32[]{:S(2)}) %all-to-all-start.5) | async-done | bytes 196640 | tf_op jit(solution)/shard_map/all_to_all | solution.py:95
  167.1 0.8 broadcast_in_dim.45
  167.9 3.5 %all-to-all-start.6 = ((bf16[8,48,512]{2,1,0:T(8,128)(2,1)}), bf16[8,48,512]{2,1,0:T(8,128)(2,1)S(1)}, u32[]{:S(2)}, u32[]{:S(2)}) async-start(bf16[8,48,512]{2,1,0:T(8,128)(2,1)} %broadcast_in_dim.45), calls=%async_computation.6 | async-start | bytes 786432 | tf_op jit(solution)/shard_map/all_to_all | solution.py:30
  171.4 0.6 constant_dynamic-slice_fusion
  172.0 1.3 fusion
  173.2 4.4 %all-to-all-done.6 = bf16[8,48,512]{2,1,0:T(8,128)(2,1)S(1)} async-done(((bf16[8,48,512]{2,1,0:T(8,128)(2,1)}), bf16[8,48,512]{2,1,0:T(8,128)(2,1)S(1)}, u32[]{:S(2)}, u32[]{:S(2)}) %all-to-all-start.6) | async-done | bytes 393248 | tf_op jit(solution)/shard_map/all_to_all | solution.py:30
  177.7 0.8 convolution_convert_fusion
  178.5 1.0 fusion.9
  (40 shorter events, 3.9 us)
Async XLA Ops:
  0.6 81.9 %copy-start = (bf16[256,1024]{1,0:T(8,128)(2,1)S(1)}, bf16[256,1024]{1,0:T(8,128)(2,1)}, u32[]{:S(2)}) copy-start(bf16[256,1024]{1,0:T(8,128)(2,1)} %param.12) | copy-start | bytes 1572868
  0.6 47.5 %copy-start.2 = (s32[384]{0:T(512)S(1)}, s32[384]{0:T(512)}, u32[]{:S(2)}) copy-start(s32[384]{0:T(512)} %param.9) | copy-start | bytes 4612
  30.1 8.6 %collective-permute-start = (bf16[16,6,1024]{2,1,0:T(8,128)(2,1)S(1)}, bf16[16,6,1024]{2,1,0:T(8,128)(2,1)S(1)}, u32[]{:S(2)}, u32[]{:S(2)}) collective-permute-start(bf16[16,6,1024]{2,1,0:T(8,128)(2,1)S(1)} %all_to_all.35), channel_id=1, source_target_pairs={{0,256},{256,0},{1,257},{257,1},{2,258},{258,2},{3,259},{259,3},{4... | collective-permute-start | bytes 589832 | tf_op jit(solution)/shard_map/ppermute | solution.py:26
  38.9 10.8 %collective-permute-start.1 = (bf16[2,16,1,6,1024]{4,3,2,1,0:T(8,128)(2,1)S(1)}, bf16[2,16,1,6,1024]{4,3,2,1,0:T(8,128)(2,1)S(1)}, u32[]{:S(2)}, u32[]{:S(2)}) collective-permute-start(bf16[2,16,1,6,1024]{4,3,2,1,0:T(8,128)(2,1)S(1)} %maximum_select_fusion.2), channel_id=1, source_target_pairs={{0,8},{8,0},{1,9},{9,1},{2,10},{10,2},{3,11},{11,3},{4,12},{12,4},... | collective-permute-start | bytes 1179656 | tf_op jit(solution)/shard_map/ppermute | solution.py:26
  50.3 2.1 %copy-start.3 = (bf16[1024,256]{1,0:T(8,128)(2,1)S(1)}, bf16[1024,256]{1,0:T(8,128)(2,1)}, u32[]{:S(2)}) copy-start(bf16[1024,256]{1,0:T(8,128)(2,1)} %param.11) | copy-start | bytes 1572868
  52.4 1.0 copy-start.4
  52.4 1.6 copy-start.5
  53.5 1.1 copy-start.6
  72.0 10.9 %copy-start.1 = (bf16[256,1024]{1,0:T(8,128)(2,1)S(1)}, bf16[256,1024]{1,0:T(8,128)(2,1)}, u32[]{:S(2)}) copy-start(bf16[256,1024]{1,0:T(8,128)(2,1)} %param.15) | copy-start | bytes 1572868
  83.4 5.8 %collective-permute-start.2 = (bf16[384,512]{1,0:T(8,128)(2,1)S(1)}, bf16[384,512]{1,0:T(8,128)(2,1)S(1)}, u32[]{:S(2)}, u32[]{:S(2)}) collective-permute-start(bf16[384,512]{1,0:T(8,128)(2,1)S(1)} %select_convert_fusion), channel_id=1, source_target_pairs={{0,8},{8,0},{1,9},{9,1},{2,10},{10,2},{3,11},{11,3},{4,12},{12,4},... | collective-permute-start | bytes 1179656 | tf_op jit(solution)/shard_map/ppermute | solution.py:26
  89.4 9.5 %collective-permute-start.3 = (bf16[384,256]{1,0:T(8,128)(2,1)S(1)}, bf16[384,256]{1,0:T(8,128)(2,1)S(1)}, u32[]{:S(2)}, u32[]{:S(2)}) collective-permute-start(bf16[384,256]{1,0:T(8,128)(2,1)S(1)} %select_convert_fusion.1), channel_id=1, source_target_pairs={{0,256},{256,0},{1,257},{257,1},{2,258},{258,2},{3,259},{259,3},{4... | collective-permute-start | bytes 589832 | tf_op jit(solution)/shard_map/ppermute | solution.py:26
  139.1 7.9 %collective-permute-start.4 = (bf16[384,256]{1,0:T(8,128)(2,1)S(1)}, bf16[384,256]{1,0:T(8,128)(2,1)S(1)}, u32[]{:S(2)}, u32[]{:S(2)}) collective-permute-start(bf16[384,256]{1,0:T(8,128)(2,1)S(1)} %bitcast.23), channel_id=1, source_target_pairs={{0,256},{256,0},{1,257},{257,1},{2,258},{258,2},{3,259},{259,3},{4... | collective-permute-start | bytes 589832 | tf_op jit(solution)/shard_map/ppermute | solution.py:26
  147.1 9.5 %collective-permute-start.5 = (bf16[384,512]{1,0:T(8,128)(2,1)S(1)}, bf16[384,512]{1,0:T(8,128)(2,1)S(1)}, u32[]{:S(2)}, u32[]{:S(2)}) collective-permute-start(bf16[384,512]{1,0:T(8,128)(2,1)S(1)} %maximum_select_fusion.3), channel_id=1, source_target_pairs={{0,8},{8,0},{1,9},{9,1},{2,10},{10,2},{3,11},{11,3},{4,12},{12,4},... | collective-permute-start | bytes 1179656 | tf_op jit(solution)/shard_map/ppermute | solution.py:26
  157.9 9.1 %all-to-all-start.5 = ((bf16[8,48,256]{2,1,0:T(8,128)(2,1)}), bf16[8,48,256]{2,1,0:T(8,128)(2,1)S(1)}, u32[]{:S(2)}, u32[]{:S(2)}) async-start(bf16[8,48,256]{2,1,0:T(8,128)(2,1)} %bitcast.6), calls=%async_computation.5 | async-start | bytes 393216 | tf_op jit(solution)/shard_map/all_to_all | solution.py:95
  167.9 9.8 %all-to-all-start.6 = ((bf16[8,48,512]{2,1,0:T(8,128)(2,1)}), bf16[8,48,512]{2,1,0:T(8,128)(2,1)S(1)}, u32[]{:S(2)}, u32[]{:S(2)}) async-start(bf16[8,48,512]{2,1,0:T(8,128)(2,1)} %broadcast_in_dim.45), calls=%async_computation.6 | async-start | bytes 786432 | tf_op jit(solution)/shard_map/all_to_all | solution.py:30

commit v2 on v1

v2 whole, which is shorter than its diff:
```python
import jax
import jax.numpy as jnp
from jax import lax
from jax.sharding import Mesh, PartitionSpec as P

YH, Z, CORE, X, YL = "yh", "z", "core", "x", "yl"
MP = (YH, Z, CORE)
DP = (X, YL)
bf16 = jnp.bfloat16
f32 = jnp.float32


def product(left, right):
    return jnp.dot(left, right, preferred_element_type=f32)


def over_rows(left, right):
    return lax.dot_general(left, right, (((0,), (0,)), ((), ())), preferred_element_type=f32)


def over_width(left, right):
    return lax.dot_general(left, right, (((1,), (1,)), ((), ())), preferred_element_type=f32)


def swap(value, axis):
    return lax.ppermute(value, axis, [(0, 1), (1, 0)])


def ordered(position, pair):
    return jnp.where(position == 0, pair, pair[::-1])


def local(table, ids, gate_weight, up_weight, down_weight, gate_probe, up_probe, down_probe):
    tokens = ids.shape[0]
    own_count, width = table.shape
    units = gate_weight.shape[1]
    scale = float(tokens) ** (-0.5)
    nz, ndp = lax.axis_size(Z), lax.axis_size(X) * lax.axis_size(YL)
    core, yh = lax.axis_index(CORE), lax.axis_index(YH)
    quarter, part = tokens // 4, tokens // 4 // ndp

    gates = jnp.stack([gate_weight, up_weight, gate_probe, up_probe])
    gates_x = swap(gates, CORE)
    down = jnp.stack([down_weight, down_probe])
    downs = jnp.stack([down, swap(down, YH)])
    downs = jnp.stack([downs, swap(downs, CORE)], axis=2)
    downs = downs.reshape(2, 2, 2 * units, width)

    rows = lax.all_to_all(jnp.broadcast_to(table[None], (nz,) + table.shape), Z, 0, 0)
    rows_x = swap(rows, YH)
    rows = rows.reshape(ndp, part, width)
    rows_x = rows_x.reshape(ndp, part, width)
    inputs = jnp.stack([rows, rows_x], axis=1).reshape(tokens // 2, width)
    inputs_x = swap(inputs, CORE)

    partials = jnp.concatenate(
        [product(inputs, w[k]).astype(bf16) for k in range(4) for w in (gates, gates_x)], axis=1
    )
    parts = lax.all_to_all(partials.reshape(ndp, 2 * part, 8 * units), DP, 0, 0)
    sums = jnp.sum(parts.astype(f32), axis=0)
    chip = 2 * units
    gate, up_value, tan_gate, tan_up = (sums[:, i * chip : (i + 1) * chip] for i in range(4))
    sigmoid_gate = jax.nn.sigmoid(gate)
    activated = gate * sigmoid_gate
    slope = sigmoid_gate * (1.0 + gate * (1.0 - sigmoid_gate))
    hidden = (activated * up_value).astype(bf16)
    tan_hidden = (slope * tan_gate * up_value + activated * tan_up).astype(bf16)

    both = jnp.concatenate(
        [hidden.reshape(2, part, chip), tan_hidden.reshape(2, part, chip)], axis=1
    )
    both = jnp.broadcast_to(ordered(yh, both)[:, None], (2, ndp, 2 * part, chip))
    both = lax.all_to_all(both.reshape(2 * ndp, 2 * part, chip), (YH,) + DP, 0, 0)
    both = ordered(yh, both.reshape(2, ndp, 2, part, chip))
    hidden = both[:, :, 0].reshape(2, quarter, chip)
    tan_hidden = both[:, :, 1].reshape(2, quarter, chip)

    partial_out = sum(
        product(tan_hidden[i], downs[i, 0]) + product(hidden[i], downs[i, 1]) for i in range(2)
    ).astype(bf16)
    side = 4
    blocks = partial_out.reshape(side, quarter // side, side, width // side).transpose(0, 2, 1, 3)
    parts = lax.all_to_all(blocks.reshape(nz, quarter // side, width // side), Z, 0, 0)
    block = jnp.sum(parts.astype(f32), axis=0).astype(bf16)
    out = lax.all_to_all(jnp.broadcast_to(block[None], (nz,) + block.shape), Z, 0, 0)
    out = out.reshape(side, side, quarter // side, width // side).transpose(0, 2, 1, 3)
    out = out.reshape(quarter, width)

    cot = jnp.stack([over_width(out, downs[i, 0]).astype(bf16) for i in range(2)])
    cot = ordered(yh, cot).reshape(2, ndp, part, 2, units).transpose(0, 1, 3, 2, 4)
    cot = lax.all_to_all(cot.reshape(2 * ndp, 2 * part, units), (YH,) + DP, 0, 0)
    cot = jnp.sum(cot.reshape(2, ndp, 2 * part, units).astype(f32), axis=1) * scale
    cot = ordered(yh, cot).reshape(2, 2, part, units).transpose(0, 2, 1, 3).reshape(2 * part, chip)
    cot_gate = (cot * up_value * slope).astype(bf16)
    cot_up = (cot * activated).astype(bf16)
    both = jnp.stack(
        [
            jnp.concatenate([cot_gate[:, :units], cot_up[:, :units]], axis=1),
            jnp.concatenate([cot_gate[:, units:], cot_up[:, units:]], axis=1),
        ]
    )
    both = jnp.broadcast_to(ordered(core, both)[:, None], (2, ndp, 2 * part, chip))
    both = lax.all_to_all(both.reshape(2 * ndp, 2 * part, chip), (CORE,) + DP, 0, 0)
    both = ordered(core, both.reshape(2, tokens // 2, chip)).reshape(tokens, chip)
    ggn = over_rows(jnp.concatenate([inputs, inputs_x]), both).astype(bf16)

    hidden = jnp.concatenate([hidden[0], swap(hidden[1], YH)])
    hidden = jnp.concatenate([hidden[:, :units], swap(hidden[:, units:], CORE)])
    out = jnp.concatenate([out, swap(out, YH)])
    out = jnp.concatenate([out, swap(out, CORE)])
    ggn_down = (over_rows(hidden, out) * scale).astype(bf16)
    wanted = lax.dynamic_slice_in_dim(ids, lax.axis_index(MP) * own_count, own_count, 0)
    holder, row = wanted // own_count, wanted % own_count
    place = (holder % 2) ^ core
    place = 2 * place + ((holder // (2 * nz)) ^ yh)
    place = nz * place + (holder // 2) % nz
    tangent_out = jnp.take(out, place * own_count + row, axis=0)
    return tangent_out, ggn[:, :units], ggn[:, units:], ggn_down


def solution(mesh):
    devices = mesh.devices.reshape(2, 16, 2, 4, 2)
    fine = Mesh(devices, (YH, Z, CORE, X, YL))
    in_specs = (
        P(MP, DP),
        P(),
        P(DP, MP),
        P(DP, MP),
        P(MP, DP),
        P(DP, MP),
        P(DP, MP),
        P(MP, DP),
    )
    out_specs = (P(MP, DP), P(DP, MP), P(DP, MP), P(MP, DP))
    return jax.shard_map(local, mesh=fine, in_specs=in_specs, out_specs=out_specs, check_vma=False)
```

time: 181 us -> 200 us (1.10)
  blocking collectives: 95.5 us -> 23.6 us
  starting transfers between devices: 42.6 us -> 79.1 us
  waiting for transfers between devices: 26.4 us -> 50.4 us
  matrix products: 6.1 us -> 24.1 us
  other arithmetic: 1.56 us -> 13.3 us
    all_to_all x5 -> x1, blocking collectives: 95.5 us -> 23.6 us  [local(): lax.all_to_all(blocks.reshape(nz, quarter // side, width // side), Z, 0, 0)]
    all_to_all x2 -> x6, starting transfers between devices: 6.85 us -> 40.1 us  [the longest x1 10.4 us: local(): lax.all_to_all(both.reshape(2 * ndp, 2 * part, chip), (CORE,) + DP, 0, 0)]
    all_to_all x2 -> x6, waiting for transfers between devices: 10.1 us -> 34.8 us  [the longest x1 12.7 us: local(): parts = lax.all_to_all(partials.reshape(ndp, 2 * part, 8 * units), DP, 0, 0)]
    dot_general x6 -> x12, matrix products: 2.94 us -> 17.8 us  [product(): return jnp.dot(left, right, preferred_element_type=f32)]
    another operation x0 -> x9, other arithmetic: none -> 11.3 us  [the longest x2 6.79 us: local(): downs = jnp.stack([downs, swap(downs, CORE)], axis=2)]
    ppermute x6 -> x9, starting transfers between devices: 35.7 us -> 39 us  [swap(): return lax.ppermute(value, axis, [(0, 1), (1, 0)])]
    dot_general x1 -> x2, matrix products: 1.09 us -> 3.36 us  [over_width(): lax.dot_general(left, right, (((1,), (1,)), ((), ())), preferred_element_...]
    ppermute x6 -> x9, waiting for transfers between devices: 16.3 us -> 15.6 us  [swap(): return lax.ppermute(value, axis, [(0, 1), (1, 0)])]
  transfers between devices with their start and end apart: 8 -> 15, of which waited for: 8 -> 7; matrix products, arithmetic and copies ran while one was open for 1% -> 16% of each run, Pallas kernels for 0% -> 0%
where the time goes in v2:
time: 200 us; the launch traced here: 198 us
  starting transfers between devices  79.1 us (40%)
  waiting for transfers between devices  50.4 us (25%)
  matrix products  24.1 us (12%)
  blocking collectives  23.6 us (12%)
  other arithmetic  13.3 us (7%)
  local copies, waits for them, and re-layouts  6.51 us (3%)
    ppermute x9, starting transfers between devices, swap(): return lax.ppermute(value, axis, [(0, 1), (1, 0)])  39 us
    all_to_all x1, blocking collectives, local(): lax.all_to_all(blocks.reshape(nz, quarter // side, width // side), Z, 0, 0)  23.6 us
    dot_general x12, matrix products, product(): return jnp.dot(left, right, preferred_element_type=f32)  17.8 us
    ppermute x9, waiting for transfers between devices, swap(): return lax.ppermute(value, axis, [(0, 1), (1, 0)])  15.6 us
    all_to_all x1, waiting for transfers between devices, local(): parts = lax.all_to_all(partials.reshape(ndp, 2 * part, 8 * units), DP, 0, 0)  12.7 us
    all_to_all x1, starting transfers between devices, local(): lax.all_to_all(both.reshape(2 * ndp, 2 * part, chip), (CORE,) + DP, 0, 0)  10.4 us
    all_to_all x1, starting transfers between devices, local(): lax.all_to_all(jnp.broadcast_to(table[None], (nz,) + table.shape), Z, 0, 0)  9.54 us
    all_to_all x1, waiting for transfers between devices, local(): lax.all_to_all(jnp.broadcast_to(table[None], (nz,) + table.shape), Z, 0, 0)  8.35 us
  transfers between devices with their start and end apart: 15, of which 7 were waited for; matrix products, arithmetic and copies ran while one was open for 16% of the time, Pallas kernels for 0%

profile of v2, /device:TPU:1, one launch (start us, length us, event | category | flops | bytes accessed | tf_op | source)
XLA Modules:
  0.0 198.3 jit_solution(14271156837125038398)
XLA Ops:
  0.7 3.3 %pad_maximum_fusion.1 = bf16[4,1024,256]{2,1,0:T(8,128)(2,1)} fusion(bf16[1,1024,256]{2,1,0:T(8,128)(2,1)} %bitcast.113, bf16[1,1024,256]{2,1,0:T(8,128)(2,1)} %bitcast.112, bf16[1,1024,256]{2,1,0:T(8,128)(2,1)} %bitcast.111, bf16[1,1024,256]{2,1,0:T(8,128)(2,1)} %bitcast.110), kind=kLoop, calls=%fused_computation.2 | loop fusion | flops 3145728 | bytes 4194304 | tf_op jit(solution)/shard_map/stack | solution.py:42
  3.9 8.8 %collective-permute-start.1 = (bf16[4,1024,256]{2,1,0:T(8,128)(2,1)}, bf16[4,1024,256]{2,1,0:T(8,128)(2,1)}, u32[]{:S(2)}, u32[]{:S(2)}) collective-permute-start(bf16[4,1024,256]{2,1,0:T(8,128)(2,1)} %pad_maximum_fusion.1), channel_id=1, source_target_pairs={{0,8},{8,0},{1,9},{9,1},{2,10},{10,2},{3,11},{11,3},{4,12},{12,4},... | collective-permute-start | bytes 6291464 | tf_op jit(solution)/shard_map/ppermute | solution.py:26
  13.5 9.5 %all-to-all-start = ((bf16[16,6,1024]{2,1,0:T(8,128)(2,1)}), bf16[16,6,1024]{2,1,0:T(8,128)(2,1)S(1)}, u32[]{:S(2)}, u32[]{:S(2)}) async-start(bf16[16,6,1024]{2,1,0:T(8,128)(2,1)} %broadcast_in_dim.18), calls=%async_computation | async-start | bytes 524288 | tf_op jit(solution)/shard_map/all_to_all | solution.py:49
  24.1 4.9 %collective-permute-start.2 = (bf16[2,256,1024]{2,1,0:T(8,128)(2,1)}, bf16[2,256,1024]{2,1,0:T(8,128)(2,1)}, u32[]{:S(2)}, u32[]{:S(2)}) collective-permute-start(bf16[2,256,1024]{2,1,0:T(8,128)(2,1)} %get-tuple-element.11), channel_id=1, source_target_pairs={{0,256},{256,0},{1,257},{257,1},{2,258},{258,2},{3,259},{259,3},{4... | collective-permute-start | bytes 3145736 | tf_op jit(solution)/shard_map/ppermute | solution.py:26
  29.1 8.4 %all-to-all-done = bf16[16,6,1024]{2,1,0:T(8,128)(2,1)S(1)} async-done(((bf16[16,6,1024]{2,1,0:T(8,128)(2,1)}), bf16[16,6,1024]{2,1,0:T(8,128)(2,1)S(1)}, u32[]{:S(2)}, u32[]{:S(2)}) %all-to-all-start) | async-done | bytes 196640 | tf_op jit(solution)/shard_map/all_to_all | solution.py:49
  37.4 4.8 %collective-permute-start = (bf16[16,6,1024]{2,1,0:T(8,128)(2,1)S(1)}, bf16[16,6,1024]{2,1,0:T(8,128)(2,1)S(1)}, u32[]{:S(2)}, u32[]{:S(2)}) collective-permute-start(bf16[16,6,1024]{2,1,0:T(8,128)(2,1)S(1)} %all-to-all-done), channel_id=1, source_target_pairs={{0,256},{256,0},{1,257},{257,1},{2,258},{258,2},{3,259},{259,3},{4... | collective-permute-start | bytes 589832 | tf_op jit(solution)/shard_map/ppermute | solution.py:26
  42.3 15.6 %collective-permute-done = bf16[16,6,1024]{2,1,0:T(8,128)(2,1)S(1)} collective-permute-done((bf16[16,6,1024]{2,1,0:T(8,128)(2,1)S(1)}, bf16[16,6,1024]{2,1,0:T(8,128)(2,1)S(1)}, u32[]{:S(2)}, u32[]{:S(2)}) %collective-permute-start) | collective-permute-done | bytes 196640 | tf_op jit(solution)/shard_map/ppermute | solution.py:26
  59.2 2.9 %fusion.34 = (bf16[2,2,1,256,1024]{4,3,2,1,0:T(8,128)(2,1)S(1)}, bf16[2,2,256,1024]{3,2,1,0:T(8,128)(2,1)}) fusion(bf16[1,2,256,1024]{3,2,1,0:T(8,128)(2,1)} %bitcast.14, bf16[1,2,256,1024]{3,2,1,0:T(8,128)(2,1)S(1)} %get-tuple-element.10), kind=kLoop, calls=%fused_computation.105 | loop fusion | flops 1048576 | bytes 6291456 | tf_op jit(solution)/shard_map/stack | solution.py:46
  62.1 3.1 %collective-permute-start.3 = (bf16[2,2,256,1024]{3,2,1,0:T(8,128)(2,1)}, bf16[2,2,256,1024]{3,2,1,0:T(8,128)(2,1)}, u32[]{:S(2)}, u32[]{:S(2)}) collective-permute-start(bf16[2,2,256,1024]{3,2,1,0:T(8,128)(2,1)} %get-tuple-element.7), channel_id=1, source_target_pairs={{0,8},{8,0},{1,9},{9,1},{2,10},{10,2},{3,11},{11,3},{4,12},{12,4},... | collective-permute-start | bytes 6291464 | tf_op jit(solution)/shard_map/ppermute | solution.py:26
  65.2 2.0 fusion.9
  68.1 2.0 fusion.7
  71.0 2.0 fusion.5
  73.9 2.0 %fusion.3 = bf16[192,2048]{1,0:T(8,128)(2,1)} fusion(bf16[192,2048]{1,0:T(8,128)(2,1)} %fusion.4, bf16[192,1024]{1,0:T(8,128)(2,1)S(1)} %reshape.82, bf16[4,1024,256]{2,1,0:T(8,128)(2,1)} %collective-permute-done.1), kind=kOutput, calls=%fused_computation.15 | convolution fusion | flops 100712448 | bytes 1015808 | tf_op jit(solution)/shard_map/dot_general | solution.py:14
  75.9 5.0 %all-to-all-start.1 = ((bf16[8,24,2048]{2,1,0:T(8,128)(2,1)}), bf16[8,24,2048]{2,1,0:T(8,128)(2,1)S(1)}, u32[]{:S(2)}, u32[]{:S(2)}) async-start(bf16[8,24,2048]{2,1,0:T(8,128)(2,1)} %bitcast.8), calls=%async_computation.1 | async-start | bytes 1572864 | tf_op jit(solution)/shard_map/all_to_all | solution.py:59
  81.0 12.7 %all-to-all-done.1 = bf16[8,24,2048]{2,1,0:T(8,128)(2,1)S(1)} async-done(((bf16[8,24,2048]{2,1,0:T(8,128)(2,1)}), bf16[8,24,2048]{2,1,0:T(8,128)(2,1)S(1)}, u32[]{:S(2)}, u32[]{:S(2)}) %all-to-all-start.1) | async-done | bytes 786464 | tf_op jit(solution)/shard_map/all_to_all | solution.py:59
  94.7 4.2 %all-to-all-start.2 = ((bf16[16,24,512]{2,1,0:T(8,128)(2,1)}), bf16[16,24,512]{2,1,0:T(8,128)(2,1)S(1)}, u32[]{:S(2)}, u32[]{:S(2)}) async-start(bf16[16,24,512]{2,1,0:T(8,128)(2,1)} %bitcast.9), calls=%async_computation.2 | async-start | bytes 786432 | tf_op jit(solution)/shard_map/all_to_all | solution.py:73
  98.9 3.9 %pad_maximum_fusion = bf16[2,2,2,256,1024]{4,3,2,1,0:T(8,128)(2,1)} fusion(bf16[2,2,1,256,1024]{4,3,2,1,0:T(8,128)(2,1)} %bitcast.17, bf16[2,2,1,256,1024]{4,3,2,1,0:T(8,128)(2,1)S(1)} %get-tuple-element.6), kind=kLoop, calls=%fused_computation.1 | loop fusion | flops 2097152 | bytes 8388608 | tf_op jit(solution)/shard_map/stack | solution.py:46
  102.9 4.0 %all-to-all-done.2 = bf16[16,24,512]{2,1,0:T(8,128)(2,1)S(1)} async-done(((bf16[16,24,512]{2,1,0:T(8,128)(2,1)}), bf16[16,24,512]{2,1,0:T(8,128)(2,1)S(1)}, u32[]{:S(2)}, u32[]{:S(2)}) %all-to-all-start.2) | async-done | bytes 393248 | tf_op jit(solution)/shard_map/all_to_all | solution.py:73
  113.8 23.6 %all_to_all.35 = bf16[16,24,256]{2,1,0:T(8,128)(2,1)S(1)} all-to-all(bf16[16,24,256]{2,1,0:T(8,128)(2,1)S(1)} %bitcast.122), channel_id=1, replica_groups=mesh['yh'=2,'z'=16,'core'=2,'x'=4,'yl'=2] {'z'}, dimensions={0} | all-to-all | bytes 393216 | tf_op jit(solution)/shard_map/all_to_all | solution.py:83
  138.2 7.0 %all-to-all-start.4 = ((bf16[16,24,256]{2,1,0:T(8,128)(2,1)}), bf16[16,24,256]{2,1,0:T(8,128)(2,1)S(1)}, u32[]{:S(2)}, u32[]{:S(2)}) async-start(bf16[16,24,256]{2,1,0:T(8,128)(2,1)} %broadcast_in_dim.39), calls=%async_computation.4 | async-start | bytes 393216 | tf_op jit(solution)/shard_map/all_to_all | solution.py:85
  146.0 4.9 %collective-permute-start.6 = (bf16[192,1024]{1,0:T(8,128)(2,1)S(1)}, bf16[192,1024]{1,0:T(8,128)(2,1)}, u32[]{:S(2)}, u32[]{:S(2)}) collective-permute-start(bf16[192,1024]{1,0:T(8,128)(2,1)S(1)} %reshape.82), channel_id=1, source_target_pairs={{0,8},{8,0},{1,9},{9,1},{2,10},{10,2},{3,11},{11,3},{4,12},{12,4},... | collective-permute-start | bytes 1179656 | tf_op jit(solution)/shard_map/ppermute | solution.py:26
  150.9 3.3 %collective-permute-start.7 = (bf16[96,512]{1,0:T(8,128)(2,1)S(1)}, bf16[96,512]{1,0:T(8,128)(2,1)S(1)}, u32[]{:S(2)}, u32[]{:S(2)}) collective-permute-start(bf16[96,512]{1,0:T(8,128)(2,1)S(1)} %squeeze.50), channel_id=1, source_target_pairs={{0,256},{256,0},{1,257},{257,1},{2,258},{258,2},{3,259},{259,3},{4... | collective-permute-start | bytes 294920 | tf_op jit(solution)/shard_map/ppermute | solution.py:26
  154.2 3.3 %all-to-all-done.4 = bf16[16,24,256]{2,1,0:T(8,128)(2,1)S(1)} async-done(((bf16[16,24,256]{2,1,0:T(8,128)(2,1)}), bf16[16,24,256]{2,1,0:T(8,128)(2,1)S(1)}, u32[]{:S(2)}, u32[]{:S(2)}) %all-to-all-start.4) | async-done | bytes 196640 | tf_op jit(solution)/shard_map/all_to_all | solution.py:85
  157.6 1.7 fusion.11
  161.9 3.9 %all-to-all-start.5 = ((bf16[16,24,256]{2,1,0:T(8,128)(2,1)}), bf16[16,24,256]{2,1,0:T(8,128)(2,1)S(1)}, u32[]{:S(2)}, u32[]{:S(2)}) async-start(bf16[16,24,256]{2,1,0:T(8,128)(2,1)} %copy.55), calls=%async_computation.5 | async-start | bytes 393216 | tf_op jit(solution)/shard_map/all_to_all | solution.py:91
  165.9 4.8 %collective-permute-start.4 = (bf16[96,1024]{1,0:T(8,128)(2,1)S(1)}, bf16[96,1024]{1,0:T(8,128)(2,1)S(1)}, u32[]{:S(2)}, u32[]{:S(2)}) collective-permute-start(bf16[96,1024]{1,0:T(8,128)(2,1)S(1)} %bitcast.116), channel_id=1, source_target_pairs={{0,256},{256,0},{1,257},{257,1},{2,258},{258,2},{3,259},{259,3},{4... | collective-permute-start | bytes 589832 | tf_op jit(solution)/shard_map/ppermute | solution.py:26
  170.7 2.2 %all-to-all-done.5 = bf16[16,24,256]{2,1,0:T(8,128)(2,1)S(1)} async-done(((bf16[16,24,256]{2,1,0:T(8,128)(2,1)}), bf16[16,24,256]{2,1,0:T(8,128)(2,1)S(1)}, u32[]{:S(2)}, u32[]{:S(2)}) %all-to-all-start.5) | async-done | bytes 196640 | tf_op jit(solution)/shard_map/all_to_all | solution.py:91
  173.9 10.4 %all-to-all-start.6 = ((bf16[16,24,512]{2,1,0:T(8,128)(2,1)}), bf16[16,24,512]{2,1,0:T(8,128)(2,1)S(1)}, u32[]{:S(2)}, u32[]{:S(2)}) async-start(bf16[16,24,512]{2,1,0:T(8,128)(2,1)} %bitcast.36), calls=%async_computation.6 | async-start | bytes 786432 | tf_op jit(solution)/shard_map/all_to_all | solution.py:103
  184.4 2.1 %collective-permute-start.8 = (bf16[192,256]{1,0:T(8,128)(2,1)S(1)}, bf16[192,256]{1,0:T(8,128)(2,1)S(1)}, u32[]{:S(2)}, u32[]{:S(2)}) collective-permute-start(bf16[192,256]{1,0:T(8,128)(2,1)S(1)} %get-tuple-element.19), channel_id=1, source_target_pairs={{0,8},{8,0},{1,9},{9,1},{2,10},{10,2},{3,11},{11,3},{4,12},{12,4},... | collective-permute-start | bytes 294920 | tf_op jit(solution)/shard_map/ppermute | solution.py:26
  186.5 2.2 %collective-permute-start.5 = (bf16[192,1024]{1,0:T(8,128)(2,1)S(1)}, bf16[192,1024]{1,0:T(8,128)(2,1)S(1)}, u32[]{:S(2)}, u32[]{:S(2)}) collective-permute-start(bf16[192,1024]{1,0:T(8,128)(2,1)S(1)} %pad_maximum_fusion.5), channel_id=1, source_target_pairs={{0,8},{8,0},{1,9},{9,1},{2,10},{10,2},{3,11},{11,3},{4,12},{12,4},... | collective-permute-start | bytes 1179656 | tf_op jit(solution)/shard_map/ppermute | solution.py:26
  188.8 4.1 %all-to-all-done.6 = bf16[16,24,512]{2,1,0:T(8,128)(2,1)S(1)} async-done(((bf16[16,24,512]{2,1,0:T(8,128)(2,1)}), bf16[16,24,512]{2,1,0:T(8,128)(2,1)S(1)}, u32[]{:S(2)}, u32[]{:S(2)}) %all-to-all-start.6) | async-done | bytes 393248 | tf_op jit(solution)/shard_map/all_to_all | solution.py:103
  193.0 1.7 convolution_convert_fusion
  (93 shorter events, 22.6 us)
Async XLA Ops:
  0.6 12.1 %copy-start.6 = (bf16[6,1024]{1,0:T(8,128)(2,1)S(1)}, bf16[6,1024]{1,0:T(8,128)(2,1)}, u32[]{:S(2)}) copy-start(bf16[6,1024]{1,0:T(8,128)(2,1)} %param.8) | copy-start | bytes 36868
  0.6 22.4 %copy-start.4 = (bf16[256,1024]{1,0:T(8,128)(2,1)S(1)}, bf16[256,1024]{1,0:T(8,128)(2,1)}, u32[]{:S(2)}) copy-start(bf16[256,1024]{1,0:T(8,128)(2,1)} %param.15) | copy-start | bytes 1572868
  0.7 22.4 %copy-start.5 = (bf16[256,1024]{1,0:T(8,128)(2,1)S(1)}, bf16[256,1024]{1,0:T(8,128)(2,1)}, u32[]{:S(2)}) copy-start(bf16[256,1024]{1,0:T(8,128)(2,1)} %param.12) | copy-start | bytes 1572868
  3.9 61.3 %collective-permute-start.1 = (bf16[4,1024,256]{2,1,0:T(8,128)(2,1)}, bf16[4,1024,256]{2,1,0:T(8,128)(2,1)}, u32[]{:S(2)}, u32[]{:S(2)}) collective-permute-start(bf16[4,1024,256]{2,1,0:T(8,128)(2,1)} %pad_maximum_fusion.1), channel_id=1, source_target_pairs={{0,8},{8,0},{1,9},{9,1},{2,10},{10,2},{3,11},{11,3},{4,12},{12,4},... | collective-permute-start | bytes 6291464 | tf_op jit(solution)/shard_map/ppermute | solution.py:26
  13.5 24.0 %all-to-all-start = ((bf16[16,6,1024]{2,1,0:T(8,128)(2,1)}), bf16[16,6,1024]{2,1,0:T(8,128)(2,1)S(1)}, u32[]{:S(2)}, u32[]{:S(2)}) async-start(bf16[16,6,1024]{2,1,0:T(8,128)(2,1)} %broadcast_in_dim.18), calls=%async_computation | async-start | bytes 524288 | tf_op jit(solution)/shard_map/all_to_all | solution.py:49
  24.1 34.1 %copy-start = (bf16[1024,256]{1,0:T(8,128)(2,1)S(1)}, bf16[1024,256]{1,0:T(8,128)(2,1)}, u32[]{:S(2)}) copy-start(bf16[1024,256]{1,0:T(8,128)(2,1)} %param.10) | copy-start | bytes 1572868
  24.1 35.1 %collective-permute-start.2 = (bf16[2,256,1024]{2,1,0:T(8,128)(2,1)}, bf16[2,256,1024]{2,1,0:T(8,128)(2,1)}, u32[]{:S(2)}, u32[]{:S(2)}) collective-permute-start(bf16[2,256,1024]{2,1,0:T(8,128)(2,1)} %get-tuple-element.11), channel_id=1, source_target_pairs={{0,256},{256,0},{1,257},{257,1},{2,258},{258,2},{3,259},{259,3},{4... | collective-permute-start | bytes 3145736 | tf_op jit(solution)/shard_map/ppermute | solution.py:26
  37.4 20.5 %collective-permute-start = (bf16[16,6,1024]{2,1,0:T(8,128)(2,1)S(1)}, bf16[16,6,1024]{2,1,0:T(8,128)(2,1)S(1)}, u32[]{:S(2)}, u32[]{:S(2)}) collective-permute-start(bf16[16,6,1024]{2,1,0:T(8,128)(2,1)S(1)} %all-to-all-done), channel_id=1, source_target_pairs={{0,256},{256,0},{1,257},{257,1},{2,258},{258,2},{3,259},{259,3},{4... | collective-permute-start | bytes 589832 | tf_op jit(solution)/shard_map/ppermute | solution.py:26
  59.2 8.0 %copy-start.1 = (bf16[1024,256]{1,0:T(8,128)(2,1)S(1)}, bf16[1024,256]{1,0:T(8,128)(2,1)}, u32[]{:S(2)}) copy-start(bf16[1024,256]{1,0:T(8,128)(2,1)} %param.11) | copy-start | bytes 1572868
  62.1 8.0 %copy-start.2 = (bf16[1024,256]{1,0:T(8,128)(2,1)S(1)}, bf16[1024,256]{1,0:T(8,128)(2,1)}, u32[]{:S(2)}) copy-start(bf16[1024,256]{1,0:T(8,128)(2,1)} %param.13) | copy-start | bytes 1572868
  62.1 36.9 %collective-permute-start.3 = (bf16[2,2,256,1024]{3,2,1,0:T(8,128)(2,1)}, bf16[2,2,256,1024]{3,2,1,0:T(8,128)(2,1)}, u32[]{:S(2)}, u32[]{:S(2)}) collective-permute-start(bf16[2,2,256,1024]{3,2,1,0:T(8,128)(2,1)} %get-tuple-element.7), channel_id=1, source_target_pairs={{0,8},{8,0},{1,9},{9,1},{2,10},{10,2},{3,11},{11,3},{4,12},{12,4},... | collective-permute-start | bytes 6291464 | tf_op jit(solution)/shard_map/ppermute | solution.py:26
  67.2 5.8 %copy-start.3 = (bf16[1024,256]{1,0:T(8,128)(2,1)S(1)}, bf16[1024,256]{1,0:T(8,128)(2,1)}, u32[]{:S(2)}) copy-start(bf16[1024,256]{1,0:T(8,128)(2,1)} %param.14) | copy-start | bytes 1572868
  75.9 17.8 %all-to-all-start.1 = ((bf16[8,24,2048]{2,1,0:T(8,128)(2,1)}), bf16[8,24,2048]{2,1,0:T(8,128)(2,1)S(1)}, u32[]{:S(2)}, u32[]{:S(2)}) async-start(bf16[8,24,2048]{2,1,0:T(8,128)(2,1)} %bitcast.8), calls=%async_computation.1 | async-start | bytes 1572864 | tf_op jit(solution)/shard_map/all_to_all | solution.py:59
  94.7 12.2 %all-to-all-start.2 = ((bf16[16,24,512]{2,1,0:T(8,128)(2,1)}), bf16[16,24,512]{2,1,0:T(8,128)(2,1)S(1)}, u32[]{:S(2)}, u32[]{:S(2)}) async-start(bf16[16,24,512]{2,1,0:T(8,128)(2,1)} %bitcast.9), calls=%async_computation.2 | async-start | bytes 786432 | tf_op jit(solution)/shard_map/all_to_all | solution.py:73
  138.2 19.3 %all-to-all-start.4 = ((bf16[16,24,256]{2,1,0:T(8,128)(2,1)}), bf16[16,24,256]{2,1,0:T(8,128)(2,1)S(1)}, u32[]{:S(2)}, u32[]{:S(2)}) async-start(bf16[16,24,256]{2,1,0:T(8,128)(2,1)} %broadcast_in_dim.39), calls=%async_computation.4 | async-start | bytes 393216 | tf_op jit(solution)/shard_map/all_to_all | solution.py:85
  146.0 47.0 %collective-permute-start.6 = (bf16[192,1024]{1,0:T(8,128)(2,1)S(1)}, bf16[192,1024]{1,0:T(8,128)(2,1)}, u32[]{:S(2)}, u32[]{:S(2)}) collective-permute-start(bf16[192,1024]{1,0:T(8,128)(2,1)S(1)} %reshape.82), channel_id=1, source_target_pairs={{0,8},{8,0},{1,9},{9,1},{2,10},{10,2},{3,11},{11,3},{4,12},{12,4},... | collective-permute-start | bytes 1179656 | tf_op jit(solution)/shard_map/ppermute | solution.py:26
  150.9 15.0 %collective-permute-start.7 = (bf16[96,512]{1,0:T(8,128)(2,1)S(1)}, bf16[96,512]{1,0:T(8,128)(2,1)S(1)}, u32[]{:S(2)}, u32[]{:S(2)}) collective-permute-start(bf16[96,512]{1,0:T(8,128)(2,1)S(1)} %squeeze.50), channel_id=1, source_target_pairs={{0,256},{256,0},{1,257},{257,1},{2,258},{258,2},{3,259},{259,3},{4... | collective-permute-start | bytes 294920 | tf_op jit(solution)/shard_map/ppermute | solution.py:26
  161.9 11.0 %all-to-all-start.5 = ((bf16[16,24,256]{2,1,0:T(8,128)(2,1)}), bf16[16,24,256]{2,1,0:T(8,128)(2,1)S(1)}, u32[]{:S(2)}, u32[]{:S(2)}) async-start(bf16[16,24,256]{2,1,0:T(8,128)(2,1)} %copy.55), calls=%async_computation.5 | async-start | bytes 393216 | tf_op jit(solution)/shard_map/all_to_all | solution.py:91
  165.9 20.6 %collective-permute-start.4 = (bf16[96,1024]{1,0:T(8,128)(2,1)S(1)}, bf16[96,1024]{1,0:T(8,128)(2,1)S(1)}, u32[]{:S(2)}, u32[]{:S(2)}) collective-permute-start(bf16[96,1024]{1,0:T(8,128)(2,1)S(1)} %bitcast.116), channel_id=1, source_target_pairs={{0,256},{256,0},{1,257},{257,1},{2,258},{258,2},{3,259},{259,3},{4... | collective-permute-start | bytes 589832 | tf_op jit(solution)/shard_map/ppermute | solution.py:26
  173.9 19.0 %all-to-all-start.6 = ((bf16[16,24,512]{2,1,0:T(8,128)(2,1)}), bf16[16,24,512]{2,1,0:T(8,128)(2,1)S(1)}, u32[]{:S(2)}, u32[]{:S(2)}) async-start(bf16[16,24,512]{2,1,0:T(8,128)(2,1)} %bitcast.36), calls=%async_computation.6 | async-start | bytes 786432 | tf_op jit(solution)/shard_map/all_to_all | solution.py:103
  184.4 12.7 %collective-permute-start.8 = (bf16[192,256]{1,0:T(8,128)(2,1)S(1)}, bf16[192,256]{1,0:T(8,128)(2,1)S(1)}, u32[]{:S(2)}, u32[]{:S(2)}) collective-permute-start(bf16[192,256]{1,0:T(8,128)(2,1)S(1)} %get-tuple-element.19), channel_id=1, source_target_pairs={{0,8},{8,0},{1,9},{9,1},{2,10},{10,2},{3,11},{11,3},{4,12},{12,4},... | collective-permute-start | bytes 294920 | tf_op jit(solution)/shard_map/ppermute | solution.py:26
  186.5 9.2 %collective-permute-start.5 = (bf16[192,1024]{1,0:T(8,128)(2,1)S(1)}, bf16[192,1024]{1,0:T(8,128)(2,1)S(1)}, u32[]{:S(2)}, u32[]{:S(2)}) collective-permute-start(bf16[192,1024]{1,0:T(8,128)(2,1)S(1)} %pad_maximum_fusion.5), channel_id=1, source_target_pairs={{0,8},{8,0},{1,9},{9,1},{2,10},{10,2},{3,11},{11,3},{4,12},{12,4},... | collective-permute-start | bytes 1179656 | tf_op jit(solution)/shard_map/ppermute | solution.py:26

commit v3 on v1

v3 whole, which is shorter than its diff:
```python
import functools

import jax
import jax.numpy as jnp
import numpy as np
from jax import lax
from jax.experimental import pallas as pl
from jax.experimental.pallas import tpu as pltpu
from jax.sharding import Mesh, PartitionSpec as P

YH, Z, CORE, X, YL = "yh", "z", "core", "x", "yl"
MP = (YH, Z, CORE)
DP = (X, YL)
NZ, NDP = 16, 8
bf16 = jnp.bfloat16
f32 = jnp.float32
MIB = 1 << 20
VMEM = pl.BlockSpec(memory_space=pltpu.VMEM)
ANY = pl.BlockSpec(memory_space=pl.ANY)


def swap(value, axis):
    return lax.ppermute(value, axis, [(0, 1), (1, 0)])


def together(*values):
    return lax.optimization_barrier(values)


def product(left, right):
    return jnp.dot(left, right, preferred_element_type=f32)


def over_rows(left, right):
    return lax.dot_general(left, right, (((0,), (0,)), ((), ())), preferred_element_type=f32)


def over_width(left, right):
    return lax.dot_general(left, right, (((1,), (1,)), ((), ())), preferred_element_type=f32)


def moved(table, values):
    return product(table, values).astype(bf16)


def one_hot(sources, count):
    table = np.zeros((len(sources), count), np.float32)
    for row, source in enumerate(sources):
        if source is not None:
            table[row, source] = 1.0
    return jnp.asarray(table, bf16)


def tables(part):
    d8, o2, h2, k2, js = range(NDP), range(2), range(2), range(2), range(part)
    pad = lambda s: s // 6 * 8 + s % 6
    return dict(
        pick=one_hot([o * 128 + pad(d * part + j) for d in d8 for o in o2 for j in js], 256),
        fan=one_hot(
            [h * 192 + (d * 2 + o) * part + j for d in d8 for o in o2 for h in h2 for j in js], 384
        ),
        kinds=one_hot(
            [d * 48 + (k * 2 + h) * part + j for k in k2 for h in h2 for d in d8 for j in js], 384
        ),
        low=one_hot([None if h else d * part + j for d in d8 for h in h2 for j in js], 96),
        high=one_hot([d * part + j if h else None for d in d8 for h in h2 for j in js], 96),
        cores=one_hot(
            [((k * 2 + o) * 2 + h) * part + j for h in h2 for k in k2 for o in o2 for j in js], 96
        ),
        last=one_hot(
            [d * 48 + (k * 2 + o) * part + j for k in k2 for d in d8 for o in o2 for j in js], 384
        ),
    )


def rows_at(position, count):
    return pl.ds(pl.multiple_of(position * count, count), count)


def fetch(refs, slots, sems):
    copies = [pltpu.make_async_copy(r, slots.at[i], sems.at[i]) for i, r in enumerate(refs)]
    for copy in copies:
        copy.start()
    return copies


def gates_kernel(own, other, pick, fan, *rest):
    weights, (inputs, out, slots, sems) = rest[:8], rest[8:]
    copies = fetch(weights, slots, sems)
    inputs[...] = moved(pick[...], jnp.concatenate([own[...], other[...]], axis=0))
    units = slots.shape[2]
    for k in range(4):
        copies[k].wait()
        mine = product(inputs[...], slots[k]).astype(bf16)
        copies[4 + k].wait()
        theirs = product(inputs[...], slots[4 + k]).astype(bf16)
        out[:, k * units : (k + 1) * units] = moved(
            fan[...], jnp.concatenate([mine, theirs], axis=0)
        )


def hidden_kernel(scale, parts, out, coef_gate, coef_up):
    yh = lax.axis_index(YH)
    sums = parts[0:48].astype(f32)
    for d in range(1, NDP):
        sums = sums + parts[48 * d : 48 * d + 48].astype(f32)
    units = sums.shape[1] // 4
    gate, up_value, tan_gate, tan_up = (sums[:, i * units : (i + 1) * units] for i in range(4))
    sigmoid_gate = 1.0 / (1.0 + jnp.exp(-gate))
    activated = gate * sigmoid_gate
    slope = sigmoid_gate * (1.0 + gate * (1.0 - sigmoid_gate))
    hidden = activated * up_value
    tan_hidden = slope * tan_gate * up_value + activated * tan_up
    coef_gate[...] = up_value * slope * scale
    coef_up[...] = activated * scale
    for o in range(2):
        block = jnp.concatenate(
            [hidden[24 * o : 24 * o + 24], tan_hidden[24 * o : 24 * o + 24]], axis=0
        ).astype(bf16)
        base = (yh if o == 0 else 1 - yh) * NDP
        for d in range(NDP):
            out[rows_at(base + d, 48), :] = block


def down_kernel(parts, kinds, *rest):
    weights, (out, hidden_own, hidden_other, slots, sems) = rest[:8], rest[8:]
    copies = fetch(weights, slots, sems)
    yh = lax.axis_index(YH)
    total = None
    for i, (position, keep) in enumerate(((yh, hidden_own), (1 - yh, hidden_other))):
        sorted_rows = moved(kinds[...], parts[rows_at(position, 384), :])
        keep[...] = sorted_rows[:192]
        for n in range(4):
            copies[4 * i + n].wait()
            left = sorted_rows[192 + 96 * n : 288 + 96 * n] if n < 2 else sorted_rows[96 * n - 192 : 96 * n - 96]
            term = product(left, slots[4 * i + n])
            total = term if total is None else total + term
    for a in range(2):
        for j in range(8):
            out[48 * (8 * a + j) : 48 * (8 * a + j) + 48, :] = total[
                48 * a : 48 * a + 48, 128 * j : 128 * j + 128
            ].astype(bf16)


def sum_kernel(parts, out):
    total = parts[0:48].astype(f32)
    for i in range(1, NZ):
        total = total + parts[48 * i : 48 * i + 48].astype(f32)
    total = total.astype(bf16)
    for i in range(NZ):
        out[48 * i : 48 * i + 48, :] = total


def cot_kernel(blocks, low, high, *rest):
    weights, (tan_out, out, slots, sems) = rest[:4], rest[4:]
    copies = fetch(weights, slots, sems)
    yh = lax.axis_index(YH)
    for a in range(2):
        for j in range(8):
            tan_out[48 * a : 48 * a + 48, 128 * j : 128 * j + 128] = blocks[
                48 * (8 * a + j) : 48 * (8 * a + j) + 48, :
            ]
    first, second = moved(low[...], tan_out[...]), moved(high[...], tan_out[...])
    for i, position in enumerate((yh, 1 - yh)):
        copies[2 * i].wait()
        copies[2 * i + 1].wait()
        total = over_width(first, slots[2 * i]) + over_width(second, slots[2 * i + 1])
        out[rows_at(position, 192), :] = total.astype(bf16)


def cot_units_kernel(parts, coef_gate, coef_up, cores, out):
    yh, core = lax.axis_index(YH), lax.axis_index(CORE)
    values = parts[...].astype(f32)
    sums = []
    for h in range(2):
        total = values[192 * h : 192 * h + 24]
        for d in range(1, NDP):
            total = total + values[192 * h + 24 * d : 192 * h + 24 * d + 24]
        sums.append(total)
    first = jnp.where(yh == 0, sums[0], sums[1])
    second = jnp.where(yh == 0, sums[1], sums[0])
    total = jnp.concatenate([first, second], axis=0)
    both = jnp.concatenate([total * coef_gate[...], total * coef_up[...]], axis=0).astype(bf16)
    both = moved(cores[...], both)
    for h in range(2):
        base = (core if h == 0 else 1 - core) * NDP
        for d in range(NDP):
            out[rows_at(base + d, 48), :] = both[48 * h : 48 * h + 48]


def ggn_kernel(parts, last, inputs, inputs_x, ggn_gate, ggn_up):
    core = lax.axis_index(CORE)
    gate, up = None, None
    for left, position in ((inputs, core), (inputs_x, 1 - core)):
        both = moved(last[...], parts[rows_at(position, 384), :])
        one, two = over_rows(left[...], both[:192]), over_rows(left[...], both[192:])
        gate, up = (one, two) if gate is None else (gate + one, up + two)
    ggn_gate[...] = gate.astype(bf16)
    ggn_up[...] = up.astype(bf16)


def ggn_down_kernel(scale, ids, own, from_y, from_core, out, out_y, out_core, ggn_down, tangent_out):
    yh, z, core = lax.axis_index(YH), lax.axis_index(Z), lax.axis_index(CORE)
    total = over_rows(own[0:96], out[...]) + over_rows(from_y[0:96], out_y[...])
    total = total + over_rows(from_core[...], out_core[...])
    ggn_down[...] = (total * scale).astype(bf16)
    own_count = tangent_out.shape[0]
    first = ((yh * NZ + z) * 2 + core) * own_count
    row = lax.broadcasted_iota(jnp.int32, (16, 384), 0)
    column = lax.broadcasted_iota(jnp.int32, (16, 384), 1)
    wanted = jnp.full((16, 384), -1, jnp.int32)
    for i in range(own_count):
        stored = ids[first + i]
        holder = stored // own_count
        place = ((holder % 2) ^ core) * 192 + ((holder // (2 * NZ)) ^ yh) * 96
        place = place + (holder // 2) % NZ * own_count + stored % own_count
        wanted = jnp.where(row == i, place, wanted)
    hot = jnp.where(wanted == column, 1.0, 0.0).astype(bf16)
    every = jnp.concatenate([out[...], out_y[...], out_core[...]], axis=0)
    tangent_out[...] = product(hot, every)[:own_count].astype(bf16)


def call(kernel, outs, args, in_specs=None, scratch=(), flops=0):
    nbytes = sum(int(np.prod(a.shape)) * a.dtype.itemsize for a in args)
    nbytes += sum(int(np.prod(s)) * jnp.dtype(t).itemsize for s, t in outs)
    return pl.pallas_call(
        kernel,
        out_shape=[jax.ShapeDtypeStruct(s, t) for s, t in outs],
        in_specs=in_specs or [VMEM] * len(args),
        out_specs=[VMEM] * len(outs),
        scratch_shapes=list(scratch),
        compiler_params=pltpu.CompilerParams(vmem_limit_bytes=28 * MIB),
        cost_estimate=pl.CostEstimate(flops=flops, bytes_accessed=nbytes, transcendentals=0),
    )(*args)


def local(table, ids, gate_weight, up_weight, down_weight, gate_probe, up_probe, down_probe):
    tokens = ids.shape[0]
    own_count, width = table.shape
    units = gate_weight.shape[1]
    scale = float(tokens) ** (-0.5)
    fixed = tables(tokens // 4 // NDP)

    padded = jnp.pad(table, ((0, 8 - own_count), (0, 0)))
    padded = jnp.broadcast_to(padded[None], (NZ,) + padded.shape)
    gates = (gate_weight, up_weight, gate_probe, up_probe)
    padded, down_early, *gates_early = together(padded, down_weight, *gates)
    rows = lax.all_to_all(padded, Z, 0, 0).reshape(NZ * 8, width)
    gates_x = [swap(w, CORE) for w in gates_early]
    down_y = swap(down_early, YH)
    rows_y = swap(rows, YH)
    dots = 2 * 192 * width * units
    slots = [pltpu.VMEM((8, width, units), bf16), pltpu.SemaphoreType.DMA((8,))]
    inputs, partials = call(
        gates_kernel,
        [((192, width), bf16), ((384, 4 * units), bf16)],
        (rows, rows_y, fixed["pick"], fixed["fan"], *gates, *gates_x),
        [VMEM] * 4 + [ANY] * 8,
        slots,
        8 * dots,
    )

    partials, probe_late, down_late, down_y = together(partials, down_probe, down_weight, down_y)
    parts = lax.all_to_all(partials.reshape(NDP, 48, 4 * units), DP, 0, 0).reshape(384, 4 * units)
    probe_y = swap(probe_late, YH)
    down_x, probe_x, down_yx = (swap(w, CORE) for w in (down_late, probe_late, down_y))
    spread, coef_gate, coef_up = call(
        functools.partial(hidden_kernel, scale),
        [((768, units), bf16), ((48, units), f32), ((48, units), f32)],
        (parts,),
    )
    spread, probe_y = together(spread, probe_y)
    parts = lax.all_to_all(spread.reshape(16, 48, units), (YH,) + DP, 0, 0).reshape(768, units)
    probe_yx = swap(probe_y, CORE)
    slots = [pltpu.VMEM((8, units, width), bf16), pltpu.SemaphoreType.DMA((8,))]
    blocks, hidden_own, hidden_other = call(
        down_kernel,
        [((768, 128), bf16), ((192, units), bf16), ((192, units), bf16)],
        (
            parts, fixed["kinds"],
            down_weight, down_x, down_probe, probe_x,
            down_y, down_yx, probe_y, probe_yx,
        ),
        [VMEM] * 2 + [ANY] * 8,
        slots,
        4 * dots,
    )

    blocks, inputs_late, hidden_other = together(blocks, inputs, hidden_other)
    parts = lax.all_to_all(blocks.reshape(NZ, 48, 128), Z, 0, 0).reshape(768, 128)
    inputs_x = swap(inputs_late, CORE)
    hidden_y = swap(hidden_other, YH)
    (spread,) = call(sum_kernel, [((768, 128), bf16)], (parts,))
    spread, hidden_y, hidden_late = together(spread, hidden_y, hidden_own)
    blocks = lax.all_to_all(spread.reshape(NZ, 48, 128), Z, 0, 0).reshape(768, 128)
    hidden_core = swap(jnp.concatenate([hidden_late[96:], hidden_y[96:]]), CORE)

    slots = [pltpu.VMEM((4, units, width), bf16), pltpu.SemaphoreType.DMA((4,))]
    out, cot = call(
        cot_kernel,
        [((96, width), bf16), ((384, units), bf16)],
        (blocks, fixed["low"], fixed["high"], down_weight, down_x, down_y, down_yx),
        [VMEM] * 3 + [ANY] * 4,
        slots,
        4 * dots,
    )
    cot, out_late = together(cot, out)
    parts = lax.all_to_all(cot.reshape(16, 24, units), (YH,) + DP, 0, 0).reshape(384, units)
    out_y = swap(out_late, YH)
    (spread,) = call(
        cot_units_kernel, [((768, units), bf16)], (parts, coef_gate, coef_up, fixed["cores"])
    )
    spread, out_y, out_late = together(spread, out_y, out)
    parts = lax.all_to_all(spread.reshape(16, 48, units), (CORE,) + DP, 0, 0).reshape(768, units)
    out_core = swap(jnp.concatenate([out_late, out_y]), CORE)
    ggn_down, tangent_out = call(
        functools.partial(ggn_down_kernel, scale),
        [((units, width), bf16), ((own_count, width), bf16)],
        (ids, hidden_own, hidden_y, hidden_core, out, out_y, out_core),
        [pl.BlockSpec(memory_space=pltpu.SMEM)] + [VMEM] * 6,
        (),
        2 * dots,
    )
    ggn_gate, ggn_up = call(
        ggn_kernel,
        [((width, units), bf16), ((width, units), bf16)],
        (parts, fixed["last"], inputs, inputs_x),
        None,
        (),
        4 * dots,
    )
    return tangent_out, ggn_gate, ggn_up, ggn_down


def solution(mesh):
    devices = mesh.devices.reshape(2, NZ, 2, 4, 2)
    fine = Mesh(devices, (YH, Z, CORE, X, YL))
    in_specs = (
        P(MP, DP),
        P(),
        P(DP, MP),
        P(DP, MP),
        P(MP, DP),
        P(DP, MP),
        P(DP, MP),
        P(MP, DP),
    )
    out_specs = (P(MP, DP), P(DP, MP), P(DP, MP), P(MP, DP))
    return jax.shard_map(local, mesh=fine, in_specs=in_specs, out_specs=out_specs, check_vma=False)
```

time: 181 us -> 197 us (1.088)
  blocking collectives: 95.5 us -> 21.5 us
  starting transfers between devices: 42.6 us -> 102 us
  waiting for transfers between devices: 26.4 us -> 45.9 us
  Pallas kernels: 0 us -> 15.6 us
  matrix products: 6.1 us -> 0 us
  local copies, waits for them, and re-layouts: 6.41 us -> 9.5 us
    all_to_all x5 -> x1, blocking collectives: 95.5 us -> 21.5 us  [local(): lax.all_to_all(spread.reshape(NZ, 48, 128), Z, 0, 0).reshape(768, 128)]
    all_to_all x2 -> x6, starting transfers between devices: 6.85 us -> 51.8 us  [the longest x1 15.9 us: local(): rows = lax.all_to_all(padded, Z, 0, 0).reshape(NZ * 8, width)]
    pallas_call x0 -> x8, Pallas kernels: none -> 15.6 us  [call(): pl.pallas_call(kernel, out_shape=[jax.ShapeDtypeStruct(s, t) for s, t in...]
    ppermute x6 -> x16, starting transfers between devices: 35.7 us -> 50.3 us  [swap(): return lax.ppermute(value, axis, [(0, 1), (1, 0)])]
    all_to_all x2 -> x6, waiting for transfers between devices: 10.1 us -> 23.3 us  [the longest x1 9.74 us: local(): lax.all_to_all(spread.reshape(16, 48, units), (YH,) + DP, 0, 0)]
    unnamed x14 -> x40, local copies, waits for them, and re-layouts: 0.5 us -> 7.98 us
    ppermute x6 -> x16, waiting for transfers between devices: 16.3 us -> 22.5 us  [swap(): return lax.ppermute(value, axis, [(0, 1), (1, 0)])]
    dot_general x9 -> x0, matrix products: 6.1 us -> none  [the longest x6 2.94 us: product(): return jnp.dot(left, right, preferred_element_type=f32)]
  transfers between devices with their start and end apart: 8 -> 22, of which waited for: 8 -> 5; matrix products, arithmetic and copies ran while one was open for 1% -> 0% of each run, Pallas kernels for 0% -> 4%
where the time goes in v3:
time: 197 us; the launch traced here: 196 us
  starting transfers between devices  102 us (52%)
  waiting for transfers between devices  45.9 us (23%)
  blocking collectives  21.5 us (11%)
  Pallas kernels  15.6 us (8%)
  local copies, waits for them, and re-layouts  9.5 us (5%)
    ppermute x16, starting transfers between devices, swap(): return lax.ppermute(value, axis, [(0, 1), (1, 0)])  50.3 us
    ppermute x16, waiting for transfers between devices, swap(): return lax.ppermute(value, axis, [(0, 1), (1, 0)])  22.5 us
    all_to_all x1, blocking collectives, local(): lax.all_to_all(spread.reshape(NZ, 48, 128), Z, 0, 0).reshape(768, 128)  21.5 us
    all_to_all x1, starting transfers between devices, local(): rows = lax.all_to_all(padded, Z, 0, 0).reshape(NZ * 8, width)  15.9 us
    pallas_call x8, Pallas kernels, call(): pl.pallas_call(kernel, out_shape=[jax.ShapeDtypeStruct(s, t) for s, t in...  15.6 us
    all_to_all x1, starting transfers between devices, local(): lax.all_to_all(blocks.reshape(NZ, 48, 128), Z, 0, 0).reshape(768, 128)  11.9 us
    all_to_all x1, waiting for transfers between devices, local(): lax.all_to_all(spread.reshape(16, 48, units), (YH,) + DP, 0, 0)  9.74 us
    all_to_all x1, waiting for transfers between devices, local(): lax.all_to_all(blocks.reshape(NZ, 48, 128), Z, 0, 0).reshape(768, 128)  9.63 us
  transfers between devices with their start and end apart: 22, of which 5 were waited for; matrix products, arithmetic and copies ran while one was open for 0% of the time, Pallas kernels for 4%

profile of v3, /device:TPU:1, one launch (start us, length us, event | category | flops | bytes accessed | tf_op | source)
XLA Modules:
  0.0 195.6 jit_solution(11284662527406819292)
XLA Ops:
  2.2 15.9 %all-to-all-start = ((bf16[16,8,1024]{2,1,0:T(8,128)(2,1)}), bf16[16,8,1024]{2,1,0:T(8,128)(2,1)S(1)}, u32[]{:S(2)}, u32[]{:S(2)}) async-start(bf16[16,8,1024]{2,1,0:T(8,128)(2,1)} %broadcast_in_dim.2), calls=%async_computation | async-start | bytes 524288 | tf_op jit(solution)/shard_map/all_to_all | solution.py:248
  18.0 2.9 %collective-permute-start.1 = (bf16[1024,256]{1,0:T(8,128)(2,1)}, bf16[1024,256]{1,0:T(8,128)(2,1)S(1)}, u32[]{:S(2)}, u32[]{:S(2)}) collective-permute-start(bf16[1024,256]{1,0:T(8,128)(2,1)} %rest_0_.3), channel_id=1, source_target_pairs={{0,8},{8,0},{1,9},{9,1},{2,10},{10,2},{3,11},{11,3},{4,12},{12,4},... | collective-permute-start | bytes 1572872 | tf_op jit(solution)/shard_map/ppermute | solution.py:23
  20.9 1.9 collective-permute-start.2
  22.8 2.4 %collective-permute-start.3 = (bf16[1024,256]{1,0:T(8,128)(2,1)}, bf16[1024,256]{1,0:T(8,128)(2,1)S(1)}, u32[]{:S(2)}, u32[]{:S(2)}) collective-permute-start(bf16[1024,256]{1,0:T(8,128)(2,1)} %rest_2_.2), channel_id=1, source_target_pairs={{0,8},{8,0},{1,9},{9,1},{2,10},{10,2},{3,11},{11,3},{4,12},{12,4},... | collective-permute-start | bytes 1572872 | tf_op jit(solution)/shard_map/ppermute | solution.py:23
  25.3 1.9 collective-permute-start.4
  27.2 4.8 %collective-permute-start.5 = (bf16[256,1024]{1,0:T(8,128)(2,1)S(1)}, bf16[256,1024]{1,0:T(8,128)(2,1)S(1)}, u32[]{:S(2)}, u32[]{:S(2)}) collective-permute-start(bf16[256,1024]{1,0:T(8,128)(2,1)S(1)} %copy-done), channel_id=1, source_target_pairs={{0,256},{256,0},{1,257},{257,1},{2,258},{258,2},{3,259},{259,3},{4... | collective-permute-start | bytes 1572872 | tf_op jit(solution)/shard_map/ppermute | solution.py:23
  32.1 3.9 %collective-permute-start = (bf16[128,1024]{1,0:T(8,128)(2,1)S(1)}, bf16[128,1024]{1,0:T(8,128)(2,1)S(1)}, u32[]{:S(2)}, u32[]{:S(2)}) collective-permute-start(bf16[128,1024]{1,0:T(8,128)(2,1)S(1)} %bitcast.15), channel_id=1, source_target_pairs={{0,256},{256,0},{1,257},{257,1},{2,258},{258,2},{3,259},{259,3},{4... | collective-permute-start | bytes 786440 | tf_op jit(solution)/shard_map/ppermute | solution.py:23
  36.0 13.2 %collective-permute-done.other = bf16[128,1024]{1,0:T(8,128)(2,1)S(1)} collective-permute-done((bf16[128,1024]{1,0:T(8,128)(2,1)S(1)}, bf16[128,1024]{1,0:T(8,128)(2,1)S(1)}, u32[]{:S(2)}, u32[]{:S(2)}) %collective-permute-start) | collective-permute-done | bytes 262176 | tf_op jit(solution)/shard_map/ppermute | solution.py:23
  54.3 5.5 %shard_map.174 = (bf16[192,1024]{1,0:T(8,128)(2,1)S(1)}, bf16[384,1024]{1,0:T(8,128)(2,1)}) custom-call(bf16[128,1024]{1,0:T(8,128)(2,1)S(1)} %bitcast.16, bf16[128,1024]{1,0:T(8,128)(2,1)S(1)} %collective-permute-done.other, bf16[192,256]{1,0:T(8,128)(2,1)S(1)} %copy-done.10, bf16[384,384]{1,0:T(8,128)(2,1)S(1)} %copy-done.8, ...), custom_call_target="tpu_custom_call" | custom-call | flops 805306368 | bytes 6291456 | tf_op jit(solution)/shard_map/pallas_call | solution.py:226
  60.6 5.2 %all-to-all-start.1 = ((bf16[8,48,1024]{2,1,0:T(8,128)(2,1)}), bf16[8,48,1024]{2,1,0:T(8,128)(2,1)S(1)}, u32[]{:S(2)}, u32[]{:S(2)}) async-start(bf16[8,48,1024]{2,1,0:T(8,128)(2,1)} %bitcast.1), calls=%async_computation.1 | async-start | bytes 1572864 | tf_op jit(solution)/shard_map/all_to_all | solution.py:264
  65.8 4.5 %collective-permute-start.6 = (bf16[256,1024]{1,0:T(8,128)(2,1)S(1)}, bf16[256,1024]{1,0:T(8,128)(2,1)}, u32[]{:S(2)}, u32[]{:S(2)}) collective-permute-start(bf16[256,1024]{1,0:T(8,128)(2,1)S(1)} %copy-done.5), channel_id=1, source_target_pairs={{0,256},{256,0},{1,257},{257,1},{2,258},{258,2},{3,259},{259,3},{4... | collective-permute-start | bytes 1572872 | tf_op jit(solution)/shard_map/ppermute | solution.py:23
  70.3 3.8 %collective-permute-start.8 = (bf16[256,1024]{1,0:T(8,128)(2,1)S(1)}, bf16[256,1024]{1,0:T(8,128)(2,1)}, u32[]{:S(2)}, u32[]{:S(2)}) collective-permute-start(bf16[256,1024]{1,0:T(8,128)(2,1)S(1)} %copy-done.5), channel_id=1, source_target_pairs={{0,8},{8,0},{1,9},{9,1},{2,10},{10,2},{3,11},{11,3},{4,12},{12,4},... | collective-permute-start | bytes 1572872 | tf_op jit(solution)/shard_map/ppermute | solution.py:23
  74.1 1.9 collective-permute-start.7
  76.0 2.4 %collective-permute-start.9 = (bf16[256,1024]{1,0:T(8,128)(2,1)S(1)}, bf16[256,1024]{1,0:T(8,128)(2,1)S(1)}, u32[]{:S(2)}, u32[]{:S(2)}) collective-permute-start(bf16[256,1024]{1,0:T(8,128)(2,1)S(1)} %collective-permute-done.5.rest_4_.rest_2_), channel_id=1, source_target_pairs={{0,8},{8,0},{1,9},{9,1},{2,10},{10,2},{3,11},{11,3},{4,12},{12,4},... | collective-permute-start | bytes 1572872 | tf_op jit(solution)/shard_map/ppermute | solution.py:23
  79.4 9.3 %collective-permute-done.6.rest_6_ = bf16[256,1024]{1,0:T(8,128)(2,1)} collective-permute-done((bf16[256,1024]{1,0:T(8,128)(2,1)S(1)}, bf16[256,1024]{1,0:T(8,128)(2,1)}, u32[]{:S(2)}, u32[]{:S(2)}) %collective-permute-start.6) | collective-permute-done | bytes 524320 | tf_op jit(solution)/shard_map/ppermute | solution.py:23
  88.7 3.3 %collective-permute-start.10 = (bf16[256,1024]{1,0:T(8,128)(2,1)}, bf16[256,1024]{1,0:T(8,128)(2,1)}, u32[]{:S(2)}, u32[]{:S(2)}) collective-permute-start(bf16[256,1024]{1,0:T(8,128)(2,1)} %collective-permute-done.6.rest_6_), channel_id=1, source_target_pairs={{0,8},{8,0},{1,9},{9,1},{2,10},{10,2},{3,11},{11,3},{4,12},{12,4},... | collective-permute-start | bytes 1572872 | tf_op jit(solution)/shard_map/ppermute | solution.py:23
  92.0 5.0 %all-to-all-start.2 = ((bf16[16,48,256]{2,1,0:T(8,128)(2,1)}), bf16[16,48,256]{2,1,0:T(8,128)(2,1)S(1)}, u32[]{:S(2)}, u32[]{:S(2)}) async-start(bf16[16,48,256]{2,1,0:T(8,128)(2,1)} %bitcast.22), calls=%async_computation.2 | async-start | bytes 786432 | tf_op jit(solution)/shard_map/all_to_all | solution.py:273
  97.1 9.7 %all-to-all-done.2 = bf16[16,48,256]{2,1,0:T(8,128)(2,1)S(1)} async-done(((bf16[16,48,256]{2,1,0:T(8,128)(2,1)}), bf16[16,48,256]{2,1,0:T(8,128)(2,1)S(1)}, u32[]{:S(2)}, u32[]{:S(2)}) %all-to-all-start.2) | async-done | bytes 393248 | tf_op jit(solution)/shard_map/all_to_all | solution.py:273
  106.8 2.4 %shard_map.176 = (bf16[768,128]{1,0:T(8,128)(2,1)S(1)}, bf16[192,256]{1,0:T(8,128)(2,1)S(1)}, bf16[192,256]{1,0:T(8,128)(2,1)S(1)}) custom-call(bf16[768,256]{1,0:T(8,128)(2,1)S(1)} %bitcast.14, bf16[384,384]{1,0:T(8,128)(2,1)S(1)} %copy-done.7, bf16[256,1024]{1,0:T(8,128)(2,1)S(1)} %copy-done, bf16[256,1024]{1,0:T(8,128)(2,1)S(1)} %collective-permute-done.7.rest_1_, ...), custom_call_target="tpu_custom_call" | custom-call | flops 402653184 | bytes 5275648 | tf_op jit(solution)/shard_map/pallas_call | solution.py:226
  110.6 11.9 %all-to-all-start.3 = ((bf16[16,48,128]{2,1,0:T(8,128)(2,1)}), bf16[16,48,128]{2,1,0:T(8,128)(2,1)S(1)}, u32[]{:S(2)}, u32[]{:S(2)}) async-start(bf16[16,48,128]{2,1,0:T(8,128)(2,1)} %bitcast.23), calls=%async_computation.3 | async-start | bytes 393216 | tf_op jit(solution)/shard_map/all_to_all | solution.py:290
  122.4 2.7 %collective-permute-start.11 = (bf16[192,256]{1,0:T(8,128)(2,1)S(1)}, bf16[192,256]{1,0:T(8,128)(2,1)S(1)}, u32[]{:S(2)}, u32[]{:S(2)}) collective-permute-start(bf16[192,256]{1,0:T(8,128)(2,1)S(1)} %copy-done.18), channel_id=1, source_target_pairs={{0,256},{256,0},{1,257},{257,1},{2,258},{258,2},{3,259},{259,3},{4... | collective-permute-start | bytes 294920 | tf_op jit(solution)/shard_map/ppermute | solution.py:23
  125.2 9.6 %all-to-all-done.3 = bf16[16,48,128]{2,1,0:T(8,128)(2,1)S(1)} async-done(((bf16[16,48,128]{2,1,0:T(8,128)(2,1)}), bf16[16,48,128]{2,1,0:T(8,128)(2,1)S(1)}, u32[]{:S(2)}, u32[]{:S(2)}) %all-to-all-start.3) | async-done | bytes 196640 | tf_op jit(solution)/shard_map/all_to_all | solution.py:290
  134.9 21.5 %all_to_all.35 = bf16[16,48,128]{2,1,0:T(8,128)(2,1)S(1)} all-to-all(bf16[16,48,128]{2,1,0:T(8,128)(2,1)S(1)} %bitcast.19), channel_id=1, replica_groups=mesh['yh'=2,'z'=16,'core'=2,'x'=4,'yl'=2] {'z'}, dimensions={0} | all-to-all | bytes 393216 | tf_op jit(solution)/shard_map/all_to_all | solution.py:295
  156.4 2.7 %shard_map.178 = (bf16[96,1024]{1,0:T(8,128)(2,1)S(1)}, bf16[384,256]{1,0:T(8,128)(2,1)}) custom-call(bf16[768,128]{1,0:T(8,128)(2,1)S(1)} %bitcast.17, bf16[192,96]{1,0:T(8,128)(2,1)S(1)} %copy-done.12, bf16[192,96]{1,0:T(8,128)(2,1)S(1)} %copy-done.11, bf16[256,1024]{1,0:T(8,128)(2,1)S(1)} %copy-done, ...), custom_call_target="tpu_custom_call" | custom-call | flops 402653184 | bytes 2760704 | tf_op jit(solution)/shard_map/pallas_call | solution.py:226
  161.0 4.4 %all-to-all-start.5 = ((bf16[16,24,256]{2,1,0:T(8,128)(2,1)}), bf16[16,24,256]{2,1,0:T(8,128)(2,1)S(1)}, u32[]{:S(2)}, u32[]{:S(2)}) async-start(bf16[16,24,256]{2,1,0:T(8,128)(2,1)} %bitcast.9), calls=%async_computation.5 | async-start | bytes 393216 | tf_op jit(solution)/shard_map/all_to_all | solution.py:308
  165.4 7.3 %collective-permute-start.15 = (bf16[192,1024]{1,0:T(8,128)(2,1)S(1)}, bf16[192,1024]{1,0:T(8,128)(2,1)S(1)}, u32[]{:S(2)}, u32[]{:S(2)}) collective-permute-start(bf16[192,1024]{1,0:T(8,128)(2,1)S(1)} %copy-done.16), channel_id=1, source_target_pairs={{0,8},{8,0},{1,9},{9,1},{2,10},{10,2},{3,11},{11,3},{4,12},{12,4},... | collective-permute-start | bytes 1179656 | tf_op jit(solution)/shard_map/ppermute | solution.py:23
  173.7 9.5 %all-to-all-start.6 = ((bf16[16,48,256]{2,1,0:T(8,128)(2,1)}), bf16[16,48,256]{2,1,0:T(8,128)(2,1)S(1)}, u32[]{:S(2)}, u32[]{:S(2)}) async-start(bf16[16,48,256]{2,1,0:T(8,128)(2,1)} %bitcast.11), calls=%async_computation.6 | async-start | bytes 786432 | tf_op jit(solution)/shard_map/all_to_all | solution.py:314
  183.2 2.2 %collective-permute-start.14 = (bf16[192,1024]{1,0:T(8,128)(2,1)S(1)}, bf16[192,1024]{1,0:T(8,128)(2,1)S(1)}, u32[]{:S(2)}, u32[]{:S(2)}) collective-permute-start(bf16[192,1024]{1,0:T(8,128)(2,1)S(1)} %pad_maximum_fusion), channel_id=1, source_target_pairs={{0,8},{8,0},{1,9},{9,1},{2,10},{10,2},{3,11},{11,3},{4,12},{12,4},... | collective-permute-start | bytes 1179656 | tf_op jit(solution)/shard_map/ppermute | solution.py:23
  185.5 2.2 %collective-permute-start.12 = (bf16[192,256]{1,0:T(8,128)(2,1)S(1)}, bf16[192,256]{1,0:T(8,128)(2,1)S(1)}, u32[]{:S(2)}, u32[]{:S(2)}) collective-permute-start(bf16[192,256]{1,0:T(8,128)(2,1)S(1)} %pad_maximum_fusion.1), channel_id=1, source_target_pairs={{0,8},{8,0},{1,9},{9,1},{2,10},{10,2},{3,11},{11,3},{4,12},{12,4},... | collective-permute-start | bytes 294920 | tf_op jit(solution)/shard_map/ppermute | solution.py:23
  187.7 4.0 %all-to-all-done.6 = bf16[16,48,256]{2,1,0:T(8,128)(2,1)S(1)} async-done(((bf16[16,48,256]{2,1,0:T(8,128)(2,1)}), bf16[16,48,256]{2,1,0:T(8,128)(2,1)S(1)}, u32[]{:S(2)}, u32[]{:S(2)}) %all-to-all-start.6) | async-done | bytes 393248 | tf_op jit(solution)/shard_map/all_to_all | solution.py:314
  191.7 2.0 %shard_map.181 = (bf16[1024,256]{1,0:T(8,128)(2,1)}, bf16[1024,256]{1,0:T(8,128)(2,1)}) custom-call(bf16[768,256]{1,0:T(8,128)(2,1)S(1)} %bitcast.21, bf16[384,384]{1,0:T(8,128)(2,1)S(1)} %copy-done.19, bf16[192,1024]{1,0:T(8,128)(2,1)S(1)} %copy-done.16, bf16[192,1024]{1,0:T(8,128)(2,1)S(1)} %collective-permute-done.15.inputs_x), custom_call_target="tpu_custom_call" | custom-call | flops 402653184 | bytes 2523136 | tf_op jit(solution)/shard_map/pallas_call | solution.py:226
  193.7 1.9 shard_map.180
  (67 shorter events, 12.6 us)
Async XLA Ops:
  0.6 26.6 %copy-start = (bf16[256,1024]{1,0:T(8,128)(2,1)S(1)}, bf16[256,1024]{1,0:T(8,128)(2,1)}, u32[]{:S(2)}) copy-start(bf16[256,1024]{1,0:T(8,128)(2,1)} %rest_0_.5) | copy-start | bytes 1572868
  2.2 47.1 %copy-start.10 = (bf16[192,256]{1,0:T(8,128)(2,1)S(1)}, bf16[192,256]{1,0:T(8,128)(2,1)}, u32[]{:S(2)}) copy-start(bf16[192,256]{1,0:T(8,128)(2,1)} %constant.17.clone.pick) | copy-start | bytes 294916
  2.2 29.9 %all-to-all-start = ((bf16[16,8,1024]{2,1,0:T(8,128)(2,1)}), bf16[16,8,1024]{2,1,0:T(8,128)(2,1)S(1)}, u32[]{:S(2)}, u32[]{:S(2)}) async-start(bf16[16,8,1024]{2,1,0:T(8,128)(2,1)} %broadcast_in_dim.2), calls=%async_computation | async-start | bytes 524288 | tf_op jit(solution)/shard_map/all_to_all | solution.py:248
  18.0 14.0 %collective-permute-start.1 = (bf16[1024,256]{1,0:T(8,128)(2,1)}, bf16[1024,256]{1,0:T(8,128)(2,1)S(1)}, u32[]{:S(2)}, u32[]{:S(2)}) collective-permute-start(bf16[1024,256]{1,0:T(8,128)(2,1)} %rest_0_.3), channel_id=1, source_target_pairs={{0,8},{8,0},{1,9},{9,1},{2,10},{10,2},{3,11},{11,3},{4,12},{12,4},... | collective-permute-start | bytes 1572872 | tf_op jit(solution)/shard_map/ppermute | solution.py:23
  20.9 15.1 %collective-permute-start.2 = (bf16[1024,256]{1,0:T(8,128)(2,1)}, bf16[1024,256]{1,0:T(8,128)(2,1)S(1)}, u32[]{:S(2)}, u32[]{:S(2)}) collective-permute-start(bf16[1024,256]{1,0:T(8,128)(2,1)} %rest_1_.1), channel_id=1, source_target_pairs={{0,8},{8,0},{1,9},{9,1},{2,10},{10,2},{3,11},{11,3},{4,12},{12,4},... | collective-permute-start | bytes 1572872 | tf_op jit(solution)/shard_map/ppermute | solution.py:23
  22.8 13.2 %collective-permute-start.3 = (bf16[1024,256]{1,0:T(8,128)(2,1)}, bf16[1024,256]{1,0:T(8,128)(2,1)S(1)}, u32[]{:S(2)}, u32[]{:S(2)}) collective-permute-start(bf16[1024,256]{1,0:T(8,128)(2,1)} %rest_2_.2), channel_id=1, source_target_pairs={{0,8},{8,0},{1,9},{9,1},{2,10},{10,2},{3,11},{11,3},{4,12},{12,4},... | collective-permute-start | bytes 1572872 | tf_op jit(solution)/shard_map/ppermute | solution.py:23
  25.3 10.8 %collective-permute-start.4 = (bf16[1024,256]{1,0:T(8,128)(2,1)}, bf16[1024,256]{1,0:T(8,128)(2,1)S(1)}, u32[]{:S(2)}, u32[]{:S(2)}) collective-permute-start(bf16[1024,256]{1,0:T(8,128)(2,1)} %rest_3_.1), channel_id=1, source_target_pairs={{0,8},{8,0},{1,9},{9,1},{2,10},{10,2},{3,11},{11,3},{4,12},{12,4},... | collective-permute-start | bytes 1572872 | tf_op jit(solution)/shard_map/ppermute | solution.py:23
  27.2 33.4 %collective-permute-start.5 = (bf16[256,1024]{1,0:T(8,128)(2,1)S(1)}, bf16[256,1024]{1,0:T(8,128)(2,1)S(1)}, u32[]{:S(2)}, u32[]{:S(2)}) collective-permute-start(bf16[256,1024]{1,0:T(8,128)(2,1)S(1)} %copy-done), channel_id=1, source_target_pairs={{0,256},{256,0},{1,257},{257,1},{2,258},{258,2},{3,259},{259,3},{4... | collective-permute-start | bytes 1572872 | tf_op jit(solution)/shard_map/ppermute | solution.py:23
  32.1 17.2 %collective-permute-start = (bf16[128,1024]{1,0:T(8,128)(2,1)S(1)}, bf16[128,1024]{1,0:T(8,128)(2,1)S(1)}, u32[]{:S(2)}, u32[]{:S(2)}) collective-permute-start(bf16[128,1024]{1,0:T(8,128)(2,1)S(1)} %bitcast.15), channel_id=1, source_target_pairs={{0,256},{256,0},{1,257},{257,1},{2,258},{258,2},{3,259},{259,3},{4... | collective-permute-start | bytes 786440 | tf_op jit(solution)/shard_map/ppermute | solution.py:23
  60.6 5.2 %copy-start.5 = (bf16[256,1024]{1,0:T(8,128)(2,1)S(1)}, bf16[256,1024]{1,0:T(8,128)(2,1)}, u32[]{:S(2)}) copy-start(bf16[256,1024]{1,0:T(8,128)(2,1)} %rest_2_.3) | copy-start | bytes 1572868
  60.6 17.9 %all-to-all-start.1 = ((bf16[8,48,1024]{2,1,0:T(8,128)(2,1)}), bf16[8,48,1024]{2,1,0:T(8,128)(2,1)S(1)}, u32[]{:S(2)}, u32[]{:S(2)}) async-start(bf16[8,48,1024]{2,1,0:T(8,128)(2,1)} %bitcast.1), calls=%async_computation.1 | async-start | bytes 1572864 | tf_op jit(solution)/shard_map/all_to_all | solution.py:264
  65.8 22.9 %collective-permute-start.6 = (bf16[256,1024]{1,0:T(8,128)(2,1)S(1)}, bf16[256,1024]{1,0:T(8,128)(2,1)}, u32[]{:S(2)}, u32[]{:S(2)}) collective-permute-start(bf16[256,1024]{1,0:T(8,128)(2,1)S(1)} %copy-done.5), channel_id=1, source_target_pairs={{0,256},{256,0},{1,257},{257,1},{2,258},{258,2},{3,259},{259,3},{4... | collective-permute-start | bytes 1572872 | tf_op jit(solution)/shard_map/ppermute | solution.py:23
  70.3 26.8 %collective-permute-start.8 = (bf16[256,1024]{1,0:T(8,128)(2,1)S(1)}, bf16[256,1024]{1,0:T(8,128)(2,1)}, u32[]{:S(2)}, u32[]{:S(2)}) collective-permute-start(bf16[256,1024]{1,0:T(8,128)(2,1)S(1)} %copy-done.5), channel_id=1, source_target_pairs={{0,8},{8,0},{1,9},{9,1},{2,10},{10,2},{3,11},{11,3},{4,12},{12,4},... | collective-permute-start | bytes 1572872 | tf_op jit(solution)/shard_map/ppermute | solution.py:23
  74.1 23.0 %collective-permute-start.7 = (bf16[256,1024]{1,0:T(8,128)(2,1)S(1)}, bf16[256,1024]{1,0:T(8,128)(2,1)S(1)}, u32[]{:S(2)}, u32[]{:S(2)}) collective-permute-start(bf16[256,1024]{1,0:T(8,128)(2,1)S(1)} %copy-done), channel_id=1, source_target_pairs={{0,8},{8,0},{1,9},{9,1},{2,10},{10,2},{3,11},{11,3},{4,12},{12,4},... | collective-permute-start | bytes 1572872 | tf_op jit(solution)/shard_map/ppermute | solution.py:23
  76.0 21.0 %collective-permute-start.9 = (bf16[256,1024]{1,0:T(8,128)(2,1)S(1)}, bf16[256,1024]{1,0:T(8,128)(2,1)S(1)}, u32[]{:S(2)}, u32[]{:S(2)}) collective-permute-start(bf16[256,1024]{1,0:T(8,128)(2,1)S(1)} %collective-permute-done.5.rest_4_.rest_2_), channel_id=1, source_target_pairs={{0,8},{8,0},{1,9},{9,1},{2,10},{10,2},{3,11},{11,3},{4,12},{12,4},... | collective-permute-start | bytes 1572872 | tf_op jit(solution)/shard_map/ppermute | solution.py:23
  88.7 18.2 %collective-permute-start.10 = (bf16[256,1024]{1,0:T(8,128)(2,1)}, bf16[256,1024]{1,0:T(8,128)(2,1)}, u32[]{:S(2)}, u32[]{:S(2)}) collective-permute-start(bf16[256,1024]{1,0:T(8,128)(2,1)} %collective-permute-done.6.rest_6_), channel_id=1, source_target_pairs={{0,8},{8,0},{1,9},{9,1},{2,10},{10,2},{3,11},{11,3},{4,12},{12,4},... | collective-permute-start | bytes 1572872 | tf_op jit(solution)/shard_map/ppermute | solution.py:23
  92.0 14.8 %copy-start.7 = (bf16[384,384]{1,0:T(8,128)(2,1)S(1)}, bf16[384,384]{1,0:T(8,128)(2,1)}, u32[]{:S(2)}) copy-start(bf16[384,384]{1,0:T(8,128)(2,1)} %constant.19.clone.kinds) | copy-start | bytes 884740
  92.0 14.8 %all-to-all-start.2 = ((bf16[16,48,256]{2,1,0:T(8,128)(2,1)}), bf16[16,48,256]{2,1,0:T(8,128)(2,1)S(1)}, u32[]{:S(2)}, u32[]{:S(2)}) async-start(bf16[16,48,256]{2,1,0:T(8,128)(2,1)} %bitcast.22), calls=%async_computation.2 | async-start | bytes 786432 | tf_op jit(solution)/shard_map/all_to_all | solution.py:273
  110.6 11.9 %copy-start.18 = (bf16[192,256]{1,0:T(8,128)(2,1)S(1)}, bf16[192,256]{1,0:T(8,128)(2,1)}, u32[]{:S(2)}) copy-start(bf16[192,256]{1,0:T(8,128)(2,1)} %copy-done.17) | copy-start | bytes 294916
  110.6 24.2 %all-to-all-start.3 = ((bf16[16,48,128]{2,1,0:T(8,128)(2,1)}), bf16[16,48,128]{2,1,0:T(8,128)(2,1)S(1)}, u32[]{:S(2)}, u32[]{:S(2)}) async-start(bf16[16,48,128]{2,1,0:T(8,128)(2,1)} %bitcast.23), calls=%async_computation.3 | async-start | bytes 393216 | tf_op jit(solution)/shard_map/all_to_all | solution.py:290
  122.4 12.4 %collective-permute-start.11 = (bf16[192,256]{1,0:T(8,128)(2,1)S(1)}, bf16[192,256]{1,0:T(8,128)(2,1)S(1)}, u32[]{:S(2)}, u32[]{:S(2)}) collective-permute-start(bf16[192,256]{1,0:T(8,128)(2,1)S(1)} %copy-done.18), channel_id=1, source_target_pairs={{0,256},{256,0},{1,257},{257,1},{2,258},{258,2},{3,259},{259,3},{4... | collective-permute-start | bytes 294920 | tf_op jit(solution)/shard_map/ppermute | solution.py:23
  134.8 21.5 %copy-start.11 = (bf16[192,96]{1,0:T(8,128)(2,1)S(1)}, bf16[192,96]{1,0:T(8,128)(2,1)}, u32[]{:S(2)}) copy-start(bf16[192,96]{1,0:T(8,128)(2,1)} %constant.21.clone.high) | copy-start | bytes 110596
  134.9 21.5 %copy-start.12 = (bf16[192,96]{1,0:T(8,128)(2,1)S(1)}, bf16[192,96]{1,0:T(8,128)(2,1)}, u32[]{:S(2)}) copy-start(bf16[192,96]{1,0:T(8,128)(2,1)} %constant.20.clone.low) | copy-start | bytes 110596
  156.4 9.0 %copy-start.16 = (bf16[192,1024]{1,0:T(8,128)(2,1)S(1)}, bf16[192,1024]{1,0:T(8,128)(2,1)}, u32[]{:S(2)}) copy-start(bf16[192,1024]{1,0:T(8,128)(2,1)} %copy-done.15) | copy-start | bytes 1179652
  159.1 14.6 %collective-permute-start.13 = (bf16[96,1024]{1,0:T(8,128)(2,1)S(1)}, bf16[96,1024]{1,0:T(8,128)(2,1)S(1)}, u32[]{:S(2)}, u32[]{:S(2)}) collective-permute-start(bf16[96,1024]{1,0:T(8,128)(2,1)S(1)} %get-tuple-element.71.out), channel_id=1, source_target_pairs={{0,256},{256,0},{1,257},{257,1},{2,258},{258,2},{3,259},{259,3},{4... | collective-permute-start | bytes 589832 | tf_op jit(solution)/shard_map/ppermute | solution.py:23
  161.0 11.7 %copy-start.13 = (bf16[96,96]{1,0:T(8,128)(2,1)S(1)}, bf16[96,96]{1,0:T(8,128)(2,1)}, u32[]{:S(2)}) copy-start(bf16[96,96]{1,0:T(8,128)(2,1)} %constant.22.clone.cores) | copy-start | bytes 55300
  161.0 11.7 %all-to-all-start.5 = ((bf16[16,24,256]{2,1,0:T(8,128)(2,1)}), bf16[16,24,256]{2,1,0:T(8,128)(2,1)S(1)}, u32[]{:S(2)}, u32[]{:S(2)}) async-start(bf16[16,24,256]{2,1,0:T(8,128)(2,1)} %bitcast.9), calls=%async_computation.5 | async-start | bytes 393216 | tf_op jit(solution)/shard_map/all_to_all | solution.py:308
  165.4 22.4 %collective-permute-start.15 = (bf16[192,1024]{1,0:T(8,128)(2,1)S(1)}, bf16[192,1024]{1,0:T(8,128)(2,1)S(1)}, u32[]{:S(2)}, u32[]{:S(2)}) collective-permute-start(bf16[192,1024]{1,0:T(8,128)(2,1)S(1)} %copy-done.16), channel_id=1, source_target_pairs={{0,8},{8,0},{1,9},{9,1},{2,10},{10,2},{3,11},{11,3},{4,12},{12,4},... | collective-permute-start | bytes 1179656 | tf_op jit(solution)/shard_map/ppermute | solution.py:23
  173.7 18.1 %all-to-all-start.6 = ((bf16[16,48,256]{2,1,0:T(8,128)(2,1)}), bf16[16,48,256]{2,1,0:T(8,128)(2,1)S(1)}, u32[]{:S(2)}, u32[]{:S(2)}) async-start(bf16[16,48,256]{2,1,0:T(8,128)(2,1)} %bitcast.11), calls=%async_computation.6 | async-start | bytes 786432 | tf_op jit(solution)/shard_map/all_to_all | solution.py:314
  183.2 8.5 %copy-start.19 = (bf16[384,384]{1,0:T(8,128)(2,1)S(1)}, bf16[384,384]{1,0:T(8,128)(2,1)}, u32[]{:S(2)}) copy-start(bf16[384,384]{1,0:T(8,128)(2,1)} %constant.23.clone.last) | copy-start | bytes 884740
  183.2 10.5 %collective-permute-start.14 = (bf16[192,1024]{1,0:T(8,128)(2,1)S(1)}, bf16[192,1024]{1,0:T(8,128)(2,1)S(1)}, u32[]{:S(2)}, u32[]{:S(2)}) collective-permute-start(bf16[192,1024]{1,0:T(8,128)(2,1)S(1)} %pad_maximum_fusion), channel_id=1, source_target_pairs={{0,8},{8,0},{1,9},{9,1},{2,10},{10,2},{3,11},{11,3},{4,12},{12,4},... | collective-permute-start | bytes 1179656 | tf_op jit(solution)/shard_map/ppermute | solution.py:23
  185.5 8.2 %collective-permute-start.12 = (bf16[192,256]{1,0:T(8,128)(2,1)S(1)}, bf16[192,256]{1,0:T(8,128)(2,1)S(1)}, u32[]{:S(2)}, u32[]{:S(2)}) collective-permute-start(bf16[192,256]{1,0:T(8,128)(2,1)S(1)} %pad_maximum_fusion.1), channel_id=1, source_target_pairs={{0,8},{8,0},{1,9},{9,1},{2,10},{10,2},{3,11},{11,3},{4,12},{12,4},... | collective-permute-start | bytes 294920 | tf_op jit(solution)/shard_map/ppermute | solution.py:23
  (10 other events, 9.9 us)

commit v4 on v3

v4 whole, which is shorter than its diff:
```python
import functools

import jax
import jax.numpy as jnp
import numpy as np
from jax import lax
from jax.experimental import pallas as pl
from jax.experimental.pallas import tpu as pltpu
from jax.sharding import Mesh, PartitionSpec as P

YH, Z, CORE, X, YL = "yh", "z", "core", "x", "yl"
MP = (YH, Z, CORE)
DP = (X, YL)
NZ, NDP = 16, 8
bf16 = jnp.bfloat16
f32 = jnp.float32
MIB = 1 << 20
VMEM = pl.BlockSpec(memory_space=pltpu.VMEM)
HBM = pl.BlockSpec(memory_space=pltpu.HBM)
ANY = pl.BlockSpec(memory_space=pl.ANY)
SMEM = pl.BlockSpec(memory_space=pltpu.SMEM)
DMA = pltpu.SemaphoreType.DMA


def swap(value, axis):
    return lax.ppermute(value, axis, [(0, 1), (1, 0)])


def product(left, right):
    return jnp.dot(left, right, preferred_element_type=f32)


def over_rows(left, right):
    return lax.dot_general(left, right, (((0,), (0,)), ((), ())), preferred_element_type=f32)


def over_width(left, right):
    return lax.dot_general(left, right, (((1,), (1,)), ((), ())), preferred_element_type=f32)


def moved(count, sources, source, values):
    row = lax.broadcasted_iota(jnp.int32, (count, sources), 0)
    column = lax.broadcasted_iota(jnp.int32, (count, sources), 1)
    q = (row * 171) >> 11
    table = jnp.where(source(q, row - 12 * q) == column, 1.0, 0.0).astype(bf16)
    return product(table, values).astype(bf16)


def pick(q, j):
    s = 12 * (q >> 1) + j
    return (q & 1) * 128 + s + 2 * ((s * 43) >> 8)


def fan(q, j):
    return (q & 1) * 192 + (q >> 1) * 12 + j


def by_half(q, j):
    return ((q & 7) * 4 + ((q >> 3) & 1) * 2 + (q >> 4)) * 12 + j


def low(q, j):
    return jnp.where((q & 1) == 0, (q >> 1) * 12 + j, -1)


def high(q, j):
    return jnp.where((q & 1) == 1, (q >> 1) * 12 + j, -1)


def by_core(q, j):
    return (((q >> 1) & 1) * 4 + (q & 1) * 2 + (q >> 2)) * 12 + j


def by_kind(q, j):
    return (((q >> 1) & 7) * 4 + (q >> 4) * 2 + (q & 1)) * 12 + j


def rows_at(position, count):
    return pl.ds(pl.multiple_of(position * count, count), count)


def start(source, target, sem):
    copy = pltpu.make_async_copy(source, target, sem)
    copy.start()
    return copy


def gates_kernel(rows, rows_y, *rest):
    own, theirs, (inputs, out, slots, buffer, in_sems, out_sems) = rest[:4], rest[4:8], rest[8:]
    copies = [start(own[k], slots.at[k], in_sems.at[k]) for k in range(4)]
    units = slots.shape[2]
    both = jnp.concatenate([rows[...], rows_y[...]], axis=0)
    inputs[...] = moved(192, 256, pick, both)
    others = [product(inputs[...], theirs[k][...]).astype(bf16) for k in range(4)]
    writes = []
    for k in range(4):
        copies[k].wait()
        mine = product(inputs[...], slots[k]).astype(bf16)
        buffer[k] = moved(384, 384, fan, jnp.concatenate([mine, others[k]], axis=0))
        target = out.at[:, k * units : (k + 1) * units]
        writes.append(start(buffer.at[k], target, out_sems.at[k]))
    for write in writes:
        write.wait()


def hidden_kernel(scale, parts, after, out, coef_gate, coef_up, buffer, sems):
    sums = parts[0:48].astype(f32)
    for d in range(1, NDP):
        sums = sums + parts[48 * d : 48 * d + 48].astype(f32)
    units = sums.shape[1] // 4
    gate, up_value, tan_gate, tan_up = (sums[:, i * units : (i + 1) * units] for i in range(4))
    sigmoid_gate = 1.0 / (1.0 + jnp.exp(-gate))
    activated = gate * sigmoid_gate
    slope = sigmoid_gate * (1.0 + gate * (1.0 - sigmoid_gate))
    buffer[:, :units] = (activated * up_value).astype(bf16)
    buffer[:, units:] = (slope * tan_gate * up_value + activated * tan_up).astype(bf16)
    writes = [start(buffer, out.at[48 * d : 48 * d + 48], sems.at[d]) for d in range(NDP)]
    coef_gate[...] = up_value * slope * scale
    coef_up[...] = activated * scale
    for write in writes:
        write.wait()


def down_kernel(parts, down, probe, down_x, probe_x, sent, kept, hidden, hidden_x, slots, sems):
    copies = [start(down, slots.at[0], sems.at[0]), start(probe, slots.at[1], sems.at[1])]
    both = moved(384, 384, by_half, parts[...])
    units = both.shape[1] // 2
    hidden[...] = both[:192, :units]
    hidden_x[...] = both[192:, :units]
    total = product(both[192:, units:], down_x[...]) + product(both[192:, :units], probe_x[...])
    for copy in copies:
        copy.wait()
    total = total + product(both[:192, units:], slots[0]) + product(both[:192, :units], slots[1])
    kept[...] = total[:96]
    sent[...] = total[96:].astype(bf16)


def add_kernel(kept, received, out, buffer, sems):
    total = (kept[...] + received[...].astype(f32)).astype(bf16)
    writes = []
    for a in range(2):
        for j in range(8):
            buffer[48 * (8 * a + j) : 48 * (8 * a + j) + 48, :] = total[
                48 * a : 48 * a + 48, 128 * j : 128 * j + 128
            ]
        span = slice(384 * a, 384 * a + 384)
        writes.append(start(buffer.at[span], out.at[span], sems.at[a]))
    for write in writes:
        write.wait()


def sum_kernel(parts, after, after_too, out, buffer, sems):
    total = parts[0:48].astype(f32)
    for i in range(1, NZ):
        total = total + parts[48 * i : 48 * i + 48].astype(f32)
    buffer[...] = total.astype(bf16)
    writes = [start(buffer, out.at[48 * i : 48 * i + 48], sems.at[i]) for i in range(NZ)]
    for write in writes:
        write.wait()


def whole(blocks):
    lines = [
        jnp.concatenate([blocks[48 * (8 * a + j) : 48 * (8 * a + j) + 48, :] for j in range(8)], axis=1)
        for a in range(2)
    ]
    return jnp.concatenate(lines, axis=0)


def cot_kernel(blocks, down, down_x, down_y, down_yx, out, slot, buffer, in_sem, out_sems):
    copy = start(down, slot, in_sem)
    yh = lax.axis_index(YH)
    tan_out = whole(blocks)
    first, second = moved(192, 96, low, tan_out), moved(192, 96, high, tan_out)
    buffer[1] = (over_width(first, down_y[...]) + over_width(second, down_yx[...])).astype(bf16)
    writes = [start(buffer.at[1], out.at[rows_at(1 - yh, 192)], out_sems.at[1])]
    total = over_width(second, down_x[...])
    copy.wait()
    buffer[0] = (total + over_width(first, slot[...])).astype(bf16)
    writes.append(start(buffer.at[0], out.at[rows_at(yh, 192)], out_sems.at[0]))
    for write in writes:
        write.wait()


def whole_kernel(blocks, after, out):
    out[...] = whole(blocks)


def cot_units_kernel(parts, coef_gate, coef_up, after, out, buffer, sems):
    yh, core = lax.axis_index(YH), lax.axis_index(CORE)
    values = parts[...].astype(f32)
    sums = []
    for h in range(2):
        total = values[192 * h : 192 * h + 24]
        for d in range(1, NDP):
            total = total + values[192 * h + 24 * d : 192 * h + 24 * d + 24]
        sums.append(total)
    first = jnp.where(yh == 0, sums[0], sums[1])
    second = jnp.where(yh == 0, sums[1], sums[0])
    total = jnp.concatenate([first, second], axis=0)
    both = jnp.concatenate([total * coef_gate[...], total * coef_up[...]], axis=0).astype(bf16)
    buffer[...] = moved(96, 96, by_core, both)
    writes = []
    for h in range(2):
        base = (core if h == 0 else 1 - core) * NDP
        for d in range(NDP):
            source = buffer.at[48 * h : 48 * h + 48]
            writes.append(start(source, out.at[rows_at(base + d, 48)], sems.at[NDP * h + d]))
    for write in writes:
        write.wait()


def ggn_kernel(parts, inputs, inputs_x, after, ggn_gate, ggn_up):
    core = lax.axis_index(CORE)
    gate, up = None, None
    for left, position in ((inputs, core), (inputs_x, 1 - core)):
        both = moved(384, 384, by_kind, parts[rows_at(position, 384), :])
        one, two = over_rows(left[...], both[:192]), over_rows(left[...], both[192:])
        gate, up = (one, two) if gate is None else (gate + one, up + two)
    ggn_gate[...] = gate.astype(bf16)
    ggn_up[...] = up.astype(bf16)


def ggn_down_kernel(scale, ids, hidden, hidden_core, out, out_y, out_core, ggn_down, tangent_out):
    yh, z, core = lax.axis_index(YH), lax.axis_index(Z), lax.axis_index(CORE)
    total = over_rows(hidden[0:96], out[...]) + over_rows(hidden[96:192], out_y[...])
    total = total + over_rows(hidden_core[...], out_core[...])
    ggn_down[...] = (total * scale).astype(bf16)
    own_count = tangent_out.shape[0]
    first = ((yh * NZ + z) * 2 + core) * own_count
    row = lax.broadcasted_iota(jnp.int32, (16, 384), 0)
    column = lax.broadcasted_iota(jnp.int32, (16, 384), 1)
    wanted = jnp.full((16, 384), -1, jnp.int32)
    for i in range(own_count):
        stored = ids[first + i]
        holder = stored // own_count
        place = ((holder % 2) ^ core) * 192 + ((holder // (2 * NZ)) ^ yh) * 96
        place = place + (holder // 2) % NZ * own_count + stored % own_count
        wanted = jnp.where(row == i, place, wanted)
    hot = jnp.where(wanted == column, 1.0, 0.0).astype(bf16)
    every = jnp.concatenate([out[...], out_y[...], out_core[...]], axis=0)
    tangent_out[...] = product(hot, every)[:own_count].astype(bf16)


def call(kernel, mib, flops, ins, outs, scratch=()):
    nbytes = sum(int(np.prod(a.shape)) * a.dtype.itemsize for a, space in ins if space is not ANY)
    nbytes += sum(int(np.prod(s)) * jnp.dtype(t).itemsize for s, t, _ in outs)
    return pl.pallas_call(
        kernel,
        out_shape=[jax.ShapeDtypeStruct(s, t) for s, t, _ in outs],
        in_specs=[space for _, space in ins],
        out_specs=[space for _, _, space in outs],
        scratch_shapes=list(scratch),
        compiler_params=pltpu.CompilerParams(vmem_limit_bytes=mib * MIB),
        cost_estimate=pl.CostEstimate(flops=flops, bytes_accessed=nbytes, transcendentals=0),
    )(*[a for a, _ in ins])


def local(table, ids, gate_weight, up_weight, down_weight, gate_probe, up_probe, down_probe):
    tokens = ids.shape[0]
    own_count, width = table.shape
    units = gate_weight.shape[1]
    scale = float(tokens) ** (-0.5)
    dots = 2 * 192 * width * units

    rows = jnp.pad(table, ((0, 8 - own_count), (0, 0)))
    rows = jnp.broadcast_to(rows[None], (NZ,) + rows.shape)
    rows = lax.all_to_all(rows, Z, 0, 0).reshape(NZ * 8, width)
    gates = (gate_weight, up_weight, gate_probe, up_probe)
    gates_x = [swap(w, CORE) for w in gates]
    rows_y = swap(rows, YH)
    inputs, partials = call(
        gates_kernel,
        20,
        8 * dots,
        [(rows, VMEM), (rows_y, VMEM)] + [(w, HBM) for w in gates] + [(w, VMEM) for w in gates_x],
        [((192, width), bf16, VMEM), ((384, 4 * units), bf16, HBM)],
        [
            pltpu.VMEM((4, width, units), bf16),
            pltpu.VMEM((4, 384, units), bf16),
            DMA((4,)),
            DMA((4,)),
        ],
    )

    parts = lax.all_to_all(partials.reshape(NDP, 48, 4 * units), DP, 0, 0).reshape(384, 4 * units)
    down_x, probe_x, inputs_x = (swap(w, CORE) for w in (down_weight, down_probe, inputs))
    spread, coef_gate, coef_up = call(
        functools.partial(hidden_kernel, scale),
        8,
        0,
        [(parts, VMEM), (inputs_x, ANY)],
        [((384, 2 * units), bf16, HBM), ((48, units), f32, VMEM), ((48, units), f32, VMEM)],
        [pltpu.VMEM((48, 2 * units), bf16), DMA((NDP,))],
    )
    parts = lax.all_to_all(spread.reshape(NDP, 48, 2 * units), DP, 0, 0).reshape(384, 2 * units)
    sent, kept, hidden, hidden_x = call(
        down_kernel,
        14,
        4 * dots,
        [(parts, VMEM), (down_weight, HBM), (down_probe, HBM), (down_x, VMEM), (probe_x, VMEM)],
        [
            ((96, width), bf16, VMEM),
            ((96, width), f32, VMEM),
            ((192, units), bf16, VMEM),
            ((192, units), bf16, VMEM),
        ],
        [pltpu.VMEM((2, units, width), bf16), DMA((2,))],
    )

    received = swap(sent, YH)
    (blocks,) = call(
        add_kernel,
        6,
        0,
        [(kept, VMEM), (received, VMEM)],
        [((768, 128), bf16, HBM)],
        [pltpu.VMEM((768, 128), bf16), DMA((2,))],
    )
    parts = lax.all_to_all(blocks.reshape(NZ, 48, 128), Z, 0, 0).reshape(768, 128)
    down_y = swap(down_weight, YH)
    hidden_core = swap(hidden_x, CORE)
    (spread,) = call(
        sum_kernel,
        4,
        0,
        [(parts, VMEM), (down_y, ANY), (hidden_core, ANY)],
        [((768, 128), bf16, HBM)],
        [pltpu.VMEM((48, 128), bf16), DMA((NZ,))],
    )
    blocks = lax.all_to_all(spread.reshape(NZ, 48, 128), Z, 0, 0).reshape(768, 128)
    down_yx = swap(down_y, CORE)

    (cot,) = call(
        cot_kernel,
        14,
        4 * dots,
        [(blocks, VMEM), (down_weight, HBM), (down_x, VMEM), (down_y, VMEM), (down_yx, VMEM)],
        [((384, units), bf16, HBM)],
        [
            pltpu.VMEM((units, width), bf16),
            pltpu.VMEM((2, 192, units), bf16),
            DMA,
            DMA((2,)),
        ],
    )
    parts = lax.all_to_all(cot.reshape(16, 24, units), (YH,) + DP, 0, 0).reshape(384, units)
    (out,) = call(
        whole_kernel, 4, 0, [(blocks, VMEM), (cot, ANY)], [((96, width), bf16, VMEM)]
    )
    out_y = swap(out, YH)
    (spread,) = call(
        cot_units_kernel,
        6,
        0,
        [(parts, VMEM), (coef_gate, VMEM), (coef_up, VMEM), (out_y, ANY)],
        [((768, units), bf16, HBM)],
        [pltpu.VMEM((96, units), bf16), DMA((16,))],
    )
    parts = lax.all_to_all(spread.reshape(16, 48, units), (CORE,) + DP, 0, 0).reshape(768, units)
    out_core = swap(jnp.concatenate([out, out_y]), CORE)
    ggn_down, tangent_out = call(
        functools.partial(ggn_down_kernel, scale),
        14,
        2 * dots,
        [
            (ids, SMEM), (hidden, VMEM), (hidden_core, VMEM),
            (out, VMEM), (out_y, VMEM), (out_core, VMEM),
        ],
        [((units, width), bf16, VMEM), ((own_count, width), bf16, VMEM)],
    )
    ggn_gate, ggn_up = call(
        ggn_kernel,
        20,
        4 * dots,
        [(parts, VMEM), (inputs, VMEM), (inputs_x, VMEM), (tangent_out, ANY)],
        [((width, units), bf16, VMEM), ((width, units), bf16, VMEM)],
    )
    return tangent_out, ggn_gate, ggn_up, ggn_down


def solution(mesh):
    devices = mesh.devices.reshape(2, NZ, 2, 4, 2)
    fine = Mesh(devices, (YH, Z, CORE, X, YL))
    in_specs = (
        P(MP, DP),
        P(),
        P(DP, MP),
        P(DP, MP),
        P(MP, DP),
        P(DP, MP),
        P(DP, MP),
        P(MP, DP),
    )
    out_specs = (P(MP, DP), P(DP, MP), P(DP, MP), P(MP, DP))
    return jax.shard_map(local, mesh=fine, in_specs=in_specs, out_specs=out_specs, check_vma=False)
```

time: 197 us -> 179 us (0.909)
  starting transfers between devices: 102 us -> 124 us
  blocking collectives: 21.5 us -> 0 us
  waiting for transfers between devices: 45.9 us -> 30.3 us
  local copies, waits for them, and re-layouts: 9.5 us -> 5.39 us
    all_to_all x1 -> x0, blocking collectives: 21.5 us -> none  [local(): lax.all_to_all(spread.reshape(NZ, 48, 128), Z, 0, 0).reshape(768, 128)]
    ppermute x16 -> x14, starting transfers between devices: 50.3 us -> 65.2 us  [swap(): return lax.ppermute(value, axis, [(0, 1), (1, 0)])]
    ppermute x16 -> x14, waiting for transfers between devices: 22.5 us -> 9.81 us  [swap(): return lax.ppermute(value, axis, [(0, 1), (1, 0)])]
    all_to_all x2 -> x3, starting transfers between devices: 20.9 us -> 32.7 us  [the longest x1 15.7 us: local(): rows = lax.all_to_all(rows, Z, 0, 0).reshape(NZ * 8, width)]
    all_to_all x1, waiting for transfers between devices: 9.63 us -> 0.01 us  [local(): lax.all_to_all(blocks.reshape(NZ, 48, 128), Z, 0, 0).reshape(768, 128)]
    all_to_all x2 -> x3, waiting for transfers between devices: 9.75 us -> 13.9 us  [the longest x1 6.54 us: local(): lax.all_to_all(spread.reshape(NDP, 48, 2 * units), DP, 0, 0)]
    unnamed x40 -> x20, local copies, waits for them, and re-layouts: 7.98 us -> 3.88 us
    all_to_all x1, starting transfers between devices: 11.9 us -> 8.67 us  [local(): lax.all_to_all(blocks.reshape(NZ, 48, 128), Z, 0, 0).reshape(768, 128)]
  transfers between devices with their start and end apart: 22 -> 21, of which waited for: 5 -> 8; matrix products, arithmetic and copies ran while one was open for 0% -> 0% of each run, Pallas kernels for 4% -> 2%
where the time goes in v4:
time: 179 us; the launch traced here: 178 us
  starting transfers between devices  124 us (69%)
  waiting for transfers between devices  30.3 us (17%)
  Pallas kernels  16.9 us (9%)
  local copies, waits for them, and re-layouts  5.39 us (3%)
    ppermute x14, starting transfers between devices, swap(): return lax.ppermute(value, axis, [(0, 1), (1, 0)])  65.2 us
    pallas_call x10, Pallas kernels, call(): pl.pallas_call(kernel, out_shape=[jax.ShapeDtypeStruct(s, t) for s, t, _...  16.9 us
    all_to_all x1, starting transfers between devices, local(): rows = lax.all_to_all(rows, Z, 0, 0).reshape(NZ * 8, width)  15.7 us
    all_to_all x1, starting transfers between devices, local(): lax.all_to_all(spread.reshape(NZ, 48, 128), Z, 0, 0).reshape(768, 128)  11.5 us
    ppermute x14, waiting for transfers between devices, swap(): return lax.ppermute(value, axis, [(0, 1), (1, 0)])  9.81 us
    all_to_all x1, starting transfers between devices, local(): lax.all_to_all(blocks.reshape(NZ, 48, 128), Z, 0, 0).reshape(768, 128)  8.67 us
    all_to_all x1, starting transfers between devices, local(): lax.all_to_all(spread.reshape(16, 48, units), (CORE,) + DP, 0, 0)  8.02 us
    all_to_all x1, waiting for transfers between devices, local(): lax.all_to_all(spread.reshape(16, 48, units), (CORE,) + DP, 0, 0)  6.58 us
  transfers between devices with their start and end apart: 21, of which 8 were waited for; matrix products, arithmetic and copies ran while one was open for 0% of the time, Pallas kernels for 2%

profile of v4, /device:TPU:1, one launch (start us, length us, event | category | flops | bytes accessed | tf_op | source)
XLA Modules:
  0.0 177.6 jit_solution(18225896998295742687)
XLA Ops:
  2.2 15.7 %all-to-all-start = ((bf16[16,8,1024]{2,1,0:T(8,128)(2,1)}), bf16[16,8,1024]{2,1,0:T(8,128)(2,1)S(1)}, u32[]{:S(2)}, u32[]{:S(2)}) async-start(bf16[16,8,1024]{2,1,0:T(8,128)(2,1)} %broadcast_in_dim.2), calls=%async_computation | async-start | bytes 524288 | tf_op jit(solution)/shard_map/all_to_all | solution.py:268
  17.9 2.9 %collective-permute-start.1 = (bf16[1024,256]{1,0:T(8,128)(2,1)S(1)}, bf16[1024,256]{1,0:T(8,128)(2,1)S(1)}, u32[]{:S(2)}, u32[]{:S(2)}) collective-permute-start(bf16[1024,256]{1,0:T(8,128)(2,1)S(1)} %copy-done.1), channel_id=1, source_target_pairs={{0,8},{8,0},{1,9},{9,1},{2,10},{10,2},{3,11},{11,3},{4,12},{12,4},... | collective-permute-start | bytes 1572872 | tf_op jit(solution)/shard_map/ppermute | solution.py:26
  20.8 1.9 %collective-permute-start.2 = (bf16[1024,256]{1,0:T(8,128)(2,1)}, bf16[1024,256]{1,0:T(8,128)(2,1)S(1)}, u32[]{:S(2)}, u32[]{:S(2)}) collective-permute-start(bf16[1024,256]{1,0:T(8,128)(2,1)} %rest_1_.1), channel_id=1, source_target_pairs={{0,8},{8,0},{1,9},{9,1},{2,10},{10,2},{3,11},{11,3},{4,12},{12,4},... | collective-permute-start | bytes 1572872 | tf_op jit(solution)/shard_map/ppermute | solution.py:26
  22.7 2.4 %collective-permute-start.3 = (bf16[1024,256]{1,0:T(8,128)(2,1)}, bf16[1024,256]{1,0:T(8,128)(2,1)S(1)}, u32[]{:S(2)}, u32[]{:S(2)}) collective-permute-start(bf16[1024,256]{1,0:T(8,128)(2,1)} %rest_2_.1), channel_id=1, source_target_pairs={{0,8},{8,0},{1,9},{9,1},{2,10},{10,2},{3,11},{11,3},{4,12},{12,4},... | collective-permute-start | bytes 1572872 | tf_op jit(solution)/shard_map/ppermute | solution.py:26
  25.1 1.9 %collective-permute-start.4 = (bf16[1024,256]{1,0:T(8,128)(2,1)}, bf16[1024,256]{1,0:T(8,128)(2,1)S(1)}, u32[]{:S(2)}, u32[]{:S(2)}) collective-permute-start(bf16[1024,256]{1,0:T(8,128)(2,1)} %rest_3_.1), channel_id=1, source_target_pairs={{0,8},{8,0},{1,9},{9,1},{2,10},{10,2},{3,11},{11,3},{4,12},{12,4},... | collective-permute-start | bytes 1572872 | tf_op jit(solution)/shard_map/ppermute | solution.py:26
  27.1 4.0 %all-to-all-done = bf16[16,8,1024]{2,1,0:T(8,128)(2,1)S(1)} async-done(((bf16[16,8,1024]{2,1,0:T(8,128)(2,1)}), bf16[16,8,1024]{2,1,0:T(8,128)(2,1)S(1)}, u32[]{:S(2)}, u32[]{:S(2)}) %all-to-all-start) | async-done | bytes 262176 | tf_op jit(solution)/shard_map/all_to_all | solution.py:268
  31.0 4.8 %collective-permute-start = (bf16[128,1024]{1,0:T(8,128)(2,1)S(1)}, bf16[128,1024]{1,0:T(8,128)(2,1)S(1)}, u32[]{:S(2)}, u32[]{:S(2)}) collective-permute-start(bf16[128,1024]{1,0:T(8,128)(2,1)S(1)} %bitcast.17), channel_id=1, source_target_pairs={{0,256},{256,0},{1,257},{257,1},{2,258},{258,2},{3,259},{259,3},{4... | collective-permute-start | bytes 786440 | tf_op jit(solution)/shard_map/ppermute | solution.py:26
  35.9 3.7 %collective-permute-done.rows_y = bf16[128,1024]{1,0:T(8,128)(2,1)S(1)} collective-permute-done((bf16[128,1024]{1,0:T(8,128)(2,1)S(1)}, bf16[128,1024]{1,0:T(8,128)(2,1)S(1)}, u32[]{:S(2)}, u32[]{:S(2)}) %collective-permute-start) | collective-permute-done | bytes 262176 | tf_op jit(solution)/shard_map/ppermute | solution.py:26
  42.8 5.1 %shard_map.111 = (bf16[192,1024]{1,0:T(8,128)(2,1)}, bf16[384,1024]{1,0:T(8,128)(2,1)}) custom-call(bf16[128,1024]{1,0:T(8,128)(2,1)S(1)} %bitcast.18, bf16[128,1024]{1,0:T(8,128)(2,1)S(1)} %collective-permute-done.rows_y, bf16[1024,256]{1,0:T(8,128)(2,1)S(1)} %copy-done.1, bf16[1024,256]{1,0:T(8,128)(2,1)S(1)} %copy-done.2, ...), custom_call_target="tpu_custom_call" | custom-call | flops 805306368 | bytes 5898240 | tf_op jit(solution)/shard_map/pallas_call | solution.py:248
  47.9 5.2 %all-to-all-start.1 = ((bf16[8,48,1024]{2,1,0:T(8,128)(2,1)}), bf16[8,48,1024]{2,1,0:T(8,128)(2,1)S(1)}, u32[]{:S(2)}, u32[]{:S(2)}) async-start(bf16[8,48,1024]{2,1,0:T(8,128)(2,1)} %bitcast.1), calls=%async_computation.1 | async-start | bytes 1572864 | tf_op jit(solution)/shard_map/all_to_all | solution.py:286
  53.1 9.5 %collective-permute-start.5 = (bf16[192,1024]{1,0:T(8,128)(2,1)}, bf16[192,1024]{1,0:T(8,128)(2,1)S(1)}, u32[]{:S(2)}, u32[]{:S(2)}) collective-permute-start(bf16[192,1024]{1,0:T(8,128)(2,1)} %get-tuple-element.18.inputs), channel_id=1, source_target_pairs={{0,8},{8,0},{1,9},{9,1},{2,10},{10,2},{3,11},{11,3},{4,12},{12,4},... | collective-permute-start | bytes 1179656 | tf_op jit(solution)/shard_map/ppermute | solution.py:26
  62.6 1.9 %collective-permute-start.7 = (bf16[256,1024]{1,0:T(8,128)(2,1)S(1)}, bf16[256,1024]{1,0:T(8,128)(2,1)S(1)}, u32[]{:S(2)}, u32[]{:S(2)}) collective-permute-start(bf16[256,1024]{1,0:T(8,128)(2,1)S(1)} %copy-done.5), channel_id=1, source_target_pairs={{0,8},{8,0},{1,9},{9,1},{2,10},{10,2},{3,11},{11,3},{4,12},{12,4},... | collective-permute-start | bytes 1572872 | tf_op jit(solution)/shard_map/ppermute | solution.py:26
  64.5 2.4 %collective-permute-start.6 = (bf16[256,1024]{1,0:T(8,128)(2,1)S(1)}, bf16[256,1024]{1,0:T(8,128)(2,1)S(1)}, u32[]{:S(2)}, u32[]{:S(2)}) collective-permute-start(bf16[256,1024]{1,0:T(8,128)(2,1)S(1)} %copy-done), channel_id=1, source_target_pairs={{0,8},{8,0},{1,9},{9,1},{2,10},{10,2},{3,11},{11,3},{4,12},{12,4},... | collective-permute-start | bytes 1572872 | tf_op jit(solution)/shard_map/ppermute | solution.py:26
  67.9 5.4 %all-to-all-start.2 = ((bf16[8,48,512]{2,1,0:T(8,128)(2,1)}), bf16[8,48,512]{2,1,0:T(8,128)(2,1)S(1)}, u32[]{:S(2)}, u32[]{:S(2)}) async-start(bf16[8,48,512]{2,1,0:T(8,128)(2,1)} %bitcast.3), calls=%async_computation.2 | async-start | bytes 786432 | tf_op jit(solution)/shard_map/all_to_all | solution.py:296
  73.4 6.5 %all-to-all-done.2 = bf16[8,48,512]{2,1,0:T(8,128)(2,1)S(1)} async-done(((bf16[8,48,512]{2,1,0:T(8,128)(2,1)}), bf16[8,48,512]{2,1,0:T(8,128)(2,1)S(1)}, u32[]{:S(2)}, u32[]{:S(2)}) %all-to-all-start.2) | async-done | bytes 393248 | tf_op jit(solution)/shard_map/all_to_all | solution.py:296
  80.9 4.5 %collective-permute-start.9 = (bf16[96,1024]{1,0:T(8,128)(2,1)S(1)}, bf16[96,1024]{1,0:T(8,128)(2,1)S(1)}, u32[]{:S(2)}, u32[]{:S(2)}) collective-permute-start(bf16[96,1024]{1,0:T(8,128)(2,1)S(1)} %get-tuple-element.23), channel_id=1, source_target_pairs={{0,256},{256,0},{1,257},{257,1},{2,258},{258,2},{3,259},{259,3},{4... | collective-permute-start | bytes 589832 | tf_op jit(solution)/shard_map/ppermute | solution.py:26
  85.5 3.4 %collective-permute-done.9.received = bf16[96,1024]{1,0:T(8,128)(2,1)S(1)} collective-permute-done((bf16[96,1024]{1,0:T(8,128)(2,1)S(1)}, bf16[96,1024]{1,0:T(8,128)(2,1)S(1)}, u32[]{:S(2)}, u32[]{:S(2)}) %collective-permute-start.9) | collective-permute-done | bytes 196640 | tf_op jit(solution)/shard_map/ppermute | solution.py:26
  89.6 8.7 %all-to-all-start.3 = ((bf16[16,48,128]{2,1,0:T(8,128)(2,1)}), bf16[16,48,128]{2,1,0:T(8,128)(2,1)S(1)}, u32[]{:S(2)}, u32[]{:S(2)}) async-start(bf16[16,48,128]{2,1,0:T(8,128)(2,1)} %bitcast.5), calls=%async_computation.3 | async-start | bytes 393216 | tf_op jit(solution)/shard_map/all_to_all | solution.py:320
  98.3 4.5 %collective-permute-start.10 = (bf16[256,1024]{1,0:T(8,128)(2,1)S(1)}, bf16[256,1024]{1,0:T(8,128)(2,1)S(1)}, u32[]{:S(2)}, u32[]{:S(2)}) collective-permute-start(bf16[256,1024]{1,0:T(8,128)(2,1)S(1)} %copy-done), channel_id=1, source_target_pairs={{0,256},{256,0},{1,257},{257,1},{2,258},{258,2},{3,259},{259,3},{4... | collective-permute-start | bytes 1572872 | tf_op jit(solution)/shard_map/ppermute | solution.py:26
  102.8 6.7 %collective-permute-start.8 = (bf16[192,256]{1,0:T(8,128)(2,1)S(1)}, bf16[192,256]{1,0:T(8,128)(2,1)S(1)}, u32[]{:S(2)}, u32[]{:S(2)}) collective-permute-start(bf16[192,256]{1,0:T(8,128)(2,1)S(1)} %copy-done.8), channel_id=1, source_target_pairs={{0,8},{8,0},{1,9},{9,1},{2,10},{10,2},{3,11},{11,3},{4,12},{12,4},... | collective-permute-start | bytes 294920 | tf_op jit(solution)/shard_map/ppermute | solution.py:26
  111.5 11.5 %all-to-all-start.4 = ((bf16[16,48,128]{2,1,0:T(8,128)(2,1)}), bf16[16,48,128]{2,1,0:T(8,128)(2,1)S(1)}, u32[]{:S(2)}, u32[]{:S(2)}) async-start(bf16[16,48,128]{2,1,0:T(8,128)(2,1)} %bitcast.7), calls=%async_computation.4 | async-start | bytes 393216 | tf_op jit(solution)/shard_map/all_to_all | solution.py:331
  123.0 7.5 %collective-permute-start.11 = (bf16[256,1024]{1,0:T(8,128)(2,1)S(1)}, bf16[256,1024]{1,0:T(8,128)(2,1)S(1)}, u32[]{:S(2)}, u32[]{:S(2)}) collective-permute-start(bf16[256,1024]{1,0:T(8,128)(2,1)S(1)} %collective-permute-done.10.after.down_y), channel_id=1, source_target_pairs={{0,8},{8,0},{1,9},{9,1},{2,10},{10,2},{3,11},{11,3},{4,12},{12,4},... | collective-permute-start | bytes 1572872 | tf_op jit(solution)/shard_map/ppermute | solution.py:26
  130.5 1.5 collective-permute-done.11.down_yx
  132.0 3.3 %all-to-all-done.4 = bf16[16,48,128]{2,1,0:T(8,128)(2,1)S(1)} async-done(((bf16[16,48,128]{2,1,0:T(8,128)(2,1)}), bf16[16,48,128]{2,1,0:T(8,128)(2,1)S(1)}, u32[]{:S(2)}, u32[]{:S(2)}) %all-to-all-start.4) | async-done | bytes 196640 | tf_op jit(solution)/shard_map/all_to_all | solution.py:331
  135.4 2.3 %shard_map.116.after = bf16[384,256]{1,0:T(8,128)(2,1)} custom-call(bf16[768,128]{1,0:T(8,128)(2,1)S(1)} %bitcast.14, bf16[256,1024]{1,0:T(8,128)(2,1)S(1)} %copy-done, bf16[256,1024]{1,0:T(8,128)(2,1)S(1)} %collective-permute-done.6.down_x, bf16[256,1024]{1,0:T(8,128)(2,1)S(1)} %collective-permute-done.10.after.down_y, ...), custom_call_target="tpu_custom_call" | custom-call | flops 402653184 | bytes 2490368 | tf_op jit(solution)/shard_map/pallas_call | solution.py:248
  137.8 4.2 %collective-permute-start.12 = (bf16[96,1024]{1,0:T(8,128)(2,1)S(1)}, bf16[96,1024]{1,0:T(8,128)(2,1)S(1)}, u32[]{:S(2)}, u32[]{:S(2)}) collective-permute-start(bf16[96,1024]{1,0:T(8,128)(2,1)S(1)} %shard_map.117.out), channel_id=1, source_target_pairs={{0,256},{256,0},{1,257},{257,1},{2,258},{258,2},{3,259},{259,3},{4... | collective-permute-start | bytes 589832 | tf_op jit(solution)/shard_map/ppermute | solution.py:26
  142.0 4.3 %all-to-all-start.5 = ((bf16[16,24,256]{2,1,0:T(8,128)(2,1)}), bf16[16,24,256]{2,1,0:T(8,128)(2,1)S(1)}, u32[]{:S(2)}, u32[]{:S(2)}) async-start(bf16[16,24,256]{2,1,0:T(8,128)(2,1)} %bitcast.9), calls=%async_computation.5 | async-start | bytes 393216 | tf_op jit(solution)/shard_map/all_to_all | solution.py:347
  146.3 10.0 %collective-permute-start.13 = (bf16[192,1024]{1,0:T(8,128)(2,1)S(1)}, bf16[192,1024]{1,0:T(8,128)(2,1)S(1)}, u32[]{:S(2)}, u32[]{:S(2)}) collective-permute-start(bf16[192,1024]{1,0:T(8,128)(2,1)S(1)} %pad_maximum_fusion), channel_id=1, source_target_pairs={{0,8},{8,0},{1,9},{9,1},{2,10},{10,2},{3,11},{11,3},{4,12},{12,4},... | collective-permute-start | bytes 1179656 | tf_op jit(solution)/shard_map/ppermute | solution.py:26
  157.4 8.0 %all-to-all-start.6 = ((bf16[16,48,256]{2,1,0:T(8,128)(2,1)}), bf16[16,48,256]{2,1,0:T(8,128)(2,1)S(1)}, u32[]{:S(2)}, u32[]{:S(2)}) async-start(bf16[16,48,256]{2,1,0:T(8,128)(2,1)} %bitcast.11), calls=%async_computation.6 | async-start | bytes 786432 | tf_op jit(solution)/shard_map/all_to_all | solution.py:360
  165.4 1.9 %shard_map.118 = (bf16[256,1024]{1,0:T(8,128)(2,1)}, bf16[6,1024]{1,0:T(8,128)(2,1)}) custom-call(s32[384]{0:T(512)S(1)} %copy-done.6, bf16[192,256]{1,0:T(8,128)(2,1)S(1)} %get-tuple-element.20.hidden, bf16[192,256]{1,0:T(8,128)(2,1)S(1)} %collective-permute-done.8.after_too.hidden_core, bf16[96,1024]{1,0:T(8,128)(2,1)S(1)} %shard_map.117.out, ...), custom_call_target="tpu_custom_call" | custom-call | flops 201326592 | bytes 1521152 | tf_op jit(solution)/shard_map/pallas_call | solution.py:248
  167.3 6.6 %all-to-all-done.6 = bf16[16,48,256]{2,1,0:T(8,128)(2,1)S(1)} async-done(((bf16[16,48,256]{2,1,0:T(8,128)(2,1)}), bf16[16,48,256]{2,1,0:T(8,128)(2,1)S(1)}, u32[]{:S(2)}, u32[]{:S(2)}) %all-to-all-start.6) | async-done | bytes 393248 | tf_op jit(solution)/shard_map/all_to_all | solution.py:360
  174.6 3.0 %shard_map.120 = (bf16[1024,256]{1,0:T(8,128)(2,1)}, bf16[1024,256]{1,0:T(8,128)(2,1)}) custom-call(bf16[768,256]{1,0:T(8,128)(2,1)S(1)} %bitcast.21, bf16[192,1024]{1,0:T(8,128)(2,1)} %get-tuple-element.18.inputs, bf16[192,1024]{1,0:T(8,128)(2,1)S(1)} %collective-permute-done.5.after.inputs_x, bf16[6,1024]{1,0:T(8,128)(2,1)S(1)} %copy-done.9), custom_call_target="tpu_custom_call" | custom-call | flops 402653184 | bytes 2228224 | tf_op jit(solution)/shard_map/pallas_call | solution.py:248
  (43 shorter events, 11.2 us)
Async XLA Ops:
  0.6 17.3 %copy-start.1 = (bf16[1024,256]{1,0:T(8,128)(2,1)S(1)}, bf16[1024,256]{1,0:T(8,128)(2,1)}, u32[]{:S(2)}) copy-start(bf16[1024,256]{1,0:T(8,128)(2,1)} %rest_0_.1) | copy-start | bytes 1572868
  2.2 28.9 %all-to-all-start = ((bf16[16,8,1024]{2,1,0:T(8,128)(2,1)}), bf16[16,8,1024]{2,1,0:T(8,128)(2,1)S(1)}, u32[]{:S(2)}, u32[]{:S(2)}) async-start(bf16[16,8,1024]{2,1,0:T(8,128)(2,1)} %broadcast_in_dim.2), calls=%async_computation | async-start | bytes 524288 | tf_op jit(solution)/shard_map/all_to_all | solution.py:268
  17.9 17.9 %collective-permute-start.1 = (bf16[1024,256]{1,0:T(8,128)(2,1)S(1)}, bf16[1024,256]{1,0:T(8,128)(2,1)S(1)}, u32[]{:S(2)}, u32[]{:S(2)}) collective-permute-start(bf16[1024,256]{1,0:T(8,128)(2,1)S(1)} %copy-done.1), channel_id=1, source_target_pairs={{0,8},{8,0},{1,9},{9,1},{2,10},{10,2},{3,11},{11,3},{4,12},{12,4},... | collective-permute-start | bytes 1572872 | tf_op jit(solution)/shard_map/ppermute | solution.py:26
  20.8 15.1 %collective-permute-start.2 = (bf16[1024,256]{1,0:T(8,128)(2,1)}, bf16[1024,256]{1,0:T(8,128)(2,1)S(1)}, u32[]{:S(2)}, u32[]{:S(2)}) collective-permute-start(bf16[1024,256]{1,0:T(8,128)(2,1)} %rest_1_.1), channel_id=1, source_target_pairs={{0,8},{8,0},{1,9},{9,1},{2,10},{10,2},{3,11},{11,3},{4,12},{12,4},... | collective-permute-start | bytes 1572872 | tf_op jit(solution)/shard_map/ppermute | solution.py:26
  22.7 13.2 %collective-permute-start.3 = (bf16[1024,256]{1,0:T(8,128)(2,1)}, bf16[1024,256]{1,0:T(8,128)(2,1)S(1)}, u32[]{:S(2)}, u32[]{:S(2)}) collective-permute-start(bf16[1024,256]{1,0:T(8,128)(2,1)} %rest_2_.1), channel_id=1, source_target_pairs={{0,8},{8,0},{1,9},{9,1},{2,10},{10,2},{3,11},{11,3},{4,12},{12,4},... | collective-permute-start | bytes 1572872 | tf_op jit(solution)/shard_map/ppermute | solution.py:26
  25.1 10.8 %collective-permute-start.4 = (bf16[1024,256]{1,0:T(8,128)(2,1)}, bf16[1024,256]{1,0:T(8,128)(2,1)S(1)}, u32[]{:S(2)}, u32[]{:S(2)}) collective-permute-start(bf16[1024,256]{1,0:T(8,128)(2,1)} %rest_3_.1), channel_id=1, source_target_pairs={{0,8},{8,0},{1,9},{9,1},{2,10},{10,2},{3,11},{11,3},{4,12},{12,4},... | collective-permute-start | bytes 1572872 | tf_op jit(solution)/shard_map/ppermute | solution.py:26
  31.0 8.6 %collective-permute-start = (bf16[128,1024]{1,0:T(8,128)(2,1)S(1)}, bf16[128,1024]{1,0:T(8,128)(2,1)S(1)}, u32[]{:S(2)}, u32[]{:S(2)}) collective-permute-start(bf16[128,1024]{1,0:T(8,128)(2,1)S(1)} %bitcast.17), channel_id=1, source_target_pairs={{0,256},{256,0},{1,257},{257,1},{2,258},{258,2},{3,259},{259,3},{4... | collective-permute-start | bytes 786440 | tf_op jit(solution)/shard_map/ppermute | solution.py:26
  39.7 1.0 copy-start.2
  40.7 1.0 copy-start.3
  41.7 1.0 copy-start.4
  47.9 14.7 %copy-start.5 = (bf16[256,1024]{1,0:T(8,128)(2,1)S(1)}, bf16[256,1024]{1,0:T(8,128)(2,1)}, u32[]{:S(2)}) copy-start(bf16[256,1024]{1,0:T(8,128)(2,1)} %probe.1) | copy-start | bytes 1572868
  47.9 16.6 %copy-start = (bf16[256,1024]{1,0:T(8,128)(2,1)S(1)}, bf16[256,1024]{1,0:T(8,128)(2,1)}, u32[]{:S(2)}) copy-start(bf16[256,1024]{1,0:T(8,128)(2,1)} %down.3) | copy-start | bytes 1572868
  47.9 19.1 %all-to-all-start.1 = ((bf16[8,48,1024]{2,1,0:T(8,128)(2,1)}), bf16[8,48,1024]{2,1,0:T(8,128)(2,1)S(1)}, u32[]{:S(2)}, u32[]{:S(2)}) async-start(bf16[8,48,1024]{2,1,0:T(8,128)(2,1)} %bitcast.1), calls=%async_computation.1 | async-start | bytes 1572864 | tf_op jit(solution)/shard_map/all_to_all | solution.py:286
  53.1 13.9 %collective-permute-start.5 = (bf16[192,1024]{1,0:T(8,128)(2,1)}, bf16[192,1024]{1,0:T(8,128)(2,1)S(1)}, u32[]{:S(2)}, u32[]{:S(2)}) collective-permute-start(bf16[192,1024]{1,0:T(8,128)(2,1)} %get-tuple-element.18.inputs), channel_id=1, source_target_pairs={{0,8},{8,0},{1,9},{9,1},{2,10},{10,2},{3,11},{11,3},{4,12},{12,4},... | collective-permute-start | bytes 1179656 | tf_op jit(solution)/shard_map/ppermute | solution.py:26
  62.6 10.8 %collective-permute-start.7 = (bf16[256,1024]{1,0:T(8,128)(2,1)S(1)}, bf16[256,1024]{1,0:T(8,128)(2,1)S(1)}, u32[]{:S(2)}, u32[]{:S(2)}) collective-permute-start(bf16[256,1024]{1,0:T(8,128)(2,1)S(1)} %copy-done.5), channel_id=1, source_target_pairs={{0,8},{8,0},{1,9},{9,1},{2,10},{10,2},{3,11},{11,3},{4,12},{12,4},... | collective-permute-start | bytes 1572872 | tf_op jit(solution)/shard_map/ppermute | solution.py:26
  64.5 8.8 %collective-permute-start.6 = (bf16[256,1024]{1,0:T(8,128)(2,1)S(1)}, bf16[256,1024]{1,0:T(8,128)(2,1)S(1)}, u32[]{:S(2)}, u32[]{:S(2)}) collective-permute-start(bf16[256,1024]{1,0:T(8,128)(2,1)S(1)} %copy-done), channel_id=1, source_target_pairs={{0,8},{8,0},{1,9},{9,1},{2,10},{10,2},{3,11},{11,3},{4,12},{12,4},... | collective-permute-start | bytes 1572872 | tf_op jit(solution)/shard_map/ppermute | solution.py:26
  67.9 12.0 %all-to-all-start.2 = ((bf16[8,48,512]{2,1,0:T(8,128)(2,1)}), bf16[8,48,512]{2,1,0:T(8,128)(2,1)S(1)}, u32[]{:S(2)}, u32[]{:S(2)}) async-start(bf16[8,48,512]{2,1,0:T(8,128)(2,1)} %bitcast.3), calls=%async_computation.2 | async-start | bytes 786432 | tf_op jit(solution)/shard_map/all_to_all | solution.py:296
  80.9 8.7 %copy-start.7 = (bf16[192,256]{1,0:T(8,128)(2,1)}, bf16[192,256]{1,0:T(8,128)(2,1)S(1)}, u32[]{:S(2)}) copy-start(bf16[192,256]{1,0:T(8,128)(2,1)S(1)} %get-tuple-element.21) | copy-start | bytes 294916
  80.9 7.9 %collective-permute-start.9 = (bf16[96,1024]{1,0:T(8,128)(2,1)S(1)}, bf16[96,1024]{1,0:T(8,128)(2,1)S(1)}, u32[]{:S(2)}, u32[]{:S(2)}) collective-permute-start(bf16[96,1024]{1,0:T(8,128)(2,1)S(1)} %get-tuple-element.23), channel_id=1, source_target_pairs={{0,256},{256,0},{1,257},{257,1},{2,258},{258,2},{3,259},{259,3},{4... | collective-permute-start | bytes 589832 | tf_op jit(solution)/shard_map/ppermute | solution.py:26
  89.6 13.2 %copy-start.8 = (bf16[192,256]{1,0:T(8,128)(2,1)S(1)}, bf16[192,256]{1,0:T(8,128)(2,1)}, u32[]{:S(2)}) copy-start(bf16[192,256]{1,0:T(8,128)(2,1)} %copy-done.7) | copy-start | bytes 294916
  89.6 21.0 %all-to-all-start.3 = ((bf16[16,48,128]{2,1,0:T(8,128)(2,1)}), bf16[16,48,128]{2,1,0:T(8,128)(2,1)S(1)}, u32[]{:S(2)}, u32[]{:S(2)}) async-start(bf16[16,48,128]{2,1,0:T(8,128)(2,1)} %bitcast.5), calls=%async_computation.3 | async-start | bytes 393216 | tf_op jit(solution)/shard_map/all_to_all | solution.py:320
  98.3 12.4 %collective-permute-start.10 = (bf16[256,1024]{1,0:T(8,128)(2,1)S(1)}, bf16[256,1024]{1,0:T(8,128)(2,1)S(1)}, u32[]{:S(2)}, u32[]{:S(2)}) collective-permute-start(bf16[256,1024]{1,0:T(8,128)(2,1)S(1)} %copy-done), channel_id=1, source_target_pairs={{0,256},{256,0},{1,257},{257,1},{2,258},{258,2},{3,259},{259,3},{4... | collective-permute-start | bytes 1572872 | tf_op jit(solution)/shard_map/ppermute | solution.py:26
  102.8 7.8 %collective-permute-start.8 = (bf16[192,256]{1,0:T(8,128)(2,1)S(1)}, bf16[192,256]{1,0:T(8,128)(2,1)S(1)}, u32[]{:S(2)}, u32[]{:S(2)}) collective-permute-start(bf16[192,256]{1,0:T(8,128)(2,1)S(1)} %copy-done.8), channel_id=1, source_target_pairs={{0,8},{8,0},{1,9},{9,1},{2,10},{10,2},{3,11},{11,3},{4,12},{12,4},... | collective-permute-start | bytes 294920 | tf_op jit(solution)/shard_map/ppermute | solution.py:26
  111.5 23.9 %all-to-all-start.4 = ((bf16[16,48,128]{2,1,0:T(8,128)(2,1)}), bf16[16,48,128]{2,1,0:T(8,128)(2,1)S(1)}, u32[]{:S(2)}, u32[]{:S(2)}) async-start(bf16[16,48,128]{2,1,0:T(8,128)(2,1)} %bitcast.7), calls=%async_computation.4 | async-start | bytes 393216 | tf_op jit(solution)/shard_map/all_to_all | solution.py:331
  123.0 9.0 %collective-permute-start.11 = (bf16[256,1024]{1,0:T(8,128)(2,1)S(1)}, bf16[256,1024]{1,0:T(8,128)(2,1)S(1)}, u32[]{:S(2)}, u32[]{:S(2)}) collective-permute-start(bf16[256,1024]{1,0:T(8,128)(2,1)S(1)} %collective-permute-done.10.after.down_y), channel_id=1, source_target_pairs={{0,8},{8,0},{1,9},{9,1},{2,10},{10,2},{3,11},{11,3},{4,12},{12,4},... | collective-permute-start | bytes 1572872 | tf_op jit(solution)/shard_map/ppermute | solution.py:26
  137.8 8.5 %collective-permute-start.12 = (bf16[96,1024]{1,0:T(8,128)(2,1)S(1)}, bf16[96,1024]{1,0:T(8,128)(2,1)S(1)}, u32[]{:S(2)}, u32[]{:S(2)}) collective-permute-start(bf16[96,1024]{1,0:T(8,128)(2,1)S(1)} %shard_map.117.out), channel_id=1, source_target_pairs={{0,256},{256,0},{1,257},{257,1},{2,258},{258,2},{3,259},{259,3},{4... | collective-permute-start | bytes 589832 | tf_op jit(solution)/shard_map/ppermute | solution.py:26
  142.0 14.3 %all-to-all-start.5 = ((bf16[16,24,256]{2,1,0:T(8,128)(2,1)}), bf16[16,24,256]{2,1,0:T(8,128)(2,1)S(1)}, u32[]{:S(2)}, u32[]{:S(2)}) async-start(bf16[16,24,256]{2,1,0:T(8,128)(2,1)} %bitcast.9), calls=%async_computation.5 | async-start | bytes 393216 | tf_op jit(solution)/shard_map/all_to_all | solution.py:347
  146.3 19.1 %collective-permute-start.13 = (bf16[192,1024]{1,0:T(8,128)(2,1)S(1)}, bf16[192,1024]{1,0:T(8,128)(2,1)S(1)}, u32[]{:S(2)}, u32[]{:S(2)}) collective-permute-start(bf16[192,1024]{1,0:T(8,128)(2,1)S(1)} %pad_maximum_fusion), channel_id=1, source_target_pairs={{0,8},{8,0},{1,9},{9,1},{2,10},{10,2},{3,11},{11,3},{4,12},{12,4},... | collective-permute-start | bytes 1179656 | tf_op jit(solution)/shard_map/ppermute | solution.py:26
  157.3 8.0 %copy-start.6 = (s32[384]{0:T(512)S(1)}, s32[384]{0:T(512)}, u32[]{:S(2)}) copy-start(s32[384]{0:T(512)} %ids.1) | copy-start | bytes 4612
  157.4 16.6 %all-to-all-start.6 = ((bf16[16,48,256]{2,1,0:T(8,128)(2,1)}), bf16[16,48,256]{2,1,0:T(8,128)(2,1)S(1)}, u32[]{:S(2)}, u32[]{:S(2)}) async-start(bf16[16,48,256]{2,1,0:T(8,128)(2,1)} %bitcast.11), calls=%async_computation.6 | async-start | bytes 786432 | tf_op jit(solution)/shard_map/all_to_all | solution.py:360
  173.9 0.7 copy-start.9

commit v5 on v4

--- a/solution.py
+++ b/solution.py
@@ -47,8 +47,7 @@
 
 
 def pick(q, j):
-    s = 12 * (q >> 1) + j
-    return (q & 1) * 128 + s + 2 * ((s * 43) >> 8)
+    return (q & 1) * 96 + (q >> 1) * 12 + j
 
 
 def fan(q, j):
@@ -85,18 +84,40 @@
     return copy
 
 
+def copies_kernel(table, out, buffer, sems):
+    count, width = table.shape
+    row = lax.broadcasted_iota(jnp.int32, (8 * count, count), 0)
+    column = lax.broadcasted_iota(jnp.int32, (8 * count, count), 1)
+    total = None
+    for n in range(8):
+        place = jnp.where(row == 8 * column + n, 1.0, 0.0).astype(bf16)
+        term = product(place, table[:, 128 * n : 128 * n + 128])
+        total = term if total is None else total + term
+    buffer[...] = total.astype(bf16)
+    writes = [start(buffer, out.at[48 * i : 48 * i + 48], sems.at[i]) for i in range(NZ)]
+    for write in writes:
+        write.wait()
+
+
 def gates_kernel(rows, rows_y, *rest):
-    own, theirs, (inputs, out, slots, buffer, in_sems, out_sems) = rest[:4], rest[4:8], rest[8:]
-    copies = [start(own[k], slots.at[k], in_sems.at[k]) for k in range(4)]
+    weights, (inputs, out, slots, buffer, in_sems, out_sems) = rest[:8], rest[8:]
+    copies = [start(weights[k], slots.at[k], in_sems.at[k]) for k in range(8)]
     units = slots.shape[2]
-    both = jnp.concatenate([rows[...], rows_y[...]], axis=0)
-    inputs[...] = moved(192, 256, pick, both)
-    others = [product(inputs[...], theirs[k][...]).astype(bf16) for k in range(4)]
+    offset = lax.broadcasted_iota(jnp.int32, (96, 768), 1)
+    offset = offset - 8 * lax.broadcasted_iota(jnp.int32, (96, 768), 0)
+    places = [jnp.where(offset == n, 1.0, 0.0).astype(bf16) for n in range(8)]
+    lines = [
+        jnp.concatenate([product(place, part[...]).astype(bf16) for place in places], axis=1)
+        for part in (rows, rows_y)
+    ]
+    inputs[...] = moved(192, 192, pick, jnp.concatenate(lines, axis=0))
     writes = []
     for k in range(4):
-        copies[k].wait()
-        mine = product(inputs[...], slots[k]).astype(bf16)
-        buffer[k] = moved(384, 384, fan, jnp.concatenate([mine, others[k]], axis=0))
+        copies[2 * k].wait()
+        mine = product(inputs[...], slots[2 * k]).astype(bf16)
+        copies[2 * k + 1].wait()
+        others = product(inputs[...], slots[2 * k + 1]).astype(bf16)
+        buffer[k] = moved(384, 384, fan, jnp.concatenate([mine, others], axis=0))
         target = out.at[:, k * units : (k + 1) * units]
         writes.append(start(buffer.at[k], target, out_sems.at[k]))
     for write in writes:
@@ -149,7 +170,7 @@
         write.wait()
 
 
-def sum_kernel(parts, after, after_too, out, buffer, sems):
+def sum_kernel(parts, after, out, buffer, sems):
     total = parts[0:48].astype(f32)
     for i in range(1, NZ):
         total = total + parts[48 * i : 48 * i + 48].astype(f32)
@@ -167,7 +188,7 @@
     return jnp.concatenate(lines, axis=0)
 
 
-def cot_kernel(blocks, down, down_x, down_y, down_yx, out, slot, buffer, in_sem, out_sems):
+def cot_kernel(blocks, down, down_x, down_y, down_yx, after, out, slot, buffer, in_sem, out_sems):
     copy = start(down, slot, in_sem)
     yh = lax.axis_index(YH)
     tan_out = whole(blocks)
@@ -263,22 +284,28 @@
     scale = float(tokens) ** (-0.5)
     dots = 2 * 192 * width * units
 
-    rows = jnp.pad(table, ((0, 8 - own_count), (0, 0)))
-    rows = jnp.broadcast_to(rows[None], (NZ,) + rows.shape)
-    rows = lax.all_to_all(rows, Z, 0, 0).reshape(NZ * 8, width)
+    (rows,) = call(
+        copies_kernel,
+        2,
+        0,
+        [(table, VMEM)],
+        [((768, 128), bf16, HBM)],
+        [pltpu.VMEM((48, 128), bf16), DMA((NZ,))],
+    )
+    rows = lax.all_to_all(rows.reshape(NZ, 48, 128), Z, 0, 0).reshape(768, 128)
     gates = (gate_weight, up_weight, gate_probe, up_probe)
     gates_x = [swap(w, CORE) for w in gates]
     rows_y = swap(rows, YH)
     inputs, partials = call(
         gates_kernel,
-        20,
+        60,
         8 * dots,
-        [(rows, VMEM), (rows_y, VMEM)] + [(w, HBM) for w in gates] + [(w, VMEM) for w in gates_x],
+        [(rows, VMEM), (rows_y, VMEM)] + [(w, HBM) for both in zip(gates, gates_x) for w in both],
         [((192, width), bf16, VMEM), ((384, 4 * units), bf16, HBM)],
         [
-            pltpu.VMEM((4, width, units), bf16),
+            pltpu.VMEM((8, width, units), bf16),
             pltpu.VMEM((4, 384, units), bf16),
-            DMA((4,)),
+            DMA((8,)),
             DMA((4,)),
         ],
     )
@@ -324,7 +351,7 @@
         sum_kernel,
         4,
         0,
-        [(parts, VMEM), (down_y, ANY), (hidden_core, ANY)],
+        [(parts, VMEM), (down_y, ANY)],
         [((768, 128), bf16, HBM)],
         [pltpu.VMEM((48, 128), bf16), DMA((NZ,))],
     )
@@ -335,7 +362,10 @@
         cot_kernel,
         14,
         4 * dots,
-        [(blocks, VMEM), (down_weight, HBM), (down_x, VMEM), (down_y, VMEM), (down_yx, VMEM)],
+        [
+            (blocks, VMEM), (down_weight, HBM), (down_x, VMEM),
+            (down_y, VMEM), (down_yx, VMEM), (hidden_core, ANY),
+        ],
         [((384, units), bf16, HBM)],
         [
             pltpu.VMEM((units, width), bf16),
@@ -346,7 +376,7 @@
     )
     parts = lax.all_to_all(cot.reshape(16, 24, units), (YH,) + DP, 0, 0).reshape(384, units)
     (out,) = call(
-        whole_kernel, 4, 0, [(blocks, VMEM), (cot, ANY)], [((96, width), bf16, VMEM)]
+        whole_kernel, 4, 100 * dots, [(blocks, VMEM), (cot, ANY)], [((96, width), bf16, VMEM)]
     )
     out_y = swap(out, YH)
     (spread,) = call(

time: 179 us -> 175 us (0.978)
  starting transfers between devices: 124 us -> 117 us
  Pallas kernels: 16.9 us -> 20.4 us
  local copies, waits for them, and re-layouts: 5.39 us -> 2.17 us
  waiting for transfers between devices: 30.3 us -> 33.3 us
    ppermute x14, waiting for transfers between devices: 9.81 us -> 15.5 us  [swap(): return lax.ppermute(value, axis, [(0, 1), (1, 0)])]
    ppermute x14, starting transfers between devices: 65.2 us -> 59.5 us  [swap(): return lax.ppermute(value, axis, [(0, 1), (1, 0)])]
    pallas_call x10 -> x11, Pallas kernels: 16.9 us -> 20.4 us  [call(): pl.pallas_call(kernel, out_shape=[jax.ShapeDtypeStruct(s, t) for s, t, _...]
    all_to_all x1, waiting for transfers between devices: 3.34 us -> 1.34 us  [local(): lax.all_to_all(spread.reshape(NZ, 48, 128), Z, 0, 0).reshape(768, 128)]
    unnamed x20 -> x28, local copies, waits for them, and re-layouts: 3.88 us -> 2.17 us
where the time goes in v5:
time: 175 us; the launch traced here: 174 us
  starting transfers between devices  117 us (67%)
  waiting for transfers between devices  33.3 us (19%)
  Pallas kernels  20.4 us (12%)
  local copies, waits for them, and re-layouts  2.17 us (1%)
    ppermute x14, starting transfers between devices, swap(): return lax.ppermute(value, axis, [(0, 1), (1, 0)])  59.5 us
    pallas_call x11, Pallas kernels, call(): pl.pallas_call(kernel, out_shape=[jax.ShapeDtypeStruct(s, t) for s, t, _...  20.4 us
    all_to_all x1, starting transfers between devices, local(): rows = lax.all_to_all(rows.reshape(NZ, 48, 128), Z, 0, 0).reshape(768, 128)  15.8 us
    ppermute x14, waiting for transfers between devices, swap(): return lax.ppermute(value, axis, [(0, 1), (1, 0)])  15.5 us
    all_to_all x1, starting transfers between devices, local(): lax.all_to_all(spread.reshape(NZ, 48, 128), Z, 0, 0).reshape(768, 128)  11.3 us
    all_to_all x1, starting transfers between devices, local(): lax.all_to_all(spread.reshape(16, 48, units), (CORE,) + DP, 0, 0)  8.13 us
    all_to_all x1, starting transfers between devices, local(): lax.all_to_all(blocks.reshape(NZ, 48, 128), Z, 0, 0).reshape(768, 128)  7.14 us
    all_to_all x1, waiting for transfers between devices, local(): lax.all_to_all(spread.reshape(16, 48, units), (CORE,) + DP, 0, 0)  6.58 us
  transfers between devices with their start and end apart: 21, of which 8 were waited for; matrix products, arithmetic and copies ran while one was open for 0% of the time, Pallas kernels for 2%

profile of v5, /device:TPU:1, one launch (start us, length us, event | category | flops | bytes accessed | tf_op | source)
XLA Modules:
  0.0 174.0 jit_solution(3198220885006512704)
XLA Ops:
  2.3 15.8 %all-to-all-start = ((bf16[16,48,128]{2,1,0:T(8,128)(2,1)}), bf16[16,48,128]{2,1,0:T(8,128)(2,1)S(1)}, u32[]{:S(2)}, u32[]{:S(2)}) async-start(bf16[16,48,128]{2,1,0:T(8,128)(2,1)} %bitcast), calls=%async_computation | async-start | bytes 393216 | tf_op jit(solution)/shard_map/all_to_all | solution.py:295
  18.1 2.9 %collective-permute-start.1 = (bf16[1024,256]{1,0:T(8,128)(2,1)S(1)}, bf16[1024,256]{1,0:T(8,128)(2,1)S(1)}, u32[]{:S(2)}, u32[]{:S(2)}) collective-permute-start(bf16[1024,256]{1,0:T(8,128)(2,1)S(1)} %copy-done.8), channel_id=1, source_target_pairs={{0,8},{8,0},{1,9},{9,1},{2,10},{10,2},{3,11},{11,3},{4,12},{12,4},... | collective-permute-start | bytes 1572872 | tf_op jit(solution)/shard_map/ppermute | solution.py:26
  21.0 1.9 %collective-permute-start.2 = (bf16[1024,256]{1,0:T(8,128)(2,1)}, bf16[1024,256]{1,0:T(8,128)(2,1)S(1)}, u32[]{:S(2)}, u32[]{:S(2)}) collective-permute-start(bf16[1024,256]{1,0:T(8,128)(2,1)} %rest_2_.1), channel_id=1, source_target_pairs={{0,8},{8,0},{1,9},{9,1},{2,10},{10,2},{3,11},{11,3},{4,12},{12,4},... | collective-permute-start | bytes 1572872 | tf_op jit(solution)/shard_map/ppermute | solution.py:26
  22.9 2.4 %collective-permute-start.3 = (bf16[1024,256]{1,0:T(8,128)(2,1)}, bf16[1024,256]{1,0:T(8,128)(2,1)S(1)}, u32[]{:S(2)}, u32[]{:S(2)}) collective-permute-start(bf16[1024,256]{1,0:T(8,128)(2,1)} %rest_4_.1), channel_id=1, source_target_pairs={{0,8},{8,0},{1,9},{9,1},{2,10},{10,2},{3,11},{11,3},{4,12},{12,4},... | collective-permute-start | bytes 1572872 | tf_op jit(solution)/shard_map/ppermute | solution.py:26
  25.3 1.9 %collective-permute-start.4 = (bf16[1024,256]{1,0:T(8,128)(2,1)}, bf16[1024,256]{1,0:T(8,128)(2,1)S(1)}, u32[]{:S(2)}, u32[]{:S(2)}) collective-permute-start(bf16[1024,256]{1,0:T(8,128)(2,1)} %rest_6_.1), channel_id=1, source_target_pairs={{0,8},{8,0},{1,9},{9,1},{2,10},{10,2},{3,11},{11,3},{4,12},{12,4},... | collective-permute-start | bytes 1572872 | tf_op jit(solution)/shard_map/ppermute | solution.py:26
  27.3 3.4 %all-to-all-done = bf16[16,48,128]{2,1,0:T(8,128)(2,1)S(1)} async-done(((bf16[16,48,128]{2,1,0:T(8,128)(2,1)}), bf16[16,48,128]{2,1,0:T(8,128)(2,1)S(1)}, u32[]{:S(2)}, u32[]{:S(2)}) %all-to-all-start) | async-done | bytes 196640 | tf_op jit(solution)/shard_map/all_to_all | solution.py:295
  30.7 4.8 %collective-permute-start = (bf16[768,128]{1,0:T(8,128)(2,1)S(1)}, bf16[768,128]{1,0:T(8,128)(2,1)S(1)}, u32[]{:S(2)}, u32[]{:S(2)}) collective-permute-start(bf16[768,128]{1,0:T(8,128)(2,1)S(1)} %bitcast.21), channel_id=1, source_target_pairs={{0,256},{256,0},{1,257},{257,1},{2,258},{258,2},{3,259},{259,3},{4... | collective-permute-start | bytes 589832 | tf_op jit(solution)/shard_map/ppermute | solution.py:26
  35.6 3.0 %collective-permute-done.rows_y = bf16[768,128]{1,0:T(8,128)(2,1)S(1)} collective-permute-done((bf16[768,128]{1,0:T(8,128)(2,1)S(1)}, bf16[768,128]{1,0:T(8,128)(2,1)S(1)}, u32[]{:S(2)}, u32[]{:S(2)}) %collective-permute-start) | collective-permute-done | bytes 196640 | tf_op jit(solution)/shard_map/ppermute | solution.py:26
  39.3 7.6 %shard_map.112 = (bf16[192,1024]{1,0:T(8,128)(2,1)}, bf16[384,1024]{1,0:T(8,128)(2,1)}) custom-call(bf16[768,128]{1,0:T(8,128)(2,1)} %bitcast.22, bf16[768,128]{1,0:T(8,128)(2,1)} %copy-done.13, bf16[1024,256]{1,0:T(8,128)(2,1)} %rest_0_.1, bf16[1024,256]{1,0:T(8,128)(2,1)} %copy-done.9, bf16[1024,256]{1,0:T(8,128)(2,1)} %rest_2_.1, ...), custom_call_target="tpu_custom_call" | custom-call | flops 805306368 | bytes 5767168 | tf_op jit(solution)/shard_map/pallas_call | solution.py:269
  46.9 5.2 %all-to-all-start.1 = ((bf16[8,48,1024]{2,1,0:T(8,128)(2,1)}), bf16[8,48,1024]{2,1,0:T(8,128)(2,1)S(1)}, u32[]{:S(2)}, u32[]{:S(2)}) async-start(bf16[8,48,1024]{2,1,0:T(8,128)(2,1)} %bitcast.23), calls=%async_computation.1 | async-start | bytes 1572864 | tf_op jit(solution)/shard_map/all_to_all | solution.py:313
  52.1 8.2 %collective-permute-start.5 = (bf16[192,1024]{1,0:T(8,128)(2,1)}, bf16[192,1024]{1,0:T(8,128)(2,1)S(1)}, u32[]{:S(2)}, u32[]{:S(2)}) collective-permute-start(bf16[192,1024]{1,0:T(8,128)(2,1)} %get-tuple-element.18.inputs), channel_id=1, source_target_pairs={{0,8},{8,0},{1,9},{9,1},{2,10},{10,2},{3,11},{11,3},{4,12},{12,4},... | collective-permute-start | bytes 1179656 | tf_op jit(solution)/shard_map/ppermute | solution.py:26
  60.3 1.9 %collective-permute-start.7 = (bf16[256,1024]{1,0:T(8,128)(2,1)S(1)}, bf16[256,1024]{1,0:T(8,128)(2,1)S(1)}, u32[]{:S(2)}, u32[]{:S(2)}) collective-permute-start(bf16[256,1024]{1,0:T(8,128)(2,1)S(1)} %copy-done.1), channel_id=1, source_target_pairs={{0,8},{8,0},{1,9},{9,1},{2,10},{10,2},{3,11},{11,3},{4,12},{12,4},... | collective-permute-start | bytes 1572872 | tf_op jit(solution)/shard_map/ppermute | solution.py:26
  62.2 2.4 %collective-permute-start.6 = (bf16[256,1024]{1,0:T(8,128)(2,1)S(1)}, bf16[256,1024]{1,0:T(8,128)(2,1)S(1)}, u32[]{:S(2)}, u32[]{:S(2)}) collective-permute-start(bf16[256,1024]{1,0:T(8,128)(2,1)S(1)} %copy-done), channel_id=1, source_target_pairs={{0,8},{8,0},{1,9},{9,1},{2,10},{10,2},{3,11},{11,3},{4,12},{12,4},... | collective-permute-start | bytes 1572872 | tf_op jit(solution)/shard_map/ppermute | solution.py:26
  65.6 5.4 %all-to-all-start.2 = ((bf16[8,48,512]{2,1,0:T(8,128)(2,1)}), bf16[8,48,512]{2,1,0:T(8,128)(2,1)S(1)}, u32[]{:S(2)}, u32[]{:S(2)}) async-start(bf16[8,48,512]{2,1,0:T(8,128)(2,1)} %bitcast.4), calls=%async_computation.2 | async-start | bytes 786432 | tf_op jit(solution)/shard_map/all_to_all | solution.py:323
  71.0 6.5 %all-to-all-done.2 = bf16[8,48,512]{2,1,0:T(8,128)(2,1)S(1)} async-done(((bf16[8,48,512]{2,1,0:T(8,128)(2,1)}), bf16[8,48,512]{2,1,0:T(8,128)(2,1)S(1)}, u32[]{:S(2)}, u32[]{:S(2)}) %all-to-all-start.2) | async-done | bytes 393248 | tf_op jit(solution)/shard_map/all_to_all | solution.py:323
  78.6 4.5 %collective-permute-start.9 = (bf16[96,1024]{1,0:T(8,128)(2,1)S(1)}, bf16[96,1024]{1,0:T(8,128)(2,1)S(1)}, u32[]{:S(2)}, u32[]{:S(2)}) collective-permute-start(bf16[96,1024]{1,0:T(8,128)(2,1)S(1)} %get-tuple-element.23), channel_id=1, source_target_pairs={{0,256},{256,0},{1,257},{257,1},{2,258},{258,2},{3,259},{259,3},{4... | collective-permute-start | bytes 589832 | tf_op jit(solution)/shard_map/ppermute | solution.py:26
  83.2 3.4 %collective-permute-done.9.received = bf16[96,1024]{1,0:T(8,128)(2,1)S(1)} collective-permute-done((bf16[96,1024]{1,0:T(8,128)(2,1)S(1)}, bf16[96,1024]{1,0:T(8,128)(2,1)S(1)}, u32[]{:S(2)}, u32[]{:S(2)}) %collective-permute-start.9) | collective-permute-done | bytes 196640 | tf_op jit(solution)/shard_map/ppermute | solution.py:26
  87.3 7.1 %all-to-all-start.3 = ((bf16[16,48,128]{2,1,0:T(8,128)(2,1)}), bf16[16,48,128]{2,1,0:T(8,128)(2,1)S(1)}, u32[]{:S(2)}, u32[]{:S(2)}) async-start(bf16[16,48,128]{2,1,0:T(8,128)(2,1)} %bitcast.6), calls=%async_computation.3 | async-start | bytes 393216 | tf_op jit(solution)/shard_map/all_to_all | solution.py:347
  94.4 4.5 %collective-permute-start.10 = (bf16[256,1024]{1,0:T(8,128)(2,1)S(1)}, bf16[256,1024]{1,0:T(8,128)(2,1)S(1)}, u32[]{:S(2)}, u32[]{:S(2)}) collective-permute-start(bf16[256,1024]{1,0:T(8,128)(2,1)S(1)} %copy-done), channel_id=1, source_target_pairs={{0,256},{256,0},{1,257},{257,1},{2,258},{258,2},{3,259},{259,3},{4... | collective-permute-start | bytes 1572872 | tf_op jit(solution)/shard_map/ppermute | solution.py:26
  99.0 7.8 %collective-permute-done.10.after.down_y = bf16[256,1024]{1,0:T(8,128)(2,1)S(1)} collective-permute-done((bf16[256,1024]{1,0:T(8,128)(2,1)S(1)}, bf16[256,1024]{1,0:T(8,128)(2,1)S(1)}, u32[]{:S(2)}, u32[]{:S(2)}) %collective-permute-start.10) | collective-permute-done | bytes 524320 | tf_op jit(solution)/shard_map/ppermute | solution.py:26
  107.6 11.3 %all-to-all-start.4 = ((bf16[16,48,128]{2,1,0:T(8,128)(2,1)}), bf16[16,48,128]{2,1,0:T(8,128)(2,1)S(1)}, u32[]{:S(2)}, u32[]{:S(2)}) async-start(bf16[16,48,128]{2,1,0:T(8,128)(2,1)} %bitcast.8), calls=%async_computation.4 | async-start | bytes 393216 | tf_op jit(solution)/shard_map/all_to_all | solution.py:358
  119.0 7.8 %collective-permute-start.11 = (bf16[256,1024]{1,0:T(8,128)(2,1)S(1)}, bf16[256,1024]{1,0:T(8,128)(2,1)S(1)}, u32[]{:S(2)}, u32[]{:S(2)}) collective-permute-start(bf16[256,1024]{1,0:T(8,128)(2,1)S(1)} %collective-permute-done.10.after.down_y), channel_id=1, source_target_pairs={{0,8},{8,0},{1,9},{9,1},{2,10},{10,2},{3,11},{11,3},{4,12},{12,4},... | collective-permute-start | bytes 1572872 | tf_op jit(solution)/shard_map/ppermute | solution.py:26
  126.8 1.9 %collective-permute-start.8 = (bf16[192,256]{1,0:T(8,128)(2,1)S(1)}, bf16[192,256]{1,0:T(8,128)(2,1)S(1)}, u32[]{:S(2)}, u32[]{:S(2)}) collective-permute-start(bf16[192,256]{1,0:T(8,128)(2,1)S(1)} %copy-done.5), channel_id=1, source_target_pairs={{0,8},{8,0},{1,9},{9,1},{2,10},{10,2},{3,11},{11,3},{4,12},{12,4},... | collective-permute-start | bytes 294920 | tf_op jit(solution)/shard_map/ppermute | solution.py:26
  130.0 1.3 all-to-all-done.4
  131.4 2.3 %shard_map.117.after = bf16[384,256]{1,0:T(8,128)(2,1)} custom-call(bf16[768,128]{1,0:T(8,128)(2,1)S(1)} %bitcast.16, bf16[256,1024]{1,0:T(8,128)(2,1)S(1)} %copy-done, bf16[256,1024]{1,0:T(8,128)(2,1)S(1)} %collective-permute-done.6.down_x, bf16[256,1024]{1,0:T(8,128)(2,1)S(1)} %collective-permute-done.10.after.down_y, ...), custom_call_target="tpu_custom_call" | custom-call | flops 402653184 | bytes 2490368 | tf_op jit(solution)/shard_map/pallas_call | solution.py:269
  133.7 4.5 %collective-permute-start.12 = (bf16[96,1024]{1,0:T(8,128)(2,1)S(1)}, bf16[96,1024]{1,0:T(8,128)(2,1)S(1)}, u32[]{:S(2)}, u32[]{:S(2)}) collective-permute-start(bf16[96,1024]{1,0:T(8,128)(2,1)S(1)} %shard_map.118.out), channel_id=1, source_target_pairs={{0,256},{256,0},{1,257},{257,1},{2,258},{258,2},{3,259},{259,3},{4... | collective-permute-start | bytes 589832 | tf_op jit(solution)/shard_map/ppermute | solution.py:26
  138.3 4.5 %all-to-all-start.5 = ((bf16[16,24,256]{2,1,0:T(8,128)(2,1)}), bf16[16,24,256]{2,1,0:T(8,128)(2,1)S(1)}, u32[]{:S(2)}, u32[]{:S(2)}) async-start(bf16[16,24,256]{2,1,0:T(8,128)(2,1)} %bitcast.10), calls=%async_computation.5 | async-start | bytes 393216 | tf_op jit(solution)/shard_map/all_to_all | solution.py:377
  142.8 9.8 %collective-permute-start.13 = (bf16[192,1024]{1,0:T(8,128)(2,1)S(1)}, bf16[192,1024]{1,0:T(8,128)(2,1)S(1)}, u32[]{:S(2)}, u32[]{:S(2)}) collective-permute-start(bf16[192,1024]{1,0:T(8,128)(2,1)S(1)} %pad_maximum_fusion), channel_id=1, source_target_pairs={{0,8},{8,0},{1,9},{9,1},{2,10},{10,2},{3,11},{11,3},{4,12},{12,4},... | collective-permute-start | bytes 1179656 | tf_op jit(solution)/shard_map/ppermute | solution.py:26
  153.7 8.1 %all-to-all-start.6 = ((bf16[16,48,256]{2,1,0:T(8,128)(2,1)}), bf16[16,48,256]{2,1,0:T(8,128)(2,1)S(1)}, u32[]{:S(2)}, u32[]{:S(2)}) async-start(bf16[16,48,256]{2,1,0:T(8,128)(2,1)} %bitcast.12), calls=%async_computation.6 | async-start | bytes 786432 | tf_op jit(solution)/shard_map/all_to_all | solution.py:390
  161.8 1.9 %shard_map.119 = (bf16[256,1024]{1,0:T(8,128)(2,1)}, bf16[6,1024]{1,0:T(8,128)(2,1)}) custom-call(s32[384]{0:T(512)S(1)} %copy-done.3, bf16[192,256]{1,0:T(8,128)(2,1)S(1)} %get-tuple-element.20.hidden, bf16[192,256]{1,0:T(8,128)(2,1)S(1)} %collective-permute-done.8.after.hidden_core, bf16[96,1024]{1,0:T(8,128)(2,1)S(1)} %shard_map.118.out, ...), custom_call_target="tpu_custom_call" | custom-call | flops 201326592 | bytes 1521152 | tf_op jit(solution)/shard_map/pallas_call | solution.py:269
  163.8 6.6 %all-to-all-done.6 = bf16[16,48,256]{2,1,0:T(8,128)(2,1)S(1)} async-done(((bf16[16,48,256]{2,1,0:T(8,128)(2,1)}), bf16[16,48,256]{2,1,0:T(8,128)(2,1)S(1)}, u32[]{:S(2)}, u32[]{:S(2)}) %all-to-all-start.6) | async-done | bytes 393248 | tf_op jit(solution)/shard_map/all_to_all | solution.py:390
  171.1 3.0 %shard_map.121 = (bf16[1024,256]{1,0:T(8,128)(2,1)}, bf16[1024,256]{1,0:T(8,128)(2,1)}) custom-call(bf16[768,256]{1,0:T(8,128)(2,1)S(1)} %bitcast.20, bf16[192,1024]{1,0:T(8,128)(2,1)} %get-tuple-element.18.inputs, bf16[192,1024]{1,0:T(8,128)(2,1)S(1)} %collective-permute-done.5.after.inputs_x, bf16[6,1024]{1,0:T(8,128)(2,1)S(1)} %copy-done.6), custom_call_target="tpu_custom_call" | custom-call | flops 402653184 | bytes 2228224 | tf_op jit(solution)/shard_map/pallas_call | solution.py:269
  (50 shorter events, 9.1 us)
Async XLA Ops:
  1.3 16.8 %copy-start.8 = (bf16[1024,256]{1,0:T(8,128)(2,1)S(1)}, bf16[1024,256]{1,0:T(8,128)(2,1)}, u32[]{:S(2)}) copy-start(bf16[1024,256]{1,0:T(8,128)(2,1)} %rest_0_.1) | copy-start | bytes 1572868
  2.3 28.3 %all-to-all-start = ((bf16[16,48,128]{2,1,0:T(8,128)(2,1)}), bf16[16,48,128]{2,1,0:T(8,128)(2,1)S(1)}, u32[]{:S(2)}, u32[]{:S(2)}) async-start(bf16[16,48,128]{2,1,0:T(8,128)(2,1)} %bitcast), calls=%async_computation | async-start | bytes 393216 | tf_op jit(solution)/shard_map/all_to_all | solution.py:295
  18.1 17.4 %collective-permute-start.1 = (bf16[1024,256]{1,0:T(8,128)(2,1)S(1)}, bf16[1024,256]{1,0:T(8,128)(2,1)S(1)}, u32[]{:S(2)}, u32[]{:S(2)}) collective-permute-start(bf16[1024,256]{1,0:T(8,128)(2,1)S(1)} %copy-done.8), channel_id=1, source_target_pairs={{0,8},{8,0},{1,9},{9,1},{2,10},{10,2},{3,11},{11,3},{4,12},{12,4},... | collective-permute-start | bytes 1572872 | tf_op jit(solution)/shard_map/ppermute | solution.py:26
  21.0 14.5 %collective-permute-start.2 = (bf16[1024,256]{1,0:T(8,128)(2,1)}, bf16[1024,256]{1,0:T(8,128)(2,1)S(1)}, u32[]{:S(2)}, u32[]{:S(2)}) collective-permute-start(bf16[1024,256]{1,0:T(8,128)(2,1)} %rest_2_.1), channel_id=1, source_target_pairs={{0,8},{8,0},{1,9},{9,1},{2,10},{10,2},{3,11},{11,3},{4,12},{12,4},... | collective-permute-start | bytes 1572872 | tf_op jit(solution)/shard_map/ppermute | solution.py:26
  22.9 12.6 %collective-permute-start.3 = (bf16[1024,256]{1,0:T(8,128)(2,1)}, bf16[1024,256]{1,0:T(8,128)(2,1)S(1)}, u32[]{:S(2)}, u32[]{:S(2)}) collective-permute-start(bf16[1024,256]{1,0:T(8,128)(2,1)} %rest_4_.1), channel_id=1, source_target_pairs={{0,8},{8,0},{1,9},{9,1},{2,10},{10,2},{3,11},{11,3},{4,12},{12,4},... | collective-permute-start | bytes 1572872 | tf_op jit(solution)/shard_map/ppermute | solution.py:26
  25.3 10.2 %collective-permute-start.4 = (bf16[1024,256]{1,0:T(8,128)(2,1)}, bf16[1024,256]{1,0:T(8,128)(2,1)S(1)}, u32[]{:S(2)}, u32[]{:S(2)}) collective-permute-start(bf16[1024,256]{1,0:T(8,128)(2,1)} %rest_6_.1), channel_id=1, source_target_pairs={{0,8},{8,0},{1,9},{9,1},{2,10},{10,2},{3,11},{11,3},{4,12},{12,4},... | collective-permute-start | bytes 1572872 | tf_op jit(solution)/shard_map/ppermute | solution.py:26
  30.7 7.9 %copy-start.7 = (bf16[16,48,128]{2,1,0:T(8,128)(2,1)}, bf16[16,48,128]{2,1,0:T(8,128)(2,1)S(1)}, u32[]{:S(2)}) copy-start(bf16[16,48,128]{2,1,0:T(8,128)(2,1)S(1)} %all-to-all-done) | copy-start | bytes 589828
  30.7 7.9 %collective-permute-start = (bf16[768,128]{1,0:T(8,128)(2,1)S(1)}, bf16[768,128]{1,0:T(8,128)(2,1)S(1)}, u32[]{:S(2)}, u32[]{:S(2)}) collective-permute-start(bf16[768,128]{1,0:T(8,128)(2,1)S(1)} %bitcast.21), channel_id=1, source_target_pairs={{0,256},{256,0},{1,257},{257,1},{2,258},{258,2},{3,259},{259,3},{4... | collective-permute-start | bytes 589832 | tf_op jit(solution)/shard_map/ppermute | solution.py:26
  35.5 3.1 %copy-start.9 = (bf16[1024,256]{1,0:T(8,128)(2,1)}, bf16[1024,256]{1,0:T(8,128)(2,1)S(1)}, u32[]{:S(2)}) copy-start(bf16[1024,256]{1,0:T(8,128)(2,1)S(1)} %collective-permute-done.1.rest_1_) | copy-start | bytes 1572868
  35.5 3.1 %copy-start.10 = (bf16[1024,256]{1,0:T(8,128)(2,1)}, bf16[1024,256]{1,0:T(8,128)(2,1)S(1)}, u32[]{:S(2)}) copy-start(bf16[1024,256]{1,0:T(8,128)(2,1)S(1)} %collective-permute-done.2.rest_3_) | copy-start | bytes 1572868
  35.5 3.0 %copy-start.11 = (bf16[1024,256]{1,0:T(8,128)(2,1)}, bf16[1024,256]{1,0:T(8,128)(2,1)S(1)}, u32[]{:S(2)}) copy-start(bf16[1024,256]{1,0:T(8,128)(2,1)S(1)} %collective-permute-done.3.rest_5_) | copy-start | bytes 1572868
  35.6 3.0 %copy-start.12 = (bf16[1024,256]{1,0:T(8,128)(2,1)}, bf16[1024,256]{1,0:T(8,128)(2,1)S(1)}, u32[]{:S(2)}) copy-start(bf16[1024,256]{1,0:T(8,128)(2,1)S(1)} %collective-permute-done.4.rest_7_) | copy-start | bytes 1572868
  46.9 13.4 %copy-start.1 = (bf16[256,1024]{1,0:T(8,128)(2,1)S(1)}, bf16[256,1024]{1,0:T(8,128)(2,1)}, u32[]{:S(2)}) copy-start(bf16[256,1024]{1,0:T(8,128)(2,1)} %probe.1) | copy-start | bytes 1572868
  46.9 15.3 %copy-start = (bf16[256,1024]{1,0:T(8,128)(2,1)S(1)}, bf16[256,1024]{1,0:T(8,128)(2,1)}, u32[]{:S(2)}) copy-start(bf16[256,1024]{1,0:T(8,128)(2,1)} %down.3) | copy-start | bytes 1572868
  46.9 17.7 %all-to-all-start.1 = ((bf16[8,48,1024]{2,1,0:T(8,128)(2,1)}), bf16[8,48,1024]{2,1,0:T(8,128)(2,1)S(1)}, u32[]{:S(2)}, u32[]{:S(2)}) async-start(bf16[8,48,1024]{2,1,0:T(8,128)(2,1)} %bitcast.23), calls=%async_computation.1 | async-start | bytes 1572864 | tf_op jit(solution)/shard_map/all_to_all | solution.py:313
  52.1 12.5 %collective-permute-start.5 = (bf16[192,1024]{1,0:T(8,128)(2,1)}, bf16[192,1024]{1,0:T(8,128)(2,1)S(1)}, u32[]{:S(2)}, u32[]{:S(2)}) collective-permute-start(bf16[192,1024]{1,0:T(8,128)(2,1)} %get-tuple-element.18.inputs), channel_id=1, source_target_pairs={{0,8},{8,0},{1,9},{9,1},{2,10},{10,2},{3,11},{11,3},{4,12},{12,4},... | collective-permute-start | bytes 1179656 | tf_op jit(solution)/shard_map/ppermute | solution.py:26
  60.3 10.8 %collective-permute-start.7 = (bf16[256,1024]{1,0:T(8,128)(2,1)S(1)}, bf16[256,1024]{1,0:T(8,128)(2,1)S(1)}, u32[]{:S(2)}, u32[]{:S(2)}) collective-permute-start(bf16[256,1024]{1,0:T(8,128)(2,1)S(1)} %copy-done.1), channel_id=1, source_target_pairs={{0,8},{8,0},{1,9},{9,1},{2,10},{10,2},{3,11},{11,3},{4,12},{12,4},... | collective-permute-start | bytes 1572872 | tf_op jit(solution)/shard_map/ppermute | solution.py:26
  62.2 8.8 %collective-permute-start.6 = (bf16[256,1024]{1,0:T(8,128)(2,1)S(1)}, bf16[256,1024]{1,0:T(8,128)(2,1)S(1)}, u32[]{:S(2)}, u32[]{:S(2)}) collective-permute-start(bf16[256,1024]{1,0:T(8,128)(2,1)S(1)} %copy-done), channel_id=1, source_target_pairs={{0,8},{8,0},{1,9},{9,1},{2,10},{10,2},{3,11},{11,3},{4,12},{12,4},... | collective-permute-start | bytes 1572872 | tf_op jit(solution)/shard_map/ppermute | solution.py:26
  65.6 12.0 %all-to-all-start.2 = ((bf16[8,48,512]{2,1,0:T(8,128)(2,1)}), bf16[8,48,512]{2,1,0:T(8,128)(2,1)S(1)}, u32[]{:S(2)}, u32[]{:S(2)}) async-start(bf16[8,48,512]{2,1,0:T(8,128)(2,1)} %bitcast.4), calls=%async_computation.2 | async-start | bytes 786432 | tf_op jit(solution)/shard_map/all_to_all | solution.py:323
  78.6 8.7 %copy-start.4 = (bf16[192,256]{1,0:T(8,128)(2,1)}, bf16[192,256]{1,0:T(8,128)(2,1)S(1)}, u32[]{:S(2)}) copy-start(bf16[192,256]{1,0:T(8,128)(2,1)S(1)} %get-tuple-element.21) | copy-start | bytes 294916
  78.6 7.9 %collective-permute-start.9 = (bf16[96,1024]{1,0:T(8,128)(2,1)S(1)}, bf16[96,1024]{1,0:T(8,128)(2,1)S(1)}, u32[]{:S(2)}, u32[]{:S(2)}) collective-permute-start(bf16[96,1024]{1,0:T(8,128)(2,1)S(1)} %get-tuple-element.23), channel_id=1, source_target_pairs={{0,256},{256,0},{1,257},{257,1},{2,258},{258,2},{3,259},{259,3},{4... | collective-permute-start | bytes 589832 | tf_op jit(solution)/shard_map/ppermute | solution.py:26
  87.3 19.5 %all-to-all-start.3 = ((bf16[16,48,128]{2,1,0:T(8,128)(2,1)}), bf16[16,48,128]{2,1,0:T(8,128)(2,1)S(1)}, u32[]{:S(2)}, u32[]{:S(2)}) async-start(bf16[16,48,128]{2,1,0:T(8,128)(2,1)} %bitcast.6), calls=%async_computation.3 | async-start | bytes 393216 | tf_op jit(solution)/shard_map/all_to_all | solution.py:347
  94.4 12.4 %collective-permute-start.10 = (bf16[256,1024]{1,0:T(8,128)(2,1)S(1)}, bf16[256,1024]{1,0:T(8,128)(2,1)S(1)}, u32[]{:S(2)}, u32[]{:S(2)}) collective-permute-start(bf16[256,1024]{1,0:T(8,128)(2,1)S(1)} %copy-done), channel_id=1, source_target_pairs={{0,256},{256,0},{1,257},{257,1},{2,258},{258,2},{3,259},{259,3},{4... | collective-permute-start | bytes 1572872 | tf_op jit(solution)/shard_map/ppermute | solution.py:26
  107.6 19.2 %copy-start.5 = (bf16[192,256]{1,0:T(8,128)(2,1)S(1)}, bf16[192,256]{1,0:T(8,128)(2,1)}, u32[]{:S(2)}) copy-start(bf16[192,256]{1,0:T(8,128)(2,1)} %copy-done.4) | copy-start | bytes 294916
  107.6 23.7 %all-to-all-start.4 = ((bf16[16,48,128]{2,1,0:T(8,128)(2,1)}), bf16[16,48,128]{2,1,0:T(8,128)(2,1)S(1)}, u32[]{:S(2)}, u32[]{:S(2)}) async-start(bf16[16,48,128]{2,1,0:T(8,128)(2,1)} %bitcast.8), calls=%async_computation.4 | async-start | bytes 393216 | tf_op jit(solution)/shard_map/all_to_all | solution.py:358
  119.0 9.8 %collective-permute-start.11 = (bf16[256,1024]{1,0:T(8,128)(2,1)S(1)}, bf16[256,1024]{1,0:T(8,128)(2,1)S(1)}, u32[]{:S(2)}, u32[]{:S(2)}) collective-permute-start(bf16[256,1024]{1,0:T(8,128)(2,1)S(1)} %collective-permute-done.10.after.down_y), channel_id=1, source_target_pairs={{0,8},{8,0},{1,9},{9,1},{2,10},{10,2},{3,11},{11,3},{4,12},{12,4},... | collective-permute-start | bytes 1572872 | tf_op jit(solution)/shard_map/ppermute | solution.py:26
  126.8 3.2 %collective-permute-start.8 = (bf16[192,256]{1,0:T(8,128)(2,1)S(1)}, bf16[192,256]{1,0:T(8,128)(2,1)S(1)}, u32[]{:S(2)}, u32[]{:S(2)}) collective-permute-start(bf16[192,256]{1,0:T(8,128)(2,1)S(1)} %copy-done.5), channel_id=1, source_target_pairs={{0,8},{8,0},{1,9},{9,1},{2,10},{10,2},{3,11},{11,3},{4,12},{12,4},... | collective-permute-start | bytes 294920 | tf_op jit(solution)/shard_map/ppermute | solution.py:26
  133.7 9.1 %collective-permute-start.12 = (bf16[96,1024]{1,0:T(8,128)(2,1)S(1)}, bf16[96,1024]{1,0:T(8,128)(2,1)S(1)}, u32[]{:S(2)}, u32[]{:S(2)}) collective-permute-start(bf16[96,1024]{1,0:T(8,128)(2,1)S(1)} %shard_map.118.out), channel_id=1, source_target_pairs={{0,256},{256,0},{1,257},{257,1},{2,258},{258,2},{3,259},{259,3},{4... | collective-permute-start | bytes 589832 | tf_op jit(solution)/shard_map/ppermute | solution.py:26
  138.3 14.3 %all-to-all-start.5 = ((bf16[16,24,256]{2,1,0:T(8,128)(2,1)}), bf16[16,24,256]{2,1,0:T(8,128)(2,1)S(1)}, u32[]{:S(2)}, u32[]{:S(2)}) async-start(bf16[16,24,256]{2,1,0:T(8,128)(2,1)} %bitcast.10), calls=%async_computation.5 | async-start | bytes 393216 | tf_op jit(solution)/shard_map/all_to_all | solution.py:377
  142.8 19.0 %collective-permute-start.13 = (bf16[192,1024]{1,0:T(8,128)(2,1)S(1)}, bf16[192,1024]{1,0:T(8,128)(2,1)S(1)}, u32[]{:S(2)}, u32[]{:S(2)}) collective-permute-start(bf16[192,1024]{1,0:T(8,128)(2,1)S(1)} %pad_maximum_fusion), channel_id=1, source_target_pairs={{0,8},{8,0},{1,9},{9,1},{2,10},{10,2},{3,11},{11,3},{4,12},{12,4},... | collective-permute-start | bytes 1179656 | tf_op jit(solution)/shard_map/ppermute | solution.py:26
  153.7 8.2 %copy-start.3 = (s32[384]{0:T(512)S(1)}, s32[384]{0:T(512)}, u32[]{:S(2)}) copy-start(s32[384]{0:T(512)} %ids.1) | copy-start | bytes 4612
  153.7 16.7 %all-to-all-start.6 = ((bf16[16,48,256]{2,1,0:T(8,128)(2,1)}), bf16[16,48,256]{2,1,0:T(8,128)(2,1)S(1)}, u32[]{:S(2)}, u32[]{:S(2)}) async-start(bf16[16,48,256]{2,1,0:T(8,128)(2,1)} %bitcast.12), calls=%async_computation.6 | async-start | bytes 786432 | tf_op jit(solution)/shard_map/all_to_all | solution.py:390
  (3 other events, 2.1 us)

commit v6 on v5

--- a/solution.py
+++ b/solution.py
@@ -46,16 +46,21 @@
     return product(table, values).astype(bf16)
 
 
+def halves_inside(values):
+    row = lax.broadcasted_iota(jnp.int32, (48, 48), 0)
+    column = lax.broadcasted_iota(jnp.int32, (48, 48), 1)
+    q = (row * 171) >> 11
+    source = ((q & 1) * 2 + (q >> 1)) * 12 + row - 12 * q
+    table = jnp.where(source == column, 1.0, 0.0)
+    return jnp.dot(table, values, precision=lax.Precision.HIGHEST, preferred_element_type=f32)
+
+
 def pick(q, j):
     return (q & 1) * 96 + (q >> 1) * 12 + j
 
 
-def fan(q, j):
-    return (q & 1) * 192 + (q >> 1) * 12 + j
-
-
 def by_half(q, j):
-    return ((q & 7) * 4 + ((q >> 3) & 1) * 2 + (q >> 4)) * 12 + j
+    return ((q & 7) * 4 + (q >> 4) * 2 + ((q >> 3) & 1)) * 12 + j
 
 
 def low(q, j):
@@ -99,32 +104,32 @@
         write.wait()
 
 
+def lines_kernel(rows, after, out, buffer):
+    buffer[...] = rows[...].astype(f32)
+    for n in range(8):
+        line = buffer[pl.ds(n, 96, stride=8), :]
+        out[:, 128 * n : 128 * n + 128] = line.astype(bf16)
+
+
 def gates_kernel(rows, rows_y, *rest):
     weights, (inputs, out, slots, buffer, in_sems, out_sems) = rest[:8], rest[8:]
     copies = [start(weights[k], slots.at[k], in_sems.at[k]) for k in range(8)]
     units = slots.shape[2]
-    offset = lax.broadcasted_iota(jnp.int32, (96, 768), 1)
-    offset = offset - 8 * lax.broadcasted_iota(jnp.int32, (96, 768), 0)
-    places = [jnp.where(offset == n, 1.0, 0.0).astype(bf16) for n in range(8)]
-    lines = [
-        jnp.concatenate([product(place, part[...]).astype(bf16) for place in places], axis=1)
-        for part in (rows, rows_y)
-    ]
-    inputs[...] = moved(192, 192, pick, jnp.concatenate(lines, axis=0))
+    inputs[...] = moved(192, 192, pick, jnp.concatenate([rows[...], rows_y[...]], axis=0))
     writes = []
     for k in range(4):
-        copies[2 * k].wait()
-        mine = product(inputs[...], slots[2 * k]).astype(bf16)
-        copies[2 * k + 1].wait()
-        others = product(inputs[...], slots[2 * k + 1]).astype(bf16)
-        buffer[k] = moved(384, 384, fan, jnp.concatenate([mine, others], axis=0))
-        target = out.at[:, k * units : (k + 1) * units]
-        writes.append(start(buffer.at[k], target, out_sems.at[k]))
-    for write in writes:
-        write.wait()
-
-
-def hidden_kernel(scale, parts, after, out, coef_gate, coef_up, buffer, sems):
+        columns = slice(k * units, (k + 1) * units)
+        for h in range(2):
+            copies[2 * k + h].wait()
+            partial = product(inputs[...], slots[2 * k + h])
+            for d in range(NDP):
+                buffer[2 * d + h, :, columns] = partial[24 * d : 24 * d + 24].astype(bf16)
+        writes.append(start(buffer.at[:, :, columns], out.at[:, :, columns], out_sems.at[k]))
+    for write in writes:
+        write.wait()
+
+
+def hidden_kernel(scale, parts, after, after_too, out, coef_gate, coef_up, buffer, sems):
     sums = parts[0:48].astype(f32)
     for d in range(1, NDP):
         sums = sums + parts[48 * d : 48 * d + 48].astype(f32)
@@ -136,8 +141,8 @@
     buffer[:, :units] = (activated * up_value).astype(bf16)
     buffer[:, units:] = (slope * tan_gate * up_value + activated * tan_up).astype(bf16)
     writes = [start(buffer, out.at[48 * d : 48 * d + 48], sems.at[d]) for d in range(NDP)]
-    coef_gate[...] = up_value * slope * scale
-    coef_up[...] = activated * scale
+    coef_gate[...] = halves_inside(up_value * slope * scale)
+    coef_up[...] = halves_inside(activated * scale)
     for write in writes:
         write.wait()
 
@@ -156,7 +161,7 @@
     sent[...] = total[96:].astype(bf16)
 
 
-def add_kernel(kept, received, out, buffer, sems):
+def add_kernel(kept, received, after, out, buffer, sems):
     total = (kept[...] + received[...].astype(f32)).astype(bf16)
     writes = []
     for a in range(2):
@@ -170,7 +175,7 @@
         write.wait()
 
 
-def sum_kernel(parts, after, out, buffer, sems):
+def sum_kernel(parts, out, buffer, sems):
     total = parts[0:48].astype(f32)
     for i in range(1, NZ):
         total = total + parts[48 * i : 48 * i + 48].astype(f32)
@@ -188,7 +193,7 @@
     return jnp.concatenate(lines, axis=0)
 
 
-def cot_kernel(blocks, down, down_x, down_y, down_yx, after, out, slot, buffer, in_sem, out_sems):
+def cot_kernel(blocks, down, down_x, down_y, down_yx, out, slot, buffer, in_sem, out_sems):
     copy = start(down, slot, in_sem)
     yh = lax.axis_index(YH)
     tan_out = whole(blocks)
@@ -231,18 +236,27 @@
         write.wait()
 
 
-def ggn_kernel(parts, inputs, inputs_x, after, ggn_gate, ggn_up):
+def ggn_kernel(parts, inputs, inputs_x, after, ggn_gate, ggn_up, buffer, sems):
     core = lax.axis_index(CORE)
-    gate, up = None, None
-    for left, position in ((inputs, core), (inputs_x, 1 - core)):
-        both = moved(384, 384, by_kind, parts[rows_at(position, 384), :])
-        one, two = over_rows(left[...], both[:192]), over_rows(left[...], both[192:])
-        gate, up = (one, two) if gate is None else (gate + one, up + two)
-    ggn_gate[...] = gate.astype(bf16)
-    ggn_up[...] = up.astype(bf16)
-
-
-def ggn_down_kernel(scale, ids, hidden, hidden_core, out, out_y, out_core, ggn_down, tangent_out):
+    sides = [
+        moved(384, 384, by_kind, parts[rows_at(position, 384), :]) for position in (core, 1 - core)
+    ]
+    width = inputs.shape[1]
+    writes = []
+    for n in range(4):
+        columns = slice(n * width // 4, (n + 1) * width // 4)
+        for k, target in enumerate((ggn_gate, ggn_up)):
+            rows = slice(192 * k, 192 * k + 192)
+            total = over_rows(inputs[:, columns], sides[0][rows])
+            total = total + over_rows(inputs_x[:, columns], sides[1][rows])
+            buffer[k, columns, :] = total.astype(bf16)
+            place = buffer.at[k, columns, :]
+            writes.append(start(place, target.at[columns, :], sems.at[2 * n + k]))
+    for write in writes:
+        write.wait()
+
+
+def ggn_down_kernel(scale, ids, hidden, hidden_core, out, out_y, out_core, ggn_down, tangent_out, flag):
     yh, z, core = lax.axis_index(YH), lax.axis_index(Z), lax.axis_index(CORE)
     total = over_rows(hidden[0:96], out[...]) + over_rows(hidden[96:192], out_y[...])
     total = total + over_rows(hidden_core[...], out_core[...])
@@ -261,6 +275,7 @@
     hot = jnp.where(wanted == column, 1.0, 0.0).astype(bf16)
     every = jnp.concatenate([out[...], out_y[...], out_core[...]], axis=0)
     tangent_out[...] = product(hot, every)[:own_count].astype(bf16)
+    flag[...] = jnp.zeros_like(flag)
 
 
 def call(kernel, mib, flops, ins, outs, scratch=()):
@@ -293,30 +308,40 @@
         [pltpu.VMEM((48, 128), bf16), DMA((NZ,))],
     )
     rows = lax.all_to_all(rows.reshape(NZ, 48, 128), Z, 0, 0).reshape(768, 128)
+    down_y = swap(down_weight, YH)
+    (rows,) = call(
+        lines_kernel,
+        4,
+        0,
+        [(rows, VMEM), (down_y, ANY)],
+        [((96, width), bf16, VMEM)],
+        [pltpu.VMEM((768, 128), f32)],
+    )
+    rows_y = swap(rows, YH)
     gates = (gate_weight, up_weight, gate_probe, up_probe)
     gates_x = [swap(w, CORE) for w in gates]
-    rows_y = swap(rows, YH)
     inputs, partials = call(
         gates_kernel,
         60,
         8 * dots,
         [(rows, VMEM), (rows_y, VMEM)] + [(w, HBM) for both in zip(gates, gates_x) for w in both],
-        [((192, width), bf16, VMEM), ((384, 4 * units), bf16, HBM)],
+        [((192, width), bf16, VMEM), ((16, 24, 4 * units), bf16, HBM)],
         [
             pltpu.VMEM((8, width, units), bf16),
-            pltpu.VMEM((4, 384, units), bf16),
+            pltpu.VMEM((16, 24, 4 * units), bf16),
             DMA((8,)),
             DMA((4,)),
         ],
     )
 
     parts = lax.all_to_all(partials.reshape(NDP, 48, 4 * units), DP, 0, 0).reshape(384, 4 * units)
-    down_x, probe_x, inputs_x = (swap(w, CORE) for w in (down_weight, down_probe, inputs))
+    swaps = (down_weight, down_probe, inputs, down_y)
+    down_x, probe_x, inputs_x, down_yx = (swap(w, CORE) for w in swaps)
     spread, coef_gate, coef_up = call(
         functools.partial(hidden_kernel, scale),
         8,
         0,
-        [(parts, VMEM), (inputs_x, ANY)],
+        [(parts, VMEM), (inputs_x, ANY), (down_yx, ANY)],
         [((384, 2 * units), bf16, HBM), ((48, units), f32, VMEM), ((48, units), f32, VMEM)],
         [pltpu.VMEM((48, 2 * units), bf16), DMA((NDP,))],
     )
@@ -336,27 +361,25 @@
     )
 
     received = swap(sent, YH)
+    hidden_core = swap(hidden_x, CORE)
     (blocks,) = call(
         add_kernel,
         6,
         0,
-        [(kept, VMEM), (received, VMEM)],
+        [(kept, VMEM), (received, VMEM), (hidden_core, ANY)],
         [((768, 128), bf16, HBM)],
         [pltpu.VMEM((768, 128), bf16), DMA((2,))],
     )
     parts = lax.all_to_all(blocks.reshape(NZ, 48, 128), Z, 0, 0).reshape(768, 128)
-    down_y = swap(down_weight, YH)
-    hidden_core = swap(hidden_x, CORE)
     (spread,) = call(
         sum_kernel,
         4,
         0,
-        [(parts, VMEM), (down_y, ANY)],
+        [(parts, VMEM)],
         [((768, 128), bf16, HBM)],
         [pltpu.VMEM((48, 128), bf16), DMA((NZ,))],
     )
     blocks = lax.all_to_all(spread.reshape(NZ, 48, 128), Z, 0, 0).reshape(768, 128)
-    down_yx = swap(down_y, CORE)
 
     (cot,) = call(
         cot_kernel,
@@ -364,7 +387,7 @@
         4 * dots,
         [
             (blocks, VMEM), (down_weight, HBM), (down_x, VMEM),
-            (down_y, VMEM), (down_yx, VMEM), (hidden_core, ANY),
+            (down_y, VMEM), (down_yx, VMEM),
         ],
         [((384, units), bf16, HBM)],
         [
@@ -376,7 +399,7 @@
     )
     parts = lax.all_to_all(cot.reshape(16, 24, units), (YH,) + DP, 0, 0).reshape(384, units)
     (out,) = call(
-        whole_kernel, 4, 100 * dots, [(blocks, VMEM), (cot, ANY)], [((96, width), bf16, VMEM)]
+        whole_kernel, 4, 0, [(blocks, VMEM), (cot, ANY)], [((96, width), bf16, VMEM)]
     )
     out_y = swap(out, YH)
     (spread,) = call(
@@ -389,7 +412,7 @@
     )
     parts = lax.all_to_all(spread.reshape(16, 48, units), (CORE,) + DP, 0, 0).reshape(768, units)
     out_core = swap(jnp.concatenate([out, out_y]), CORE)
-    ggn_down, tangent_out = call(
+    ggn_down, tangent_out, flag = call(
         functools.partial(ggn_down_kernel, scale),
         14,
         2 * dots,
@@ -397,14 +420,19 @@
             (ids, SMEM), (hidden, VMEM), (hidden_core, VMEM),
             (out, VMEM), (out_y, VMEM), (out_core, VMEM),
         ],
-        [((units, width), bf16, VMEM), ((own_count, width), bf16, VMEM)],
+        [
+            ((units, width), bf16, VMEM),
+            ((own_count, width), bf16, VMEM),
+            ((8, 128), f32, VMEM),
+        ],
     )
     ggn_gate, ggn_up = call(
         ggn_kernel,
         20,
         4 * dots,
-        [(parts, VMEM), (inputs, VMEM), (inputs_x, VMEM), (tangent_out, ANY)],
-        [((width, units), bf16, VMEM), ((width, units), bf16, VMEM)],
+        [(parts, VMEM), (inputs, VMEM), (inputs_x, VMEM), (flag, ANY)],
+        [((width, units), bf16, HBM), ((width, units), bf16, HBM)],
+        [pltpu.VMEM((2, width, units), bf16), DMA((8,))],
     )
     return tangent_out, ggn_gate, ggn_up, ggn_down
 

time: 175 us -> 180 us (1.029)
  blocking collectives: 0 us -> 43.5 us
  starting transfers between devices: 117 us -> 90.6 us
  waiting for transfers between devices: 33.3 us -> 19.8 us
    all_to_all x0 -> x2, blocking collectives: none -> 43.5 us  [the longest x1 23.6 us: local(): lax.all_to_all(blocks.reshape(NZ, 48, 128), Z, 0, 0).reshape(768, 128)]
    all_to_all x2 -> x0, starting transfers between devices: 18.5 us -> none  [the longest x1 11.3 us: local(): lax.all_to_all(spread.reshape(NZ, 48, 128), Z, 0, 0).reshape(768, 128)]
    ppermute x14, waiting for transfers between devices: 15.5 us -> 5.56 us  [swap(): return lax.ppermute(value, axis, [(0, 1), (1, 0)])]
    ppermute x14, starting transfers between devices: 59.5 us -> 51.2 us  [swap(): return lax.ppermute(value, axis, [(0, 1), (1, 0)])]
    all_to_all x1, waiting for transfers between devices: 3.4 us -> 0.01 us  [local(): rows = lax.all_to_all(rows.reshape(NZ, 48, 128), Z, 0, 0).reshape(768, 128)]
    pallas_call x11 -> x12, Pallas kernels: 20.4 us -> 19.5 us  [call(): pl.pallas_call(kernel, out_shape=[jax.ShapeDtypeStruct(s, t) for s, t, _...]
  transfers between devices with their start and end apart: 21 -> 19, of which waited for: 8 -> 5; matrix products, arithmetic and copies ran while one was open for 0% -> 0% of each run, Pallas kernels for 2% -> 2%
where the time goes in v6:
time: 180 us; the launch traced here: 178 us
  starting transfers between devices  90.6 us (50%)
  blocking collectives  43.5 us (24%)
  waiting for transfers between devices  19.8 us (11%)
  Pallas kernels  19.5 us (11%)
  local copies, waits for them, and re-layouts  3.96 us (2%)
    ppermute x14, starting transfers between devices, swap(): return lax.ppermute(value, axis, [(0, 1), (1, 0)])  51.2 us
    all_to_all x1, blocking collectives, local(): lax.all_to_all(blocks.reshape(NZ, 48, 128), Z, 0, 0).reshape(768, 128)  23.6 us
    all_to_all x1, blocking collectives, local(): lax.all_to_all(spread.reshape(NZ, 48, 128), Z, 0, 0).reshape(768, 128)  19.9 us
    pallas_call x12, Pallas kernels, call(): pl.pallas_call(kernel, out_shape=[jax.ShapeDtypeStruct(s, t) for s, t, _...  19.5 us
    all_to_all x1, starting transfers between devices, local(): rows = lax.all_to_all(rows.reshape(NZ, 48, 128), Z, 0, 0).reshape(768, 128)  15.8 us
    all_to_all x1, starting transfers between devices, local(): lax.all_to_all(spread.reshape(16, 48, units), (CORE,) + DP, 0, 0)  8.07 us
    all_to_all x1, waiting for transfers between devices, local(): lax.all_to_all(spread.reshape(NDP, 48, 2 * units), DP, 0, 0)  7.63 us
    all_to_all x1, waiting for transfers between devices, local(): lax.all_to_all(spread.reshape(16, 48, units), (CORE,) + DP, 0, 0)  6.57 us
  transfers between devices with their start and end apart: 19, of which 5 were waited for; matrix products, arithmetic and copies ran while one was open for 0% of the time, Pallas kernels for 2%

profile of v6, /device:TPU:1, one launch (start us, length us, event | category | flops | bytes accessed | tf_op | source)
XLA Modules:
  0.0 178.5 jit_solution(7744574612437337013)
XLA Ops:
  2.4 15.8 %all-to-all-start = ((bf16[16,48,128]{2,1,0:T(8,128)(2,1)}), bf16[16,48,128]{2,1,0:T(8,128)(2,1)S(1)}, u32[]{:S(2)}, u32[]{:S(2)}) async-start(bf16[16,48,128]{2,1,0:T(8,128)(2,1)} %bitcast), calls=%async_computation | async-start | bytes 393216 | tf_op jit(solution)/shard_map/all_to_all | solution.py:310
  18.2 4.8 %collective-permute-start = (bf16[256,1024]{1,0:T(8,128)(2,1)S(1)}, bf16[256,1024]{1,0:T(8,128)(2,1)S(1)}, u32[]{:S(2)}, u32[]{:S(2)}) collective-permute-start(bf16[256,1024]{1,0:T(8,128)(2,1)S(1)} %copy-done), channel_id=1, source_target_pairs={{0,256},{256,0},{1,257},{257,1},{2,258},{258,2},{3,259},{259,3},{4... | collective-permute-start | bytes 1572872 | tf_op jit(solution)/shard_map/ppermute | solution.py:26
  23.0 3.1 %collective-permute-start.2 = (bf16[1024,256]{1,0:T(8,128)(2,1)}, bf16[1024,256]{1,0:T(8,128)(2,1)S(1)}, u32[]{:S(2)}, u32[]{:S(2)}) collective-permute-start(bf16[1024,256]{1,0:T(8,128)(2,1)} %rest_0_.1), channel_id=1, source_target_pairs={{0,8},{8,0},{1,9},{9,1},{2,10},{10,2},{3,11},{11,3},{4,12},{12,4},... | collective-permute-start | bytes 1572872 | tf_op jit(solution)/shard_map/ppermute | solution.py:26
  26.2 1.9 %collective-permute-start.3 = (bf16[1024,256]{1,0:T(8,128)(2,1)}, bf16[1024,256]{1,0:T(8,128)(2,1)S(1)}, u32[]{:S(2)}, u32[]{:S(2)}) collective-permute-start(bf16[1024,256]{1,0:T(8,128)(2,1)} %rest_2_.1), channel_id=1, source_target_pairs={{0,8},{8,0},{1,9},{9,1},{2,10},{10,2},{3,11},{11,3},{4,12},{12,4},... | collective-permute-start | bytes 1572872 | tf_op jit(solution)/shard_map/ppermute | solution.py:26
  28.1 2.4 %collective-permute-start.4 = (bf16[1024,256]{1,0:T(8,128)(2,1)}, bf16[1024,256]{1,0:T(8,128)(2,1)S(1)}, u32[]{:S(2)}, u32[]{:S(2)}) collective-permute-start(bf16[1024,256]{1,0:T(8,128)(2,1)} %rest_4_.1), channel_id=1, source_target_pairs={{0,8},{8,0},{1,9},{9,1},{2,10},{10,2},{3,11},{11,3},{4,12},{12,4},... | collective-permute-start | bytes 1572872 | tf_op jit(solution)/shard_map/ppermute | solution.py:26
  30.5 1.9 %collective-permute-start.5 = (bf16[1024,256]{1,0:T(8,128)(2,1)}, bf16[1024,256]{1,0:T(8,128)(2,1)S(1)}, u32[]{:S(2)}, u32[]{:S(2)}) collective-permute-start(bf16[1024,256]{1,0:T(8,128)(2,1)} %rest_6_.1), channel_id=1, source_target_pairs={{0,8},{8,0},{1,9},{9,1},{2,10},{10,2},{3,11},{11,3},{4,12},{12,4},... | collective-permute-start | bytes 1572872 | tf_op jit(solution)/shard_map/ppermute | solution.py:26
  32.4 1.6 collective-permute-done.after.down_y
  34.2 4.8 %collective-permute-start.1 = (bf16[96,1024]{1,0:T(8,128)(2,1)S(1)}, bf16[96,1024]{1,0:T(8,128)(2,1)S(1)}, u32[]{:S(2)}, u32[]{:S(2)}) collective-permute-start(bf16[96,1024]{1,0:T(8,128)(2,1)S(1)} %shard_map.112.rows), channel_id=1, source_target_pairs={{0,256},{256,0},{1,257},{257,1},{2,258},{258,2},{3,259},{259,3},{4... | collective-permute-start | bytes 589832 | tf_op jit(solution)/shard_map/ppermute | solution.py:26
  39.1 3.0 %collective-permute-done.1.rows_y = bf16[96,1024]{1,0:T(8,128)(2,1)S(1)} collective-permute-done((bf16[96,1024]{1,0:T(8,128)(2,1)S(1)}, bf16[96,1024]{1,0:T(8,128)(2,1)S(1)}, u32[]{:S(2)}, u32[]{:S(2)}) %collective-permute-start.1) | collective-permute-done | bytes 196640 | tf_op jit(solution)/shard_map/ppermute | solution.py:26
  42.8 6.5 %shard_map.113 = (bf16[192,1024]{1,0:T(8,128)(2,1)}, bf16[16,24,1024]{2,1,0:T(8,128)(2,1)}) custom-call(bf16[96,1024]{1,0:T(8,128)(2,1)} %copy-done.1, bf16[96,1024]{1,0:T(8,128)(2,1)} %copy-done.13, bf16[1024,256]{1,0:T(8,128)(2,1)} %rest_0_.1, bf16[1024,256]{1,0:T(8,128)(2,1)} %copy-done.9, bf16[1024,256]{1,0:T(8,128)(2,1)} %rest_2_.1, ...), custom_call_target="tpu_custom_call" | custom-call | flops 805306368 | bytes 5767168 | tf_op jit(solution)/shard_map/pallas_call | solution.py:284
  49.3 5.2 %all-to-all-start.1 = ((bf16[8,48,1024]{2,1,0:T(8,128)(2,1)}), bf16[8,48,1024]{2,1,0:T(8,128)(2,1)S(1)}, u32[]{:S(2)}, u32[]{:S(2)}) async-start(bf16[8,48,1024]{2,1,0:T(8,128)(2,1)} %bitcast.25), calls=%async_computation.1 | async-start | bytes 1572864 | tf_op jit(solution)/shard_map/all_to_all | solution.py:337
  54.4 5.2 %collective-permute-start.7 = (bf16[256,1024]{1,0:T(8,128)(2,1)S(1)}, bf16[256,1024]{1,0:T(8,128)(2,1)S(1)}, u32[]{:S(2)}, u32[]{:S(2)}) collective-permute-start(bf16[256,1024]{1,0:T(8,128)(2,1)S(1)} %collective-permute-done.after.down_y), channel_id=1, source_target_pairs={{0,8},{8,0},{1,9},{9,1},{2,10},{10,2},{3,11},{11,3},{4,12},{12,4},... | collective-permute-start | bytes 1572872 | tf_op jit(solution)/shard_map/ppermute | solution.py:26
  59.7 1.9 %collective-permute-start.6 = (bf16[192,1024]{1,0:T(8,128)(2,1)}, bf16[192,1024]{1,0:T(8,128)(2,1)S(1)}, u32[]{:S(2)}, u32[]{:S(2)}) collective-permute-start(bf16[192,1024]{1,0:T(8,128)(2,1)} %get-tuple-element.19.inputs), channel_id=1, source_target_pairs={{0,8},{8,0},{1,9},{9,1},{2,10},{10,2},{3,11},{11,3},{4,12},{12,4},... | collective-permute-start | bytes 1179656 | tf_op jit(solution)/shard_map/ppermute | solution.py:26
  61.6 2.4 %collective-permute-start.8 = (bf16[256,1024]{1,0:T(8,128)(2,1)S(1)}, bf16[256,1024]{1,0:T(8,128)(2,1)S(1)}, u32[]{:S(2)}, u32[]{:S(2)}) collective-permute-start(bf16[256,1024]{1,0:T(8,128)(2,1)S(1)} %copy-done), channel_id=1, source_target_pairs={{0,8},{8,0},{1,9},{9,1},{2,10},{10,2},{3,11},{11,3},{4,12},{12,4},... | collective-permute-start | bytes 1572872 | tf_op jit(solution)/shard_map/ppermute | solution.py:26
  64.0 1.9 %collective-permute-start.9 = (bf16[256,1024]{1,0:T(8,128)(2,1)S(1)}, bf16[256,1024]{1,0:T(8,128)(2,1)}, u32[]{:S(2)}, u32[]{:S(2)}) collective-permute-start(bf16[256,1024]{1,0:T(8,128)(2,1)S(1)} %copy-done.2), channel_id=1, source_target_pairs={{0,8},{8,0},{1,9},{9,1},{2,10},{10,2},{3,11},{11,3},{4,12},{12,4},... | collective-permute-start | bytes 1572872 | tf_op jit(solution)/shard_map/ppermute | solution.py:26
  66.7 1.0 copy-done.5
  69.4 5.4 %all-to-all-start.2 = ((bf16[8,48,512]{2,1,0:T(8,128)(2,1)}), bf16[8,48,512]{2,1,0:T(8,128)(2,1)S(1)}, u32[]{:S(2)}, u32[]{:S(2)}) async-start(bf16[8,48,512]{2,1,0:T(8,128)(2,1)} %bitcast.24), calls=%async_computation.2 | async-start | bytes 786432 | tf_op jit(solution)/shard_map/all_to_all | solution.py:348
  74.9 7.6 %all-to-all-done.2 = bf16[8,48,512]{2,1,0:T(8,128)(2,1)S(1)} async-done(((bf16[8,48,512]{2,1,0:T(8,128)(2,1)}), bf16[8,48,512]{2,1,0:T(8,128)(2,1)S(1)}, u32[]{:S(2)}, u32[]{:S(2)}) %all-to-all-start.2) | async-done | bytes 393248 | tf_op jit(solution)/shard_map/all_to_all | solution.py:348
  82.5 2.1 %shard_map.115 = (bf16[96,1024]{1,0:T(8,128)(2,1)S(1)}, f32[96,1024]{1,0:T(8,128)S(1)}, bf16[192,256]{1,0:T(8,128)(2,1)S(1)}, bf16[192,256]{1,0:T(8,128)(2,1)S(1)}) custom-call(bf16[384,512]{1,0:T(8,128)(2,1)S(1)} %bitcast.17, bf16[256,1024]{1,0:T(8,128)(2,1)S(1)} %copy-done, bf16[256,1024]{1,0:T(8,128)(2,1)S(1)} %copy-done.2, ...), custom_call_target="tpu_custom_call" | custom-call | flops 402653184 | bytes 3276800 | tf_op jit(solution)/shard_map/pallas_call | solution.py:284
  84.6 4.5 %collective-permute-start.11 = (bf16[96,1024]{1,0:T(8,128)(2,1)S(1)}, bf16[96,1024]{1,0:T(8,128)(2,1)S(1)}, u32[]{:S(2)}, u32[]{:S(2)}) collective-permute-start(bf16[96,1024]{1,0:T(8,128)(2,1)S(1)} %get-tuple-element.24), channel_id=1, source_target_pairs={{0,256},{256,0},{1,257},{257,1},{2,258},{258,2},{3,259},{259,3},{4... | collective-permute-start | bytes 589832 | tf_op jit(solution)/shard_map/ppermute | solution.py:26
  89.1 3.7 %collective-permute-start.10 = (bf16[192,256]{1,0:T(8,128)(2,1)S(1)}, bf16[192,256]{1,0:T(8,128)(2,1)S(1)}, u32[]{:S(2)}, u32[]{:S(2)}) collective-permute-start(bf16[192,256]{1,0:T(8,128)(2,1)S(1)} %get-tuple-element.22), channel_id=1, source_target_pairs={{0,8},{8,0},{1,9},{9,1},{2,10},{10,2},{3,11},{11,3},{4,12},{12,4},... | collective-permute-start | bytes 294920 | tf_op jit(solution)/shard_map/ppermute | solution.py:26
  94.0 23.6 %all_to_all.35 = bf16[16,48,128]{2,1,0:T(8,128)(2,1)S(1)} all-to-all(bf16[16,48,128]{2,1,0:T(8,128)(2,1)S(1)} %bitcast.20), channel_id=1, replica_groups=mesh['yh'=2,'z'=16,'core'=2,'x'=4,'yl'=2] {'z'}, dimensions={0} | all-to-all | bytes 393216 | tf_op jit(solution)/shard_map/all_to_all | solution.py:373
  118.1 19.9 %all_to_all.36 = bf16[16,48,128]{2,1,0:T(8,128)(2,1)S(1)} all-to-all(bf16[16,48,128]{2,1,0:T(8,128)(2,1)S(1)} %bitcast.22), channel_id=1, replica_groups=mesh['yh'=2,'z'=16,'core'=2,'x'=4,'yl'=2] {'z'}, dimensions={0} | all-to-all | bytes 393216 | tf_op jit(solution)/shard_map/all_to_all | solution.py:382
  138.0 2.3 %shard_map.118.after = bf16[384,256]{1,0:T(8,128)(2,1)} custom-call(bf16[768,128]{1,0:T(8,128)(2,1)S(1)} %bitcast.15, bf16[256,1024]{1,0:T(8,128)(2,1)S(1)} %copy-done, bf16[256,1024]{1,0:T(8,128)(2,1)S(1)} %collective-permute-done.8.down_x, bf16[256,1024]{1,0:T(8,128)(2,1)S(1)} %collective-permute-done.after.down_y, ...), custom_call_target="tpu_custom_call" | custom-call | flops 402653184 | bytes 2490368 | tf_op jit(solution)/shard_map/pallas_call | solution.py:284
  140.4 3.0 %collective-permute-start.12 = (bf16[96,1024]{1,0:T(8,128)(2,1)S(1)}, bf16[96,1024]{1,0:T(8,128)(2,1)S(1)}, u32[]{:S(2)}, u32[]{:S(2)}) collective-permute-start(bf16[96,1024]{1,0:T(8,128)(2,1)S(1)} %shard_map.119.out), channel_id=1, source_target_pairs={{0,256},{256,0},{1,257},{257,1},{2,258},{258,2},{3,259},{259,3},{4... | collective-permute-start | bytes 589832 | tf_op jit(solution)/shard_map/ppermute | solution.py:26
  143.4 4.9 %all-to-all-start.5 = ((bf16[16,24,256]{2,1,0:T(8,128)(2,1)}), bf16[16,24,256]{2,1,0:T(8,128)(2,1)S(1)}, u32[]{:S(2)}, u32[]{:S(2)}) async-start(bf16[16,24,256]{2,1,0:T(8,128)(2,1)} %bitcast.10), calls=%async_computation.5 | async-start | bytes 393216 | tf_op jit(solution)/shard_map/all_to_all | solution.py:400
  148.4 9.5 %collective-permute-start.13 = (bf16[192,1024]{1,0:T(8,128)(2,1)S(1)}, bf16[192,1024]{1,0:T(8,128)(2,1)S(1)}, u32[]{:S(2)}, u32[]{:S(2)}) collective-permute-start(bf16[192,1024]{1,0:T(8,128)(2,1)S(1)} %pad_maximum_fusion), channel_id=1, source_target_pairs={{0,8},{8,0},{1,9},{9,1},{2,10},{10,2},{3,11},{11,3},{4,12},{12,4},... | collective-permute-start | bytes 1179656 | tf_op jit(solution)/shard_map/ppermute | solution.py:26
  158.0 1.1 shard_map.121
  159.0 8.1 %all-to-all-start.6 = ((bf16[16,48,256]{2,1,0:T(8,128)(2,1)}), bf16[16,48,256]{2,1,0:T(8,128)(2,1)S(1)}, u32[]{:S(2)}, u32[]{:S(2)}) async-start(bf16[16,48,256]{2,1,0:T(8,128)(2,1)} %bitcast.12), calls=%async_computation.6 | async-start | bytes 786432 | tf_op jit(solution)/shard_map/all_to_all | solution.py:413
  167.1 1.9 %shard_map.120 = (bf16[256,1024]{1,0:T(8,128)(2,1)}, bf16[6,1024]{1,0:T(8,128)(2,1)}, f32[8,128]{1,0:T(8,128)S(1)}) custom-call(s32[384]{0:T(512)S(1)} %copy-done.8, bf16[192,256]{1,0:T(8,128)(2,1)S(1)} %get-tuple-element.21.hidden, bf16[192,256]{1,0:T(8,128)(2,1)S(1)} %collective-permute-done.10.after.hidden_core, bf16[96,1024]{1,0:T(8,128)(2,1)S(1)} %shard_map.119.out, ...), custom_call_target="tpu_custom_call" | custom-call | flops 201326592 | bytes 1525248 | tf_op jit(solution)/shard_map/pallas_call | solution.py:284
  169.1 6.6 %all-to-all-done.6 = bf16[16,48,256]{2,1,0:T(8,128)(2,1)S(1)} async-done(((bf16[16,48,256]{2,1,0:T(8,128)(2,1)}), bf16[16,48,256]{2,1,0:T(8,128)(2,1)S(1)}, u32[]{:S(2)}, u32[]{:S(2)}) %all-to-all-start.6) | async-done | bytes 393248 | tf_op jit(solution)/shard_map/all_to_all | solution.py:413
  175.6 2.8 %shard_map.122 = (bf16[1024,256]{1,0:T(8,128)(2,1)}, bf16[1024,256]{1,0:T(8,128)(2,1)}) custom-call(bf16[768,256]{1,0:T(8,128)(2,1)S(1)} %bitcast.23, bf16[192,1024]{1,0:T(8,128)(2,1)} %get-tuple-element.19.inputs, bf16[192,1024]{1,0:T(8,128)(2,1)S(1)} %copy-done.6, f32[8,128]{1,0:T(8,128)S(1)} %get-tuple-element.28.after), custom_call_target="tpu_custom_call" | custom-call | flops 402653184 | bytes 2228224 | tf_op jit(solution)/shard_map/pallas_call | solution.py:284
  (49 shorter events, 6.8 us)
Async XLA Ops:
  0.6 17.5 %copy-start = (bf16[256,1024]{1,0:T(8,128)(2,1)S(1)}, bf16[256,1024]{1,0:T(8,128)(2,1)}, u32[]{:S(2)}) copy-start(bf16[256,1024]{1,0:T(8,128)(2,1)} %down.3) | copy-start | bytes 1572868
  0.6 0.8 copy-start.7
  2.4 31.6 %all-to-all-start = ((bf16[16,48,128]{2,1,0:T(8,128)(2,1)}), bf16[16,48,128]{2,1,0:T(8,128)(2,1)S(1)}, u32[]{:S(2)}, u32[]{:S(2)}) async-start(bf16[16,48,128]{2,1,0:T(8,128)(2,1)} %bitcast), calls=%async_computation | async-start | bytes 393216 | tf_op jit(solution)/shard_map/all_to_all | solution.py:310
  18.2 15.9 %collective-permute-start = (bf16[256,1024]{1,0:T(8,128)(2,1)S(1)}, bf16[256,1024]{1,0:T(8,128)(2,1)S(1)}, u32[]{:S(2)}, u32[]{:S(2)}) collective-permute-start(bf16[256,1024]{1,0:T(8,128)(2,1)S(1)} %copy-done), channel_id=1, source_target_pairs={{0,256},{256,0},{1,257},{257,1},{2,258},{258,2},{3,259},{259,3},{4... | collective-permute-start | bytes 1572872 | tf_op jit(solution)/shard_map/ppermute | solution.py:26
  23.0 16.0 %collective-permute-start.2 = (bf16[1024,256]{1,0:T(8,128)(2,1)}, bf16[1024,256]{1,0:T(8,128)(2,1)S(1)}, u32[]{:S(2)}, u32[]{:S(2)}) collective-permute-start(bf16[1024,256]{1,0:T(8,128)(2,1)} %rest_0_.1), channel_id=1, source_target_pairs={{0,8},{8,0},{1,9},{9,1},{2,10},{10,2},{3,11},{11,3},{4,12},{12,4},... | collective-permute-start | bytes 1572872 | tf_op jit(solution)/shard_map/ppermute | solution.py:26
  26.2 12.9 %collective-permute-start.3 = (bf16[1024,256]{1,0:T(8,128)(2,1)}, bf16[1024,256]{1,0:T(8,128)(2,1)S(1)}, u32[]{:S(2)}, u32[]{:S(2)}) collective-permute-start(bf16[1024,256]{1,0:T(8,128)(2,1)} %rest_2_.1), channel_id=1, source_target_pairs={{0,8},{8,0},{1,9},{9,1},{2,10},{10,2},{3,11},{11,3},{4,12},{12,4},... | collective-permute-start | bytes 1572872 | tf_op jit(solution)/shard_map/ppermute | solution.py:26
  28.1 11.0 %collective-permute-start.4 = (bf16[1024,256]{1,0:T(8,128)(2,1)}, bf16[1024,256]{1,0:T(8,128)(2,1)S(1)}, u32[]{:S(2)}, u32[]{:S(2)}) collective-permute-start(bf16[1024,256]{1,0:T(8,128)(2,1)} %rest_4_.1), channel_id=1, source_target_pairs={{0,8},{8,0},{1,9},{9,1},{2,10},{10,2},{3,11},{11,3},{4,12},{12,4},... | collective-permute-start | bytes 1572872 | tf_op jit(solution)/shard_map/ppermute | solution.py:26
  30.5 8.6 %collective-permute-start.5 = (bf16[1024,256]{1,0:T(8,128)(2,1)}, bf16[1024,256]{1,0:T(8,128)(2,1)S(1)}, u32[]{:S(2)}, u32[]{:S(2)}) collective-permute-start(bf16[1024,256]{1,0:T(8,128)(2,1)} %rest_6_.1), channel_id=1, source_target_pairs={{0,8},{8,0},{1,9},{9,1},{2,10},{10,2},{3,11},{11,3},{4,12},{12,4},... | collective-permute-start | bytes 1572872 | tf_op jit(solution)/shard_map/ppermute | solution.py:26
  34.2 7.9 %copy-start.1 = (bf16[96,1024]{1,0:T(8,128)(2,1)}, bf16[96,1024]{1,0:T(8,128)(2,1)S(1)}, u32[]{:S(2)}) copy-start(bf16[96,1024]{1,0:T(8,128)(2,1)S(1)} %shard_map.112.rows) | copy-start | bytes 589828
  34.2 7.9 %collective-permute-start.1 = (bf16[96,1024]{1,0:T(8,128)(2,1)S(1)}, bf16[96,1024]{1,0:T(8,128)(2,1)S(1)}, u32[]{:S(2)}, u32[]{:S(2)}) collective-permute-start(bf16[96,1024]{1,0:T(8,128)(2,1)S(1)} %shard_map.112.rows), channel_id=1, source_target_pairs={{0,256},{256,0},{1,257},{257,1},{2,258},{258,2},{3,259},{259,3},{4... | collective-permute-start | bytes 589832 | tf_op jit(solution)/shard_map/ppermute | solution.py:26
  39.0 3.1 %copy-start.9 = (bf16[1024,256]{1,0:T(8,128)(2,1)}, bf16[1024,256]{1,0:T(8,128)(2,1)S(1)}, u32[]{:S(2)}) copy-start(bf16[1024,256]{1,0:T(8,128)(2,1)S(1)} %collective-permute-done.2.rest_1_) | copy-start | bytes 1572868
  39.0 3.1 %copy-start.10 = (bf16[1024,256]{1,0:T(8,128)(2,1)}, bf16[1024,256]{1,0:T(8,128)(2,1)S(1)}, u32[]{:S(2)}) copy-start(bf16[1024,256]{1,0:T(8,128)(2,1)S(1)} %collective-permute-done.3.rest_3_) | copy-start | bytes 1572868
  39.1 3.0 %copy-start.11 = (bf16[1024,256]{1,0:T(8,128)(2,1)}, bf16[1024,256]{1,0:T(8,128)(2,1)S(1)}, u32[]{:S(2)}) copy-start(bf16[1024,256]{1,0:T(8,128)(2,1)S(1)} %collective-permute-done.4.rest_5_) | copy-start | bytes 1572868
  39.1 3.0 %copy-start.12 = (bf16[1024,256]{1,0:T(8,128)(2,1)}, bf16[1024,256]{1,0:T(8,128)(2,1)S(1)}, u32[]{:S(2)}) copy-start(bf16[1024,256]{1,0:T(8,128)(2,1)S(1)} %collective-permute-done.5.rest_7_) | copy-start | bytes 1572868
  49.3 14.7 %copy-start.2 = (bf16[256,1024]{1,0:T(8,128)(2,1)S(1)}, bf16[256,1024]{1,0:T(8,128)(2,1)}, u32[]{:S(2)}) copy-start(bf16[256,1024]{1,0:T(8,128)(2,1)} %probe.1) | copy-start | bytes 1572868
  49.3 17.4 %all-to-all-start.1 = ((bf16[8,48,1024]{2,1,0:T(8,128)(2,1)}), bf16[8,48,1024]{2,1,0:T(8,128)(2,1)S(1)}, u32[]{:S(2)}, u32[]{:S(2)}) async-start(bf16[8,48,1024]{2,1,0:T(8,128)(2,1)} %bitcast.25), calls=%async_computation.1 | async-start | bytes 1572864 | tf_op jit(solution)/shard_map/all_to_all | solution.py:337
  54.4 11.5 %collective-permute-start.7 = (bf16[256,1024]{1,0:T(8,128)(2,1)S(1)}, bf16[256,1024]{1,0:T(8,128)(2,1)S(1)}, u32[]{:S(2)}, u32[]{:S(2)}) collective-permute-start(bf16[256,1024]{1,0:T(8,128)(2,1)S(1)} %collective-permute-done.after.down_y), channel_id=1, source_target_pairs={{0,8},{8,0},{1,9},{9,1},{2,10},{10,2},{3,11},{11,3},{4,12},{12,4},... | collective-permute-start | bytes 1572872 | tf_op jit(solution)/shard_map/ppermute | solution.py:26
  59.7 6.3 %collective-permute-start.6 = (bf16[192,1024]{1,0:T(8,128)(2,1)}, bf16[192,1024]{1,0:T(8,128)(2,1)S(1)}, u32[]{:S(2)}, u32[]{:S(2)}) collective-permute-start(bf16[192,1024]{1,0:T(8,128)(2,1)} %get-tuple-element.19.inputs), channel_id=1, source_target_pairs={{0,8},{8,0},{1,9},{9,1},{2,10},{10,2},{3,11},{11,3},{4,12},{12,4},... | collective-permute-start | bytes 1179656 | tf_op jit(solution)/shard_map/ppermute | solution.py:26
  61.6 13.3 %collective-permute-start.8 = (bf16[256,1024]{1,0:T(8,128)(2,1)S(1)}, bf16[256,1024]{1,0:T(8,128)(2,1)S(1)}, u32[]{:S(2)}, u32[]{:S(2)}) collective-permute-start(bf16[256,1024]{1,0:T(8,128)(2,1)S(1)} %copy-done), channel_id=1, source_target_pairs={{0,8},{8,0},{1,9},{9,1},{2,10},{10,2},{3,11},{11,3},{4,12},{12,4},... | collective-permute-start | bytes 1572872 | tf_op jit(solution)/shard_map/ppermute | solution.py:26
  64.0 10.8 %collective-permute-start.9 = (bf16[256,1024]{1,0:T(8,128)(2,1)S(1)}, bf16[256,1024]{1,0:T(8,128)(2,1)}, u32[]{:S(2)}, u32[]{:S(2)}) collective-permute-start(bf16[256,1024]{1,0:T(8,128)(2,1)S(1)} %copy-done.2), channel_id=1, source_target_pairs={{0,8},{8,0},{1,9},{9,1},{2,10},{10,2},{3,11},{11,3},{4,12},{12,4},... | collective-permute-start | bytes 1572872 | tf_op jit(solution)/shard_map/ppermute | solution.py:26
  66.0 0.7 copy-start.4
  66.7 1.0 copy-start.5
  68.7 0.7 copy-start.3
  69.4 13.1 %all-to-all-start.2 = ((bf16[8,48,512]{2,1,0:T(8,128)(2,1)}), bf16[8,48,512]{2,1,0:T(8,128)(2,1)S(1)}, u32[]{:S(2)}, u32[]{:S(2)}) async-start(bf16[8,48,512]{2,1,0:T(8,128)(2,1)} %bitcast.24), calls=%async_computation.2 | async-start | bytes 786432 | tf_op jit(solution)/shard_map/all_to_all | solution.py:348
  84.6 9.1 %collective-permute-start.11 = (bf16[96,1024]{1,0:T(8,128)(2,1)S(1)}, bf16[96,1024]{1,0:T(8,128)(2,1)S(1)}, u32[]{:S(2)}, u32[]{:S(2)}) collective-permute-start(bf16[96,1024]{1,0:T(8,128)(2,1)S(1)} %get-tuple-element.24), channel_id=1, source_target_pairs={{0,256},{256,0},{1,257},{257,1},{2,258},{258,2},{3,259},{259,3},{4... | collective-permute-start | bytes 589832 | tf_op jit(solution)/shard_map/ppermute | solution.py:26
  89.1 4.6 %collective-permute-start.10 = (bf16[192,256]{1,0:T(8,128)(2,1)S(1)}, bf16[192,256]{1,0:T(8,128)(2,1)S(1)}, u32[]{:S(2)}, u32[]{:S(2)}) collective-permute-start(bf16[192,256]{1,0:T(8,128)(2,1)S(1)} %get-tuple-element.22), channel_id=1, source_target_pairs={{0,8},{8,0},{1,9},{9,1},{2,10},{10,2},{3,11},{11,3},{4,12},{12,4},... | collective-permute-start | bytes 294920 | tf_op jit(solution)/shard_map/ppermute | solution.py:26
  140.4 8.0 %collective-permute-start.12 = (bf16[96,1024]{1,0:T(8,128)(2,1)S(1)}, bf16[96,1024]{1,0:T(8,128)(2,1)S(1)}, u32[]{:S(2)}, u32[]{:S(2)}) collective-permute-start(bf16[96,1024]{1,0:T(8,128)(2,1)S(1)} %shard_map.119.out), channel_id=1, source_target_pairs={{0,256},{256,0},{1,257},{257,1},{2,258},{258,2},{3,259},{259,3},{4... | collective-permute-start | bytes 589832 | tf_op jit(solution)/shard_map/ppermute | solution.py:26
  143.4 14.5 %all-to-all-start.5 = ((bf16[16,24,256]{2,1,0:T(8,128)(2,1)}), bf16[16,24,256]{2,1,0:T(8,128)(2,1)S(1)}, u32[]{:S(2)}, u32[]{:S(2)}) async-start(bf16[16,24,256]{2,1,0:T(8,128)(2,1)} %bitcast.10), calls=%async_computation.5 | async-start | bytes 393216 | tf_op jit(solution)/shard_map/all_to_all | solution.py:400
  148.4 18.7 %collective-permute-start.13 = (bf16[192,1024]{1,0:T(8,128)(2,1)S(1)}, bf16[192,1024]{1,0:T(8,128)(2,1)S(1)}, u32[]{:S(2)}, u32[]{:S(2)}) collective-permute-start(bf16[192,1024]{1,0:T(8,128)(2,1)S(1)} %pad_maximum_fusion), channel_id=1, source_target_pairs={{0,8},{8,0},{1,9},{9,1},{2,10},{10,2},{3,11},{11,3},{4,12},{12,4},... | collective-permute-start | bytes 1179656 | tf_op jit(solution)/shard_map/ppermute | solution.py:26
  159.0 8.1 %copy-start.8 = (s32[384]{0:T(512)S(1)}, s32[384]{0:T(512)}, u32[]{:S(2)}) copy-start(s32[384]{0:T(512)} %ids.1) | copy-start | bytes 4612
  159.0 16.6 %all-to-all-start.6 = ((bf16[16,48,256]{2,1,0:T(8,128)(2,1)}), bf16[16,48,256]{2,1,0:T(8,128)(2,1)S(1)}, u32[]{:S(2)}, u32[]{:S(2)}) async-start(bf16[16,48,256]{2,1,0:T(8,128)(2,1)} %bitcast.12), calls=%async_computation.6 | async-start | bytes 786432 | tf_op jit(solution)/shard_map/all_to_all | solution.py:413
  167.1 8.5 %copy-start.6 = (bf16[192,1024]{1,0:T(8,128)(2,1)S(1)}, bf16[192,1024]{1,0:T(8,128)(2,1)}, u32[]{:S(2)}) copy-start(bf16[192,1024]{1,0:T(8,128)(2,1)} %copy-done.4) | copy-start | bytes 1179652
  (1 other events, 0.7 us)

commit v7 on v6

--- a/solution.py
+++ b/solution.py
@@ -104,6 +104,18 @@
         write.wait()
 
 
+def pack_kernel(*refs):
+    gates, downs, (all_gates, all_downs, sems) = refs[:4], refs[4:6], refs[6:]
+    copies = []
+    for packed, parts in ((all_gates, gates), (all_downs, downs)):
+        for part in parts:
+            count = part.shape[0]
+            first = len(copies) % 4 * count
+            copies.append(start(part, packed.at[first : first + count], sems.at[len(copies)]))
+    for copy in copies:
+        copy.wait()
+
+
 def lines_kernel(rows, after, out, buffer):
     buffer[...] = rows[...].astype(f32)
     for n in range(8):
@@ -112,11 +124,15 @@
 
 
 def gates_kernel(rows, rows_y, *rest):
-    weights, (inputs, out, slots, buffer, in_sems, out_sems) = rest[:8], rest[8:]
-    copies = [start(weights[k], slots.at[k], in_sems.at[k]) for k in range(8)]
-    units = slots.shape[2]
+    own, theirs, (kept, out, inputs, slots, buffer, in_sems, out_sems) = rest[:4], rest[4], rest[5:]
+    width, units = own[0].shape
+    copies = []
+    for k in range(4):
+        copies.append(start(own[k], slots.at[2 * k], in_sems.at[2 * k]))
+        part = theirs.at[k * width : (k + 1) * width]
+        copies.append(start(part, slots.at[2 * k + 1], in_sems.at[2 * k + 1]))
     inputs[...] = moved(192, 192, pick, jnp.concatenate([rows[...], rows_y[...]], axis=0))
-    writes = []
+    writes = [start(inputs, kept, out_sems.at[4])]
     for k in range(4):
         columns = slice(k * units, (k + 1) * units)
         for h in range(2):
@@ -129,7 +145,7 @@
         write.wait()
 
 
-def hidden_kernel(scale, parts, after, after_too, out, coef_gate, coef_up, buffer, sems):
+def hidden_kernel(scale, parts, out, coef_gate, coef_up, buffer, sems):
     sums = parts[0:48].astype(f32)
     for d in range(1, NDP):
         sums = sums + parts[48 * d : 48 * d + 48].astype(f32)
@@ -147,13 +163,13 @@
         write.wait()
 
 
-def down_kernel(parts, down, probe, down_x, probe_x, sent, kept, hidden, hidden_x, slots, sems):
+def down_kernel(parts, down, probe, theirs, after, after_too, sent, kept, hidden, hidden_x, slots, sems):
     copies = [start(down, slots.at[0], sems.at[0]), start(probe, slots.at[1], sems.at[1])]
     both = moved(384, 384, by_half, parts[...])
     units = both.shape[1] // 2
     hidden[...] = both[:192, :units]
     hidden_x[...] = both[192:, :units]
-    total = product(both[192:, units:], down_x[...]) + product(both[192:, :units], probe_x[...])
+    total = product(both[192:, units:], theirs[:units]) + product(both[192:, :units], theirs[units:])
     for copy in copies:
         copy.wait()
     total = total + product(both[:192, units:], slots[0]) + product(both[:192, :units], slots[1])
@@ -193,14 +209,14 @@
     return jnp.concatenate(lines, axis=0)
 
 
-def cot_kernel(blocks, down, down_x, down_y, down_yx, out, slot, buffer, in_sem, out_sems):
+def cot_kernel(blocks, down, theirs, down_y, down_yx, out, slot, buffer, in_sem, out_sems):
     copy = start(down, slot, in_sem)
     yh = lax.axis_index(YH)
     tan_out = whole(blocks)
     first, second = moved(192, 96, low, tan_out), moved(192, 96, high, tan_out)
     buffer[1] = (over_width(first, down_y[...]) + over_width(second, down_yx[...])).astype(bf16)
     writes = [start(buffer.at[1], out.at[rows_at(1 - yh, 192)], out_sems.at[1])]
-    total = over_width(second, down_x[...])
+    total = over_width(second, theirs[: slot.shape[0]])
     copy.wait()
     buffer[0] = (total + over_width(first, slot[...])).astype(bf16)
     writes.append(start(buffer.at[0], out.at[rows_at(yh, 192)], out_sems.at[0]))
@@ -283,7 +299,9 @@
     nbytes += sum(int(np.prod(s)) * jnp.dtype(t).itemsize for s, t, _ in outs)
     return pl.pallas_call(
         kernel,
-        out_shape=[jax.ShapeDtypeStruct(s, t) for s, t, _ in outs],
+        out_shape=[
+            pltpu.HBM(s, t) if space is HBM else jax.ShapeDtypeStruct(s, t) for s, t, space in outs
+        ],
         in_specs=[space for _, space in ins],
         out_specs=[space for _, _, space in outs],
         scratch_shapes=list(scratch),
@@ -319,29 +337,38 @@
     )
     rows_y = swap(rows, YH)
     gates = (gate_weight, up_weight, gate_probe, up_probe)
-    gates_x = [swap(w, CORE) for w in gates]
+    downs = (down_weight, down_probe)
+    all_gates, all_downs = call(
+        pack_kernel,
+        60,
+        0,
+        [(w, HBM) for w in gates + downs],
+        [((4 * width, units), bf16, HBM), ((2 * units, width), bf16, HBM)],
+        [DMA((6,))],
+    )
+    gates_x, downs_x = swap(all_gates, CORE), swap(all_downs, CORE)
     inputs, partials = call(
         gates_kernel,
         60,
         8 * dots,
-        [(rows, VMEM), (rows_y, VMEM)] + [(w, HBM) for both in zip(gates, gates_x) for w in both],
-        [((192, width), bf16, VMEM), ((16, 24, 4 * units), bf16, HBM)],
-        [
+        [(rows, VMEM), (rows_y, VMEM)] + [(w, HBM) for w in gates] + [(gates_x, HBM)],
+        [((192, width), bf16, HBM), ((16, 24, 4 * units), bf16, HBM)],
+        [
+            pltpu.VMEM((192, width), bf16),
             pltpu.VMEM((8, width, units), bf16),
             pltpu.VMEM((16, 24, 4 * units), bf16),
             DMA((8,)),
-            DMA((4,)),
+            DMA((5,)),
         ],
     )
 
     parts = lax.all_to_all(partials.reshape(NDP, 48, 4 * units), DP, 0, 0).reshape(384, 4 * units)
-    swaps = (down_weight, down_probe, inputs, down_y)
-    down_x, probe_x, inputs_x, down_yx = (swap(w, CORE) for w in swaps)
+    inputs_x, down_yx = swap(inputs, CORE), swap(down_y, CORE)
     spread, coef_gate, coef_up = call(
         functools.partial(hidden_kernel, scale),
         8,
         0,
-        [(parts, VMEM), (inputs_x, ANY), (down_yx, ANY)],
+        [(parts, VMEM)],
         [((384, 2 * units), bf16, HBM), ((48, units), f32, VMEM), ((48, units), f32, VMEM)],
         [pltpu.VMEM((48, 2 * units), bf16), DMA((NDP,))],
     )
@@ -350,7 +377,10 @@
         down_kernel,
         14,
         4 * dots,
-        [(parts, VMEM), (down_weight, HBM), (down_probe, HBM), (down_x, VMEM), (probe_x, VMEM)],
+        [
+            (parts, VMEM), (down_weight, HBM), (down_probe, HBM), (downs_x, VMEM),
+            (inputs_x, ANY), (down_yx, ANY),
+        ],
         [
             ((96, width), bf16, VMEM),
             ((96, width), f32, VMEM),
@@ -386,7 +416,7 @@
         14,
         4 * dots,
         [
-            (blocks, VMEM), (down_weight, HBM), (down_x, VMEM),
+            (blocks, VMEM), (down_weight, HBM), (downs_x, VMEM),
             (down_y, VMEM), (down_yx, VMEM),
         ],
         [((384, units), bf16, HBM)],

time: 180 us -> 275 us (1.53)
  Pallas kernels: 19.5 us -> 116 us
  waiting for transfers between devices: 19.8 us -> 31.2 us
  starting transfers between devices: 90.6 us -> 81.1 us
    pallas_call x12 -> x13, Pallas kernels: 19.5 us -> 116 us  [call(): pl.pallas_call(kernel, out_shape=[pltpu.HBM(s, t) if space is HBM else ja...]
    ppermute x14 -> x10, waiting for transfers between devices: 5.56 us -> 14.3 us  [swap(): return lax.ppermute(value, axis, [(0, 1), (1, 0)])]
    all_to_all x1, starting transfers between devices: 15.8 us -> 9.56 us  [local(): rows = lax.all_to_all(rows.reshape(NZ, 48, 128), Z, 0, 0).reshape(768, 128)]
    all_to_all x1, waiting for transfers between devices: 0.01 us -> 4.02 us  [local(): lax.all_to_all(partials.reshape(NDP, 48, 4 * units), DP, 0, 0)]
    ppermute x14 -> x10, starting transfers between devices: 51.2 us -> 49.1 us  [swap(): return lax.ppermute(value, axis, [(0, 1), (1, 0)])]
  transfers between devices with their start and end apart: 19 -> 15, of which waited for: 5 -> 7; matrix products, arithmetic and copies ran while one was open for 0% -> 0% of each run, Pallas kernels for 2% -> 4%
where the time goes in v7:
time: 275 us; the launch traced here: 274 us
  Pallas kernels  116 us (42%)
  starting transfers between devices  81.1 us (29%)
  blocking collectives  43.3 us (16%)
  waiting for transfers between devices  31.2 us (11%)
    pallas_call x13, Pallas kernels, call(): pl.pallas_call(kernel, out_shape=[pltpu.HBM(s, t) if space is HBM else ja...  116 us
    ppermute x10, starting transfers between devices, swap(): return lax.ppermute(value, axis, [(0, 1), (1, 0)])  49.1 us
    all_to_all x1, blocking collectives, local(): lax.all_to_all(blocks.reshape(NZ, 48, 128), Z, 0, 0).reshape(768, 128)  23.2 us
    all_to_all x1, blocking collectives, local(): lax.all_to_all(spread.reshape(NZ, 48, 128), Z, 0, 0).reshape(768, 128)  20.2 us
    ppermute x10, waiting for transfers between devices, swap(): return lax.ppermute(value, axis, [(0, 1), (1, 0)])  14.3 us
    all_to_all x1, starting transfers between devices, local(): rows = lax.all_to_all(rows.reshape(NZ, 48, 128), Z, 0, 0).reshape(768, 128)  9.56 us
    all_to_all x1, starting transfers between devices, local(): lax.all_to_all(spread.reshape(16, 48, units), (CORE,) + DP, 0, 0)  7.17 us
    all_to_all x1, waiting for transfers between devices, local(): lax.all_to_all(spread.reshape(16, 48, units), (CORE,) + DP, 0, 0)  6.58 us
  transfers between devices with their start and end apart: 15, of which 7 were waited for; matrix products, arithmetic and copies ran while one was open for 0% of the time, Pallas kernels for 4%

profile of v7, /device:TPU:1, one launch (start us, length us, event | category | flops | bytes accessed | tf_op | source)
XLA Modules:
  0.0 274.1 jit_solution(2598753247110354062)
XLA Ops:
  0.7 96.5 %shard_map.113 = (bf16[4096,256]{1,0:T(8,128)(2,1)}, bf16[512,1024]{1,0:T(8,128)(2,1)}) custom-call(bf16[1024,256]{1,0:T(8,128)(2,1)} %rest_0_.1, bf16[1024,256]{1,0:T(8,128)(2,1)} %rest_1_.1, bf16[1024,256]{1,0:T(8,128)(2,1)} %rest_2_.1, bf16[1024,256]{1,0:T(8,128)(2,1)} %rest_3_.1, bf16[256,1024]{1,0:T(8,128)(2,1)} %down.3, bf16[256,1024]{1,0:T(8,128)(2,1)} %probe.1), custom_call_target="tpu_custom_call" | custom-call | bytes 6291456 | tf_op jit(solution)/shard_map/pallas_call | solution.py:300
  97.1 8.8 %collective-permute-start.2 = (bf16[4096,256]{1,0:T(8,128)(2,1)}, bf16[4096,256]{1,0:T(8,128)(2,1)}, u32[]{:S(2)}, u32[]{:S(2)}) collective-permute-start(bf16[4096,256]{1,0:T(8,128)(2,1)} %get-tuple-element.20), channel_id=1, source_target_pairs={{0,8},{8,0},{1,9},{9,1},{2,10},{10,2},{3,11},{11,3},{4,12},{12,4},... | collective-permute-start | bytes 6291464 | tf_op jit(solution)/shard_map/ppermute | solution.py:26
  105.9 1.0 shard_map.111
  106.9 9.6 %all-to-all-start = ((bf16[16,48,128]{2,1,0:T(8,128)(2,1)}), bf16[16,48,128]{2,1,0:T(8,128)(2,1)S(1)}, u32[]{:S(2)}, u32[]{:S(2)}) async-start(bf16[16,48,128]{2,1,0:T(8,128)(2,1)} %bitcast.26), calls=%async_computation | async-start | bytes 393216 | tf_op jit(solution)/shard_map/all_to_all | solution.py:328
  116.5 4.8 %collective-permute-start = (bf16[256,1024]{1,0:T(8,128)(2,1)S(1)}, bf16[256,1024]{1,0:T(8,128)(2,1)S(1)}, u32[]{:S(2)}, u32[]{:S(2)}) collective-permute-start(bf16[256,1024]{1,0:T(8,128)(2,1)S(1)} %copy-done), channel_id=1, source_target_pairs={{0,256},{256,0},{1,257},{257,1},{2,258},{258,2},{3,259},{259,3},{4... | collective-permute-start | bytes 1572872 | tf_op jit(solution)/shard_map/ppermute | solution.py:26
  121.3 11.8 %collective-permute-done.after.down_y = bf16[256,1024]{1,0:T(8,128)(2,1)S(1)} collective-permute-done((bf16[256,1024]{1,0:T(8,128)(2,1)S(1)}, bf16[256,1024]{1,0:T(8,128)(2,1)S(1)}, u32[]{:S(2)}, u32[]{:S(2)}) %collective-permute-start) | collective-permute-done | bytes 524320 | tf_op jit(solution)/shard_map/ppermute | solution.py:26
  133.2 4.8 %collective-permute-start.1 = (bf16[96,1024]{1,0:T(8,128)(2,1)S(1)}, bf16[96,1024]{1,0:T(8,128)(2,1)S(1)}, u32[]{:S(2)}, u32[]{:S(2)}) collective-permute-start(bf16[96,1024]{1,0:T(8,128)(2,1)S(1)} %shard_map.112.rows), channel_id=1, source_target_pairs={{0,256},{256,0},{1,257},{257,1},{2,258},{258,2},{3,259},{259,3},{4... | collective-permute-start | bytes 589832 | tf_op jit(solution)/shard_map/ppermute | solution.py:26
  138.1 3.3 %collective-permute-start.3 = (bf16[512,1024]{1,0:T(8,128)(2,1)}, bf16[512,1024]{1,0:T(8,128)(2,1)S(1)}, u32[]{:S(2)}, u32[]{:S(2)}) collective-permute-start(bf16[512,1024]{1,0:T(8,128)(2,1)} %get-tuple-element.23), channel_id=1, source_target_pairs={{0,8},{8,0},{1,9},{9,1},{2,10},{10,2},{3,11},{11,3},{4,12},{12,4},... | collective-permute-start | bytes 3145736 | tf_op jit(solution)/shard_map/ppermute | solution.py:26
  142.6 5.7 %shard_map.114 = (bf16[192,1024]{1,0:T(8,128)(2,1)}, bf16[16,24,1024]{2,1,0:T(8,128)(2,1)}) custom-call(bf16[96,1024]{1,0:T(8,128)(2,1)} %copy-done.3, bf16[96,1024]{1,0:T(8,128)(2,1)} %copy-done.7, bf16[1024,256]{1,0:T(8,128)(2,1)} %rest_0_.1, bf16[1024,256]{1,0:T(8,128)(2,1)} %rest_1_.1, bf16[1024,256]{1,0:T(8,128)(2,1)} %rest_2_.1, ...), custom_call_target="tpu_custom_call" | custom-call | flops 805306368 | bytes 5767168 | tf_op jit(solution)/shard_map/pallas_call | solution.py:300
  148.3 5.2 %all-to-all-start.1 = ((bf16[8,48,1024]{2,1,0:T(8,128)(2,1)}), bf16[8,48,1024]{2,1,0:T(8,128)(2,1)S(1)}, u32[]{:S(2)}, u32[]{:S(2)}) async-start(bf16[8,48,1024]{2,1,0:T(8,128)(2,1)} %bitcast.25), calls=%async_computation.1 | async-start | bytes 1572864 | tf_op jit(solution)/shard_map/all_to_all | solution.py:365
  153.5 4.2 %collective-permute-start.5 = (bf16[256,1024]{1,0:T(8,128)(2,1)S(1)}, bf16[256,1024]{1,0:T(8,128)(2,1)}, u32[]{:S(2)}, u32[]{:S(2)}) collective-permute-start(bf16[256,1024]{1,0:T(8,128)(2,1)S(1)} %collective-permute-done.after.down_y), channel_id=1, source_target_pairs={{0,8},{8,0},{1,9},{9,1},{2,10},{10,2},{3,11},{11,3},{4,12},{12,4},... | collective-permute-start | bytes 1572872 | tf_op jit(solution)/shard_map/ppermute | solution.py:26
  157.7 1.9 collective-permute-start.4
  159.6 4.0 %all-to-all-done.1 = bf16[8,48,1024]{2,1,0:T(8,128)(2,1)S(1)} async-done(((bf16[8,48,1024]{2,1,0:T(8,128)(2,1)}), bf16[8,48,1024]{2,1,0:T(8,128)(2,1)S(1)}, u32[]{:S(2)}, u32[]{:S(2)}) %all-to-all-start.1) | async-done | bytes 786464 | tf_op jit(solution)/shard_map/all_to_all | solution.py:365
  163.7 0.9 shard_map.115
  164.6 5.0 %all-to-all-start.2 = ((bf16[8,48,512]{2,1,0:T(8,128)(2,1)}), bf16[8,48,512]{2,1,0:T(8,128)(2,1)S(1)}, u32[]{:S(2)}, u32[]{:S(2)}) async-start(bf16[8,48,512]{2,1,0:T(8,128)(2,1)} %bitcast.28), calls=%async_computation.2 | async-start | bytes 786432 | tf_op jit(solution)/shard_map/all_to_all | solution.py:375
  169.7 6.3 %all-to-all-done.2 = bf16[8,48,512]{2,1,0:T(8,128)(2,1)S(1)} async-done(((bf16[8,48,512]{2,1,0:T(8,128)(2,1)}), bf16[8,48,512]{2,1,0:T(8,128)(2,1)S(1)}, u32[]{:S(2)}, u32[]{:S(2)}) %all-to-all-start.2) | async-done | bytes 393248 | tf_op jit(solution)/shard_map/all_to_all | solution.py:375
  176.0 1.0 shard_map.116
  177.1 4.5 %collective-permute-start.7 = (bf16[96,1024]{1,0:T(8,128)(2,1)S(1)}, bf16[96,1024]{1,0:T(8,128)(2,1)S(1)}, u32[]{:S(2)}, u32[]{:S(2)}) collective-permute-start(bf16[96,1024]{1,0:T(8,128)(2,1)S(1)} %get-tuple-element.28), channel_id=1, source_target_pairs={{0,256},{256,0},{1,257},{257,1},{2,258},{258,2},{3,259},{259,3},{4... | collective-permute-start | bytes 589832 | tf_op jit(solution)/shard_map/ppermute | solution.py:26
  181.6 5.2 %collective-permute-start.6 = (bf16[192,256]{1,0:T(8,128)(2,1)S(1)}, bf16[192,256]{1,0:T(8,128)(2,1)S(1)}, u32[]{:S(2)}, u32[]{:S(2)}) collective-permute-start(bf16[192,256]{1,0:T(8,128)(2,1)S(1)} %get-tuple-element.26), channel_id=1, source_target_pairs={{0,8},{8,0},{1,9},{9,1},{2,10},{10,2},{3,11},{11,3},{4,12},{12,4},... | collective-permute-start | bytes 294920 | tf_op jit(solution)/shard_map/ppermute | solution.py:26
  186.8 0.9 collective-permute-done.6.after.hidden_core
  188.5 23.2 %all_to_all.35 = bf16[16,48,128]{2,1,0:T(8,128)(2,1)S(1)} all-to-all(bf16[16,48,128]{2,1,0:T(8,128)(2,1)} %bitcast.24), channel_id=1, replica_groups=mesh['yh'=2,'z'=16,'core'=2,'x'=4,'yl'=2] {'z'}, dimensions={0} | all-to-all | bytes 393216 | tf_op jit(solution)/shard_map/all_to_all | solution.py:403
  212.5 20.2 %all_to_all.36 = bf16[16,48,128]{2,1,0:T(8,128)(2,1)S(1)} all-to-all(bf16[16,48,128]{2,1,0:T(8,128)(2,1)} %bitcast.27), channel_id=1, replica_groups=mesh['yh'=2,'z'=16,'core'=2,'x'=4,'yl'=2] {'z'}, dimensions={0} | all-to-all | bytes 393216 | tf_op jit(solution)/shard_map/all_to_all | solution.py:412
  232.6 3.4 %shard_map.119.after = bf16[384,256]{1,0:T(8,128)(2,1)} custom-call(bf16[768,128]{1,0:T(8,128)(2,1)S(1)} %bitcast.16, bf16[256,1024]{1,0:T(8,128)(2,1)S(1)} %copy-done, bf16[512,1024]{1,0:T(8,128)(2,1)S(1)} %collective-permute-done.3.theirs, bf16[256,1024]{1,0:T(8,128)(2,1)S(1)} %collective-permute-done.after.down_y, ...), custom_call_target="tpu_custom_call" | custom-call | flops 402653184 | bytes 3014656 | tf_op jit(solution)/shard_map/pallas_call | solution.py:300
  237.0 2.1 collective-permute-start.8
  239.0 5.0 %all-to-all-start.5 = ((bf16[16,24,256]{2,1,0:T(8,128)(2,1)}), bf16[16,24,256]{2,1,0:T(8,128)(2,1)S(1)}, u32[]{:S(2)}, u32[]{:S(2)}) async-start(bf16[16,24,256]{2,1,0:T(8,128)(2,1)} %bitcast.15), calls=%async_computation.5 | async-start | bytes 393216 | tf_op jit(solution)/shard_map/all_to_all | solution.py:430
  244.1 1.0 collective-permute-done.8.out_y.after
  245.1 9.4 %collective-permute-start.9 = (bf16[192,1024]{1,0:T(8,128)(2,1)S(1)}, bf16[192,1024]{1,0:T(8,128)(2,1)S(1)}, u32[]{:S(2)}, u32[]{:S(2)}) collective-permute-start(bf16[192,1024]{1,0:T(8,128)(2,1)S(1)} %pad_maximum_fusion), channel_id=1, source_target_pairs={{0,8},{8,0},{1,9},{9,1},{2,10},{10,2},{3,11},{11,3},{4,12},{12,4},... | collective-permute-start | bytes 1179656 | tf_op jit(solution)/shard_map/ppermute | solution.py:26
  254.5 1.1 shard_map.122
  255.6 7.2 %all-to-all-start.6 = ((bf16[16,48,256]{2,1,0:T(8,128)(2,1)}), bf16[16,48,256]{2,1,0:T(8,128)(2,1)S(1)}, u32[]{:S(2)}, u32[]{:S(2)}) async-start(bf16[16,48,256]{2,1,0:T(8,128)(2,1)} %bitcast.23), calls=%async_computation.6 | async-start | bytes 786432 | tf_op jit(solution)/shard_map/all_to_all | solution.py:443
  262.8 1.9 shard_map.121
  264.7 6.6 %all-to-all-done.6 = bf16[16,48,256]{2,1,0:T(8,128)(2,1)S(1)} async-done(((bf16[16,48,256]{2,1,0:T(8,128)(2,1)}), bf16[16,48,256]{2,1,0:T(8,128)(2,1)S(1)}, u32[]{:S(2)}, u32[]{:S(2)}) %all-to-all-start.6) | async-done | bytes 393248 | tf_op jit(solution)/shard_map/all_to_all | solution.py:443
  271.3 2.8 %shard_map.123 = (bf16[1024,256]{1,0:T(8,128)(2,1)}, bf16[1024,256]{1,0:T(8,128)(2,1)}) custom-call(bf16[768,256]{1,0:T(8,128)(2,1)S(1)} %bitcast.22, bf16[192,1024]{1,0:T(8,128)(2,1)S(1)} %copy-done.6, bf16[192,1024]{1,0:T(8,128)(2,1)} %collective-permute-done.4.after.inputs_x, f32[8,128]{1,0:T(8,128)S(1)} %get-tuple-element.32.after), custom_call_target="tpu_custom_call" | custom-call | flops 402653184 | bytes 2228224 | tf_op jit(solution)/shard_map/pallas_call | solution.py:300
  (30 shorter events, 3.9 us)
Async XLA Ops:
  0.6 115.8 %copy-start = (bf16[256,1024]{1,0:T(8,128)(2,1)S(1)}, bf16[256,1024]{1,0:T(8,128)(2,1)}, u32[]{:S(2)}) copy-start(bf16[256,1024]{1,0:T(8,128)(2,1)} %down.3) | copy-start | bytes 1572868
  0.6 105.3 %copy-start.4 = (bf16[6,1024]{1,0:T(8,128)(2,1)S(1)}, bf16[6,1024]{1,0:T(8,128)(2,1)}, u32[]{:S(2)}) copy-start(bf16[6,1024]{1,0:T(8,128)(2,1)} %table.1) | copy-start | bytes 36868
  97.1 44.8 %collective-permute-start.2 = (bf16[4096,256]{1,0:T(8,128)(2,1)}, bf16[4096,256]{1,0:T(8,128)(2,1)}, u32[]{:S(2)}, u32[]{:S(2)}) collective-permute-start(bf16[4096,256]{1,0:T(8,128)(2,1)} %get-tuple-element.20), channel_id=1, source_target_pairs={{0,8},{8,0},{1,9},{9,1},{2,10},{10,2},{3,11},{11,3},{4,12},{12,4},... | collective-permute-start | bytes 6291464 | tf_op jit(solution)/shard_map/ppermute | solution.py:26
  106.9 26.2 %all-to-all-start = ((bf16[16,48,128]{2,1,0:T(8,128)(2,1)}), bf16[16,48,128]{2,1,0:T(8,128)(2,1)S(1)}, u32[]{:S(2)}, u32[]{:S(2)}) async-start(bf16[16,48,128]{2,1,0:T(8,128)(2,1)} %bitcast.26), calls=%async_computation | async-start | bytes 393216 | tf_op jit(solution)/shard_map/all_to_all | solution.py:328
  116.5 16.6 %collective-permute-start = (bf16[256,1024]{1,0:T(8,128)(2,1)S(1)}, bf16[256,1024]{1,0:T(8,128)(2,1)S(1)}, u32[]{:S(2)}, u32[]{:S(2)}) collective-permute-start(bf16[256,1024]{1,0:T(8,128)(2,1)S(1)} %copy-done), channel_id=1, source_target_pairs={{0,256},{256,0},{1,257},{257,1},{2,258},{258,2},{3,259},{259,3},{4... | collective-permute-start | bytes 1572872 | tf_op jit(solution)/shard_map/ppermute | solution.py:26
  133.2 8.7 %copy-start.3 = (bf16[96,1024]{1,0:T(8,128)(2,1)}, bf16[96,1024]{1,0:T(8,128)(2,1)S(1)}, u32[]{:S(2)}) copy-start(bf16[96,1024]{1,0:T(8,128)(2,1)S(1)} %shard_map.112.rows) | copy-start | bytes 589828
  133.2 8.7 %collective-permute-start.1 = (bf16[96,1024]{1,0:T(8,128)(2,1)S(1)}, bf16[96,1024]{1,0:T(8,128)(2,1)S(1)}, u32[]{:S(2)}, u32[]{:S(2)}) collective-permute-start(bf16[96,1024]{1,0:T(8,128)(2,1)S(1)} %shard_map.112.rows), channel_id=1, source_target_pairs={{0,256},{256,0},{1,257},{257,1},{2,258},{258,2},{3,259},{259,3},{4... | collective-permute-start | bytes 589832 | tf_op jit(solution)/shard_map/ppermute | solution.py:26
  138.1 31.6 %collective-permute-start.3 = (bf16[512,1024]{1,0:T(8,128)(2,1)}, bf16[512,1024]{1,0:T(8,128)(2,1)S(1)}, u32[]{:S(2)}, u32[]{:S(2)}) collective-permute-start(bf16[512,1024]{1,0:T(8,128)(2,1)} %get-tuple-element.23), channel_id=1, source_target_pairs={{0,8},{8,0},{1,9},{9,1},{2,10},{10,2},{3,11},{11,3},{4,12},{12,4},... | collective-permute-start | bytes 3145736 | tf_op jit(solution)/shard_map/ppermute | solution.py:26
  141.9 0.7 copy-start.7
  148.3 27.7 %copy-start.1 = (bf16[256,1024]{1,0:T(8,128)(2,1)S(1)}, bf16[256,1024]{1,0:T(8,128)(2,1)}, u32[]{:S(2)}) copy-start(bf16[256,1024]{1,0:T(8,128)(2,1)} %probe.1) | copy-start | bytes 1572868
  148.3 15.3 %all-to-all-start.1 = ((bf16[8,48,1024]{2,1,0:T(8,128)(2,1)}), bf16[8,48,1024]{2,1,0:T(8,128)(2,1)S(1)}, u32[]{:S(2)}, u32[]{:S(2)}) async-start(bf16[8,48,1024]{2,1,0:T(8,128)(2,1)} %bitcast.25), calls=%async_computation.1 | async-start | bytes 1572864 | tf_op jit(solution)/shard_map/all_to_all | solution.py:365
  153.5 16.2 %collective-permute-start.5 = (bf16[256,1024]{1,0:T(8,128)(2,1)S(1)}, bf16[256,1024]{1,0:T(8,128)(2,1)}, u32[]{:S(2)}, u32[]{:S(2)}) collective-permute-start(bf16[256,1024]{1,0:T(8,128)(2,1)S(1)} %collective-permute-done.after.down_y), channel_id=1, source_target_pairs={{0,8},{8,0},{1,9},{9,1},{2,10},{10,2},{3,11},{11,3},{4,12},{12,4},... | collective-permute-start | bytes 1572872 | tf_op jit(solution)/shard_map/ppermute | solution.py:26
  157.7 12.0 %collective-permute-start.4 = (bf16[192,1024]{1,0:T(8,128)(2,1)}, bf16[192,1024]{1,0:T(8,128)(2,1)}, u32[]{:S(2)}, u32[]{:S(2)}) collective-permute-start(bf16[192,1024]{1,0:T(8,128)(2,1)} %get-tuple-element.24.inputs), channel_id=1, source_target_pairs={{0,8},{8,0},{1,9},{9,1},{2,10},{10,2},{3,11},{11,3},{4,12},{12,4},... | collective-permute-start | bytes 1179656 | tf_op jit(solution)/shard_map/ppermute | solution.py:26
  164.6 11.4 %all-to-all-start.2 = ((bf16[8,48,512]{2,1,0:T(8,128)(2,1)}), bf16[8,48,512]{2,1,0:T(8,128)(2,1)S(1)}, u32[]{:S(2)}, u32[]{:S(2)}) async-start(bf16[8,48,512]{2,1,0:T(8,128)(2,1)} %bitcast.28), calls=%async_computation.2 | async-start | bytes 786432 | tf_op jit(solution)/shard_map/all_to_all | solution.py:375
  177.1 10.7 %collective-permute-start.7 = (bf16[96,1024]{1,0:T(8,128)(2,1)S(1)}, bf16[96,1024]{1,0:T(8,128)(2,1)S(1)}, u32[]{:S(2)}, u32[]{:S(2)}) collective-permute-start(bf16[96,1024]{1,0:T(8,128)(2,1)S(1)} %get-tuple-element.28), channel_id=1, source_target_pairs={{0,256},{256,0},{1,257},{257,1},{2,258},{258,2},{3,259},{259,3},{4... | collective-permute-start | bytes 589832 | tf_op jit(solution)/shard_map/ppermute | solution.py:26
  181.6 6.2 %collective-permute-start.6 = (bf16[192,256]{1,0:T(8,128)(2,1)S(1)}, bf16[192,256]{1,0:T(8,128)(2,1)S(1)}, u32[]{:S(2)}, u32[]{:S(2)}) collective-permute-start(bf16[192,256]{1,0:T(8,128)(2,1)S(1)} %get-tuple-element.26), channel_id=1, source_target_pairs={{0,8},{8,0},{1,9},{9,1},{2,10},{10,2},{3,11},{11,3},{4,12},{12,4},... | collective-permute-start | bytes 294920 | tf_op jit(solution)/shard_map/ppermute | solution.py:26
  236.0 0.9 copy-start.2
  236.9 25.8 %copy-start.5 = (s32[384]{0:T(512)S(1)}, s32[384]{0:T(512)}, u32[]{:S(2)}) copy-start(s32[384]{0:T(512)} %ids.1) | copy-start | bytes 4612
  237.0 34.3 %copy-start.6 = (bf16[192,1024]{1,0:T(8,128)(2,1)S(1)}, bf16[192,1024]{1,0:T(8,128)(2,1)}, u32[]{:S(2)}) copy-start(bf16[192,1024]{1,0:T(8,128)(2,1)} %get-tuple-element.24.inputs) | copy-start | bytes 1179652
  237.0 8.1 %collective-permute-start.8 = (bf16[96,1024]{1,0:T(8,128)(2,1)S(1)}, bf16[96,1024]{1,0:T(8,128)(2,1)S(1)}, u32[]{:S(2)}, u32[]{:S(2)}) collective-permute-start(bf16[96,1024]{1,0:T(8,128)(2,1)S(1)} %shard_map.120.out), channel_id=1, source_target_pairs={{0,256},{256,0},{1,257},{257,1},{2,258},{258,2},{3,259},{259,3},{4... | collective-permute-start | bytes 589832 | tf_op jit(solution)/shard_map/ppermute | solution.py:26
  239.0 15.5 %all-to-all-start.5 = ((bf16[16,24,256]{2,1,0:T(8,128)(2,1)}), bf16[16,24,256]{2,1,0:T(8,128)(2,1)S(1)}, u32[]{:S(2)}, u32[]{:S(2)}) async-start(bf16[16,24,256]{2,1,0:T(8,128)(2,1)} %bitcast.15), calls=%async_computation.5 | async-start | bytes 393216 | tf_op jit(solution)/shard_map/all_to_all | solution.py:430
  245.1 17.7 %collective-permute-start.9 = (bf16[192,1024]{1,0:T(8,128)(2,1)S(1)}, bf16[192,1024]{1,0:T(8,128)(2,1)S(1)}, u32[]{:S(2)}, u32[]{:S(2)}) collective-permute-start(bf16[192,1024]{1,0:T(8,128)(2,1)S(1)} %pad_maximum_fusion), channel_id=1, source_target_pairs={{0,8},{8,0},{1,9},{9,1},{2,10},{10,2},{3,11},{11,3},{4,12},{12,4},... | collective-permute-start | bytes 1179656 | tf_op jit(solution)/shard_map/ppermute | solution.py:26
  255.6 15.7 %all-to-all-start.6 = ((bf16[16,48,256]{2,1,0:T(8,128)(2,1)}), bf16[16,48,256]{2,1,0:T(8,128)(2,1)S(1)}, u32[]{:S(2)}, u32[]{:S(2)}) async-start(bf16[16,48,256]{2,1,0:T(8,128)(2,1)} %bitcast.23), calls=%async_computation.6 | async-start | bytes 786432 | tf_op jit(solution)/shard_map/all_to_all | solution.py:443

commit v8 on v6

--- a/solution.py
+++ b/solution.py
@@ -46,33 +46,12 @@
     return product(table, values).astype(bf16)
 
 
-def halves_inside(values):
-    row = lax.broadcasted_iota(jnp.int32, (48, 48), 0)
-    column = lax.broadcasted_iota(jnp.int32, (48, 48), 1)
-    q = (row * 171) >> 11
-    source = ((q & 1) * 2 + (q >> 1)) * 12 + row - 12 * q
-    table = jnp.where(source == column, 1.0, 0.0)
-    return jnp.dot(table, values, precision=lax.Precision.HIGHEST, preferred_element_type=f32)
-
-
 def pick(q, j):
     return (q & 1) * 96 + (q >> 1) * 12 + j
 
 
 def by_half(q, j):
     return ((q & 7) * 4 + (q >> 4) * 2 + ((q >> 3) & 1)) * 12 + j
-
-
-def low(q, j):
-    return jnp.where((q & 1) == 0, (q >> 1) * 12 + j, -1)
-
-
-def high(q, j):
-    return jnp.where((q & 1) == 1, (q >> 1) * 12 + j, -1)
-
-
-def by_core(q, j):
-    return (((q >> 1) & 1) * 4 + (q & 1) * 2 + (q >> 2)) * 12 + j
 
 
 def by_kind(q, j):
@@ -104,7 +83,7 @@
         write.wait()
 
 
-def lines_kernel(rows, after, out, buffer):
+def lines_kernel(rows, out, buffer):
     buffer[...] = rows[...].astype(f32)
     for n in range(8):
         line = buffer[pl.ds(n, 96, stride=8), :]
@@ -112,24 +91,29 @@
 
 
 def gates_kernel(rows, rows_y, *rest):
-    weights, (inputs, out, slots, buffer, in_sems, out_sems) = rest[:8], rest[8:]
-    copies = [start(weights[k], slots.at[k], in_sems.at[k]) for k in range(8)]
+    weights, (kept, out, inputs, slots, buffer, in_sems, out_sems) = rest[:8], rest[8:]
     units = slots.shape[2]
+    ahead = 3
+    copies = [start(weights[n], slots.at[n], in_sems.at[n]) for n in range(ahead)]
     inputs[...] = moved(192, 192, pick, jnp.concatenate([rows[...], rows_y[...]], axis=0))
-    writes = []
-    for k in range(4):
+    writes = [start(inputs, kept, out_sems.at[4])]
+    for n in range(8):
+        copies[n].wait()
+        if n + ahead < 8:
+            copies.append(start(weights[n + ahead], slots.at[n + ahead], in_sems.at[n + ahead]))
+        k, h = n // 2, n % 2
         columns = slice(k * units, (k + 1) * units)
-        for h in range(2):
-            copies[2 * k + h].wait()
-            partial = product(inputs[...], slots[2 * k + h])
-            for d in range(NDP):
-                buffer[2 * d + h, :, columns] = partial[24 * d : 24 * d + 24].astype(bf16)
-        writes.append(start(buffer.at[:, :, columns], out.at[:, :, columns], out_sems.at[k]))
-    for write in writes:
-        write.wait()
-
-
-def hidden_kernel(scale, parts, after, after_too, out, coef_gate, coef_up, buffer, sems):
+        partial = product(inputs[...], slots[n])
+        for d in range(NDP):
+            buffer[2 * d + h, :, columns] = partial[24 * d : 24 * d + 24].astype(bf16)
+        if h:
+            place, target = buffer.at[:, :, columns], out.at[:, :, columns]
+            writes.append(start(place, target, out_sems.at[k]))
+    for write in writes:
+        write.wait()
+
+
+def hidden_kernel(scale, parts, after, out, coef_gate, coef_up, buffer, sems):
     sums = parts[0:48].astype(f32)
     for d in range(1, NDP):
         sums = sums + parts[48 * d : 48 * d + 48].astype(f32)
@@ -141,8 +125,8 @@
     buffer[:, :units] = (activated * up_value).astype(bf16)
     buffer[:, units:] = (slope * tan_gate * up_value + activated * tan_up).astype(bf16)
     writes = [start(buffer, out.at[48 * d : 48 * d + 48], sems.at[d]) for d in range(NDP)]
-    coef_gate[...] = halves_inside(up_value * slope * scale)
-    coef_up[...] = halves_inside(activated * scale)
+    coef_gate[...] = up_value * slope * scale
+    coef_up[...] = activated * scale
     for write in writes:
         write.wait()
 
@@ -193,41 +177,32 @@
     return jnp.concatenate(lines, axis=0)
 
 
-def cot_kernel(blocks, down, down_x, down_y, down_yx, out, slot, buffer, in_sem, out_sems):
+def cot_kernel(blocks, blocks_y, down, down_x, tan_out, out, slot, buffer, in_sem, out_sem):
     copy = start(down, slot, in_sem)
-    yh = lax.axis_index(YH)
-    tan_out = whole(blocks)
-    first, second = moved(192, 96, low, tan_out), moved(192, 96, high, tan_out)
-    buffer[1] = (over_width(first, down_y[...]) + over_width(second, down_yx[...])).astype(bf16)
-    writes = [start(buffer.at[1], out.at[rows_at(1 - yh, 192)], out_sems.at[1])]
-    total = over_width(second, down_x[...])
-    copy.wait()
-    buffer[0] = (total + over_width(first, slot[...])).astype(bf16)
-    writes.append(start(buffer.at[0], out.at[rows_at(yh, 192)], out_sems.at[0]))
-    for write in writes:
-        write.wait()
-
-
-def whole_kernel(blocks, after, out):
-    out[...] = whole(blocks)
-
-
-def cot_units_kernel(parts, coef_gate, coef_up, after, out, buffer, sems):
-    yh, core = lax.axis_index(YH), lax.axis_index(CORE)
-    values = parts[...].astype(f32)
-    sums = []
-    for h in range(2):
-        total = values[192 * h : 192 * h + 24]
-        for d in range(1, NDP):
-            total = total + values[192 * h + 24 * d : 192 * h + 24 * d + 24]
-        sums.append(total)
-    first = jnp.where(yh == 0, sums[0], sums[1])
-    second = jnp.where(yh == 0, sums[1], sums[0])
-    total = jnp.concatenate([first, second], axis=0)
-    both = jnp.concatenate([total * coef_gate[...], total * coef_up[...]], axis=0).astype(bf16)
-    buffer[...] = moved(96, 96, by_core, both)
+    tan_out[:96] = whole(blocks)
+    tan_out[96:] = whole(blocks_y)
+    left = moved(192, 192, pick, tan_out[...])
+    for h in (1, 0):
+        if h == 0:
+            copy.wait()
+        total = over_width(left, down_x[...] if h else slot[...])
+        for d in range(NDP):
+            buffer[2 * d + h] = total[24 * d : 24 * d + 24].astype(bf16)
+    write = start(buffer, out, out_sem)
+    write.wait()
+
+
+def cot_units_kernel(parts, coef_gate, coef_up, out, buffer, sems):
+    core = lax.axis_index(CORE)
+    total = parts[0:48].astype(f32)
+    for d in range(1, NDP):
+        total = total + parts[48 * d : 48 * d + 48].astype(f32)
+    cot_gate, cot_up = total * coef_gate[...], total * coef_up[...]
     writes = []
     for h in range(2):
+        rows = slice(24 * h, 24 * h + 24)
+        block = jnp.concatenate([cot_gate[rows], cot_up[rows]], axis=0)
+        buffer[48 * h : 48 * h + 48, :] = block.astype(bf16)
         base = (core if h == 0 else 1 - core) * NDP
         for d in range(NDP):
             source = buffer.at[48 * h : 48 * h + 48]
@@ -256,10 +231,9 @@
         write.wait()
 
 
-def ggn_down_kernel(scale, ids, hidden, hidden_core, out, out_y, out_core, ggn_down, tangent_out, flag):
+def ggn_down_kernel(scale, ids, hidden, hidden_core, out, out_core, ggn_down, tangent_out, flag):
     yh, z, core = lax.axis_index(YH), lax.axis_index(Z), lax.axis_index(CORE)
-    total = over_rows(hidden[0:96], out[...]) + over_rows(hidden[96:192], out_y[...])
-    total = total + over_rows(hidden_core[...], out_core[...])
+    total = over_rows(hidden[...], out[...]) + over_rows(hidden_core[...], out_core[...])
     ggn_down[...] = (total * scale).astype(bf16)
     own_count = tangent_out.shape[0]
     first = ((yh * NZ + z) * 2 + core) * own_count
@@ -273,7 +247,7 @@
         place = place + (holder // 2) % NZ * own_count + stored % own_count
         wanted = jnp.where(row == i, place, wanted)
     hot = jnp.where(wanted == column, 1.0, 0.0).astype(bf16)
-    every = jnp.concatenate([out[...], out_y[...], out_core[...]], axis=0)
+    every = jnp.concatenate([out[...], out_core[...]], axis=0)
     tangent_out[...] = product(hot, every)[:own_count].astype(bf16)
     flag[...] = jnp.zeros_like(flag)
 
@@ -283,7 +257,9 @@
     nbytes += sum(int(np.prod(s)) * jnp.dtype(t).itemsize for s, t, _ in outs)
     return pl.pallas_call(
         kernel,
-        out_shape=[jax.ShapeDtypeStruct(s, t) for s, t, _ in outs],
+        out_shape=[
+            pltpu.HBM(s, t) if space is HBM else jax.ShapeDtypeStruct(s, t) for s, t, space in outs
+        ],
         in_specs=[space for _, space in ins],
         out_specs=[space for _, _, space in outs],
         scratch_shapes=list(scratch),
@@ -308,12 +284,11 @@
         [pltpu.VMEM((48, 128), bf16), DMA((NZ,))],
     )
     rows = lax.all_to_all(rows.reshape(NZ, 48, 128), Z, 0, 0).reshape(768, 128)
-    down_y = swap(down_weight, YH)
     (rows,) = call(
         lines_kernel,
         4,
         0,
-        [(rows, VMEM), (down_y, ANY)],
+        [(rows, VMEM)],
         [((96, width), bf16, VMEM)],
         [pltpu.VMEM((768, 128), f32)],
     )
@@ -325,23 +300,23 @@
         60,
         8 * dots,
         [(rows, VMEM), (rows_y, VMEM)] + [(w, HBM) for both in zip(gates, gates_x) for w in both],
-        [((192, width), bf16, VMEM), ((16, 24, 4 * units), bf16, HBM)],
+        [((192, width), bf16, HBM), ((16, 24, 4 * units), bf16, HBM)],
         [
+            pltpu.VMEM((192, width), bf16),
             pltpu.VMEM((8, width, units), bf16),
             pltpu.VMEM((16, 24, 4 * units), bf16),
             DMA((8,)),
-            DMA((4,)),
+            DMA((5,)),
         ],
     )
 
     parts = lax.all_to_all(partials.reshape(NDP, 48, 4 * units), DP, 0, 0).reshape(384, 4 * units)
-    swaps = (down_weight, down_probe, inputs, down_y)
-    down_x, probe_x, inputs_x, down_yx = (swap(w, CORE) for w in swaps)
+    down_x, probe_x, inputs_x = (swap(w, CORE) for w in (down_weight, down_probe, inputs))
     spread, coef_gate, coef_up = call(
         functools.partial(hidden_kernel, scale),
         8,
         0,
-        [(parts, VMEM), (inputs_x, ANY), (down_yx, ANY)],
+        [(parts, VMEM), (inputs_x, ANY)],
         [((384, 2 * units), bf16, HBM), ((48, units), f32, VMEM), ((48, units), f32, VMEM)],
         [pltpu.VMEM((48, 2 * units), bf16), DMA((NDP,))],
     )
@@ -381,45 +356,31 @@
     )
     blocks = lax.all_to_all(spread.reshape(NZ, 48, 128), Z, 0, 0).reshape(768, 128)
 
-    (cot,) = call(
+    blocks_y = swap(blocks, YH)
+    out, cot = call(
         cot_kernel,
         14,
         4 * dots,
-        [
-            (blocks, VMEM), (down_weight, HBM), (down_x, VMEM),
-            (down_y, VMEM), (down_yx, VMEM),
-        ],
-        [((384, units), bf16, HBM)],
-        [
-            pltpu.VMEM((units, width), bf16),
-            pltpu.VMEM((2, 192, units), bf16),
-            DMA,
-            DMA((2,)),
-        ],
-    )
-    parts = lax.all_to_all(cot.reshape(16, 24, units), (YH,) + DP, 0, 0).reshape(384, units)
-    (out,) = call(
-        whole_kernel, 4, 0, [(blocks, VMEM), (cot, ANY)], [((96, width), bf16, VMEM)]
-    )
-    out_y = swap(out, YH)
+        [(blocks, VMEM), (blocks_y, VMEM), (down_weight, HBM), (down_x, VMEM)],
+        [((192, width), bf16, VMEM), ((16, 24, units), bf16, HBM)],
+        [pltpu.VMEM((units, width), bf16), pltpu.VMEM((16, 24, units), bf16), DMA, DMA],
+    )
+    parts = lax.all_to_all(cot.reshape(NDP, 48, units), DP, 0, 0).reshape(384, units)
+    out_core = swap(out, CORE)
     (spread,) = call(
         cot_units_kernel,
         6,
         0,
-        [(parts, VMEM), (coef_gate, VMEM), (coef_up, VMEM), (out_y, ANY)],
+        [(parts, VMEM), (coef_gate, VMEM), (coef_up, VMEM)],
         [((768, units), bf16, HBM)],
         [pltpu.VMEM((96, units), bf16), DMA((16,))],
     )
     parts = lax.all_to_all(spread.reshape(16, 48, units), (CORE,) + DP, 0, 0).reshape(768, units)
-    out_core = swap(jnp.concatenate([out, out_y]), CORE)
     ggn_down, tangent_out, flag = call(
         functools.partial(ggn_down_kernel, scale),
         14,
         2 * dots,
-        [
-            (ids, SMEM), (hidden, VMEM), (hidden_core, VMEM),
-            (out, VMEM), (out_y, VMEM), (out_core, VMEM),
-        ],
+        [(ids, SMEM), (hidden, VMEM), (hidden_core, VMEM), (out, VMEM), (out_core, VMEM)],
         [
             ((units, width), bf16, VMEM),
             ((own_count, width), bf16, VMEM),

time: 180 us -> 172 us (0.956)
  waiting for transfers between devices: 19.8 us -> 26.6 us
  starting transfers between devices: 90.6 us -> 84.3 us
  blocking collectives: 43.5 us -> 40 us
  local copies, waits for them, and re-layouts: 3.96 us -> 1.44 us
  Pallas kernels: 19.5 us -> 17.7 us
    ppermute x14 -> x12, starting transfers between devices: 51.2 us -> 46.4 us  [swap(): return lax.ppermute(value, axis, [(0, 1), (1, 0)])]
    ppermute x14 -> x12, waiting for transfers between devices: 5.56 us -> 9.93 us  [swap(): return lax.ppermute(value, axis, [(0, 1), (1, 0)])]
    all_to_all x1, blocking collectives: 23.6 us -> 19.8 us  [local(): lax.all_to_all(blocks.reshape(NZ, 48, 128), Z, 0, 0).reshape(768, 128)]
    all_to_all x1, waiting for transfers between devices: 0.01 us -> 3.4 us  [local(): rows = lax.all_to_all(rows.reshape(NZ, 48, 128), Z, 0, 0).reshape(768, 128)]
    unnamed x28 -> x22, local copies, waits for them, and re-layouts: 3.96 us -> 1.44 us
    pallas_call x12 -> x11, Pallas kernels: 19.5 us -> 17.7 us  [call(): pl.pallas_call(kernel, out_shape=[pltpu.HBM(s, t) if space is HBM else ja...]
  transfers between devices with their start and end apart: 19 -> 17, of which waited for: 5 -> 6; matrix products, arithmetic and copies ran while one was open for 0% -> 0% of each run, Pallas kernels for 2% -> 2%
where the time goes in v8:
time: 172 us; the launch traced here: 171 us
  starting transfers between devices  84.3 us (49%)
  blocking collectives  40 us (23%)
  waiting for transfers between devices  26.6 us (15%)
  Pallas kernels  17.7 us (10%)
    ppermute x12, starting transfers between devices, swap(): return lax.ppermute(value, axis, [(0, 1), (1, 0)])  46.4 us
    all_to_all x1, blocking collectives, local(): lax.all_to_all(spread.reshape(NZ, 48, 128), Z, 0, 0).reshape(768, 128)  20.2 us
    all_to_all x1, blocking collectives, local(): lax.all_to_all(blocks.reshape(NZ, 48, 128), Z, 0, 0).reshape(768, 128)  19.8 us
    pallas_call x11, Pallas kernels, call(): pl.pallas_call(kernel, out_shape=[pltpu.HBM(s, t) if space is HBM else ja...  17.7 us
    all_to_all x1, starting transfers between devices, local(): rows = lax.all_to_all(rows.reshape(NZ, 48, 128), Z, 0, 0).reshape(768, 128)  15.8 us
    ppermute x12, waiting for transfers between devices, swap(): return lax.ppermute(value, axis, [(0, 1), (1, 0)])  9.93 us
    all_to_all x1, starting transfers between devices, local(): lax.all_to_all(spread.reshape(16, 48, units), (CORE,) + DP, 0, 0)  8.08 us
    all_to_all x1, waiting for transfers between devices, local(): lax.all_to_all(spread.reshape(16, 48, units), (CORE,) + DP, 0, 0)  6.71 us
  transfers between devices with their start and end apart: 17, of which 6 were waited for; matrix products, arithmetic and copies ran while one was open for 0% of the time, Pallas kernels for 2%

profile of v8, /device:TPU:1, one launch (start us, length us, event | category | flops | bytes accessed | tf_op | source)
XLA Modules:
  0.0 171.0 jit_solution(8152369936578176072)
XLA Ops:
  1.4 1.0 shard_map.111
  2.3 15.8 %all-to-all-start = ((bf16[16,48,128]{2,1,0:T(8,128)(2,1)}), bf16[16,48,128]{2,1,0:T(8,128)(2,1)S(1)}, u32[]{:S(2)}, u32[]{:S(2)}) async-start(bf16[16,48,128]{2,1,0:T(8,128)(2,1)} %bitcast.25), calls=%async_computation | async-start | bytes 393216 | tf_op jit(solution)/shard_map/all_to_all | solution.py:286
  18.1 2.9 %collective-permute-start.1 = (bf16[1024,256]{1,0:T(8,128)(2,1)S(1)}, bf16[1024,256]{1,0:T(8,128)(2,1)S(1)}, u32[]{:S(2)}, u32[]{:S(2)}) collective-permute-start(bf16[1024,256]{1,0:T(8,128)(2,1)S(1)} %copy-done.5), channel_id=1, source_target_pairs={{0,8},{8,0},{1,9},{9,1},{2,10},{10,2},{3,11},{11,3},{4,12},{12,4},... | collective-permute-start | bytes 1572872 | tf_op jit(solution)/shard_map/ppermute | solution.py:26
  21.0 1.9 %collective-permute-start.2 = (bf16[1024,256]{1,0:T(8,128)(2,1)}, bf16[1024,256]{1,0:T(8,128)(2,1)S(1)}, u32[]{:S(2)}, u32[]{:S(2)}) collective-permute-start(bf16[1024,256]{1,0:T(8,128)(2,1)} %rest_2_.1), channel_id=1, source_target_pairs={{0,8},{8,0},{1,9},{9,1},{2,10},{10,2},{3,11},{11,3},{4,12},{12,4},... | collective-permute-start | bytes 1572872 | tf_op jit(solution)/shard_map/ppermute | solution.py:26
  22.9 2.4 %collective-permute-start.3 = (bf16[1024,256]{1,0:T(8,128)(2,1)}, bf16[1024,256]{1,0:T(8,128)(2,1)S(1)}, u32[]{:S(2)}, u32[]{:S(2)}) collective-permute-start(bf16[1024,256]{1,0:T(8,128)(2,1)} %rest_4_.1), channel_id=1, source_target_pairs={{0,8},{8,0},{1,9},{9,1},{2,10},{10,2},{3,11},{11,3},{4,12},{12,4},... | collective-permute-start | bytes 1572872 | tf_op jit(solution)/shard_map/ppermute | solution.py:26
  25.3 1.9 %collective-permute-start.4 = (bf16[1024,256]{1,0:T(8,128)(2,1)}, bf16[1024,256]{1,0:T(8,128)(2,1)S(1)}, u32[]{:S(2)}, u32[]{:S(2)}) collective-permute-start(bf16[1024,256]{1,0:T(8,128)(2,1)} %rest_6_.1), channel_id=1, source_target_pairs={{0,8},{8,0},{1,9},{9,1},{2,10},{10,2},{3,11},{11,3},{4,12},{12,4},... | collective-permute-start | bytes 1572872 | tf_op jit(solution)/shard_map/ppermute | solution.py:26
  27.3 3.4 %all-to-all-done = bf16[16,48,128]{2,1,0:T(8,128)(2,1)S(1)} async-done(((bf16[16,48,128]{2,1,0:T(8,128)(2,1)}), bf16[16,48,128]{2,1,0:T(8,128)(2,1)S(1)}, u32[]{:S(2)}, u32[]{:S(2)}) %all-to-all-start) | async-done | bytes 196640 | tf_op jit(solution)/shard_map/all_to_all | solution.py:286
  30.8 4.8 %collective-permute-start = (bf16[96,1024]{1,0:T(8,128)(2,1)S(1)}, bf16[96,1024]{1,0:T(8,128)(2,1)S(1)}, u32[]{:S(2)}, u32[]{:S(2)}) collective-permute-start(bf16[96,1024]{1,0:T(8,128)(2,1)S(1)} %shard_map.112.rows), channel_id=1, source_target_pairs={{0,256},{256,0},{1,257},{257,1},{2,258},{258,2},{3,259},{259,3},{4... | collective-permute-start | bytes 589832 | tf_op jit(solution)/shard_map/ppermute | solution.py:26
  35.7 3.0 %collective-permute-done.rows_y = bf16[96,1024]{1,0:T(8,128)(2,1)S(1)} collective-permute-done((bf16[96,1024]{1,0:T(8,128)(2,1)S(1)}, bf16[96,1024]{1,0:T(8,128)(2,1)S(1)}, u32[]{:S(2)}, u32[]{:S(2)}) %collective-permute-start) | collective-permute-done | bytes 196640 | tf_op jit(solution)/shard_map/ppermute | solution.py:26
  39.4 5.9 %shard_map.113 = (bf16[192,1024]{1,0:T(8,128)(2,1)}, bf16[16,24,1024]{2,1,0:T(8,128)(2,1)}) custom-call(bf16[96,1024]{1,0:T(8,128)(2,1)} %copy-done, bf16[96,1024]{1,0:T(8,128)(2,1)} %copy-done.10, bf16[1024,256]{1,0:T(8,128)(2,1)} %rest_0_.1, bf16[1024,256]{1,0:T(8,128)(2,1)} %copy-done.6, bf16[1024,256]{1,0:T(8,128)(2,1)} %rest_2_.1, ...), custom_call_target="tpu_custom_call" | custom-call | flops 805306368 | bytes 5767168 | tf_op jit(solution)/shard_map/pallas_call | solution.py:258
  45.3 5.2 %all-to-all-start.1 = ((bf16[8,48,1024]{2,1,0:T(8,128)(2,1)}), bf16[8,48,1024]{2,1,0:T(8,128)(2,1)S(1)}, u32[]{:S(2)}, u32[]{:S(2)}) async-start(bf16[8,48,1024]{2,1,0:T(8,128)(2,1)} %bitcast.24), calls=%async_computation.1 | async-start | bytes 1572864 | tf_op jit(solution)/shard_map/all_to_all | solution.py:313
  50.5 8.2 %collective-permute-start.5 = (bf16[192,1024]{1,0:T(8,128)(2,1)}, bf16[192,1024]{1,0:T(8,128)(2,1)S(1)}, u32[]{:S(2)}, u32[]{:S(2)}) collective-permute-start(bf16[192,1024]{1,0:T(8,128)(2,1)} %get-tuple-element.21.inputs), channel_id=1, source_target_pairs={{0,8},{8,0},{1,9},{9,1},{2,10},{10,2},{3,11},{11,3},{4,12},{12,4},... | collective-permute-start | bytes 1179656 | tf_op jit(solution)/shard_map/ppermute | solution.py:26
  58.7 1.9 %collective-permute-start.7 = (bf16[256,1024]{1,0:T(8,128)(2,1)S(1)}, bf16[256,1024]{1,0:T(8,128)(2,1)S(1)}, u32[]{:S(2)}, u32[]{:S(2)}) collective-permute-start(bf16[256,1024]{1,0:T(8,128)(2,1)S(1)} %copy-done.1), channel_id=1, source_target_pairs={{0,8},{8,0},{1,9},{9,1},{2,10},{10,2},{3,11},{11,3},{4,12},{12,4},... | collective-permute-start | bytes 1572872 | tf_op jit(solution)/shard_map/ppermute | solution.py:26
  60.6 2.4 %collective-permute-start.6 = (bf16[256,1024]{1,0:T(8,128)(2,1)S(1)}, bf16[256,1024]{1,0:T(8,128)(2,1)S(1)}, u32[]{:S(2)}, u32[]{:S(2)}) collective-permute-start(bf16[256,1024]{1,0:T(8,128)(2,1)S(1)} %copy-done.2), channel_id=1, source_target_pairs={{0,8},{8,0},{1,9},{9,1},{2,10},{10,2},{3,11},{11,3},{4,12},{12,4},... | collective-permute-start | bytes 1572872 | tf_op jit(solution)/shard_map/ppermute | solution.py:26
  63.1 0.9 shard_map.114
  64.0 5.4 %all-to-all-start.2 = ((bf16[8,48,512]{2,1,0:T(8,128)(2,1)}), bf16[8,48,512]{2,1,0:T(8,128)(2,1)S(1)}, u32[]{:S(2)}, u32[]{:S(2)}) async-start(bf16[8,48,512]{2,1,0:T(8,128)(2,1)} %bitcast.27), calls=%async_computation.2 | async-start | bytes 786432 | tf_op jit(solution)/shard_map/all_to_all | solution.py:323
  69.5 6.5 %all-to-all-done.2 = bf16[8,48,512]{2,1,0:T(8,128)(2,1)S(1)} async-done(((bf16[8,48,512]{2,1,0:T(8,128)(2,1)}), bf16[8,48,512]{2,1,0:T(8,128)(2,1)S(1)}, u32[]{:S(2)}, u32[]{:S(2)}) %all-to-all-start.2) | async-done | bytes 393248 | tf_op jit(solution)/shard_map/all_to_all | solution.py:323
  76.0 1.0 shard_map.115
  77.0 4.5 %collective-permute-start.9 = (bf16[96,1024]{1,0:T(8,128)(2,1)S(1)}, bf16[96,1024]{1,0:T(8,128)(2,1)S(1)}, u32[]{:S(2)}, u32[]{:S(2)}) collective-permute-start(bf16[96,1024]{1,0:T(8,128)(2,1)S(1)} %get-tuple-element.26), channel_id=1, source_target_pairs={{0,256},{256,0},{1,257},{257,1},{2,258},{258,2},{3,259},{259,3},{4... | collective-permute-start | bytes 589832 | tf_op jit(solution)/shard_map/ppermute | solution.py:26
  81.6 4.9 %collective-permute-start.8 = (bf16[192,256]{1,0:T(8,128)(2,1)S(1)}, bf16[192,256]{1,0:T(8,128)(2,1)S(1)}, u32[]{:S(2)}, u32[]{:S(2)}) collective-permute-start(bf16[192,256]{1,0:T(8,128)(2,1)S(1)} %get-tuple-element.24), channel_id=1, source_target_pairs={{0,8},{8,0},{1,9},{9,1},{2,10},{10,2},{3,11},{11,3},{4,12},{12,4},... | collective-permute-start | bytes 294920 | tf_op jit(solution)/shard_map/ppermute | solution.py:26
  86.5 0.9 collective-permute-done.8.after.hidden_core
  88.1 19.8 %all_to_all.35 = bf16[16,48,128]{2,1,0:T(8,128)(2,1)S(1)} all-to-all(bf16[16,48,128]{2,1,0:T(8,128)(2,1)} %bitcast.23), channel_id=1, replica_groups=mesh['yh'=2,'z'=16,'core'=2,'x'=4,'yl'=2] {'z'}, dimensions={0} | all-to-all | bytes 393216 | tf_op jit(solution)/shard_map/all_to_all | solution.py:348
  108.8 20.2 %all_to_all.36 = bf16[16,48,128]{2,1,0:T(8,128)(2,1)S(1)} all-to-all(bf16[16,48,128]{2,1,0:T(8,128)(2,1)} %bitcast.26), channel_id=1, replica_groups=mesh['yh'=2,'z'=16,'core'=2,'x'=4,'yl'=2] {'z'}, dimensions={0} | all-to-all | bytes 393216 | tf_op jit(solution)/shard_map/all_to_all | solution.py:357
  128.9 1.9 %collective-permute-start.10 = (bf16[768,128]{1,0:T(8,128)(2,1)S(1)}, bf16[768,128]{1,0:T(8,128)(2,1)S(1)}, u32[]{:S(2)}, u32[]{:S(2)}) collective-permute-start(bf16[768,128]{1,0:T(8,128)(2,1)S(1)} %bitcast.20), channel_id=1, source_target_pairs={{0,256},{256,0},{1,257},{257,1},{2,258},{258,2},{3,259},{259,3},{4... | collective-permute-start | bytes 589832 | tf_op jit(solution)/shard_map/ppermute | solution.py:26
  130.8 6.0 %collective-permute-done.10.blocks_y = bf16[768,128]{1,0:T(8,128)(2,1)S(1)} collective-permute-done((bf16[768,128]{1,0:T(8,128)(2,1)S(1)}, bf16[768,128]{1,0:T(8,128)(2,1)S(1)}, u32[]{:S(2)}, u32[]{:S(2)}) %collective-permute-start.10) | collective-permute-done | bytes 196640 | tf_op jit(solution)/shard_map/ppermute | solution.py:26
  136.8 1.7 %shard_map.118 = (bf16[192,1024]{1,0:T(8,128)(2,1)S(1)}, bf16[16,24,256]{2,1,0:T(8,128)(2,1)}) custom-call(bf16[768,128]{1,0:T(8,128)(2,1)S(1)} %bitcast.21, bf16[768,128]{1,0:T(8,128)(2,1)S(1)} %collective-permute-done.10.blocks_y, bf16[256,1024]{1,0:T(8,128)(2,1)S(1)} %copy-done.2, bf16[256,1024]{1,0:T(8,128)(2,1)S(1)} %collective-permute-done.6.down_x), custom_call_target="tpu_custom_call" | custom-call | flops 402653184 | bytes 2031616 | tf_op jit(solution)/shard_map/pallas_call | solution.py:258
  138.6 3.4 %all-to-all-start.5 = ((bf16[8,48,256]{2,1,0:T(8,128)(2,1)}), bf16[8,48,256]{2,1,0:T(8,128)(2,1)S(1)}, u32[]{:S(2)}, u32[]{:S(2)}) async-start(bf16[8,48,256]{2,1,0:T(8,128)(2,1)} %bitcast.28), calls=%async_computation.5 | async-start | bytes 393216 | tf_op jit(solution)/shard_map/all_to_all | solution.py:368
  142.0 8.7 %collective-permute-start.11 = (bf16[192,1024]{1,0:T(8,128)(2,1)S(1)}, bf16[192,1024]{1,0:T(8,128)(2,1)S(1)}, u32[]{:S(2)}, u32[]{:S(2)}) collective-permute-start(bf16[192,1024]{1,0:T(8,128)(2,1)S(1)} %get-tuple-element.27.out), channel_id=1, source_target_pairs={{0,8},{8,0},{1,9},{9,1},{2,10},{10,2},{3,11},{11,3},{4,12},{12,4},... | collective-permute-start | bytes 1179656 | tf_op jit(solution)/shard_map/ppermute | solution.py:26
  151.5 8.1 %all-to-all-start.6 = ((bf16[16,48,256]{2,1,0:T(8,128)(2,1)}), bf16[16,48,256]{2,1,0:T(8,128)(2,1)S(1)}, u32[]{:S(2)}, u32[]{:S(2)}) async-start(bf16[16,48,256]{2,1,0:T(8,128)(2,1)} %bitcast.22), calls=%async_computation.6 | async-start | bytes 786432 | tf_op jit(solution)/shard_map/all_to_all | solution.py:378
  159.6 1.8 %shard_map.119 = (bf16[256,1024]{1,0:T(8,128)(2,1)}, bf16[6,1024]{1,0:T(8,128)(2,1)}, f32[8,128]{1,0:T(8,128)S(1)}) custom-call(s32[384]{0:T(512)S(1)} %copy-done.4, bf16[192,256]{1,0:T(8,128)(2,1)S(1)} %get-tuple-element.23.hidden, bf16[192,256]{1,0:T(8,128)(2,1)S(1)} %collective-permute-done.8.after.hidden_core, ...), custom_call_target="tpu_custom_call" | custom-call | flops 201326592 | bytes 1525248 | tf_op jit(solution)/shard_map/pallas_call | solution.py:258
  161.5 6.7 %all-to-all-done.6 = bf16[16,48,256]{2,1,0:T(8,128)(2,1)S(1)} async-done(((bf16[16,48,256]{2,1,0:T(8,128)(2,1)}), bf16[16,48,256]{2,1,0:T(8,128)(2,1)S(1)}, u32[]{:S(2)}, u32[]{:S(2)}) %all-to-all-start.6) | async-done | bytes 393248 | tf_op jit(solution)/shard_map/all_to_all | solution.py:378
  168.2 2.8 %shard_map.121 = (bf16[1024,256]{1,0:T(8,128)(2,1)}, bf16[1024,256]{1,0:T(8,128)(2,1)}) custom-call(bf16[768,256]{1,0:T(8,128)(2,1)S(1)} %bitcast.19, bf16[192,1024]{1,0:T(8,128)(2,1)} %get-tuple-element.21.inputs, bf16[192,1024]{1,0:T(8,128)(2,1)S(1)} %collective-permute-done.5.after.inputs_x, f32[8,128]{1,0:T(8,128)S(1)} %get-tuple-element.32.after), custom_call_target="tpu_custom_call" | custom-call | flops 402653184 | bytes 2228224 | tf_op jit(solution)/shard_map/pallas_call | solution.py:258
  (37 shorter events, 4.0 us)
Async XLA Ops:
  0.6 0.7 copy-start.3
  1.3 16.8 %copy-start.5 = (bf16[1024,256]{1,0:T(8,128)(2,1)S(1)}, bf16[1024,256]{1,0:T(8,128)(2,1)}, u32[]{:S(2)}) copy-start(bf16[1024,256]{1,0:T(8,128)(2,1)} %rest_0_.1) | copy-start | bytes 1572868
  2.3 28.3 %all-to-all-start = ((bf16[16,48,128]{2,1,0:T(8,128)(2,1)}), bf16[16,48,128]{2,1,0:T(8,128)(2,1)S(1)}, u32[]{:S(2)}, u32[]{:S(2)}) async-start(bf16[16,48,128]{2,1,0:T(8,128)(2,1)} %bitcast.25), calls=%async_computation | async-start | bytes 393216 | tf_op jit(solution)/shard_map/all_to_all | solution.py:286
  18.1 17.5 %collective-permute-start.1 = (bf16[1024,256]{1,0:T(8,128)(2,1)S(1)}, bf16[1024,256]{1,0:T(8,128)(2,1)S(1)}, u32[]{:S(2)}, u32[]{:S(2)}) collective-permute-start(bf16[1024,256]{1,0:T(8,128)(2,1)S(1)} %copy-done.5), channel_id=1, source_target_pairs={{0,8},{8,0},{1,9},{9,1},{2,10},{10,2},{3,11},{11,3},{4,12},{12,4},... | collective-permute-start | bytes 1572872 | tf_op jit(solution)/shard_map/ppermute | solution.py:26
  21.0 14.7 %collective-permute-start.2 = (bf16[1024,256]{1,0:T(8,128)(2,1)}, bf16[1024,256]{1,0:T(8,128)(2,1)S(1)}, u32[]{:S(2)}, u32[]{:S(2)}) collective-permute-start(bf16[1024,256]{1,0:T(8,128)(2,1)} %rest_2_.1), channel_id=1, source_target_pairs={{0,8},{8,0},{1,9},{9,1},{2,10},{10,2},{3,11},{11,3},{4,12},{12,4},... | collective-permute-start | bytes 1572872 | tf_op jit(solution)/shard_map/ppermute | solution.py:26
  22.9 12.7 %collective-permute-start.3 = (bf16[1024,256]{1,0:T(8,128)(2,1)}, bf16[1024,256]{1,0:T(8,128)(2,1)S(1)}, u32[]{:S(2)}, u32[]{:S(2)}) collective-permute-start(bf16[1024,256]{1,0:T(8,128)(2,1)} %rest_4_.1), channel_id=1, source_target_pairs={{0,8},{8,0},{1,9},{9,1},{2,10},{10,2},{3,11},{11,3},{4,12},{12,4},... | collective-permute-start | bytes 1572872 | tf_op jit(solution)/shard_map/ppermute | solution.py:26
  25.3 10.4 %collective-permute-start.4 = (bf16[1024,256]{1,0:T(8,128)(2,1)}, bf16[1024,256]{1,0:T(8,128)(2,1)S(1)}, u32[]{:S(2)}, u32[]{:S(2)}) collective-permute-start(bf16[1024,256]{1,0:T(8,128)(2,1)} %rest_6_.1), channel_id=1, source_target_pairs={{0,8},{8,0},{1,9},{9,1},{2,10},{10,2},{3,11},{11,3},{4,12},{12,4},... | collective-permute-start | bytes 1572872 | tf_op jit(solution)/shard_map/ppermute | solution.py:26
  30.8 7.9 %copy-start = (bf16[96,1024]{1,0:T(8,128)(2,1)}, bf16[96,1024]{1,0:T(8,128)(2,1)S(1)}, u32[]{:S(2)}) copy-start(bf16[96,1024]{1,0:T(8,128)(2,1)S(1)} %shard_map.112.rows) | copy-start | bytes 589828
  30.8 7.9 %collective-permute-start = (bf16[96,1024]{1,0:T(8,128)(2,1)S(1)}, bf16[96,1024]{1,0:T(8,128)(2,1)S(1)}, u32[]{:S(2)}, u32[]{:S(2)}) collective-permute-start(bf16[96,1024]{1,0:T(8,128)(2,1)S(1)} %shard_map.112.rows), channel_id=1, source_target_pairs={{0,256},{256,0},{1,257},{257,1},{2,258},{258,2},{3,259},{259,3},{4... | collective-permute-start | bytes 589832 | tf_op jit(solution)/shard_map/ppermute | solution.py:26
  35.6 3.1 %copy-start.6 = (bf16[1024,256]{1,0:T(8,128)(2,1)}, bf16[1024,256]{1,0:T(8,128)(2,1)S(1)}, u32[]{:S(2)}) copy-start(bf16[1024,256]{1,0:T(8,128)(2,1)S(1)} %collective-permute-done.1.rest_1_) | copy-start | bytes 1572868
  35.6 3.1 %copy-start.7 = (bf16[1024,256]{1,0:T(8,128)(2,1)}, bf16[1024,256]{1,0:T(8,128)(2,1)S(1)}, u32[]{:S(2)}) copy-start(bf16[1024,256]{1,0:T(8,128)(2,1)S(1)} %collective-permute-done.2.rest_3_) | copy-start | bytes 1572868
  35.7 3.0 %copy-start.8 = (bf16[1024,256]{1,0:T(8,128)(2,1)}, bf16[1024,256]{1,0:T(8,128)(2,1)S(1)}, u32[]{:S(2)}) copy-start(bf16[1024,256]{1,0:T(8,128)(2,1)S(1)} %collective-permute-done.3.rest_5_) | copy-start | bytes 1572868
  35.7 3.0 %copy-start.9 = (bf16[1024,256]{1,0:T(8,128)(2,1)}, bf16[1024,256]{1,0:T(8,128)(2,1)S(1)}, u32[]{:S(2)}) copy-start(bf16[1024,256]{1,0:T(8,128)(2,1)S(1)} %collective-permute-done.4.rest_7_) | copy-start | bytes 1572868
  38.7 0.7 copy-start.10
  45.3 13.4 %copy-start.1 = (bf16[256,1024]{1,0:T(8,128)(2,1)S(1)}, bf16[256,1024]{1,0:T(8,128)(2,1)}, u32[]{:S(2)}) copy-start(bf16[256,1024]{1,0:T(8,128)(2,1)} %probe.1) | copy-start | bytes 1572868
  45.3 15.3 %copy-start.2 = (bf16[256,1024]{1,0:T(8,128)(2,1)S(1)}, bf16[256,1024]{1,0:T(8,128)(2,1)}, u32[]{:S(2)}) copy-start(bf16[256,1024]{1,0:T(8,128)(2,1)} %down.3) | copy-start | bytes 1572868
  45.3 17.7 %all-to-all-start.1 = ((bf16[8,48,1024]{2,1,0:T(8,128)(2,1)}), bf16[8,48,1024]{2,1,0:T(8,128)(2,1)S(1)}, u32[]{:S(2)}, u32[]{:S(2)}) async-start(bf16[8,48,1024]{2,1,0:T(8,128)(2,1)} %bitcast.24), calls=%async_computation.1 | async-start | bytes 1572864 | tf_op jit(solution)/shard_map/all_to_all | solution.py:313
  50.5 12.5 %collective-permute-start.5 = (bf16[192,1024]{1,0:T(8,128)(2,1)}, bf16[192,1024]{1,0:T(8,128)(2,1)S(1)}, u32[]{:S(2)}, u32[]{:S(2)}) collective-permute-start(bf16[192,1024]{1,0:T(8,128)(2,1)} %get-tuple-element.21.inputs), channel_id=1, source_target_pairs={{0,8},{8,0},{1,9},{9,1},{2,10},{10,2},{3,11},{11,3},{4,12},{12,4},... | collective-permute-start | bytes 1179656 | tf_op jit(solution)/shard_map/ppermute | solution.py:26
  58.7 10.8 %collective-permute-start.7 = (bf16[256,1024]{1,0:T(8,128)(2,1)S(1)}, bf16[256,1024]{1,0:T(8,128)(2,1)S(1)}, u32[]{:S(2)}, u32[]{:S(2)}) collective-permute-start(bf16[256,1024]{1,0:T(8,128)(2,1)S(1)} %copy-done.1), channel_id=1, source_target_pairs={{0,8},{8,0},{1,9},{9,1},{2,10},{10,2},{3,11},{11,3},{4,12},{12,4},... | collective-permute-start | bytes 1572872 | tf_op jit(solution)/shard_map/ppermute | solution.py:26
  60.6 8.8 %collective-permute-start.6 = (bf16[256,1024]{1,0:T(8,128)(2,1)S(1)}, bf16[256,1024]{1,0:T(8,128)(2,1)S(1)}, u32[]{:S(2)}, u32[]{:S(2)}) collective-permute-start(bf16[256,1024]{1,0:T(8,128)(2,1)S(1)} %copy-done.2), channel_id=1, source_target_pairs={{0,8},{8,0},{1,9},{9,1},{2,10},{10,2},{3,11},{11,3},{4,12},{12,4},... | collective-permute-start | bytes 1572872 | tf_op jit(solution)/shard_map/ppermute | solution.py:26
  64.0 12.0 %all-to-all-start.2 = ((bf16[8,48,512]{2,1,0:T(8,128)(2,1)}), bf16[8,48,512]{2,1,0:T(8,128)(2,1)S(1)}, u32[]{:S(2)}, u32[]{:S(2)}) async-start(bf16[8,48,512]{2,1,0:T(8,128)(2,1)} %bitcast.27), calls=%async_computation.2 | async-start | bytes 786432 | tf_op jit(solution)/shard_map/all_to_all | solution.py:323
  77.0 10.4 %collective-permute-start.9 = (bf16[96,1024]{1,0:T(8,128)(2,1)S(1)}, bf16[96,1024]{1,0:T(8,128)(2,1)S(1)}, u32[]{:S(2)}, u32[]{:S(2)}) collective-permute-start(bf16[96,1024]{1,0:T(8,128)(2,1)S(1)} %get-tuple-element.26), channel_id=1, source_target_pairs={{0,256},{256,0},{1,257},{257,1},{2,258},{258,2},{3,259},{259,3},{4... | collective-permute-start | bytes 589832 | tf_op jit(solution)/shard_map/ppermute | solution.py:26
  81.6 5.8 %collective-permute-start.8 = (bf16[192,256]{1,0:T(8,128)(2,1)S(1)}, bf16[192,256]{1,0:T(8,128)(2,1)S(1)}, u32[]{:S(2)}, u32[]{:S(2)}) collective-permute-start(bf16[192,256]{1,0:T(8,128)(2,1)S(1)} %get-tuple-element.24), channel_id=1, source_target_pairs={{0,8},{8,0},{1,9},{9,1},{2,10},{10,2},{3,11},{11,3},{4,12},{12,4},... | collective-permute-start | bytes 294920 | tf_op jit(solution)/shard_map/ppermute | solution.py:26
  128.9 7.9 %collective-permute-start.10 = (bf16[768,128]{1,0:T(8,128)(2,1)S(1)}, bf16[768,128]{1,0:T(8,128)(2,1)S(1)}, u32[]{:S(2)}, u32[]{:S(2)}) collective-permute-start(bf16[768,128]{1,0:T(8,128)(2,1)S(1)} %bitcast.20), channel_id=1, source_target_pairs={{0,256},{256,0},{1,257},{257,1},{2,258},{258,2},{3,259},{259,3},{4... | collective-permute-start | bytes 589832 | tf_op jit(solution)/shard_map/ppermute | solution.py:26
  138.6 12.1 %all-to-all-start.5 = ((bf16[8,48,256]{2,1,0:T(8,128)(2,1)}), bf16[8,48,256]{2,1,0:T(8,128)(2,1)S(1)}, u32[]{:S(2)}, u32[]{:S(2)}) async-start(bf16[8,48,256]{2,1,0:T(8,128)(2,1)} %bitcast.28), calls=%async_computation.5 | async-start | bytes 393216 | tf_op jit(solution)/shard_map/all_to_all | solution.py:368
  142.0 17.7 %collective-permute-start.11 = (bf16[192,1024]{1,0:T(8,128)(2,1)S(1)}, bf16[192,1024]{1,0:T(8,128)(2,1)S(1)}, u32[]{:S(2)}, u32[]{:S(2)}) collective-permute-start(bf16[192,1024]{1,0:T(8,128)(2,1)S(1)} %get-tuple-element.27.out), channel_id=1, source_target_pairs={{0,8},{8,0},{1,9},{9,1},{2,10},{10,2},{3,11},{11,3},{4,12},{12,4},... | collective-permute-start | bytes 1179656 | tf_op jit(solution)/shard_map/ppermute | solution.py:26
  151.5 8.1 %copy-start.4 = (s32[384]{0:T(512)S(1)}, s32[384]{0:T(512)}, u32[]{:S(2)}) copy-start(s32[384]{0:T(512)} %ids.1) | copy-start | bytes 4612
  151.5 16.6 %all-to-all-start.6 = ((bf16[16,48,256]{2,1,0:T(8,128)(2,1)}), bf16[16,48,256]{2,1,0:T(8,128)(2,1)S(1)}, u32[]{:S(2)}, u32[]{:S(2)}) async-start(bf16[16,48,256]{2,1,0:T(8,128)(2,1)} %bitcast.22), calls=%async_computation.6 | async-start | bytes 786432 | tf_op jit(solution)/shard_map/all_to_all | solution.py:378

commit v9 on v8

--- a/solution.py
+++ b/solution.py
@@ -91,24 +91,23 @@
 
 
 def gates_kernel(rows, rows_y, *rest):
-    weights, (kept, out, inputs, slots, buffer, in_sems, out_sems) = rest[:8], rest[8:]
+    own, theirs, rest = rest[:4], rest[4:8], rest[8:]
+    kept, out, inputs, slots, buffer, in_sems, out_sems = rest
     units = slots.shape[2]
-    ahead = 3
-    copies = [start(weights[n], slots.at[n], in_sems.at[n]) for n in range(ahead)]
+    copies = [start(own[k], slots.at[k], in_sems.at[k]) for k in range(4)]
     inputs[...] = moved(192, 192, pick, jnp.concatenate([rows[...], rows_y[...]], axis=0))
     writes = [start(inputs, kept, out_sems.at[4])]
-    for n in range(8):
-        copies[n].wait()
-        if n + ahead < 8:
-            copies.append(start(weights[n + ahead], slots.at[n + ahead], in_sems.at[n + ahead]))
-        k, h = n // 2, n % 2
-        columns = slice(k * units, (k + 1) * units)
-        partial = product(inputs[...], slots[n])
-        for d in range(NDP):
-            buffer[2 * d + h, :, columns] = partial[24 * d : 24 * d + 24].astype(bf16)
-        if h:
-            place, target = buffer.at[:, :, columns], out.at[:, :, columns]
-            writes.append(start(place, target, out_sems.at[k]))
+    for h in (1, 0):
+        for k in range(4):
+            columns = slice(k * units, (k + 1) * units)
+            if h == 0:
+                copies[k].wait()
+            partial = product(inputs[...], theirs[k][...] if h else slots[k])
+            for d in range(NDP):
+                buffer[2 * d + h, :, columns] = partial[24 * d : 24 * d + 24].astype(bf16)
+            if h == 0:
+                place, target = buffer.at[:, :, columns], out.at[:, :, columns]
+                writes.append(start(place, target, out_sems.at[k]))
     for write in writes:
         write.wait()
 
@@ -145,28 +144,22 @@
     sent[...] = total[96:].astype(bf16)
 
 
-def add_kernel(kept, received, after, out, buffer, sems):
+def add_kernel(kept, received, after, out):
     total = (kept[...] + received[...].astype(f32)).astype(bf16)
-    writes = []
     for a in range(2):
         for j in range(8):
-            buffer[48 * (8 * a + j) : 48 * (8 * a + j) + 48, :] = total[
+            out[48 * (8 * a + j) : 48 * (8 * a + j) + 48, :] = total[
                 48 * a : 48 * a + 48, 128 * j : 128 * j + 128
             ]
-        span = slice(384 * a, 384 * a + 384)
-        writes.append(start(buffer.at[span], out.at[span], sems.at[a]))
-    for write in writes:
-        write.wait()
-
-
-def sum_kernel(parts, out, buffer, sems):
+
+
+def sum_kernel(parts, out):
     total = parts[0:48].astype(f32)
     for i in range(1, NZ):
         total = total + parts[48 * i : 48 * i + 48].astype(f32)
-    buffer[...] = total.astype(bf16)
-    writes = [start(buffer, out.at[48 * i : 48 * i + 48], sems.at[i]) for i in range(NZ)]
-    for write in writes:
-        write.wait()
+    total = total.astype(bf16)
+    for i in range(NZ):
+        out[48 * i : 48 * i + 48, :] = total
 
 
 def whole(blocks):
@@ -263,7 +256,7 @@
         in_specs=[space for _, space in ins],
         out_specs=[space for _, _, space in outs],
         scratch_shapes=list(scratch),
-        compiler_params=pltpu.CompilerParams(vmem_limit_bytes=mib * MIB),
+        compiler_params=pltpu.CompilerParams(vmem_limit_bytes=int(mib * MIB)),
         cost_estimate=pl.CostEstimate(flops=flops, bytes_accessed=nbytes, transcendentals=0),
     )(*[a for a, _ in ins])
 
@@ -297,15 +290,15 @@
     gates_x = [swap(w, CORE) for w in gates]
     inputs, partials = call(
         gates_kernel,
-        60,
+        58.5,
         8 * dots,
-        [(rows, VMEM), (rows_y, VMEM)] + [(w, HBM) for both in zip(gates, gates_x) for w in both],
+        [(rows, VMEM), (rows_y, VMEM)] + [(w, HBM) for w in gates] + [(w, VMEM) for w in gates_x],
         [((192, width), bf16, HBM), ((16, 24, 4 * units), bf16, HBM)],
         [
             pltpu.VMEM((192, width), bf16),
-            pltpu.VMEM((8, width, units), bf16),
+            pltpu.VMEM((4, width, units), bf16),
             pltpu.VMEM((16, 24, 4 * units), bf16),
-            DMA((8,)),
+            DMA((4,)),
             DMA((5,)),
         ],
     )
@@ -342,8 +335,7 @@
         6,
         0,
         [(kept, VMEM), (received, VMEM), (hidden_core, ANY)],
-        [((768, 128), bf16, HBM)],
-        [pltpu.VMEM((768, 128), bf16), DMA((2,))],
+        [((768, 128), bf16, VMEM)],
     )
     parts = lax.all_to_all(blocks.reshape(NZ, 48, 128), Z, 0, 0).reshape(768, 128)
     (spread,) = call(
@@ -351,8 +343,7 @@
         4,
         0,
         [(parts, VMEM)],
-        [((768, 128), bf16, HBM)],
-        [pltpu.VMEM((48, 128), bf16), DMA((NZ,))],
+        [((768, 128), bf16, VMEM)],
     )
     blocks = lax.all_to_all(spread.reshape(NZ, 48, 128), Z, 0, 0).reshape(768, 128)
 

time: 172 us -> 169 us (0.983)
  Pallas kernels: 17.7 us -> 15.3 us
    pallas_call x11, Pallas kernels: 17.7 us -> 15.3 us  [call(): pl.pallas_call(kernel, out_shape=[pltpu.HBM(s, t) if space is HBM else ja...]
where the time goes in v9:
time: 169 us; the launch traced here: 168 us
  starting transfers between devices  84.3 us (50%)
  blocking collectives  39.5 us (23%)
  waiting for transfers between devices  26.6 us (16%)
  Pallas kernels  15.3 us (9%)
    ppermute x12, starting transfers between devices, swap(): return lax.ppermute(value, axis, [(0, 1), (1, 0)])  46.4 us
    all_to_all x1, blocking collectives, local(): lax.all_to_all(spread.reshape(NZ, 48, 128), Z, 0, 0).reshape(768, 128)  19.9 us
    all_to_all x1, blocking collectives, local(): lax.all_to_all(blocks.reshape(NZ, 48, 128), Z, 0, 0).reshape(768, 128)  19.6 us
    all_to_all x1, starting transfers between devices, local(): rows = lax.all_to_all(rows.reshape(NZ, 48, 128), Z, 0, 0).reshape(768, 128)  15.8 us
    pallas_call x11, Pallas kernels, call(): pl.pallas_call(kernel, out_shape=[pltpu.HBM(s, t) if space is HBM else ja...  15.3 us
    ppermute x12, waiting for transfers between devices, swap(): return lax.ppermute(value, axis, [(0, 1), (1, 0)])  9.93 us
    all_to_all x1, starting transfers between devices, local(): lax.all_to_all(spread.reshape(16, 48, units), (CORE,) + DP, 0, 0)  8.08 us
    all_to_all x1, waiting for transfers between devices, local(): lax.all_to_all(spread.reshape(16, 48, units), (CORE,) + DP, 0, 0)  6.71 us
  transfers between devices with their start and end apart: 17, of which 6 were waited for; matrix products, arithmetic and copies ran while one was open for 0% of the time, Pallas kernels for 2%

profile of v9, /device:TPU:1, one launch (start us, length us, event | category | flops | bytes accessed | tf_op | source)
XLA Modules:
  0.0 168.1 jit_solution(16161378016466105851)
XLA Ops:
  1.4 1.0 shard_map.111
  2.3 15.8 %all-to-all-start = ((bf16[16,48,128]{2,1,0:T(8,128)(2,1)}), bf16[16,48,128]{2,1,0:T(8,128)(2,1)S(1)}, u32[]{:S(2)}, u32[]{:S(2)}) async-start(bf16[16,48,128]{2,1,0:T(8,128)(2,1)} %bitcast.26), calls=%async_computation | async-start | bytes 393216 | tf_op jit(solution)/shard_map/all_to_all | solution.py:279
  18.1 2.9 %collective-permute-start.1 = (bf16[1024,256]{1,0:T(8,128)(2,1)S(1)}, bf16[1024,256]{1,0:T(8,128)(2,1)S(1)}, u32[]{:S(2)}, u32[]{:S(2)}) collective-permute-start(bf16[1024,256]{1,0:T(8,128)(2,1)S(1)} %copy-done.5), channel_id=1, source_target_pairs={{0,8},{8,0},{1,9},{9,1},{2,10},{10,2},{3,11},{11,3},{4,12},{12,4},... | collective-permute-start | bytes 1572872 | tf_op jit(solution)/shard_map/ppermute | solution.py:26
  21.0 1.9 %collective-permute-start.2 = (bf16[1024,256]{1,0:T(8,128)(2,1)}, bf16[1024,256]{1,0:T(8,128)(2,1)S(1)}, u32[]{:S(2)}, u32[]{:S(2)}) collective-permute-start(bf16[1024,256]{1,0:T(8,128)(2,1)} %rest_1_.1), channel_id=1, source_target_pairs={{0,8},{8,0},{1,9},{9,1},{2,10},{10,2},{3,11},{11,3},{4,12},{12,4},... | collective-permute-start | bytes 1572872 | tf_op jit(solution)/shard_map/ppermute | solution.py:26
  22.9 2.4 %collective-permute-start.3 = (bf16[1024,256]{1,0:T(8,128)(2,1)}, bf16[1024,256]{1,0:T(8,128)(2,1)S(1)}, u32[]{:S(2)}, u32[]{:S(2)}) collective-permute-start(bf16[1024,256]{1,0:T(8,128)(2,1)} %rest_2_.1), channel_id=1, source_target_pairs={{0,8},{8,0},{1,9},{9,1},{2,10},{10,2},{3,11},{11,3},{4,12},{12,4},... | collective-permute-start | bytes 1572872 | tf_op jit(solution)/shard_map/ppermute | solution.py:26
  25.3 1.9 %collective-permute-start.4 = (bf16[1024,256]{1,0:T(8,128)(2,1)}, bf16[1024,256]{1,0:T(8,128)(2,1)S(1)}, u32[]{:S(2)}, u32[]{:S(2)}) collective-permute-start(bf16[1024,256]{1,0:T(8,128)(2,1)} %rest_3_.1), channel_id=1, source_target_pairs={{0,8},{8,0},{1,9},{9,1},{2,10},{10,2},{3,11},{11,3},{4,12},{12,4},... | collective-permute-start | bytes 1572872 | tf_op jit(solution)/shard_map/ppermute | solution.py:26
  27.3 3.4 %all-to-all-done = bf16[16,48,128]{2,1,0:T(8,128)(2,1)S(1)} async-done(((bf16[16,48,128]{2,1,0:T(8,128)(2,1)}), bf16[16,48,128]{2,1,0:T(8,128)(2,1)S(1)}, u32[]{:S(2)}, u32[]{:S(2)}) %all-to-all-start) | async-done | bytes 196640 | tf_op jit(solution)/shard_map/all_to_all | solution.py:279
  30.8 4.8 %collective-permute-start = (bf16[96,1024]{1,0:T(8,128)(2,1)S(1)}, bf16[96,1024]{1,0:T(8,128)(2,1)S(1)}, u32[]{:S(2)}, u32[]{:S(2)}) collective-permute-start(bf16[96,1024]{1,0:T(8,128)(2,1)S(1)} %shard_map.112.rows), channel_id=1, source_target_pairs={{0,256},{256,0},{1,257},{257,1},{2,258},{258,2},{3,259},{259,3},{4... | collective-permute-start | bytes 589832 | tf_op jit(solution)/shard_map/ppermute | solution.py:26
  35.7 3.0 %collective-permute-done.rows_y = bf16[96,1024]{1,0:T(8,128)(2,1)S(1)} collective-permute-done((bf16[96,1024]{1,0:T(8,128)(2,1)S(1)}, bf16[96,1024]{1,0:T(8,128)(2,1)S(1)}, u32[]{:S(2)}, u32[]{:S(2)}) %collective-permute-start) | collective-permute-done | bytes 196640 | tf_op jit(solution)/shard_map/ppermute | solution.py:26
  39.4 4.9 %shard_map.113 = (bf16[192,1024]{1,0:T(8,128)(2,1)}, bf16[16,24,1024]{2,1,0:T(8,128)(2,1)}) custom-call(bf16[96,1024]{1,0:T(8,128)(2,1)} %copy-done, bf16[96,1024]{1,0:T(8,128)(2,1)} %copy-done.10, bf16[1024,256]{1,0:T(8,128)(2,1)} %rest_0_.1, bf16[1024,256]{1,0:T(8,128)(2,1)} %rest_1_.1, bf16[1024,256]{1,0:T(8,128)(2,1)} %rest_2_.1, ...), custom_call_target="tpu_custom_call" | custom-call | flops 805306368 | bytes 5767168 | tf_op jit(solution)/shard_map/pallas_call | solution.py:251
  44.4 5.2 %all-to-all-start.1 = ((bf16[8,48,1024]{2,1,0:T(8,128)(2,1)}), bf16[8,48,1024]{2,1,0:T(8,128)(2,1)S(1)}, u32[]{:S(2)}, u32[]{:S(2)}) async-start(bf16[8,48,1024]{2,1,0:T(8,128)(2,1)} %bitcast.25), calls=%async_computation.1 | async-start | bytes 1572864 | tf_op jit(solution)/shard_map/all_to_all | solution.py:306
  49.5 8.2 %collective-permute-start.5 = (bf16[192,1024]{1,0:T(8,128)(2,1)}, bf16[192,1024]{1,0:T(8,128)(2,1)S(1)}, u32[]{:S(2)}, u32[]{:S(2)}) collective-permute-start(bf16[192,1024]{1,0:T(8,128)(2,1)} %get-tuple-element.21.inputs), channel_id=1, source_target_pairs={{0,8},{8,0},{1,9},{9,1},{2,10},{10,2},{3,11},{11,3},{4,12},{12,4},... | collective-permute-start | bytes 1179656 | tf_op jit(solution)/shard_map/ppermute | solution.py:26
  57.7 1.9 %collective-permute-start.7 = (bf16[256,1024]{1,0:T(8,128)(2,1)S(1)}, bf16[256,1024]{1,0:T(8,128)(2,1)S(1)}, u32[]{:S(2)}, u32[]{:S(2)}) collective-permute-start(bf16[256,1024]{1,0:T(8,128)(2,1)S(1)} %copy-done.1), channel_id=1, source_target_pairs={{0,8},{8,0},{1,9},{9,1},{2,10},{10,2},{3,11},{11,3},{4,12},{12,4},... | collective-permute-start | bytes 1572872 | tf_op jit(solution)/shard_map/ppermute | solution.py:26
  59.7 2.4 %collective-permute-start.6 = (bf16[256,1024]{1,0:T(8,128)(2,1)S(1)}, bf16[256,1024]{1,0:T(8,128)(2,1)S(1)}, u32[]{:S(2)}, u32[]{:S(2)}) collective-permute-start(bf16[256,1024]{1,0:T(8,128)(2,1)S(1)} %copy-done.2), channel_id=1, source_target_pairs={{0,8},{8,0},{1,9},{9,1},{2,10},{10,2},{3,11},{11,3},{4,12},{12,4},... | collective-permute-start | bytes 1572872 | tf_op jit(solution)/shard_map/ppermute | solution.py:26
  62.1 0.9 shard_map.114
  63.0 5.4 %all-to-all-start.2 = ((bf16[8,48,512]{2,1,0:T(8,128)(2,1)}), bf16[8,48,512]{2,1,0:T(8,128)(2,1)S(1)}, u32[]{:S(2)}, u32[]{:S(2)}) async-start(bf16[8,48,512]{2,1,0:T(8,128)(2,1)} %bitcast.27), calls=%async_computation.2 | async-start | bytes 786432 | tf_op jit(solution)/shard_map/all_to_all | solution.py:316
  68.5 6.5 %all-to-all-done.2 = bf16[8,48,512]{2,1,0:T(8,128)(2,1)S(1)} async-done(((bf16[8,48,512]{2,1,0:T(8,128)(2,1)}), bf16[8,48,512]{2,1,0:T(8,128)(2,1)S(1)}, u32[]{:S(2)}, u32[]{:S(2)}) %all-to-all-start.2) | async-done | bytes 393248 | tf_op jit(solution)/shard_map/all_to_all | solution.py:316
  75.0 1.0 shard_map.115
  76.1 4.5 %collective-permute-start.9 = (bf16[96,1024]{1,0:T(8,128)(2,1)S(1)}, bf16[96,1024]{1,0:T(8,128)(2,1)S(1)}, u32[]{:S(2)}, u32[]{:S(2)}) collective-permute-start(bf16[96,1024]{1,0:T(8,128)(2,1)S(1)} %get-tuple-element.26), channel_id=1, source_target_pairs={{0,256},{256,0},{1,257},{257,1},{2,258},{258,2},{3,259},{259,3},{4... | collective-permute-start | bytes 589832 | tf_op jit(solution)/shard_map/ppermute | solution.py:26
  80.6 4.9 %collective-permute-start.8 = (bf16[192,256]{1,0:T(8,128)(2,1)S(1)}, bf16[192,256]{1,0:T(8,128)(2,1)S(1)}, u32[]{:S(2)}, u32[]{:S(2)}) collective-permute-start(bf16[192,256]{1,0:T(8,128)(2,1)S(1)} %get-tuple-element.24), channel_id=1, source_target_pairs={{0,8},{8,0},{1,9},{9,1},{2,10},{10,2},{3,11},{11,3},{4,12},{12,4},... | collective-permute-start | bytes 294920 | tf_op jit(solution)/shard_map/ppermute | solution.py:26
  85.5 0.9 collective-permute-done.8.after.hidden_core
  86.5 19.6 %all_to_all.35 = bf16[16,48,128]{2,1,0:T(8,128)(2,1)S(1)} all-to-all(bf16[16,48,128]{2,1,0:T(8,128)(2,1)S(1)} %bitcast.16), channel_id=1, replica_groups=mesh['yh'=2,'z'=16,'core'=2,'x'=4,'yl'=2] {'z'}, dimensions={0} | all-to-all | bytes 393216 | tf_op jit(solution)/shard_map/all_to_all | solution.py:340
  106.1 19.9 %all_to_all.36 = bf16[16,48,128]{2,1,0:T(8,128)(2,1)S(1)} all-to-all(bf16[16,48,128]{2,1,0:T(8,128)(2,1)S(1)} %bitcast.19), channel_id=1, replica_groups=mesh['yh'=2,'z'=16,'core'=2,'x'=4,'yl'=2] {'z'}, dimensions={0} | all-to-all | bytes 393216 | tf_op jit(solution)/shard_map/all_to_all | solution.py:348
  126.0 1.9 %collective-permute-start.10 = (bf16[768,128]{1,0:T(8,128)(2,1)S(1)}, bf16[768,128]{1,0:T(8,128)(2,1)S(1)}, u32[]{:S(2)}, u32[]{:S(2)}) collective-permute-start(bf16[768,128]{1,0:T(8,128)(2,1)S(1)} %bitcast.22), channel_id=1, source_target_pairs={{0,256},{256,0},{1,257},{257,1},{2,258},{258,2},{3,259},{259,3},{4... | collective-permute-start | bytes 589832 | tf_op jit(solution)/shard_map/ppermute | solution.py:26
  128.0 6.0 %collective-permute-done.10.blocks_y = bf16[768,128]{1,0:T(8,128)(2,1)S(1)} collective-permute-done((bf16[768,128]{1,0:T(8,128)(2,1)S(1)}, bf16[768,128]{1,0:T(8,128)(2,1)S(1)}, u32[]{:S(2)}, u32[]{:S(2)}) %collective-permute-start.10) | collective-permute-done | bytes 196640 | tf_op jit(solution)/shard_map/ppermute | solution.py:26
  134.0 1.7 %shard_map.118 = (bf16[192,1024]{1,0:T(8,128)(2,1)S(1)}, bf16[16,24,256]{2,1,0:T(8,128)(2,1)}) custom-call(bf16[768,128]{1,0:T(8,128)(2,1)S(1)} %bitcast.23, bf16[768,128]{1,0:T(8,128)(2,1)S(1)} %collective-permute-done.10.blocks_y, bf16[256,1024]{1,0:T(8,128)(2,1)S(1)} %copy-done.2, bf16[256,1024]{1,0:T(8,128)(2,1)S(1)} %collective-permute-done.6.down_x), custom_call_target="tpu_custom_call" | custom-call | flops 402653184 | bytes 2031616 | tf_op jit(solution)/shard_map/pallas_call | solution.py:251
  135.7 3.4 %all-to-all-start.5 = ((bf16[8,48,256]{2,1,0:T(8,128)(2,1)}), bf16[8,48,256]{2,1,0:T(8,128)(2,1)S(1)}, u32[]{:S(2)}, u32[]{:S(2)}) async-start(bf16[8,48,256]{2,1,0:T(8,128)(2,1)} %bitcast.28), calls=%async_computation.5 | async-start | bytes 393216 | tf_op jit(solution)/shard_map/all_to_all | solution.py:359
  139.1 8.7 %collective-permute-start.11 = (bf16[192,1024]{1,0:T(8,128)(2,1)S(1)}, bf16[192,1024]{1,0:T(8,128)(2,1)S(1)}, u32[]{:S(2)}, u32[]{:S(2)}) collective-permute-start(bf16[192,1024]{1,0:T(8,128)(2,1)S(1)} %get-tuple-element.27.out), channel_id=1, source_target_pairs={{0,8},{8,0},{1,9},{9,1},{2,10},{10,2},{3,11},{11,3},{4,12},{12,4},... | collective-permute-start | bytes 1179656 | tf_op jit(solution)/shard_map/ppermute | solution.py:26
  148.7 8.1 %all-to-all-start.6 = ((bf16[16,48,256]{2,1,0:T(8,128)(2,1)}), bf16[16,48,256]{2,1,0:T(8,128)(2,1)S(1)}, u32[]{:S(2)}, u32[]{:S(2)}) async-start(bf16[16,48,256]{2,1,0:T(8,128)(2,1)} %bitcast.24), calls=%async_computation.6 | async-start | bytes 786432 | tf_op jit(solution)/shard_map/all_to_all | solution.py:369
  156.8 1.8 %shard_map.119 = (bf16[256,1024]{1,0:T(8,128)(2,1)}, bf16[6,1024]{1,0:T(8,128)(2,1)}, f32[8,128]{1,0:T(8,128)S(1)}) custom-call(s32[384]{0:T(512)S(1)} %copy-done.4, bf16[192,256]{1,0:T(8,128)(2,1)S(1)} %get-tuple-element.23.hidden, bf16[192,256]{1,0:T(8,128)(2,1)S(1)} %collective-permute-done.8.after.hidden_core, ...), custom_call_target="tpu_custom_call" | custom-call | flops 201326592 | bytes 1525248 | tf_op jit(solution)/shard_map/pallas_call | solution.py:251
  158.6 6.7 %all-to-all-done.6 = bf16[16,48,256]{2,1,0:T(8,128)(2,1)S(1)} async-done(((bf16[16,48,256]{2,1,0:T(8,128)(2,1)}), bf16[16,48,256]{2,1,0:T(8,128)(2,1)S(1)}, u32[]{:S(2)}, u32[]{:S(2)}) %all-to-all-start.6) | async-done | bytes 393248 | tf_op jit(solution)/shard_map/all_to_all | solution.py:369
  165.3 2.8 %shard_map.121 = (bf16[1024,256]{1,0:T(8,128)(2,1)}, bf16[1024,256]{1,0:T(8,128)(2,1)}) custom-call(bf16[768,256]{1,0:T(8,128)(2,1)S(1)} %bitcast.21, bf16[192,1024]{1,0:T(8,128)(2,1)} %get-tuple-element.21.inputs, bf16[192,1024]{1,0:T(8,128)(2,1)S(1)} %collective-permute-done.5.after.inputs_x, f32[8,128]{1,0:T(8,128)S(1)} %get-tuple-element.32.after), custom_call_target="tpu_custom_call" | custom-call | flops 402653184 | bytes 2228224 | tf_op jit(solution)/shard_map/pallas_call | solution.py:251
  (37 shorter events, 2.5 us)
Async XLA Ops:
  0.6 0.7 copy-start.3
  1.3 16.8 %copy-start.5 = (bf16[1024,256]{1,0:T(8,128)(2,1)S(1)}, bf16[1024,256]{1,0:T(8,128)(2,1)}, u32[]{:S(2)}) copy-start(bf16[1024,256]{1,0:T(8,128)(2,1)} %rest_0_.1) | copy-start | bytes 1572868
  2.3 28.3 %all-to-all-start = ((bf16[16,48,128]{2,1,0:T(8,128)(2,1)}), bf16[16,48,128]{2,1,0:T(8,128)(2,1)S(1)}, u32[]{:S(2)}, u32[]{:S(2)}) async-start(bf16[16,48,128]{2,1,0:T(8,128)(2,1)} %bitcast.26), calls=%async_computation | async-start | bytes 393216 | tf_op jit(solution)/shard_map/all_to_all | solution.py:279
  18.1 17.5 %collective-permute-start.1 = (bf16[1024,256]{1,0:T(8,128)(2,1)S(1)}, bf16[1024,256]{1,0:T(8,128)(2,1)S(1)}, u32[]{:S(2)}, u32[]{:S(2)}) collective-permute-start(bf16[1024,256]{1,0:T(8,128)(2,1)S(1)} %copy-done.5), channel_id=1, source_target_pairs={{0,8},{8,0},{1,9},{9,1},{2,10},{10,2},{3,11},{11,3},{4,12},{12,4},... | collective-permute-start | bytes 1572872 | tf_op jit(solution)/shard_map/ppermute | solution.py:26
  21.0 14.7 %collective-permute-start.2 = (bf16[1024,256]{1,0:T(8,128)(2,1)}, bf16[1024,256]{1,0:T(8,128)(2,1)S(1)}, u32[]{:S(2)}, u32[]{:S(2)}) collective-permute-start(bf16[1024,256]{1,0:T(8,128)(2,1)} %rest_1_.1), channel_id=1, source_target_pairs={{0,8},{8,0},{1,9},{9,1},{2,10},{10,2},{3,11},{11,3},{4,12},{12,4},... | collective-permute-start | bytes 1572872 | tf_op jit(solution)/shard_map/ppermute | solution.py:26
  22.9 12.7 %collective-permute-start.3 = (bf16[1024,256]{1,0:T(8,128)(2,1)}, bf16[1024,256]{1,0:T(8,128)(2,1)S(1)}, u32[]{:S(2)}, u32[]{:S(2)}) collective-permute-start(bf16[1024,256]{1,0:T(8,128)(2,1)} %rest_2_.1), channel_id=1, source_target_pairs={{0,8},{8,0},{1,9},{9,1},{2,10},{10,2},{3,11},{11,3},{4,12},{12,4},... | collective-permute-start | bytes 1572872 | tf_op jit(solution)/shard_map/ppermute | solution.py:26
  25.3 10.4 %collective-permute-start.4 = (bf16[1024,256]{1,0:T(8,128)(2,1)}, bf16[1024,256]{1,0:T(8,128)(2,1)S(1)}, u32[]{:S(2)}, u32[]{:S(2)}) collective-permute-start(bf16[1024,256]{1,0:T(8,128)(2,1)} %rest_3_.1), channel_id=1, source_target_pairs={{0,8},{8,0},{1,9},{9,1},{2,10},{10,2},{3,11},{11,3},{4,12},{12,4},... | collective-permute-start | bytes 1572872 | tf_op jit(solution)/shard_map/ppermute | solution.py:26
  30.8 7.9 %copy-start = (bf16[96,1024]{1,0:T(8,128)(2,1)}, bf16[96,1024]{1,0:T(8,128)(2,1)S(1)}, u32[]{:S(2)}) copy-start(bf16[96,1024]{1,0:T(8,128)(2,1)S(1)} %shard_map.112.rows) | copy-start | bytes 589828
  30.8 7.9 %collective-permute-start = (bf16[96,1024]{1,0:T(8,128)(2,1)S(1)}, bf16[96,1024]{1,0:T(8,128)(2,1)S(1)}, u32[]{:S(2)}, u32[]{:S(2)}) collective-permute-start(bf16[96,1024]{1,0:T(8,128)(2,1)S(1)} %shard_map.112.rows), channel_id=1, source_target_pairs={{0,256},{256,0},{1,257},{257,1},{2,258},{258,2},{3,259},{259,3},{4... | collective-permute-start | bytes 589832 | tf_op jit(solution)/shard_map/ppermute | solution.py:26
  35.6 3.1 %copy-start.6 = (bf16[1024,256]{1,0:T(8,128)(2,1)}, bf16[1024,256]{1,0:T(8,128)(2,1)S(1)}, u32[]{:S(2)}) copy-start(bf16[1024,256]{1,0:T(8,128)(2,1)S(1)} %collective-permute-done.1.rest_4_) | copy-start | bytes 1572868
  35.6 3.1 %copy-start.7 = (bf16[1024,256]{1,0:T(8,128)(2,1)}, bf16[1024,256]{1,0:T(8,128)(2,1)S(1)}, u32[]{:S(2)}) copy-start(bf16[1024,256]{1,0:T(8,128)(2,1)S(1)} %collective-permute-done.2.rest_5_) | copy-start | bytes 1572868
  35.7 3.0 %copy-start.8 = (bf16[1024,256]{1,0:T(8,128)(2,1)}, bf16[1024,256]{1,0:T(8,128)(2,1)S(1)}, u32[]{:S(2)}) copy-start(bf16[1024,256]{1,0:T(8,128)(2,1)S(1)} %collective-permute-done.3.rest_6_) | copy-start | bytes 1572868
  35.7 3.0 %copy-start.9 = (bf16[1024,256]{1,0:T(8,128)(2,1)}, bf16[1024,256]{1,0:T(8,128)(2,1)S(1)}, u32[]{:S(2)}) copy-start(bf16[1024,256]{1,0:T(8,128)(2,1)S(1)} %collective-permute-done.4.rest_7_) | copy-start | bytes 1572868
  38.7 0.7 copy-start.10
  44.3 13.4 %copy-start.1 = (bf16[256,1024]{1,0:T(8,128)(2,1)S(1)}, bf16[256,1024]{1,0:T(8,128)(2,1)}, u32[]{:S(2)}) copy-start(bf16[256,1024]{1,0:T(8,128)(2,1)} %probe.1) | copy-start | bytes 1572868
  44.3 15.3 %copy-start.2 = (bf16[256,1024]{1,0:T(8,128)(2,1)S(1)}, bf16[256,1024]{1,0:T(8,128)(2,1)}, u32[]{:S(2)}) copy-start(bf16[256,1024]{1,0:T(8,128)(2,1)} %down.3) | copy-start | bytes 1572868
  44.4 17.7 %all-to-all-start.1 = ((bf16[8,48,1024]{2,1,0:T(8,128)(2,1)}), bf16[8,48,1024]{2,1,0:T(8,128)(2,1)S(1)}, u32[]{:S(2)}, u32[]{:S(2)}) async-start(bf16[8,48,1024]{2,1,0:T(8,128)(2,1)} %bitcast.25), calls=%async_computation.1 | async-start | bytes 1572864 | tf_op jit(solution)/shard_map/all_to_all | solution.py:306
  49.5 12.5 %collective-permute-start.5 = (bf16[192,1024]{1,0:T(8,128)(2,1)}, bf16[192,1024]{1,0:T(8,128)(2,1)S(1)}, u32[]{:S(2)}, u32[]{:S(2)}) collective-permute-start(bf16[192,1024]{1,0:T(8,128)(2,1)} %get-tuple-element.21.inputs), channel_id=1, source_target_pairs={{0,8},{8,0},{1,9},{9,1},{2,10},{10,2},{3,11},{11,3},{4,12},{12,4},... | collective-permute-start | bytes 1179656 | tf_op jit(solution)/shard_map/ppermute | solution.py:26
  57.7 10.8 %collective-permute-start.7 = (bf16[256,1024]{1,0:T(8,128)(2,1)S(1)}, bf16[256,1024]{1,0:T(8,128)(2,1)S(1)}, u32[]{:S(2)}, u32[]{:S(2)}) collective-permute-start(bf16[256,1024]{1,0:T(8,128)(2,1)S(1)} %copy-done.1), channel_id=1, source_target_pairs={{0,8},{8,0},{1,9},{9,1},{2,10},{10,2},{3,11},{11,3},{4,12},{12,4},... | collective-permute-start | bytes 1572872 | tf_op jit(solution)/shard_map/ppermute | solution.py:26
  59.7 8.8 %collective-permute-start.6 = (bf16[256,1024]{1,0:T(8,128)(2,1)S(1)}, bf16[256,1024]{1,0:T(8,128)(2,1)S(1)}, u32[]{:S(2)}, u32[]{:S(2)}) collective-permute-start(bf16[256,1024]{1,0:T(8,128)(2,1)S(1)} %copy-done.2), channel_id=1, source_target_pairs={{0,8},{8,0},{1,9},{9,1},{2,10},{10,2},{3,11},{11,3},{4,12},{12,4},... | collective-permute-start | bytes 1572872 | tf_op jit(solution)/shard_map/ppermute | solution.py:26
  63.0 12.0 %all-to-all-start.2 = ((bf16[8,48,512]{2,1,0:T(8,128)(2,1)}), bf16[8,48,512]{2,1,0:T(8,128)(2,1)S(1)}, u32[]{:S(2)}, u32[]{:S(2)}) async-start(bf16[8,48,512]{2,1,0:T(8,128)(2,1)} %bitcast.27), calls=%async_computation.2 | async-start | bytes 786432 | tf_op jit(solution)/shard_map/all_to_all | solution.py:316
  76.1 10.3 %collective-permute-start.9 = (bf16[96,1024]{1,0:T(8,128)(2,1)S(1)}, bf16[96,1024]{1,0:T(8,128)(2,1)S(1)}, u32[]{:S(2)}, u32[]{:S(2)}) collective-permute-start(bf16[96,1024]{1,0:T(8,128)(2,1)S(1)} %get-tuple-element.26), channel_id=1, source_target_pairs={{0,256},{256,0},{1,257},{257,1},{2,258},{258,2},{3,259},{259,3},{4... | collective-permute-start | bytes 589832 | tf_op jit(solution)/shard_map/ppermute | solution.py:26
  80.6 5.8 %collective-permute-start.8 = (bf16[192,256]{1,0:T(8,128)(2,1)S(1)}, bf16[192,256]{1,0:T(8,128)(2,1)S(1)}, u32[]{:S(2)}, u32[]{:S(2)}) collective-permute-start(bf16[192,256]{1,0:T(8,128)(2,1)S(1)} %get-tuple-element.24), channel_id=1, source_target_pairs={{0,8},{8,0},{1,9},{9,1},{2,10},{10,2},{3,11},{11,3},{4,12},{12,4},... | collective-permute-start | bytes 294920 | tf_op jit(solution)/shard_map/ppermute | solution.py:26
  126.0 7.9 %collective-permute-start.10 = (bf16[768,128]{1,0:T(8,128)(2,1)S(1)}, bf16[768,128]{1,0:T(8,128)(2,1)S(1)}, u32[]{:S(2)}, u32[]{:S(2)}) collective-permute-start(bf16[768,128]{1,0:T(8,128)(2,1)S(1)} %bitcast.22), channel_id=1, source_target_pairs={{0,256},{256,0},{1,257},{257,1},{2,258},{258,2},{3,259},{259,3},{4... | collective-permute-start | bytes 589832 | tf_op jit(solution)/shard_map/ppermute | solution.py:26
  135.7 12.1 %all-to-all-start.5 = ((bf16[8,48,256]{2,1,0:T(8,128)(2,1)}), bf16[8,48,256]{2,1,0:T(8,128)(2,1)S(1)}, u32[]{:S(2)}, u32[]{:S(2)}) async-start(bf16[8,48,256]{2,1,0:T(8,128)(2,1)} %bitcast.28), calls=%async_computation.5 | async-start | bytes 393216 | tf_op jit(solution)/shard_map/all_to_all | solution.py:359
  139.1 17.7 %collective-permute-start.11 = (bf16[192,1024]{1,0:T(8,128)(2,1)S(1)}, bf16[192,1024]{1,0:T(8,128)(2,1)S(1)}, u32[]{:S(2)}, u32[]{:S(2)}) collective-permute-start(bf16[192,1024]{1,0:T(8,128)(2,1)S(1)} %get-tuple-element.27.out), channel_id=1, source_target_pairs={{0,8},{8,0},{1,9},{9,1},{2,10},{10,2},{3,11},{11,3},{4,12},{12,4},... | collective-permute-start | bytes 1179656 | tf_op jit(solution)/shard_map/ppermute | solution.py:26
  148.7 8.1 %copy-start.4 = (s32[384]{0:T(512)S(1)}, s32[384]{0:T(512)}, u32[]{:S(2)}) copy-start(s32[384]{0:T(512)} %ids.1) | copy-start | bytes 4612
  148.7 16.6 %all-to-all-start.6 = ((bf16[16,48,256]{2,1,0:T(8,128)(2,1)}), bf16[16,48,256]{2,1,0:T(8,128)(2,1)S(1)}, u32[]{:S(2)}, u32[]{:S(2)}) async-start(bf16[16,48,256]{2,1,0:T(8,128)(2,1)} %bitcast.24), calls=%async_computation.6 | async-start | bytes 786432 | tf_op jit(solution)/shard_map/all_to_all | solution.py:369

commit v10 on v9

--- a/solution.py
+++ b/solution.py
@@ -204,19 +204,21 @@
         write.wait()
 
 
-def ggn_kernel(parts, inputs, inputs_x, after, ggn_gate, ggn_up, buffer, sems):
+def ggn_kernel(parts, inputs, inputs_x, after, ggn_gate, ggn_up, own, buffer, in_sem, sems):
+    copy = start(inputs, own, in_sem)
     core = lax.axis_index(CORE)
     sides = [
         moved(384, 384, by_kind, parts[rows_at(position, 384), :]) for position in (core, 1 - core)
     ]
     width = inputs.shape[1]
+    copy.wait()
     writes = []
     for n in range(4):
         columns = slice(n * width // 4, (n + 1) * width // 4)
         for k, target in enumerate((ggn_gate, ggn_up)):
             rows = slice(192 * k, 192 * k + 192)
-            total = over_rows(inputs[:, columns], sides[0][rows])
-            total = total + over_rows(inputs_x[:, columns], sides[1][rows])
+            total = over_rows(inputs_x[:, columns], sides[1][rows])
+            total = total + over_rows(own[:, columns], sides[0][rows])
             buffer[k, columns, :] = total.astype(bf16)
             place = buffer.at[k, columns, :]
             writes.append(start(place, target.at[columns, :], sems.at[2 * n + k]))
@@ -290,7 +292,7 @@
     gates_x = [swap(w, CORE) for w in gates]
     inputs, partials = call(
         gates_kernel,
-        58.5,
+        57.25,
         8 * dots,
         [(rows, VMEM), (rows_y, VMEM)] + [(w, HBM) for w in gates] + [(w, VMEM) for w in gates_x],
         [((192, width), bf16, HBM), ((16, 24, 4 * units), bf16, HBM)],
@@ -382,9 +384,14 @@
         ggn_kernel,
         20,
         4 * dots,
-        [(parts, VMEM), (inputs, VMEM), (inputs_x, VMEM), (flag, ANY)],
+        [(parts, VMEM), (inputs, HBM), (inputs_x, VMEM), (flag, ANY)],
         [((width, units), bf16, HBM), ((width, units), bf16, HBM)],
-        [pltpu.VMEM((2, width, units), bf16), DMA((8,))],
+        [
+            pltpu.VMEM((192, width), bf16),
+            pltpu.VMEM((2, width, units), bf16),
+            DMA,
+            DMA((8,)),
+        ],
     )
     return tangent_out, ggn_gate, ggn_up, ggn_down
 

time: 169 us -> 169 us (level)
  no operation moved by 1% of the time
where the time goes in v10:
time: 169 us; the launch traced here: 168 us
  starting transfers between devices  84.3 us (50%)
  blocking collectives  39.5 us (23%)
  waiting for transfers between devices  26.6 us (16%)
  Pallas kernels  15 us (9%)
    ppermute x12, starting transfers between devices, swap(): return lax.ppermute(value, axis, [(0, 1), (1, 0)])  46.4 us
    all_to_all x1, blocking collectives, local(): lax.all_to_all(spread.reshape(NZ, 48, 128), Z, 0, 0).reshape(768, 128)  19.9 us
    all_to_all x1, blocking collectives, local(): lax.all_to_all(blocks.reshape(NZ, 48, 128), Z, 0, 0).reshape(768, 128)  19.6 us
    all_to_all x1, starting transfers between devices, local(): rows = lax.all_to_all(rows.reshape(NZ, 48, 128), Z, 0, 0).reshape(768, 128)  15.8 us
    pallas_call x11, Pallas kernels, call(): pl.pallas_call(kernel, out_shape=[pltpu.HBM(s, t) if space is HBM else ja...  15 us
    ppermute x12, waiting for transfers between devices, swap(): return lax.ppermute(value, axis, [(0, 1), (1, 0)])  9.93 us
    all_to_all x1, starting transfers between devices, local(): lax.all_to_all(spread.reshape(16, 48, units), (CORE,) + DP, 0, 0)  8.08 us
    all_to_all x1, waiting for transfers between devices, local(): lax.all_to_all(spread.reshape(16, 48, units), (CORE,) + DP, 0, 0)  6.71 us
  transfers between devices with their start and end apart: 17, of which 6 were waited for; matrix products, arithmetic and copies ran while one was open for 0% of the time, Pallas kernels for 2%

profile of v10, /device:TPU:1, one launch (start us, length us, event | category | flops | bytes accessed | tf_op | source)
XLA Modules:
  0.0 167.9 jit_solution(12141783393687926681)
XLA Ops:
  1.4 1.0 shard_map.111
  2.3 15.8 %all-to-all-start = ((bf16[16,48,128]{2,1,0:T(8,128)(2,1)}), bf16[16,48,128]{2,1,0:T(8,128)(2,1)S(1)}, u32[]{:S(2)}, u32[]{:S(2)}) async-start(bf16[16,48,128]{2,1,0:T(8,128)(2,1)} %bitcast.26), calls=%async_computation | async-start | bytes 393216 | tf_op jit(solution)/shard_map/all_to_all | solution.py:281
  18.1 2.9 %collective-permute-start.1 = (bf16[1024,256]{1,0:T(8,128)(2,1)S(1)}, bf16[1024,256]{1,0:T(8,128)(2,1)S(1)}, u32[]{:S(2)}, u32[]{:S(2)}) collective-permute-start(bf16[1024,256]{1,0:T(8,128)(2,1)S(1)} %copy-done.5), channel_id=1, source_target_pairs={{0,8},{8,0},{1,9},{9,1},{2,10},{10,2},{3,11},{11,3},{4,12},{12,4},... | collective-permute-start | bytes 1572872 | tf_op jit(solution)/shard_map/ppermute | solution.py:26
  21.0 1.9 %collective-permute-start.2 = (bf16[1024,256]{1,0:T(8,128)(2,1)}, bf16[1024,256]{1,0:T(8,128)(2,1)S(1)}, u32[]{:S(2)}, u32[]{:S(2)}) collective-permute-start(bf16[1024,256]{1,0:T(8,128)(2,1)} %rest_1_.1), channel_id=1, source_target_pairs={{0,8},{8,0},{1,9},{9,1},{2,10},{10,2},{3,11},{11,3},{4,12},{12,4},... | collective-permute-start | bytes 1572872 | tf_op jit(solution)/shard_map/ppermute | solution.py:26
  22.9 2.4 %collective-permute-start.3 = (bf16[1024,256]{1,0:T(8,128)(2,1)}, bf16[1024,256]{1,0:T(8,128)(2,1)S(1)}, u32[]{:S(2)}, u32[]{:S(2)}) collective-permute-start(bf16[1024,256]{1,0:T(8,128)(2,1)} %rest_2_.1), channel_id=1, source_target_pairs={{0,8},{8,0},{1,9},{9,1},{2,10},{10,2},{3,11},{11,3},{4,12},{12,4},... | collective-permute-start | bytes 1572872 | tf_op jit(solution)/shard_map/ppermute | solution.py:26
  25.3 1.9 %collective-permute-start.4 = (bf16[1024,256]{1,0:T(8,128)(2,1)}, bf16[1024,256]{1,0:T(8,128)(2,1)S(1)}, u32[]{:S(2)}, u32[]{:S(2)}) collective-permute-start(bf16[1024,256]{1,0:T(8,128)(2,1)} %rest_3_.1), channel_id=1, source_target_pairs={{0,8},{8,0},{1,9},{9,1},{2,10},{10,2},{3,11},{11,3},{4,12},{12,4},... | collective-permute-start | bytes 1572872 | tf_op jit(solution)/shard_map/ppermute | solution.py:26
  27.3 3.4 %all-to-all-done = bf16[16,48,128]{2,1,0:T(8,128)(2,1)S(1)} async-done(((bf16[16,48,128]{2,1,0:T(8,128)(2,1)}), bf16[16,48,128]{2,1,0:T(8,128)(2,1)S(1)}, u32[]{:S(2)}, u32[]{:S(2)}) %all-to-all-start) | async-done | bytes 196640 | tf_op jit(solution)/shard_map/all_to_all | solution.py:281
  30.8 4.8 %collective-permute-start = (bf16[96,1024]{1,0:T(8,128)(2,1)S(1)}, bf16[96,1024]{1,0:T(8,128)(2,1)S(1)}, u32[]{:S(2)}, u32[]{:S(2)}) collective-permute-start(bf16[96,1024]{1,0:T(8,128)(2,1)S(1)} %shard_map.112.rows), channel_id=1, source_target_pairs={{0,256},{256,0},{1,257},{257,1},{2,258},{258,2},{3,259},{259,3},{4... | collective-permute-start | bytes 589832 | tf_op jit(solution)/shard_map/ppermute | solution.py:26
  35.7 3.0 %collective-permute-done.rows_y = bf16[96,1024]{1,0:T(8,128)(2,1)S(1)} collective-permute-done((bf16[96,1024]{1,0:T(8,128)(2,1)S(1)}, bf16[96,1024]{1,0:T(8,128)(2,1)S(1)}, u32[]{:S(2)}, u32[]{:S(2)}) %collective-permute-start) | collective-permute-done | bytes 196640 | tf_op jit(solution)/shard_map/ppermute | solution.py:26
  39.4 4.9 %shard_map.113 = (bf16[192,1024]{1,0:T(8,128)(2,1)}, bf16[16,24,1024]{2,1,0:T(8,128)(2,1)}) custom-call(bf16[96,1024]{1,0:T(8,128)(2,1)} %copy-done, bf16[96,1024]{1,0:T(8,128)(2,1)} %copy-done.10, bf16[1024,256]{1,0:T(8,128)(2,1)} %rest_0_.1, bf16[1024,256]{1,0:T(8,128)(2,1)} %rest_1_.1, bf16[1024,256]{1,0:T(8,128)(2,1)} %rest_2_.1, ...), custom_call_target="tpu_custom_call" | custom-call | flops 805306368 | bytes 5767168 | tf_op jit(solution)/shard_map/pallas_call | solution.py:253
  44.4 5.2 %all-to-all-start.1 = ((bf16[8,48,1024]{2,1,0:T(8,128)(2,1)}), bf16[8,48,1024]{2,1,0:T(8,128)(2,1)S(1)}, u32[]{:S(2)}, u32[]{:S(2)}) async-start(bf16[8,48,1024]{2,1,0:T(8,128)(2,1)} %bitcast.25), calls=%async_computation.1 | async-start | bytes 1572864 | tf_op jit(solution)/shard_map/all_to_all | solution.py:308
  49.5 8.2 %collective-permute-start.5 = (bf16[192,1024]{1,0:T(8,128)(2,1)}, bf16[192,1024]{1,0:T(8,128)(2,1)S(1)}, u32[]{:S(2)}, u32[]{:S(2)}) collective-permute-start(bf16[192,1024]{1,0:T(8,128)(2,1)} %get-tuple-element.21.inputs), channel_id=1, source_target_pairs={{0,8},{8,0},{1,9},{9,1},{2,10},{10,2},{3,11},{11,3},{4,12},{12,4},... | collective-permute-start | bytes 1179656 | tf_op jit(solution)/shard_map/ppermute | solution.py:26
  57.7 1.9 %collective-permute-start.7 = (bf16[256,1024]{1,0:T(8,128)(2,1)S(1)}, bf16[256,1024]{1,0:T(8,128)(2,1)S(1)}, u32[]{:S(2)}, u32[]{:S(2)}) collective-permute-start(bf16[256,1024]{1,0:T(8,128)(2,1)S(1)} %copy-done.1), channel_id=1, source_target_pairs={{0,8},{8,0},{1,9},{9,1},{2,10},{10,2},{3,11},{11,3},{4,12},{12,4},... | collective-permute-start | bytes 1572872 | tf_op jit(solution)/shard_map/ppermute | solution.py:26
  59.7 2.4 %collective-permute-start.6 = (bf16[256,1024]{1,0:T(8,128)(2,1)S(1)}, bf16[256,1024]{1,0:T(8,128)(2,1)S(1)}, u32[]{:S(2)}, u32[]{:S(2)}) collective-permute-start(bf16[256,1024]{1,0:T(8,128)(2,1)S(1)} %copy-done.2), channel_id=1, source_target_pairs={{0,8},{8,0},{1,9},{9,1},{2,10},{10,2},{3,11},{11,3},{4,12},{12,4},... | collective-permute-start | bytes 1572872 | tf_op jit(solution)/shard_map/ppermute | solution.py:26
  62.1 0.9 shard_map.114
  63.0 5.4 %all-to-all-start.2 = ((bf16[8,48,512]{2,1,0:T(8,128)(2,1)}), bf16[8,48,512]{2,1,0:T(8,128)(2,1)S(1)}, u32[]{:S(2)}, u32[]{:S(2)}) async-start(bf16[8,48,512]{2,1,0:T(8,128)(2,1)} %bitcast.27), calls=%async_computation.2 | async-start | bytes 786432 | tf_op jit(solution)/shard_map/all_to_all | solution.py:318
  68.5 6.5 %all-to-all-done.2 = bf16[8,48,512]{2,1,0:T(8,128)(2,1)S(1)} async-done(((bf16[8,48,512]{2,1,0:T(8,128)(2,1)}), bf16[8,48,512]{2,1,0:T(8,128)(2,1)S(1)}, u32[]{:S(2)}, u32[]{:S(2)}) %all-to-all-start.2) | async-done | bytes 393248 | tf_op jit(solution)/shard_map/all_to_all | solution.py:318
  75.0 1.0 shard_map.115
  76.1 4.5 %collective-permute-start.9 = (bf16[96,1024]{1,0:T(8,128)(2,1)S(1)}, bf16[96,1024]{1,0:T(8,128)(2,1)S(1)}, u32[]{:S(2)}, u32[]{:S(2)}) collective-permute-start(bf16[96,1024]{1,0:T(8,128)(2,1)S(1)} %get-tuple-element.26), channel_id=1, source_target_pairs={{0,256},{256,0},{1,257},{257,1},{2,258},{258,2},{3,259},{259,3},{4... | collective-permute-start | bytes 589832 | tf_op jit(solution)/shard_map/ppermute | solution.py:26
  80.6 4.9 %collective-permute-start.8 = (bf16[192,256]{1,0:T(8,128)(2,1)S(1)}, bf16[192,256]{1,0:T(8,128)(2,1)S(1)}, u32[]{:S(2)}, u32[]{:S(2)}) collective-permute-start(bf16[192,256]{1,0:T(8,128)(2,1)S(1)} %get-tuple-element.24), channel_id=1, source_target_pairs={{0,8},{8,0},{1,9},{9,1},{2,10},{10,2},{3,11},{11,3},{4,12},{12,4},... | collective-permute-start | bytes 294920 | tf_op jit(solution)/shard_map/ppermute | solution.py:26
  85.5 0.9 collective-permute-done.8.after.hidden_core
  86.5 19.6 %all_to_all.35 = bf16[16,48,128]{2,1,0:T(8,128)(2,1)S(1)} all-to-all(bf16[16,48,128]{2,1,0:T(8,128)(2,1)S(1)} %bitcast.16), channel_id=1, replica_groups=mesh['yh'=2,'z'=16,'core'=2,'x'=4,'yl'=2] {'z'}, dimensions={0} | all-to-all | bytes 393216 | tf_op jit(solution)/shard_map/all_to_all | solution.py:342
  106.1 19.9 %all_to_all.36 = bf16[16,48,128]{2,1,0:T(8,128)(2,1)S(1)} all-to-all(bf16[16,48,128]{2,1,0:T(8,128)(2,1)S(1)} %bitcast.19), channel_id=1, replica_groups=mesh['yh'=2,'z'=16,'core'=2,'x'=4,'yl'=2] {'z'}, dimensions={0} | all-to-all | bytes 393216 | tf_op jit(solution)/shard_map/all_to_all | solution.py:350
  126.0 1.9 %collective-permute-start.10 = (bf16[768,128]{1,0:T(8,128)(2,1)S(1)}, bf16[768,128]{1,0:T(8,128)(2,1)S(1)}, u32[]{:S(2)}, u32[]{:S(2)}) collective-permute-start(bf16[768,128]{1,0:T(8,128)(2,1)S(1)} %bitcast.22), channel_id=1, source_target_pairs={{0,256},{256,0},{1,257},{257,1},{2,258},{258,2},{3,259},{259,3},{4... | collective-permute-start | bytes 589832 | tf_op jit(solution)/shard_map/ppermute | solution.py:26
  128.0 6.0 %collective-permute-done.10.blocks_y = bf16[768,128]{1,0:T(8,128)(2,1)S(1)} collective-permute-done((bf16[768,128]{1,0:T(8,128)(2,1)S(1)}, bf16[768,128]{1,0:T(8,128)(2,1)S(1)}, u32[]{:S(2)}, u32[]{:S(2)}) %collective-permute-start.10) | collective-permute-done | bytes 196640 | tf_op jit(solution)/shard_map/ppermute | solution.py:26
  134.0 1.7 %shard_map.118 = (bf16[192,1024]{1,0:T(8,128)(2,1)S(1)}, bf16[16,24,256]{2,1,0:T(8,128)(2,1)}) custom-call(bf16[768,128]{1,0:T(8,128)(2,1)S(1)} %bitcast.23, bf16[768,128]{1,0:T(8,128)(2,1)S(1)} %collective-permute-done.10.blocks_y, bf16[256,1024]{1,0:T(8,128)(2,1)S(1)} %copy-done.2, bf16[256,1024]{1,0:T(8,128)(2,1)S(1)} %collective-permute-done.6.down_x), custom_call_target="tpu_custom_call" | custom-call | flops 402653184 | bytes 2031616 | tf_op jit(solution)/shard_map/pallas_call | solution.py:253
  135.7 3.4 %all-to-all-start.5 = ((bf16[8,48,256]{2,1,0:T(8,128)(2,1)}), bf16[8,48,256]{2,1,0:T(8,128)(2,1)S(1)}, u32[]{:S(2)}, u32[]{:S(2)}) async-start(bf16[8,48,256]{2,1,0:T(8,128)(2,1)} %bitcast.28), calls=%async_computation.5 | async-start | bytes 393216 | tf_op jit(solution)/shard_map/all_to_all | solution.py:361
  139.1 8.7 %collective-permute-start.11 = (bf16[192,1024]{1,0:T(8,128)(2,1)S(1)}, bf16[192,1024]{1,0:T(8,128)(2,1)S(1)}, u32[]{:S(2)}, u32[]{:S(2)}) collective-permute-start(bf16[192,1024]{1,0:T(8,128)(2,1)S(1)} %get-tuple-element.27.out), channel_id=1, source_target_pairs={{0,8},{8,0},{1,9},{9,1},{2,10},{10,2},{3,11},{11,3},{4,12},{12,4},... | collective-permute-start | bytes 1179656 | tf_op jit(solution)/shard_map/ppermute | solution.py:26
  148.7 8.1 %all-to-all-start.6 = ((bf16[16,48,256]{2,1,0:T(8,128)(2,1)}), bf16[16,48,256]{2,1,0:T(8,128)(2,1)S(1)}, u32[]{:S(2)}, u32[]{:S(2)}) async-start(bf16[16,48,256]{2,1,0:T(8,128)(2,1)} %bitcast.24), calls=%async_computation.6 | async-start | bytes 786432 | tf_op jit(solution)/shard_map/all_to_all | solution.py:371
  156.8 1.8 %shard_map.119 = (bf16[256,1024]{1,0:T(8,128)(2,1)}, bf16[6,1024]{1,0:T(8,128)(2,1)}, f32[8,128]{1,0:T(8,128)S(1)}) custom-call(s32[384]{0:T(512)S(1)} %copy-done.4, bf16[192,256]{1,0:T(8,128)(2,1)S(1)} %get-tuple-element.23.hidden, bf16[192,256]{1,0:T(8,128)(2,1)S(1)} %collective-permute-done.8.after.hidden_core, ...), custom_call_target="tpu_custom_call" | custom-call | flops 201326592 | bytes 1525248 | tf_op jit(solution)/shard_map/pallas_call | solution.py:253
  158.6 6.7 %all-to-all-done.6 = bf16[16,48,256]{2,1,0:T(8,128)(2,1)S(1)} async-done(((bf16[16,48,256]{2,1,0:T(8,128)(2,1)}), bf16[16,48,256]{2,1,0:T(8,128)(2,1)S(1)}, u32[]{:S(2)}, u32[]{:S(2)}) %all-to-all-start.6) | async-done | bytes 393248 | tf_op jit(solution)/shard_map/all_to_all | solution.py:371
  165.3 2.6 %shard_map.121 = (bf16[1024,256]{1,0:T(8,128)(2,1)}, bf16[1024,256]{1,0:T(8,128)(2,1)}) custom-call(bf16[768,256]{1,0:T(8,128)(2,1)S(1)} %bitcast.21, bf16[192,1024]{1,0:T(8,128)(2,1)} %get-tuple-element.21.inputs, bf16[192,1024]{1,0:T(8,128)(2,1)S(1)} %collective-permute-done.5.after.inputs_x, f32[8,128]{1,0:T(8,128)S(1)} %get-tuple-element.32.after), custom_call_target="tpu_custom_call" | custom-call | flops 402653184 | bytes 2228224 | tf_op jit(solution)/shard_map/pallas_call | solution.py:253
  (37 shorter events, 2.5 us)
Async XLA Ops:
  0.6 0.7 copy-start.3
  1.3 16.8 %copy-start.5 = (bf16[1024,256]{1,0:T(8,128)(2,1)S(1)}, bf16[1024,256]{1,0:T(8,128)(2,1)}, u32[]{:S(2)}) copy-start(bf16[1024,256]{1,0:T(8,128)(2,1)} %rest_0_.1) | copy-start | bytes 1572868
  2.3 28.3 %all-to-all-start = ((bf16[16,48,128]{2,1,0:T(8,128)(2,1)}), bf16[16,48,128]{2,1,0:T(8,128)(2,1)S(1)}, u32[]{:S(2)}, u32[]{:S(2)}) async-start(bf16[16,48,128]{2,1,0:T(8,128)(2,1)} %bitcast.26), calls=%async_computation | async-start | bytes 393216 | tf_op jit(solution)/shard_map/all_to_all | solution.py:281
  18.1 17.5 %collective-permute-start.1 = (bf16[1024,256]{1,0:T(8,128)(2,1)S(1)}, bf16[1024,256]{1,0:T(8,128)(2,1)S(1)}, u32[]{:S(2)}, u32[]{:S(2)}) collective-permute-start(bf16[1024,256]{1,0:T(8,128)(2,1)S(1)} %copy-done.5), channel_id=1, source_target_pairs={{0,8},{8,0},{1,9},{9,1},{2,10},{10,2},{3,11},{11,3},{4,12},{12,4},... | collective-permute-start | bytes 1572872 | tf_op jit(solution)/shard_map/ppermute | solution.py:26
  21.0 14.7 %collective-permute-start.2 = (bf16[1024,256]{1,0:T(8,128)(2,1)}, bf16[1024,256]{1,0:T(8,128)(2,1)S(1)}, u32[]{:S(2)}, u32[]{:S(2)}) collective-permute-start(bf16[1024,256]{1,0:T(8,128)(2,1)} %rest_1_.1), channel_id=1, source_target_pairs={{0,8},{8,0},{1,9},{9,1},{2,10},{10,2},{3,11},{11,3},{4,12},{12,4},... | collective-permute-start | bytes 1572872 | tf_op jit(solution)/shard_map/ppermute | solution.py:26
  22.9 12.7 %collective-permute-start.3 = (bf16[1024,256]{1,0:T(8,128)(2,1)}, bf16[1024,256]{1,0:T(8,128)(2,1)S(1)}, u32[]{:S(2)}, u32[]{:S(2)}) collective-permute-start(bf16[1024,256]{1,0:T(8,128)(2,1)} %rest_2_.1), channel_id=1, source_target_pairs={{0,8},{8,0},{1,9},{9,1},{2,10},{10,2},{3,11},{11,3},{4,12},{12,4},... | collective-permute-start | bytes 1572872 | tf_op jit(solution)/shard_map/ppermute | solution.py:26
  25.3 10.4 %collective-permute-start.4 = (bf16[1024,256]{1,0:T(8,128)(2,1)}, bf16[1024,256]{1,0:T(8,128)(2,1)S(1)}, u32[]{:S(2)}, u32[]{:S(2)}) collective-permute-start(bf16[1024,256]{1,0:T(8,128)(2,1)} %rest_3_.1), channel_id=1, source_target_pairs={{0,8},{8,0},{1,9},{9,1},{2,10},{10,2},{3,11},{11,3},{4,12},{12,4},... | collective-permute-start | bytes 1572872 | tf_op jit(solution)/shard_map/ppermute | solution.py:26
  30.8 7.9 %copy-start = (bf16[96,1024]{1,0:T(8,128)(2,1)}, bf16[96,1024]{1,0:T(8,128)(2,1)S(1)}, u32[]{:S(2)}) copy-start(bf16[96,1024]{1,0:T(8,128)(2,1)S(1)} %shard_map.112.rows) | copy-start | bytes 589828
  30.8 7.9 %collective-permute-start = (bf16[96,1024]{1,0:T(8,128)(2,1)S(1)}, bf16[96,1024]{1,0:T(8,128)(2,1)S(1)}, u32[]{:S(2)}, u32[]{:S(2)}) collective-permute-start(bf16[96,1024]{1,0:T(8,128)(2,1)S(1)} %shard_map.112.rows), channel_id=1, source_target_pairs={{0,256},{256,0},{1,257},{257,1},{2,258},{258,2},{3,259},{259,3},{4... | collective-permute-start | bytes 589832 | tf_op jit(solution)/shard_map/ppermute | solution.py:26
  35.6 3.1 %copy-start.6 = (bf16[1024,256]{1,0:T(8,128)(2,1)}, bf16[1024,256]{1,0:T(8,128)(2,1)S(1)}, u32[]{:S(2)}) copy-start(bf16[1024,256]{1,0:T(8,128)(2,1)S(1)} %collective-permute-done.1.rest_4_) | copy-start | bytes 1572868
  35.6 3.1 %copy-start.7 = (bf16[1024,256]{1,0:T(8,128)(2,1)}, bf16[1024,256]{1,0:T(8,128)(2,1)S(1)}, u32[]{:S(2)}) copy-start(bf16[1024,256]{1,0:T(8,128)(2,1)S(1)} %collective-permute-done.2.rest_5_) | copy-start | bytes 1572868
  35.7 3.0 %copy-start.8 = (bf16[1024,256]{1,0:T(8,128)(2,1)}, bf16[1024,256]{1,0:T(8,128)(2,1)S(1)}, u32[]{:S(2)}) copy-start(bf16[1024,256]{1,0:T(8,128)(2,1)S(1)} %collective-permute-done.3.rest_6_) | copy-start | bytes 1572868
  35.7 3.0 %copy-start.9 = (bf16[1024,256]{1,0:T(8,128)(2,1)}, bf16[1024,256]{1,0:T(8,128)(2,1)S(1)}, u32[]{:S(2)}) copy-start(bf16[1024,256]{1,0:T(8,128)(2,1)S(1)} %collective-permute-done.4.rest_7_) | copy-start | bytes 1572868
  38.7 0.7 copy-start.10
  44.3 13.4 %copy-start.1 = (bf16[256,1024]{1,0:T(8,128)(2,1)S(1)}, bf16[256,1024]{1,0:T(8,128)(2,1)}, u32[]{:S(2)}) copy-start(bf16[256,1024]{1,0:T(8,128)(2,1)} %probe.1) | copy-start | bytes 1572868
  44.3 15.3 %copy-start.2 = (bf16[256,1024]{1,0:T(8,128)(2,1)S(1)}, bf16[256,1024]{1,0:T(8,128)(2,1)}, u32[]{:S(2)}) copy-start(bf16[256,1024]{1,0:T(8,128)(2,1)} %down.3) | copy-start | bytes 1572868
  44.4 17.7 %all-to-all-start.1 = ((bf16[8,48,1024]{2,1,0:T(8,128)(2,1)}), bf16[8,48,1024]{2,1,0:T(8,128)(2,1)S(1)}, u32[]{:S(2)}, u32[]{:S(2)}) async-start(bf16[8,48,1024]{2,1,0:T(8,128)(2,1)} %bitcast.25), calls=%async_computation.1 | async-start | bytes 1572864 | tf_op jit(solution)/shard_map/all_to_all | solution.py:308
  49.5 12.5 %collective-permute-start.5 = (bf16[192,1024]{1,0:T(8,128)(2,1)}, bf16[192,1024]{1,0:T(8,128)(2,1)S(1)}, u32[]{:S(2)}, u32[]{:S(2)}) collective-permute-start(bf16[192,1024]{1,0:T(8,128)(2,1)} %get-tuple-element.21.inputs), channel_id=1, source_target_pairs={{0,8},{8,0},{1,9},{9,1},{2,10},{10,2},{3,11},{11,3},{4,12},{12,4},... | collective-permute-start | bytes 1179656 | tf_op jit(solution)/shard_map/ppermute | solution.py:26
  57.7 10.8 %collective-permute-start.7 = (bf16[256,1024]{1,0:T(8,128)(2,1)S(1)}, bf16[256,1024]{1,0:T(8,128)(2,1)S(1)}, u32[]{:S(2)}, u32[]{:S(2)}) collective-permute-start(bf16[256,1024]{1,0:T(8,128)(2,1)S(1)} %copy-done.1), channel_id=1, source_target_pairs={{0,8},{8,0},{1,9},{9,1},{2,10},{10,2},{3,11},{11,3},{4,12},{12,4},... | collective-permute-start | bytes 1572872 | tf_op jit(solution)/shard_map/ppermute | solution.py:26
  59.7 8.8 %collective-permute-start.6 = (bf16[256,1024]{1,0:T(8,128)(2,1)S(1)}, bf16[256,1024]{1,0:T(8,128)(2,1)S(1)}, u32[]{:S(2)}, u32[]{:S(2)}) collective-permute-start(bf16[256,1024]{1,0:T(8,128)(2,1)S(1)} %copy-done.2), channel_id=1, source_target_pairs={{0,8},{8,0},{1,9},{9,1},{2,10},{10,2},{3,11},{11,3},{4,12},{12,4},... | collective-permute-start | bytes 1572872 | tf_op jit(solution)/shard_map/ppermute | solution.py:26
  63.0 12.0 %all-to-all-start.2 = ((bf16[8,48,512]{2,1,0:T(8,128)(2,1)}), bf16[8,48,512]{2,1,0:T(8,128)(2,1)S(1)}, u32[]{:S(2)}, u32[]{:S(2)}) async-start(bf16[8,48,512]{2,1,0:T(8,128)(2,1)} %bitcast.27), calls=%async_computation.2 | async-start | bytes 786432 | tf_op jit(solution)/shard_map/all_to_all | solution.py:318
  76.1 10.3 %collective-permute-start.9 = (bf16[96,1024]{1,0:T(8,128)(2,1)S(1)}, bf16[96,1024]{1,0:T(8,128)(2,1)S(1)}, u32[]{:S(2)}, u32[]{:S(2)}) collective-permute-start(bf16[96,1024]{1,0:T(8,128)(2,1)S(1)} %get-tuple-element.26), channel_id=1, source_target_pairs={{0,256},{256,0},{1,257},{257,1},{2,258},{258,2},{3,259},{259,3},{4... | collective-permute-start | bytes 589832 | tf_op jit(solution)/shard_map/ppermute | solution.py:26
  80.6 5.8 %collective-permute-start.8 = (bf16[192,256]{1,0:T(8,128)(2,1)S(1)}, bf16[192,256]{1,0:T(8,128)(2,1)S(1)}, u32[]{:S(2)}, u32[]{:S(2)}) collective-permute-start(bf16[192,256]{1,0:T(8,128)(2,1)S(1)} %get-tuple-element.24), channel_id=1, source_target_pairs={{0,8},{8,0},{1,9},{9,1},{2,10},{10,2},{3,11},{11,3},{4,12},{12,4},... | collective-permute-start | bytes 294920 | tf_op jit(solution)/shard_map/ppermute | solution.py:26
  126.0 7.9 %collective-permute-start.10 = (bf16[768,128]{1,0:T(8,128)(2,1)S(1)}, bf16[768,128]{1,0:T(8,128)(2,1)S(1)}, u32[]{:S(2)}, u32[]{:S(2)}) collective-permute-start(bf16[768,128]{1,0:T(8,128)(2,1)S(1)} %bitcast.22), channel_id=1, source_target_pairs={{0,256},{256,0},{1,257},{257,1},{2,258},{258,2},{3,259},{259,3},{4... | collective-permute-start | bytes 589832 | tf_op jit(solution)/shard_map/ppermute | solution.py:26
  135.7 12.1 %all-to-all-start.5 = ((bf16[8,48,256]{2,1,0:T(8,128)(2,1)}), bf16[8,48,256]{2,1,0:T(8,128)(2,1)S(1)}, u32[]{:S(2)}, u32[]{:S(2)}) async-start(bf16[8,48,256]{2,1,0:T(8,128)(2,1)} %bitcast.28), calls=%async_computation.5 | async-start | bytes 393216 | tf_op jit(solution)/shard_map/all_to_all | solution.py:361
  139.1 17.7 %collective-permute-start.11 = (bf16[192,1024]{1,0:T(8,128)(2,1)S(1)}, bf16[192,1024]{1,0:T(8,128)(2,1)S(1)}, u32[]{:S(2)}, u32[]{:S(2)}) collective-permute-start(bf16[192,1024]{1,0:T(8,128)(2,1)S(1)} %get-tuple-element.27.out), channel_id=1, source_target_pairs={{0,8},{8,0},{1,9},{9,1},{2,10},{10,2},{3,11},{11,3},{4,12},{12,4},... | collective-permute-start | bytes 1179656 | tf_op jit(solution)/shard_map/ppermute | solution.py:26
  148.7 8.1 %copy-start.4 = (s32[384]{0:T(512)S(1)}, s32[384]{0:T(512)}, u32[]{:S(2)}) copy-start(s32[384]{0:T(512)} %ids.1) | copy-start | bytes 4612
  148.7 16.6 %all-to-all-start.6 = ((bf16[16,48,256]{2,1,0:T(8,128)(2,1)}), bf16[16,48,256]{2,1,0:T(8,128)(2,1)S(1)}, u32[]{:S(2)}, u32[]{:S(2)}) async-start(bf16[16,48,256]{2,1,0:T(8,128)(2,1)} %bitcast.24), calls=%async_computation.6 | async-start | bytes 786432 | tf_op jit(solution)/shard_map/all_to_all | solution.py:371

commit v11 on v10

--- a/solution.py
+++ b/solution.py
@@ -90,24 +90,22 @@
         out[:, 128 * n : 128 * n + 128] = line.astype(bf16)
 
 
-def gates_kernel(rows, rows_y, *rest):
-    own, theirs, rest = rest[:4], rest[4:8], rest[8:]
-    kept, out, inputs, slots, buffer, in_sems, out_sems = rest
-    units = slots.shape[2]
-    copies = [start(own[k], slots.at[k], in_sems.at[k]) for k in range(4)]
+def ready_kernel(first, second, third, fourth, flag):
+    flag[...] = jnp.zeros_like(flag)
+
+
+def gates_kernel(rows, rows_y, after, *rest):
+    own, theirs, (kept, out, inputs, buffer, sems) = rest[:4], rest[4:8], rest[8:]
+    units = own[0].shape[1]
     inputs[...] = moved(192, 192, pick, jnp.concatenate([rows[...], rows_y[...]], axis=0))
-    writes = [start(inputs, kept, out_sems.at[4])]
-    for h in (1, 0):
-        for k in range(4):
-            columns = slice(k * units, (k + 1) * units)
-            if h == 0:
-                copies[k].wait()
-            partial = product(inputs[...], theirs[k][...] if h else slots[k])
+    writes = [start(inputs, kept, sems.at[4])]
+    for k in range(4):
+        columns = slice(k * units, (k + 1) * units)
+        for h, weights in enumerate((own, theirs)):
+            partial = product(inputs[...], weights[k][...])
             for d in range(NDP):
                 buffer[2 * d + h, :, columns] = partial[24 * d : 24 * d + 24].astype(bf16)
-            if h == 0:
-                place, target = buffer.at[:, :, columns], out.at[:, :, columns]
-                writes.append(start(place, target, out_sems.at[k]))
+        writes.append(start(buffer.at[:, :, columns], out.at[:, :, columns], sems.at[k]))
     for write in writes:
         write.wait()
 
@@ -290,17 +288,16 @@
     rows_y = swap(rows, YH)
     gates = (gate_weight, up_weight, gate_probe, up_probe)
     gates_x = [swap(w, CORE) for w in gates]
+    (flag,) = call(ready_kernel, 2, 0, [(w, ANY) for w in gates], [((8, 128), f32, VMEM)])
     inputs, partials = call(
         gates_kernel,
-        57.25,
+        14,
         8 * dots,
-        [(rows, VMEM), (rows_y, VMEM)] + [(w, HBM) for w in gates] + [(w, VMEM) for w in gates_x],
+        [(rows, VMEM), (rows_y, VMEM), (flag, ANY)] + [(w, VMEM) for w in (*gates, *gates_x)],
         [((192, width), bf16, HBM), ((16, 24, 4 * units), bf16, HBM)],
         [
             pltpu.VMEM((192, width), bf16),
-            pltpu.VMEM((4, width, units), bf16),
             pltpu.VMEM((16, 24, 4 * units), bf16),
-            DMA((4,)),
             DMA((5,)),
         ],
     )

time: 169 us -> 165 us (0.976)
  local copies, waits for them, and re-layouts: 1.44 us -> 5.21 us
  Pallas kernels: 15 us -> 12 us
  waiting for transfers between devices: 26.6 us -> 23.6 us
    unnamed x22, local copies, waits for them, and re-layouts: 1.44 us -> 5.21 us
    pallas_call x11 -> x12, Pallas kernels: 15 us -> 12 us  [call(): pl.pallas_call(kernel, out_shape=[pltpu.HBM(s, t) if space is HBM else ja...]
    ppermute x12, waiting for transfers between devices: 9.93 us -> 6.94 us  [swap(): return lax.ppermute(value, axis, [(0, 1), (1, 0)])]
  transfers between devices with their start and end apart: 17 -> 17, of which waited for: 6 -> 5; matrix products, arithmetic and copies ran while one was open for 0% -> 0% of each run, Pallas kernels for 2% -> 2%
where the time goes in v11:
time: 165 us; the launch traced here: 164 us
  starting transfers between devices  82.9 us (50%)
  blocking collectives  39.5 us (24%)
  waiting for transfers between devices  23.6 us (14%)
  Pallas kernels  12 us (7%)
  local copies, waits for them, and re-layouts  5.21 us (3%)
    ppermute x12, starting transfers between devices, swap(): return lax.ppermute(value, axis, [(0, 1), (1, 0)])  45.9 us
    all_to_all x1, blocking collectives, local(): lax.all_to_all(spread.reshape(NZ, 48, 128), Z, 0, 0).reshape(768, 128)  19.9 us
    all_to_all x1, blocking collectives, local(): lax.all_to_all(blocks.reshape(NZ, 48, 128), Z, 0, 0).reshape(768, 128)  19.6 us
    all_to_all x1, starting transfers between devices, local(): rows = lax.all_to_all(rows.reshape(NZ, 48, 128), Z, 0, 0).reshape(768, 128)  15.8 us
    pallas_call x12, Pallas kernels, call(): pl.pallas_call(kernel, out_shape=[pltpu.HBM(s, t) if space is HBM else ja...  12 us
    all_to_all x1, starting transfers between devices, local(): lax.all_to_all(spread.reshape(16, 48, units), (CORE,) + DP, 0, 0)  8.08 us
    ppermute x12, waiting for transfers between devices, swap(): return lax.ppermute(value, axis, [(0, 1), (1, 0)])  6.94 us
    all_to_all x1, waiting for transfers between devices, local(): lax.all_to_all(spread.reshape(16, 48, units), (CORE,) + DP, 0, 0)  6.71 us
  transfers between devices with their start and end apart: 17, of which 5 were waited for; matrix products, arithmetic and copies ran while one was open for 0% of the time, Pallas kernels for 2%

profile of v11, /device:TPU:1, one launch (start us, length us, event | category | flops | bytes accessed | tf_op | source)
XLA Modules:
  0.0 164.2 jit_solution(18182318420694394748)
XLA Ops:
  1.4 1.0 shard_map.111
  2.4 15.8 %all-to-all-start = ((bf16[16,48,128]{2,1,0:T(8,128)(2,1)}), bf16[16,48,128]{2,1,0:T(8,128)(2,1)S(1)}, u32[]{:S(2)}, u32[]{:S(2)}) async-start(bf16[16,48,128]{2,1,0:T(8,128)(2,1)} %bitcast.26), calls=%async_computation | async-start | bytes 393216 | tf_op jit(solution)/shard_map/all_to_all | solution.py:279
  18.2 2.9 %collective-permute-start.1 = (bf16[1024,256]{1,0:T(8,128)(2,1)S(1)}, bf16[1024,256]{1,0:T(8,128)(2,1)S(1)}, u32[]{:S(2)}, u32[]{:S(2)}) collective-permute-start(bf16[1024,256]{1,0:T(8,128)(2,1)S(1)} %copy-done), channel_id=1, source_target_pairs={{0,8},{8,0},{1,9},{9,1},{2,10},{10,2},{3,11},{11,3},{4,12},{12,4},... | collective-permute-start | bytes 1572872 | tf_op jit(solution)/shard_map/ppermute | solution.py:26
  21.1 1.9 %collective-permute-start.2 = (bf16[1024,256]{1,0:T(8,128)(2,1)}, bf16[1024,256]{1,0:T(8,128)(2,1)S(1)}, u32[]{:S(2)}, u32[]{:S(2)}) collective-permute-start(bf16[1024,256]{1,0:T(8,128)(2,1)} %rest_1_.1), channel_id=1, source_target_pairs={{0,8},{8,0},{1,9},{9,1},{2,10},{10,2},{3,11},{11,3},{4,12},{12,4},... | collective-permute-start | bytes 1572872 | tf_op jit(solution)/shard_map/ppermute | solution.py:26
  23.0 2.4 %collective-permute-start.3 = (bf16[1024,256]{1,0:T(8,128)(2,1)}, bf16[1024,256]{1,0:T(8,128)(2,1)S(1)}, u32[]{:S(2)}, u32[]{:S(2)}) collective-permute-start(bf16[1024,256]{1,0:T(8,128)(2,1)} %rest_2_.1), channel_id=1, source_target_pairs={{0,8},{8,0},{1,9},{9,1},{2,10},{10,2},{3,11},{11,3},{4,12},{12,4},... | collective-permute-start | bytes 1572872 | tf_op jit(solution)/shard_map/ppermute | solution.py:26
  25.4 1.9 %collective-permute-start.4 = (bf16[1024,256]{1,0:T(8,128)(2,1)}, bf16[1024,256]{1,0:T(8,128)(2,1)S(1)}, u32[]{:S(2)}, u32[]{:S(2)}) collective-permute-start(bf16[1024,256]{1,0:T(8,128)(2,1)} %rest_3_.1), channel_id=1, source_target_pairs={{0,8},{8,0},{1,9},{9,1},{2,10},{10,2},{3,11},{11,3},{4,12},{12,4},... | collective-permute-start | bytes 1572872 | tf_op jit(solution)/shard_map/ppermute | solution.py:26
  27.3 3.4 %all-to-all-done = bf16[16,48,128]{2,1,0:T(8,128)(2,1)S(1)} async-done(((bf16[16,48,128]{2,1,0:T(8,128)(2,1)}), bf16[16,48,128]{2,1,0:T(8,128)(2,1)S(1)}, u32[]{:S(2)}, u32[]{:S(2)}) %all-to-all-start) | async-done | bytes 196640 | tf_op jit(solution)/shard_map/all_to_all | solution.py:279
  30.8 4.8 %collective-permute-start = (bf16[96,1024]{1,0:T(8,128)(2,1)S(1)}, bf16[96,1024]{1,0:T(8,128)(2,1)S(1)}, u32[]{:S(2)}, u32[]{:S(2)}) collective-permute-start(bf16[96,1024]{1,0:T(8,128)(2,1)S(1)} %shard_map.112.rows), channel_id=1, source_target_pairs={{0,256},{256,0},{1,257},{257,1},{2,258},{258,2},{3,259},{259,3},{4... | collective-permute-start | bytes 589832 | tf_op jit(solution)/shard_map/ppermute | solution.py:26
  35.7 1.0 copy-done.1
  36.7 1.0 copy-done.3
  37.8 1.0 copy-done.5
  40.2 1.9 %shard_map.114 = (bf16[192,1024]{1,0:T(8,128)(2,1)}, bf16[16,24,1024]{2,1,0:T(8,128)(2,1)}) custom-call(bf16[96,1024]{1,0:T(8,128)(2,1)S(1)} %shard_map.112.rows, bf16[96,1024]{1,0:T(8,128)(2,1)S(1)} %collective-permute-done.rows_y, f32[8,128]{1,0:T(8,128)S(1)} %shard_map.113.after, bf16[1024,256]{1,0:T(8,128)(2,1)S(1)} %copy-done, ...), custom_call_target="tpu_custom_call" | custom-call | flops 805306368 | bytes 5767168 | tf_op jit(solution)/shard_map/pallas_call | solution.py:251
  42.0 4.3 %all-to-all-start.1 = ((bf16[8,48,1024]{2,1,0:T(8,128)(2,1)}), bf16[8,48,1024]{2,1,0:T(8,128)(2,1)S(1)}, u32[]{:S(2)}, u32[]{:S(2)}) async-start(bf16[8,48,1024]{2,1,0:T(8,128)(2,1)} %bitcast.25), calls=%async_computation.1 | async-start | bytes 1572864 | tf_op jit(solution)/shard_map/all_to_all | solution.py:305
  46.3 7.7 %collective-permute-start.5 = (bf16[192,1024]{1,0:T(8,128)(2,1)}, bf16[192,1024]{1,0:T(8,128)(2,1)S(1)}, u32[]{:S(2)}, u32[]{:S(2)}) collective-permute-start(bf16[192,1024]{1,0:T(8,128)(2,1)} %get-tuple-element.21.inputs), channel_id=1, source_target_pairs={{0,8},{8,0},{1,9},{9,1},{2,10},{10,2},{3,11},{11,3},{4,12},{12,4},... | collective-permute-start | bytes 1179656 | tf_op jit(solution)/shard_map/ppermute | solution.py:26
  54.0 1.9 %collective-permute-start.6 = (bf16[256,1024]{1,0:T(8,128)(2,1)S(1)}, bf16[256,1024]{1,0:T(8,128)(2,1)S(1)}, u32[]{:S(2)}, u32[]{:S(2)}) collective-permute-start(bf16[256,1024]{1,0:T(8,128)(2,1)S(1)} %copy-done.8), channel_id=1, source_target_pairs={{0,8},{8,0},{1,9},{9,1},{2,10},{10,2},{3,11},{11,3},{4,12},{12,4},... | collective-permute-start | bytes 1572872 | tf_op jit(solution)/shard_map/ppermute | solution.py:26
  55.9 2.4 %collective-permute-start.7 = (bf16[256,1024]{1,0:T(8,128)(2,1)S(1)}, bf16[256,1024]{1,0:T(8,128)(2,1)S(1)}, u32[]{:S(2)}, u32[]{:S(2)}) collective-permute-start(bf16[256,1024]{1,0:T(8,128)(2,1)S(1)} %copy-done.7), channel_id=1, source_target_pairs={{0,8},{8,0},{1,9},{9,1},{2,10},{10,2},{3,11},{11,3},{4,12},{12,4},... | collective-permute-start | bytes 1572872 | tf_op jit(solution)/shard_map/ppermute | solution.py:26
  59.3 5.4 %all-to-all-start.2 = ((bf16[8,48,512]{2,1,0:T(8,128)(2,1)}), bf16[8,48,512]{2,1,0:T(8,128)(2,1)S(1)}, u32[]{:S(2)}, u32[]{:S(2)}) async-start(bf16[8,48,512]{2,1,0:T(8,128)(2,1)} %bitcast.27), calls=%async_computation.2 | async-start | bytes 786432 | tf_op jit(solution)/shard_map/all_to_all | solution.py:315
  64.8 6.5 %all-to-all-done.2 = bf16[8,48,512]{2,1,0:T(8,128)(2,1)S(1)} async-done(((bf16[8,48,512]{2,1,0:T(8,128)(2,1)}), bf16[8,48,512]{2,1,0:T(8,128)(2,1)S(1)}, u32[]{:S(2)}, u32[]{:S(2)}) %all-to-all-start.2) | async-done | bytes 393248 | tf_op jit(solution)/shard_map/all_to_all | solution.py:315
  71.3 1.1 shard_map.116
  72.4 4.5 %collective-permute-start.9 = (bf16[96,1024]{1,0:T(8,128)(2,1)S(1)}, bf16[96,1024]{1,0:T(8,128)(2,1)S(1)}, u32[]{:S(2)}, u32[]{:S(2)}) collective-permute-start(bf16[96,1024]{1,0:T(8,128)(2,1)S(1)} %get-tuple-element.26), channel_id=1, source_target_pairs={{0,256},{256,0},{1,257},{257,1},{2,258},{258,2},{3,259},{259,3},{4... | collective-permute-start | bytes 589832 | tf_op jit(solution)/shard_map/ppermute | solution.py:26
  76.9 4.9 %collective-permute-start.8 = (bf16[192,256]{1,0:T(8,128)(2,1)S(1)}, bf16[192,256]{1,0:T(8,128)(2,1)S(1)}, u32[]{:S(2)}, u32[]{:S(2)}) collective-permute-start(bf16[192,256]{1,0:T(8,128)(2,1)S(1)} %get-tuple-element.24), channel_id=1, source_target_pairs={{0,8},{8,0},{1,9},{9,1},{2,10},{10,2},{3,11},{11,3},{4,12},{12,4},... | collective-permute-start | bytes 294920 | tf_op jit(solution)/shard_map/ppermute | solution.py:26
  82.8 19.6 %all_to_all.35 = bf16[16,48,128]{2,1,0:T(8,128)(2,1)S(1)} all-to-all(bf16[16,48,128]{2,1,0:T(8,128)(2,1)S(1)} %bitcast.16), channel_id=1, replica_groups=mesh['yh'=2,'z'=16,'core'=2,'x'=4,'yl'=2] {'z'}, dimensions={0} | all-to-all | bytes 393216 | tf_op jit(solution)/shard_map/all_to_all | solution.py:339
  102.4 19.9 %all_to_all.36 = bf16[16,48,128]{2,1,0:T(8,128)(2,1)S(1)} all-to-all(bf16[16,48,128]{2,1,0:T(8,128)(2,1)S(1)} %bitcast.19), channel_id=1, replica_groups=mesh['yh'=2,'z'=16,'core'=2,'x'=4,'yl'=2] {'z'}, dimensions={0} | all-to-all | bytes 393216 | tf_op jit(solution)/shard_map/all_to_all | solution.py:347
  122.3 1.9 %collective-permute-start.10 = (bf16[768,128]{1,0:T(8,128)(2,1)S(1)}, bf16[768,128]{1,0:T(8,128)(2,1)S(1)}, u32[]{:S(2)}, u32[]{:S(2)}) collective-permute-start(bf16[768,128]{1,0:T(8,128)(2,1)S(1)} %bitcast.22), channel_id=1, source_target_pairs={{0,256},{256,0},{1,257},{257,1},{2,258},{258,2},{3,259},{259,3},{4... | collective-permute-start | bytes 589832 | tf_op jit(solution)/shard_map/ppermute | solution.py:26
  124.3 6.0 %collective-permute-done.10.blocks_y = bf16[768,128]{1,0:T(8,128)(2,1)S(1)} collective-permute-done((bf16[768,128]{1,0:T(8,128)(2,1)S(1)}, bf16[768,128]{1,0:T(8,128)(2,1)S(1)}, u32[]{:S(2)}, u32[]{:S(2)}) %collective-permute-start.10) | collective-permute-done | bytes 196640 | tf_op jit(solution)/shard_map/ppermute | solution.py:26
  130.2 1.7 %shard_map.119 = (bf16[192,1024]{1,0:T(8,128)(2,1)S(1)}, bf16[16,24,256]{2,1,0:T(8,128)(2,1)}) custom-call(bf16[768,128]{1,0:T(8,128)(2,1)S(1)} %bitcast.23, bf16[768,128]{1,0:T(8,128)(2,1)S(1)} %collective-permute-done.10.blocks_y, bf16[256,1024]{1,0:T(8,128)(2,1)S(1)} %copy-done.8, bf16[256,1024]{1,0:T(8,128)(2,1)S(1)} %collective-permute-done.6.down_x), custom_call_target="tpu_custom_call" | custom-call | flops 402653184 | bytes 2031616 | tf_op jit(solution)/shard_map/pallas_call | solution.py:251
  132.0 3.4 %all-to-all-start.5 = ((bf16[8,48,256]{2,1,0:T(8,128)(2,1)}), bf16[8,48,256]{2,1,0:T(8,128)(2,1)S(1)}, u32[]{:S(2)}, u32[]{:S(2)}) async-start(bf16[8,48,256]{2,1,0:T(8,128)(2,1)} %bitcast.28), calls=%async_computation.5 | async-start | bytes 393216 | tf_op jit(solution)/shard_map/all_to_all | solution.py:358
  135.4 8.7 %collective-permute-start.11 = (bf16[192,1024]{1,0:T(8,128)(2,1)S(1)}, bf16[192,1024]{1,0:T(8,128)(2,1)S(1)}, u32[]{:S(2)}, u32[]{:S(2)}) collective-permute-start(bf16[192,1024]{1,0:T(8,128)(2,1)S(1)} %get-tuple-element.27.out), channel_id=1, source_target_pairs={{0,8},{8,0},{1,9},{9,1},{2,10},{10,2},{3,11},{11,3},{4,12},{12,4},... | collective-permute-start | bytes 1179656 | tf_op jit(solution)/shard_map/ppermute | solution.py:26
  145.0 8.1 %all-to-all-start.6 = ((bf16[16,48,256]{2,1,0:T(8,128)(2,1)}), bf16[16,48,256]{2,1,0:T(8,128)(2,1)S(1)}, u32[]{:S(2)}, u32[]{:S(2)}) async-start(bf16[16,48,256]{2,1,0:T(8,128)(2,1)} %bitcast.24), calls=%async_computation.6 | async-start | bytes 786432 | tf_op jit(solution)/shard_map/all_to_all | solution.py:368
  153.1 1.8 %shard_map.120 = (bf16[256,1024]{1,0:T(8,128)(2,1)}, bf16[6,1024]{1,0:T(8,128)(2,1)}, f32[8,128]{1,0:T(8,128)S(1)}) custom-call(s32[384]{0:T(512)S(1)} %copy-done.10, bf16[192,256]{1,0:T(8,128)(2,1)S(1)} %get-tuple-element.23.hidden, bf16[192,256]{1,0:T(8,128)(2,1)S(1)} %collective-permute-done.8.after.hidden_core, ...), custom_call_target="tpu_custom_call" | custom-call | flops 201326592 | bytes 1525248 | tf_op jit(solution)/shard_map/pallas_call | solution.py:251
  154.9 6.7 %all-to-all-done.6 = bf16[16,48,256]{2,1,0:T(8,128)(2,1)S(1)} async-done(((bf16[16,48,256]{2,1,0:T(8,128)(2,1)}), bf16[16,48,256]{2,1,0:T(8,128)(2,1)S(1)}, u32[]{:S(2)}, u32[]{:S(2)}) %all-to-all-start.6) | async-done | bytes 393248 | tf_op jit(solution)/shard_map/all_to_all | solution.py:368
  161.6 2.6 %shard_map.122 = (bf16[1024,256]{1,0:T(8,128)(2,1)}, bf16[1024,256]{1,0:T(8,128)(2,1)}) custom-call(bf16[768,256]{1,0:T(8,128)(2,1)S(1)} %bitcast.21, bf16[192,1024]{1,0:T(8,128)(2,1)} %get-tuple-element.21.inputs, bf16[192,1024]{1,0:T(8,128)(2,1)S(1)} %collective-permute-done.5.after.inputs_x, f32[8,128]{1,0:T(8,128)S(1)} %get-tuple-element.32.after), custom_call_target="tpu_custom_call" | custom-call | flops 402653184 | bytes 2228224 | tf_op jit(solution)/shard_map/pallas_call | solution.py:251
  (38 shorter events, 5.0 us)
Async XLA Ops:
  0.6 17.5 %copy-start = (bf16[1024,256]{1,0:T(8,128)(2,1)S(1)}, bf16[1024,256]{1,0:T(8,128)(2,1)}, u32[]{:S(2)}) copy-start(bf16[1024,256]{1,0:T(8,128)(2,1)} %rest_0_.1) | copy-start | bytes 1572868
  0.6 0.8 copy-start.9
  2.4 28.3 %all-to-all-start = ((bf16[16,48,128]{2,1,0:T(8,128)(2,1)}), bf16[16,48,128]{2,1,0:T(8,128)(2,1)S(1)}, u32[]{:S(2)}, u32[]{:S(2)}) async-start(bf16[16,48,128]{2,1,0:T(8,128)(2,1)} %bitcast.26), calls=%async_computation | async-start | bytes 393216 | tf_op jit(solution)/shard_map/all_to_all | solution.py:279
  18.2 20.6 %collective-permute-start.1 = (bf16[1024,256]{1,0:T(8,128)(2,1)S(1)}, bf16[1024,256]{1,0:T(8,128)(2,1)S(1)}, u32[]{:S(2)}, u32[]{:S(2)}) collective-permute-start(bf16[1024,256]{1,0:T(8,128)(2,1)S(1)} %copy-done), channel_id=1, source_target_pairs={{0,8},{8,0},{1,9},{9,1},{2,10},{10,2},{3,11},{11,3},{4,12},{12,4},... | collective-permute-start | bytes 1572872 | tf_op jit(solution)/shard_map/ppermute | solution.py:26
  21.1 17.8 %collective-permute-start.2 = (bf16[1024,256]{1,0:T(8,128)(2,1)}, bf16[1024,256]{1,0:T(8,128)(2,1)S(1)}, u32[]{:S(2)}, u32[]{:S(2)}) collective-permute-start(bf16[1024,256]{1,0:T(8,128)(2,1)} %rest_1_.1), channel_id=1, source_target_pairs={{0,8},{8,0},{1,9},{9,1},{2,10},{10,2},{3,11},{11,3},{4,12},{12,4},... | collective-permute-start | bytes 1572872 | tf_op jit(solution)/shard_map/ppermute | solution.py:26
  23.0 15.9 %collective-permute-start.3 = (bf16[1024,256]{1,0:T(8,128)(2,1)}, bf16[1024,256]{1,0:T(8,128)(2,1)S(1)}, u32[]{:S(2)}, u32[]{:S(2)}) collective-permute-start(bf16[1024,256]{1,0:T(8,128)(2,1)} %rest_2_.1), channel_id=1, source_target_pairs={{0,8},{8,0},{1,9},{9,1},{2,10},{10,2},{3,11},{11,3},{4,12},{12,4},... | collective-permute-start | bytes 1572872 | tf_op jit(solution)/shard_map/ppermute | solution.py:26
  25.4 13.4 %collective-permute-start.4 = (bf16[1024,256]{1,0:T(8,128)(2,1)}, bf16[1024,256]{1,0:T(8,128)(2,1)S(1)}, u32[]{:S(2)}, u32[]{:S(2)}) collective-permute-start(bf16[1024,256]{1,0:T(8,128)(2,1)} %rest_3_.1), channel_id=1, source_target_pairs={{0,8},{8,0},{1,9},{9,1},{2,10},{10,2},{3,11},{11,3},{4,12},{12,4},... | collective-permute-start | bytes 1572872 | tf_op jit(solution)/shard_map/ppermute | solution.py:26
  30.8 8.0 %collective-permute-start = (bf16[96,1024]{1,0:T(8,128)(2,1)S(1)}, bf16[96,1024]{1,0:T(8,128)(2,1)S(1)}, u32[]{:S(2)}, u32[]{:S(2)}) collective-permute-start(bf16[96,1024]{1,0:T(8,128)(2,1)S(1)} %shard_map.112.rows), channel_id=1, source_target_pairs={{0,256},{256,0},{1,257},{257,1},{2,258},{258,2},{3,259},{259,3},{4... | collective-permute-start | bytes 589832 | tf_op jit(solution)/shard_map/ppermute | solution.py:26
  35.7 1.0 copy-start.1
  36.7 1.0 copy-start.3
  37.8 1.0 copy-start.5
  38.8 1.0 copy-start.2
  38.8 1.2 copy-start.4
  38.8 1.4 copy-start.6
  42.0 12.0 %copy-start.8 = (bf16[256,1024]{1,0:T(8,128)(2,1)S(1)}, bf16[256,1024]{1,0:T(8,128)(2,1)}, u32[]{:S(2)}) copy-start(bf16[256,1024]{1,0:T(8,128)(2,1)} %down.3) | copy-start | bytes 1572868
  42.0 13.9 %copy-start.7 = (bf16[256,1024]{1,0:T(8,128)(2,1)S(1)}, bf16[256,1024]{1,0:T(8,128)(2,1)}, u32[]{:S(2)}) copy-start(bf16[256,1024]{1,0:T(8,128)(2,1)} %probe.1) | copy-start | bytes 1572868
  42.0 16.3 %all-to-all-start.1 = ((bf16[8,48,1024]{2,1,0:T(8,128)(2,1)}), bf16[8,48,1024]{2,1,0:T(8,128)(2,1)S(1)}, u32[]{:S(2)}, u32[]{:S(2)}) async-start(bf16[8,48,1024]{2,1,0:T(8,128)(2,1)} %bitcast.25), calls=%async_computation.1 | async-start | bytes 1572864 | tf_op jit(solution)/shard_map/all_to_all | solution.py:305
  46.3 12.1 %collective-permute-start.5 = (bf16[192,1024]{1,0:T(8,128)(2,1)}, bf16[192,1024]{1,0:T(8,128)(2,1)S(1)}, u32[]{:S(2)}, u32[]{:S(2)}) collective-permute-start(bf16[192,1024]{1,0:T(8,128)(2,1)} %get-tuple-element.21.inputs), channel_id=1, source_target_pairs={{0,8},{8,0},{1,9},{9,1},{2,10},{10,2},{3,11},{11,3},{4,12},{12,4},... | collective-permute-start | bytes 1179656 | tf_op jit(solution)/shard_map/ppermute | solution.py:26
  54.0 10.8 %collective-permute-start.6 = (bf16[256,1024]{1,0:T(8,128)(2,1)S(1)}, bf16[256,1024]{1,0:T(8,128)(2,1)S(1)}, u32[]{:S(2)}, u32[]{:S(2)}) collective-permute-start(bf16[256,1024]{1,0:T(8,128)(2,1)S(1)} %copy-done.8), channel_id=1, source_target_pairs={{0,8},{8,0},{1,9},{9,1},{2,10},{10,2},{3,11},{11,3},{4,12},{12,4},... | collective-permute-start | bytes 1572872 | tf_op jit(solution)/shard_map/ppermute | solution.py:26
  55.9 8.8 %collective-permute-start.7 = (bf16[256,1024]{1,0:T(8,128)(2,1)S(1)}, bf16[256,1024]{1,0:T(8,128)(2,1)S(1)}, u32[]{:S(2)}, u32[]{:S(2)}) collective-permute-start(bf16[256,1024]{1,0:T(8,128)(2,1)S(1)} %copy-done.7), channel_id=1, source_target_pairs={{0,8},{8,0},{1,9},{9,1},{2,10},{10,2},{3,11},{11,3},{4,12},{12,4},... | collective-permute-start | bytes 1572872 | tf_op jit(solution)/shard_map/ppermute | solution.py:26
  59.3 12.0 %all-to-all-start.2 = ((bf16[8,48,512]{2,1,0:T(8,128)(2,1)}), bf16[8,48,512]{2,1,0:T(8,128)(2,1)S(1)}, u32[]{:S(2)}, u32[]{:S(2)}) async-start(bf16[8,48,512]{2,1,0:T(8,128)(2,1)} %bitcast.27), calls=%async_computation.2 | async-start | bytes 786432 | tf_op jit(solution)/shard_map/all_to_all | solution.py:315
  72.4 10.3 %collective-permute-start.9 = (bf16[96,1024]{1,0:T(8,128)(2,1)S(1)}, bf16[96,1024]{1,0:T(8,128)(2,1)S(1)}, u32[]{:S(2)}, u32[]{:S(2)}) collective-permute-start(bf16[96,1024]{1,0:T(8,128)(2,1)S(1)} %get-tuple-element.26), channel_id=1, source_target_pairs={{0,256},{256,0},{1,257},{257,1},{2,258},{258,2},{3,259},{259,3},{4... | collective-permute-start | bytes 589832 | tf_op jit(solution)/shard_map/ppermute | solution.py:26
  76.9 5.8 %collective-permute-start.8 = (bf16[192,256]{1,0:T(8,128)(2,1)S(1)}, bf16[192,256]{1,0:T(8,128)(2,1)S(1)}, u32[]{:S(2)}, u32[]{:S(2)}) collective-permute-start(bf16[192,256]{1,0:T(8,128)(2,1)S(1)} %get-tuple-element.24), channel_id=1, source_target_pairs={{0,8},{8,0},{1,9},{9,1},{2,10},{10,2},{3,11},{11,3},{4,12},{12,4},... | collective-permute-start | bytes 294920 | tf_op jit(solution)/shard_map/ppermute | solution.py:26
  122.3 7.9 %collective-permute-start.10 = (bf16[768,128]{1,0:T(8,128)(2,1)S(1)}, bf16[768,128]{1,0:T(8,128)(2,1)S(1)}, u32[]{:S(2)}, u32[]{:S(2)}) collective-permute-start(bf16[768,128]{1,0:T(8,128)(2,1)S(1)} %bitcast.22), channel_id=1, source_target_pairs={{0,256},{256,0},{1,257},{257,1},{2,258},{258,2},{3,259},{259,3},{4... | collective-permute-start | bytes 589832 | tf_op jit(solution)/shard_map/ppermute | solution.py:26
  132.0 12.1 %all-to-all-start.5 = ((bf16[8,48,256]{2,1,0:T(8,128)(2,1)}), bf16[8,48,256]{2,1,0:T(8,128)(2,1)S(1)}, u32[]{:S(2)}, u32[]{:S(2)}) async-start(bf16[8,48,256]{2,1,0:T(8,128)(2,1)} %bitcast.28), calls=%async_computation.5 | async-start | bytes 393216 | tf_op jit(solution)/shard_map/all_to_all | solution.py:358
  135.4 17.7 %collective-permute-start.11 = (bf16[192,1024]{1,0:T(8,128)(2,1)S(1)}, bf16[192,1024]{1,0:T(8,128)(2,1)S(1)}, u32[]{:S(2)}, u32[]{:S(2)}) collective-permute-start(bf16[192,1024]{1,0:T(8,128)(2,1)S(1)} %get-tuple-element.27.out), channel_id=1, source_target_pairs={{0,8},{8,0},{1,9},{9,1},{2,10},{10,2},{3,11},{11,3},{4,12},{12,4},... | collective-permute-start | bytes 1179656 | tf_op jit(solution)/shard_map/ppermute | solution.py:26
  145.0 8.1 %copy-start.10 = (s32[384]{0:T(512)S(1)}, s32[384]{0:T(512)}, u32[]{:S(2)}) copy-start(s32[384]{0:T(512)} %ids.1) | copy-start | bytes 4612
  145.0 16.6 %all-to-all-start.6 = ((bf16[16,48,256]{2,1,0:T(8,128)(2,1)}), bf16[16,48,256]{2,1,0:T(8,128)(2,1)S(1)}, u32[]{:S(2)}, u32[]{:S(2)}) async-start(bf16[16,48,256]{2,1,0:T(8,128)(2,1)} %bitcast.24), calls=%async_computation.6 | async-start | bytes 786432 | tf_op jit(solution)/shard_map/all_to_all | solution.py:368

commit v12 on v11

--- a/solution.py
+++ b/solution.py
@@ -52,10 +52,6 @@
 
 def by_half(q, j):
     return ((q & 7) * 4 + (q >> 4) * 2 + ((q >> 3) & 1)) * 12 + j
-
-
-def by_kind(q, j):
-    return (((q >> 1) & 7) * 4 + (q >> 4) * 2 + (q & 1)) * 12 + j
 
 
 def rows_at(position, count):
@@ -168,19 +164,15 @@
     return jnp.concatenate(lines, axis=0)
 
 
-def cot_kernel(blocks, blocks_y, down, down_x, tan_out, out, slot, buffer, in_sem, out_sem):
-    copy = start(down, slot, in_sem)
-    tan_out[:96] = whole(blocks)
-    tan_out[96:] = whole(blocks_y)
-    left = moved(192, 192, pick, tan_out[...])
+def cot_kernel(blocks, blocks_y, down, down_x, out, slot, sem):
+    copy = start(down, slot, sem)
+    left = moved(192, 192, pick, jnp.concatenate([whole(blocks), whole(blocks_y)], axis=0))
     for h in (1, 0):
         if h == 0:
             copy.wait()
         total = over_width(left, down_x[...] if h else slot[...])
         for d in range(NDP):
-            buffer[2 * d + h] = total[24 * d : 24 * d + 24].astype(bf16)
-    write = start(buffer, out, out_sem)
-    write.wait()
+            out[2 * d + h] = total[24 * d : 24 * d + 24].astype(bf16)
 
 
 def cot_units_kernel(parts, coef_gate, coef_up, out, buffer, sems):
@@ -205,9 +197,11 @@
 def ggn_kernel(parts, inputs, inputs_x, after, ggn_gate, ggn_up, own, buffer, in_sem, sems):
     copy = start(inputs, own, in_sem)
     core = lax.axis_index(CORE)
-    sides = [
-        moved(384, 384, by_kind, parts[rows_at(position, 384), :]) for position in (core, 1 - core)
-    ]
+    sides = []
+    for position in (core, 1 - core):
+        both = parts[rows_at(position, 384), :].astype(f32)
+        lines = [both[48 * d + 24 * k : 48 * d + 24 * k + 24] for k in range(2) for d in range(NDP)]
+        sides.append(jnp.concatenate(lines, axis=0).astype(bf16))
     width = inputs.shape[1]
     copy.wait()
     writes = []
@@ -224,9 +218,11 @@
         write.wait()
 
 
-def ggn_down_kernel(scale, ids, hidden, hidden_core, out, out_core, ggn_down, tangent_out, flag):
+def ggn_down_kernel(scale, ids, hidden, hidden_core, *rest):
+    blocks, (ggn_down, tangent_out, flag) = rest[:4], rest[4:]
     yh, z, core = lax.axis_index(YH), lax.axis_index(Z), lax.axis_index(CORE)
-    total = over_rows(hidden[...], out[...]) + over_rows(hidden_core[...], out_core[...])
+    every = jnp.concatenate([whole(b) for b in blocks], axis=0)
+    total = over_rows(hidden[...], every[:192]) + over_rows(hidden_core[...], every[192:])
     ggn_down[...] = (total * scale).astype(bf16)
     own_count = tangent_out.shape[0]
     first = ((yh * NZ + z) * 2 + core) * own_count
@@ -240,7 +236,6 @@
         place = place + (holder // 2) % NZ * own_count + stored % own_count
         wanted = jnp.where(row == i, place, wanted)
     hot = jnp.where(wanted == column, 1.0, 0.0).astype(bf16)
-    every = jnp.concatenate([out[...], out_core[...]], axis=0)
     tangent_out[...] = product(hot, every)[:own_count].astype(bf16)
     flag[...] = jnp.zeros_like(flag)
 
@@ -347,16 +342,15 @@
     blocks = lax.all_to_all(spread.reshape(NZ, 48, 128), Z, 0, 0).reshape(768, 128)
 
     blocks_y = swap(blocks, YH)
-    out, cot = call(
+    (cot,) = call(
         cot_kernel,
         14,
         4 * dots,
         [(blocks, VMEM), (blocks_y, VMEM), (down_weight, HBM), (down_x, VMEM)],
-        [((192, width), bf16, VMEM), ((16, 24, units), bf16, HBM)],
-        [pltpu.VMEM((units, width), bf16), pltpu.VMEM((16, 24, units), bf16), DMA, DMA],
+        [((16, 24, units), bf16, VMEM)],
+        [pltpu.VMEM((units, width), bf16), DMA],
     )
     parts = lax.all_to_all(cot.reshape(NDP, 48, units), DP, 0, 0).reshape(384, units)
-    out_core = swap(out, CORE)
     (spread,) = call(
         cot_units_kernel,
         6,
@@ -366,11 +360,13 @@
         [pltpu.VMEM((96, units), bf16), DMA((16,))],
     )
     parts = lax.all_to_all(spread.reshape(16, 48, units), (CORE,) + DP, 0, 0).reshape(768, units)
+    blocks_x, blocks_yx = swap(blocks, CORE), swap(blocks_y, CORE)
     ggn_down, tangent_out, flag = call(
         functools.partial(ggn_down_kernel, scale),
         14,
         2 * dots,
-        [(ids, SMEM), (hidden, VMEM), (hidden_core, VMEM), (out, VMEM), (out_core, VMEM)],
+        [(ids, SMEM), (hidden, VMEM), (hidden_core, VMEM)]
+        + [(b, VMEM) for b in (blocks, blocks_y, blocks_x, blocks_yx)],
         [
             ((units, width), bf16, VMEM),
             ((own_count, width), bf16, VMEM),

time: 165 us -> 164 us (level)
  blocking collectives: 39.5 us -> 47.5 us
  waiting for transfers between devices: 23.6 us -> 19.3 us
  starting transfers between devices: 82.9 us -> 78.9 us
    all_to_all x0 -> x1, blocking collectives: none -> 7.92 us  [local(): lax.all_to_all(cot.reshape(NDP, 48, units), DP, 0, 0).reshape(384, units)]
    all_to_all x1, waiting for transfers between devices: 6.71 us -> 1.3 us  [local(): lax.all_to_all(spread.reshape(16, 48, units), (CORE,) + DP, 0, 0)]
    ppermute x12 -> x13, starting transfers between devices: 45.9 us -> 41.6 us  [swap(): return lax.ppermute(value, axis, [(0, 1), (1, 0)])]
    all_to_all x1, starting transfers between devices: 8.08 us -> 11.8 us  [local(): lax.all_to_all(spread.reshape(16, 48, units), (CORE,) + DP, 0, 0)]
    all_to_all x1 -> x0, starting transfers between devices: 3.4 us -> none  [local(): lax.all_to_all(cot.reshape(NDP, 48, units), DP, 0, 0).reshape(384, units)]
    ppermute x12 -> x13, waiting for transfers between devices: 6.94 us -> 8.02 us  [swap(): return lax.ppermute(value, axis, [(0, 1), (1, 0)])]
  transfers between devices with their start and end apart: 17 -> 17, of which waited for: 5 -> 6; matrix products, arithmetic and copies ran while one was open for 0% -> 0% of each run, Pallas kernels for 2% -> 2%
where the time goes in v12:
time: 164 us; the launch traced here: 163 us
  starting transfers between devices  78.9 us (48%)
  blocking collectives  47.5 us (29%)
  waiting for transfers between devices  19.3 us (12%)
  Pallas kernels  11.3 us (7%)
  local copies, waits for them, and re-layouts  5.21 us (3%)
    ppermute x13, starting transfers between devices, swap(): return lax.ppermute(value, axis, [(0, 1), (1, 0)])  41.6 us
    all_to_all x1, blocking collectives, local(): lax.all_to_all(spread.reshape(NZ, 48, 128), Z, 0, 0).reshape(768, 128)  19.9 us
    all_to_all x1, blocking collectives, local(): lax.all_to_all(blocks.reshape(NZ, 48, 128), Z, 0, 0).reshape(768, 128)  19.6 us
    all_to_all x1, starting transfers between devices, local(): rows = lax.all_to_all(rows.reshape(NZ, 48, 128), Z, 0, 0).reshape(768, 128)  15.8 us
    all_to_all x1, starting transfers between devices, local(): lax.all_to_all(spread.reshape(16, 48, units), (CORE,) + DP, 0, 0)  11.8 us
    pallas_call x12, Pallas kernels, call(): pl.pallas_call(kernel, out_shape=[pltpu.HBM(s, t) if space is HBM else ja...  11.3 us
    ppermute x13, waiting for transfers between devices, swap(): return lax.ppermute(value, axis, [(0, 1), (1, 0)])  8.02 us
    all_to_all x1, blocking collectives, local(): lax.all_to_all(cot.reshape(NDP, 48, units), DP, 0, 0).reshape(384, units)  7.92 us
  transfers between devices with their start and end apart: 17, of which 6 were waited for; matrix products, arithmetic and copies ran while one was open for 0% of the time, Pallas kernels for 2%

profile of v12, /device:TPU:1, one launch (start us, length us, event | category | flops | bytes accessed | tf_op | source)
XLA Modules:
  0.0 163.0 jit_solution(5477190735400429257)
XLA Ops:
  2.4 15.8 %all-to-all-start = ((bf16[16,48,128]{2,1,0:T(8,128)(2,1)}), bf16[16,48,128]{2,1,0:T(8,128)(2,1)S(1)}, u32[]{:S(2)}, u32[]{:S(2)}) async-start(bf16[16,48,128]{2,1,0:T(8,128)(2,1)} %bitcast.29), calls=%async_computation | async-start | bytes 393216 | tf_op jit(solution)/shard_map/all_to_all | solution.py:274
  18.2 2.9 %collective-permute-start.1 = (bf16[1024,256]{1,0:T(8,128)(2,1)S(1)}, bf16[1024,256]{1,0:T(8,128)(2,1)S(1)}, u32[]{:S(2)}, u32[]{:S(2)}) collective-permute-start(bf16[1024,256]{1,0:T(8,128)(2,1)S(1)} %copy-done.1), channel_id=1, source_target_pairs={{0,8},{8,0},{1,9},{9,1},{2,10},{10,2},{3,11},{11,3},{4,12},{12,4},... | collective-permute-start | bytes 1572872 | tf_op jit(solution)/shard_map/ppermute | solution.py:26
  21.1 1.9 %collective-permute-start.2 = (bf16[1024,256]{1,0:T(8,128)(2,1)}, bf16[1024,256]{1,0:T(8,128)(2,1)S(1)}, u32[]{:S(2)}, u32[]{:S(2)}) collective-permute-start(bf16[1024,256]{1,0:T(8,128)(2,1)} %rest_1_.1), channel_id=1, source_target_pairs={{0,8},{8,0},{1,9},{9,1},{2,10},{10,2},{3,11},{11,3},{4,12},{12,4},... | collective-permute-start | bytes 1572872 | tf_op jit(solution)/shard_map/ppermute | solution.py:26
  23.0 2.4 %collective-permute-start.3 = (bf16[1024,256]{1,0:T(8,128)(2,1)}, bf16[1024,256]{1,0:T(8,128)(2,1)S(1)}, u32[]{:S(2)}, u32[]{:S(2)}) collective-permute-start(bf16[1024,256]{1,0:T(8,128)(2,1)} %rest_2_.1), channel_id=1, source_target_pairs={{0,8},{8,0},{1,9},{9,1},{2,10},{10,2},{3,11},{11,3},{4,12},{12,4},... | collective-permute-start | bytes 1572872 | tf_op jit(solution)/shard_map/ppermute | solution.py:26
  25.4 1.9 %collective-permute-start.4 = (bf16[1024,256]{1,0:T(8,128)(2,1)}, bf16[1024,256]{1,0:T(8,128)(2,1)S(1)}, u32[]{:S(2)}, u32[]{:S(2)}) collective-permute-start(bf16[1024,256]{1,0:T(8,128)(2,1)} %rest_3_.1), channel_id=1, source_target_pairs={{0,8},{8,0},{1,9},{9,1},{2,10},{10,2},{3,11},{11,3},{4,12},{12,4},... | collective-permute-start | bytes 1572872 | tf_op jit(solution)/shard_map/ppermute | solution.py:26
  27.3 3.4 %all-to-all-done = bf16[16,48,128]{2,1,0:T(8,128)(2,1)S(1)} async-done(((bf16[16,48,128]{2,1,0:T(8,128)(2,1)}), bf16[16,48,128]{2,1,0:T(8,128)(2,1)S(1)}, u32[]{:S(2)}, u32[]{:S(2)}) %all-to-all-start) | async-done | bytes 196640 | tf_op jit(solution)/shard_map/all_to_all | solution.py:274
  30.8 4.8 %collective-permute-start = (bf16[96,1024]{1,0:T(8,128)(2,1)S(1)}, bf16[96,1024]{1,0:T(8,128)(2,1)S(1)}, u32[]{:S(2)}, u32[]{:S(2)}) collective-permute-start(bf16[96,1024]{1,0:T(8,128)(2,1)S(1)} %shard_map.112.rows), channel_id=1, source_target_pairs={{0,256},{256,0},{1,257},{257,1},{2,258},{258,2},{3,259},{259,3},{4... | collective-permute-start | bytes 589832 | tf_op jit(solution)/shard_map/ppermute | solution.py:26
  35.7 1.0 copy-done.2
  36.7 1.0 copy-done.4
  37.8 1.0 copy-done.6
  40.2 1.9 %shard_map.114 = (bf16[192,1024]{1,0:T(8,128)(2,1)}, bf16[16,24,1024]{2,1,0:T(8,128)(2,1)}) custom-call(bf16[96,1024]{1,0:T(8,128)(2,1)S(1)} %shard_map.112.rows, bf16[96,1024]{1,0:T(8,128)(2,1)S(1)} %collective-permute-done.rows_y, f32[8,128]{1,0:T(8,128)S(1)} %shard_map.113.after, bf16[1024,256]{1,0:T(8,128)(2,1)S(1)} %copy-done.1, ...), custom_call_target="tpu_custom_call" | custom-call | flops 805306368 | bytes 5767168 | tf_op jit(solution)/shard_map/pallas_call | solution.py:246
  42.0 4.3 %all-to-all-start.1 = ((bf16[8,48,1024]{2,1,0:T(8,128)(2,1)}), bf16[8,48,1024]{2,1,0:T(8,128)(2,1)S(1)}, u32[]{:S(2)}, u32[]{:S(2)}) async-start(bf16[8,48,1024]{2,1,0:T(8,128)(2,1)} %bitcast.28), calls=%async_computation.1 | async-start | bytes 1572864 | tf_op jit(solution)/shard_map/all_to_all | solution.py:300
  46.3 7.7 %collective-permute-start.5 = (bf16[192,1024]{1,0:T(8,128)(2,1)}, bf16[192,1024]{1,0:T(8,128)(2,1)S(1)}, u32[]{:S(2)}, u32[]{:S(2)}) collective-permute-start(bf16[192,1024]{1,0:T(8,128)(2,1)} %get-tuple-element.19.inputs), channel_id=1, source_target_pairs={{0,8},{8,0},{1,9},{9,1},{2,10},{10,2},{3,11},{11,3},{4,12},{12,4},... | collective-permute-start | bytes 1179656 | tf_op jit(solution)/shard_map/ppermute | solution.py:26
  54.0 1.9 %collective-permute-start.6 = (bf16[256,1024]{1,0:T(8,128)(2,1)S(1)}, bf16[256,1024]{1,0:T(8,128)(2,1)S(1)}, u32[]{:S(2)}, u32[]{:S(2)}) collective-permute-start(bf16[256,1024]{1,0:T(8,128)(2,1)S(1)} %copy-done), channel_id=1, source_target_pairs={{0,8},{8,0},{1,9},{9,1},{2,10},{10,2},{3,11},{11,3},{4,12},{12,4},... | collective-permute-start | bytes 1572872 | tf_op jit(solution)/shard_map/ppermute | solution.py:26
  56.0 2.4 %collective-permute-start.7 = (bf16[256,1024]{1,0:T(8,128)(2,1)S(1)}, bf16[256,1024]{1,0:T(8,128)(2,1)S(1)}, u32[]{:S(2)}, u32[]{:S(2)}) collective-permute-start(bf16[256,1024]{1,0:T(8,128)(2,1)S(1)} %copy-done.8), channel_id=1, source_target_pairs={{0,8},{8,0},{1,9},{9,1},{2,10},{10,2},{3,11},{11,3},{4,12},{12,4},... | collective-permute-start | bytes 1572872 | tf_op jit(solution)/shard_map/ppermute | solution.py:26
  59.3 5.4 %all-to-all-start.2 = ((bf16[8,48,512]{2,1,0:T(8,128)(2,1)}), bf16[8,48,512]{2,1,0:T(8,128)(2,1)S(1)}, u32[]{:S(2)}, u32[]{:S(2)}) async-start(bf16[8,48,512]{2,1,0:T(8,128)(2,1)} %bitcast.30), calls=%async_computation.2 | async-start | bytes 786432 | tf_op jit(solution)/shard_map/all_to_all | solution.py:310
  64.8 6.5 %all-to-all-done.2 = bf16[8,48,512]{2,1,0:T(8,128)(2,1)S(1)} async-done(((bf16[8,48,512]{2,1,0:T(8,128)(2,1)}), bf16[8,48,512]{2,1,0:T(8,128)(2,1)S(1)}, u32[]{:S(2)}, u32[]{:S(2)}) %all-to-all-start.2) | async-done | bytes 393248 | tf_op jit(solution)/shard_map/all_to_all | solution.py:310
  71.3 1.0 shard_map.116
  72.4 4.5 %collective-permute-start.9 = (bf16[96,1024]{1,0:T(8,128)(2,1)S(1)}, bf16[96,1024]{1,0:T(8,128)(2,1)S(1)}, u32[]{:S(2)}, u32[]{:S(2)}) collective-permute-start(bf16[96,1024]{1,0:T(8,128)(2,1)S(1)} %get-tuple-element.24), channel_id=1, source_target_pairs={{0,256},{256,0},{1,257},{257,1},{2,258},{258,2},{3,259},{259,3},{4... | collective-permute-start | bytes 589832 | tf_op jit(solution)/shard_map/ppermute | solution.py:26
  76.9 4.9 %collective-permute-start.8 = (bf16[192,256]{1,0:T(8,128)(2,1)S(1)}, bf16[192,256]{1,0:T(8,128)(2,1)S(1)}, u32[]{:S(2)}, u32[]{:S(2)}) collective-permute-start(bf16[192,256]{1,0:T(8,128)(2,1)S(1)} %get-tuple-element.22), channel_id=1, source_target_pairs={{0,8},{8,0},{1,9},{9,1},{2,10},{10,2},{3,11},{11,3},{4,12},{12,4},... | collective-permute-start | bytes 294920 | tf_op jit(solution)/shard_map/ppermute | solution.py:26
  82.8 19.6 %all_to_all.35 = bf16[16,48,128]{2,1,0:T(8,128)(2,1)S(1)} all-to-all(bf16[16,48,128]{2,1,0:T(8,128)(2,1)S(1)} %bitcast.20), channel_id=1, replica_groups=mesh['yh'=2,'z'=16,'core'=2,'x'=4,'yl'=2] {'z'}, dimensions={0} | all-to-all | bytes 393216 | tf_op jit(solution)/shard_map/all_to_all | solution.py:334
  102.4 19.9 %all_to_all.36 = bf16[16,48,128]{2,1,0:T(8,128)(2,1)S(1)} all-to-all(bf16[16,48,128]{2,1,0:T(8,128)(2,1)S(1)} %bitcast.24), channel_id=1, replica_groups=mesh['yh'=2,'z'=16,'core'=2,'x'=4,'yl'=2] {'z'}, dimensions={0} | all-to-all | bytes 393216 | tf_op jit(solution)/shard_map/all_to_all | solution.py:342
  122.4 1.9 %collective-permute-start.10 = (bf16[768,128]{1,0:T(8,128)(2,1)S(1)}, bf16[768,128]{1,0:T(8,128)(2,1)S(1)}, u32[]{:S(2)}, u32[]{:S(2)}) collective-permute-start(bf16[768,128]{1,0:T(8,128)(2,1)S(1)} %bitcast.15), channel_id=1, source_target_pairs={{0,256},{256,0},{1,257},{257,1},{2,258},{258,2},{3,259},{259,3},{4... | collective-permute-start | bytes 589832 | tf_op jit(solution)/shard_map/ppermute | solution.py:26
  124.3 6.0 %collective-permute-done.10.rest_1_.blocks_y = bf16[768,128]{1,0:T(8,128)(2,1)S(1)} collective-permute-done((bf16[768,128]{1,0:T(8,128)(2,1)S(1)}, bf16[768,128]{1,0:T(8,128)(2,1)S(1)}, u32[]{:S(2)}, u32[]{:S(2)}) %collective-permute-start.10) | collective-permute-done | bytes 196640 | tf_op jit(solution)/shard_map/ppermute | solution.py:26
  131.3 7.9 %all_to_all.37 = bf16[8,48,256]{2,1,0:T(8,128)(2,1)S(1)} all-to-all(bf16[8,48,256]{2,1,0:T(8,128)(2,1)S(1)} %bitcast.21), channel_id=1, replica_groups=mesh['yh'=2,'z'=16,'core'=2,'x'=4,'yl'=2] {'x','yl'}, dimensions={0} | all-to-all | bytes 393216 | tf_op jit(solution)/shard_map/all_to_all | solution.py:353
  140.1 11.8 %all-to-all-start.6 = ((bf16[16,48,256]{2,1,0:T(8,128)(2,1)}), bf16[16,48,256]{2,1,0:T(8,128)(2,1)S(1)}, u32[]{:S(2)}, u32[]{:S(2)}) async-start(bf16[16,48,256]{2,1,0:T(8,128)(2,1)} %bitcast.27), calls=%async_computation.6 | async-start | bytes 786432 | tf_op jit(solution)/shard_map/all_to_all | solution.py:362
  152.0 2.1 %collective-permute-start.11 = (bf16[768,128]{1,0:T(8,128)(2,1)S(1)}, bf16[768,128]{1,0:T(8,128)(2,1)S(1)}, u32[]{:S(2)}, u32[]{:S(2)}) collective-permute-start(bf16[768,128]{1,0:T(8,128)(2,1)S(1)} %bitcast.17), channel_id=1, source_target_pairs={{0,8},{8,0},{1,9},{9,1},{2,10},{10,2},{3,11},{11,3},{4,12},{12,4},... | collective-permute-start | bytes 589832 | tf_op jit(solution)/shard_map/ppermute | solution.py:26
  154.0 2.2 %collective-permute-start.12 = (bf16[768,128]{1,0:T(8,128)(2,1)S(1)}, bf16[768,128]{1,0:T(8,128)(2,1)S(1)}, u32[]{:S(2)}, u32[]{:S(2)}) collective-permute-start(bf16[768,128]{1,0:T(8,128)(2,1)S(1)} %collective-permute-done.10.rest_1_.blocks_y), channel_id=1, source_target_pairs={{0,8},{8,0},{1,9},{9,1},{2,10},{10,2},{3,11},{11,3},{4,12},{12,4},... | collective-permute-start | bytes 589832 | tf_op jit(solution)/shard_map/ppermute | solution.py:26
  156.3 1.1 collective-permute-done.12.rest_3_
  157.4 1.8 %shard_map.119 = (bf16[256,1024]{1,0:T(8,128)(2,1)}, bf16[6,1024]{1,0:T(8,128)(2,1)}, f32[8,128]{1,0:T(8,128)S(1)}) custom-call(s32[384]{0:T(512)S(1)} %copy-done.10, bf16[192,256]{1,0:T(8,128)(2,1)S(1)} %get-tuple-element.21.hidden, bf16[192,256]{1,0:T(8,128)(2,1)S(1)} %collective-permute-done.8.after.hidden_core, bf16[768,128]{1,0:T(8,128)(2,1)S(1)} %bitcast.18, ...), custom_call_target="tpu_custom_call" | custom-call | flops 201326592 | bytes 1525248 | tf_op jit(solution)/shard_map/pallas_call | solution.py:246
  159.2 1.3 all-to-all-done.6
  160.5 2.5 %shard_map.122 = (bf16[1024,256]{1,0:T(8,128)(2,1)}, bf16[1024,256]{1,0:T(8,128)(2,1)}) custom-call(bf16[768,256]{1,0:T(8,128)(2,1)S(1)} %bitcast.26, bf16[192,1024]{1,0:T(8,128)(2,1)} %get-tuple-element.19.inputs, bf16[192,1024]{1,0:T(8,128)(2,1)S(1)} %collective-permute-done.5.after.inputs_x, f32[8,128]{1,0:T(8,128)S(1)} %get-tuple-element.28.after), custom_call_target="tpu_custom_call" | custom-call | flops 402653184 | bytes 2228224 | tf_op jit(solution)/shard_map/pallas_call | solution.py:246
  (39 shorter events, 7.1 us)
Async XLA Ops:
  0.6 17.5 %copy-start.1 = (bf16[1024,256]{1,0:T(8,128)(2,1)S(1)}, bf16[1024,256]{1,0:T(8,128)(2,1)}, u32[]{:S(2)}) copy-start(bf16[1024,256]{1,0:T(8,128)(2,1)} %rest_0_.1) | copy-start | bytes 1572868
  0.6 0.8 copy-start.9
  2.4 28.3 %all-to-all-start = ((bf16[16,48,128]{2,1,0:T(8,128)(2,1)}), bf16[16,48,128]{2,1,0:T(8,128)(2,1)S(1)}, u32[]{:S(2)}, u32[]{:S(2)}) async-start(bf16[16,48,128]{2,1,0:T(8,128)(2,1)} %bitcast.29), calls=%async_computation | async-start | bytes 393216 | tf_op jit(solution)/shard_map/all_to_all | solution.py:274
  18.2 20.6 %collective-permute-start.1 = (bf16[1024,256]{1,0:T(8,128)(2,1)S(1)}, bf16[1024,256]{1,0:T(8,128)(2,1)S(1)}, u32[]{:S(2)}, u32[]{:S(2)}) collective-permute-start(bf16[1024,256]{1,0:T(8,128)(2,1)S(1)} %copy-done.1), channel_id=1, source_target_pairs={{0,8},{8,0},{1,9},{9,1},{2,10},{10,2},{3,11},{11,3},{4,12},{12,4},... | collective-permute-start | bytes 1572872 | tf_op jit(solution)/shard_map/ppermute | solution.py:26
  21.1 17.8 %collective-permute-start.2 = (bf16[1024,256]{1,0:T(8,128)(2,1)}, bf16[1024,256]{1,0:T(8,128)(2,1)S(1)}, u32[]{:S(2)}, u32[]{:S(2)}) collective-permute-start(bf16[1024,256]{1,0:T(8,128)(2,1)} %rest_1_.1), channel_id=1, source_target_pairs={{0,8},{8,0},{1,9},{9,1},{2,10},{10,2},{3,11},{11,3},{4,12},{12,4},... | collective-permute-start | bytes 1572872 | tf_op jit(solution)/shard_map/ppermute | solution.py:26
  23.0 15.9 %collective-permute-start.3 = (bf16[1024,256]{1,0:T(8,128)(2,1)}, bf16[1024,256]{1,0:T(8,128)(2,1)S(1)}, u32[]{:S(2)}, u32[]{:S(2)}) collective-permute-start(bf16[1024,256]{1,0:T(8,128)(2,1)} %rest_2_.1), channel_id=1, source_target_pairs={{0,8},{8,0},{1,9},{9,1},{2,10},{10,2},{3,11},{11,3},{4,12},{12,4},... | collective-permute-start | bytes 1572872 | tf_op jit(solution)/shard_map/ppermute | solution.py:26
  25.4 13.4 %collective-permute-start.4 = (bf16[1024,256]{1,0:T(8,128)(2,1)}, bf16[1024,256]{1,0:T(8,128)(2,1)S(1)}, u32[]{:S(2)}, u32[]{:S(2)}) collective-permute-start(bf16[1024,256]{1,0:T(8,128)(2,1)} %rest_3_.1), channel_id=1, source_target_pairs={{0,8},{8,0},{1,9},{9,1},{2,10},{10,2},{3,11},{11,3},{4,12},{12,4},... | collective-permute-start | bytes 1572872 | tf_op jit(solution)/shard_map/ppermute | solution.py:26
  30.8 8.0 %collective-permute-start = (bf16[96,1024]{1,0:T(8,128)(2,1)S(1)}, bf16[96,1024]{1,0:T(8,128)(2,1)S(1)}, u32[]{:S(2)}, u32[]{:S(2)}) collective-permute-start(bf16[96,1024]{1,0:T(8,128)(2,1)S(1)} %shard_map.112.rows), channel_id=1, source_target_pairs={{0,256},{256,0},{1,257},{257,1},{2,258},{258,2},{3,259},{259,3},{4... | collective-permute-start | bytes 589832 | tf_op jit(solution)/shard_map/ppermute | solution.py:26
  35.7 1.0 copy-start.2
  36.7 1.0 copy-start.4
  37.8 1.0 copy-start.6
  38.8 1.0 copy-start.3
  38.8 1.2 copy-start.5
  38.8 1.4 copy-start.7
  42.0 12.0 %copy-start = (bf16[256,1024]{1,0:T(8,128)(2,1)S(1)}, bf16[256,1024]{1,0:T(8,128)(2,1)}, u32[]{:S(2)}) copy-start(bf16[256,1024]{1,0:T(8,128)(2,1)} %down.3) | copy-start | bytes 1572868
  42.0 13.9 %copy-start.8 = (bf16[256,1024]{1,0:T(8,128)(2,1)S(1)}, bf16[256,1024]{1,0:T(8,128)(2,1)}, u32[]{:S(2)}) copy-start(bf16[256,1024]{1,0:T(8,128)(2,1)} %probe.1) | copy-start | bytes 1572868
  42.0 16.3 %all-to-all-start.1 = ((bf16[8,48,1024]{2,1,0:T(8,128)(2,1)}), bf16[8,48,1024]{2,1,0:T(8,128)(2,1)S(1)}, u32[]{:S(2)}, u32[]{:S(2)}) async-start(bf16[8,48,1024]{2,1,0:T(8,128)(2,1)} %bitcast.28), calls=%async_computation.1 | async-start | bytes 1572864 | tf_op jit(solution)/shard_map/all_to_all | solution.py:300
  46.3 12.1 %collective-permute-start.5 = (bf16[192,1024]{1,0:T(8,128)(2,1)}, bf16[192,1024]{1,0:T(8,128)(2,1)S(1)}, u32[]{:S(2)}, u32[]{:S(2)}) collective-permute-start(bf16[192,1024]{1,0:T(8,128)(2,1)} %get-tuple-element.19.inputs), channel_id=1, source_target_pairs={{0,8},{8,0},{1,9},{9,1},{2,10},{10,2},{3,11},{11,3},{4,12},{12,4},... | collective-permute-start | bytes 1179656 | tf_op jit(solution)/shard_map/ppermute | solution.py:26
  54.0 10.8 %collective-permute-start.6 = (bf16[256,1024]{1,0:T(8,128)(2,1)S(1)}, bf16[256,1024]{1,0:T(8,128)(2,1)S(1)}, u32[]{:S(2)}, u32[]{:S(2)}) collective-permute-start(bf16[256,1024]{1,0:T(8,128)(2,1)S(1)} %copy-done), channel_id=1, source_target_pairs={{0,8},{8,0},{1,9},{9,1},{2,10},{10,2},{3,11},{11,3},{4,12},{12,4},... | collective-permute-start | bytes 1572872 | tf_op jit(solution)/shard_map/ppermute | solution.py:26
  56.0 8.8 %collective-permute-start.7 = (bf16[256,1024]{1,0:T(8,128)(2,1)S(1)}, bf16[256,1024]{1,0:T(8,128)(2,1)S(1)}, u32[]{:S(2)}, u32[]{:S(2)}) collective-permute-start(bf16[256,1024]{1,0:T(8,128)(2,1)S(1)} %copy-done.8), channel_id=1, source_target_pairs={{0,8},{8,0},{1,9},{9,1},{2,10},{10,2},{3,11},{11,3},{4,12},{12,4},... | collective-permute-start | bytes 1572872 | tf_op jit(solution)/shard_map/ppermute | solution.py:26
  59.3 12.0 %all-to-all-start.2 = ((bf16[8,48,512]{2,1,0:T(8,128)(2,1)}), bf16[8,48,512]{2,1,0:T(8,128)(2,1)S(1)}, u32[]{:S(2)}, u32[]{:S(2)}) async-start(bf16[8,48,512]{2,1,0:T(8,128)(2,1)} %bitcast.30), calls=%async_computation.2 | async-start | bytes 786432 | tf_op jit(solution)/shard_map/all_to_all | solution.py:310
  72.4 10.4 %collective-permute-start.9 = (bf16[96,1024]{1,0:T(8,128)(2,1)S(1)}, bf16[96,1024]{1,0:T(8,128)(2,1)S(1)}, u32[]{:S(2)}, u32[]{:S(2)}) collective-permute-start(bf16[96,1024]{1,0:T(8,128)(2,1)S(1)} %get-tuple-element.24), channel_id=1, source_target_pairs={{0,256},{256,0},{1,257},{257,1},{2,258},{258,2},{3,259},{259,3},{4... | collective-permute-start | bytes 589832 | tf_op jit(solution)/shard_map/ppermute | solution.py:26
  76.9 5.8 %collective-permute-start.8 = (bf16[192,256]{1,0:T(8,128)(2,1)S(1)}, bf16[192,256]{1,0:T(8,128)(2,1)S(1)}, u32[]{:S(2)}, u32[]{:S(2)}) collective-permute-start(bf16[192,256]{1,0:T(8,128)(2,1)S(1)} %get-tuple-element.22), channel_id=1, source_target_pairs={{0,8},{8,0},{1,9},{9,1},{2,10},{10,2},{3,11},{11,3},{4,12},{12,4},... | collective-permute-start | bytes 294920 | tf_op jit(solution)/shard_map/ppermute | solution.py:26
  122.4 7.9 %collective-permute-start.10 = (bf16[768,128]{1,0:T(8,128)(2,1)S(1)}, bf16[768,128]{1,0:T(8,128)(2,1)S(1)}, u32[]{:S(2)}, u32[]{:S(2)}) collective-permute-start(bf16[768,128]{1,0:T(8,128)(2,1)S(1)} %bitcast.15), channel_id=1, source_target_pairs={{0,256},{256,0},{1,257},{257,1},{2,258},{258,2},{3,259},{259,3},{4... | collective-permute-start | bytes 589832 | tf_op jit(solution)/shard_map/ppermute | solution.py:26
  140.1 17.3 %copy-start.10 = (s32[384]{0:T(512)S(1)}, s32[384]{0:T(512)}, u32[]{:S(2)}) copy-start(s32[384]{0:T(512)} %ids.1) | copy-start | bytes 4612
  140.1 20.4 %all-to-all-start.6 = ((bf16[16,48,256]{2,1,0:T(8,128)(2,1)}), bf16[16,48,256]{2,1,0:T(8,128)(2,1)S(1)}, u32[]{:S(2)}, u32[]{:S(2)}) async-start(bf16[16,48,256]{2,1,0:T(8,128)(2,1)} %bitcast.27), calls=%async_computation.6 | async-start | bytes 786432 | tf_op jit(solution)/shard_map/all_to_all | solution.py:362
  152.0 4.3 %collective-permute-start.11 = (bf16[768,128]{1,0:T(8,128)(2,1)S(1)}, bf16[768,128]{1,0:T(8,128)(2,1)S(1)}, u32[]{:S(2)}, u32[]{:S(2)}) collective-permute-start(bf16[768,128]{1,0:T(8,128)(2,1)S(1)} %bitcast.17), channel_id=1, source_target_pairs={{0,8},{8,0},{1,9},{9,1},{2,10},{10,2},{3,11},{11,3},{4,12},{12,4},... | collective-permute-start | bytes 589832 | tf_op jit(solution)/shard_map/ppermute | solution.py:26
  154.0 3.3 %collective-permute-start.12 = (bf16[768,128]{1,0:T(8,128)(2,1)S(1)}, bf16[768,128]{1,0:T(8,128)(2,1)S(1)}, u32[]{:S(2)}, u32[]{:S(2)}) collective-permute-start(bf16[768,128]{1,0:T(8,128)(2,1)S(1)} %collective-permute-done.10.rest_1_.blocks_y), channel_id=1, source_target_pairs={{0,8},{8,0},{1,9},{9,1},{2,10},{10,2},{3,11},{11,3},{4,12},{12,4},... | collective-permute-start | bytes 589832 | tf_op jit(solution)/shard_map/ppermute | solution.py:26

commit v13 on v12

--- a/solution.py
+++ b/solution.py
@@ -164,7 +164,7 @@
     return jnp.concatenate(lines, axis=0)
 
 
-def cot_kernel(blocks, blocks_y, down, down_x, out, slot, sem):
+def cot_kernel(blocks, blocks_y, down, down_x, after, out, slot, sem):
     copy = start(down, slot, sem)
     left = moved(192, 192, pick, jnp.concatenate([whole(blocks), whole(blocks_y)], axis=0))
     for h in (1, 0):
@@ -341,12 +341,15 @@
     )
     blocks = lax.all_to_all(spread.reshape(NZ, 48, 128), Z, 0, 0).reshape(768, 128)
 
-    blocks_y = swap(blocks, YH)
+    blocks_y, blocks_x = swap(blocks, YH), swap(blocks, CORE)
     (cot,) = call(
         cot_kernel,
         14,
         4 * dots,
-        [(blocks, VMEM), (blocks_y, VMEM), (down_weight, HBM), (down_x, VMEM)],
+        [
+            (blocks, VMEM), (blocks_y, VMEM), (down_weight, HBM), (down_x, VMEM),
+            (blocks_x, ANY),
+        ],
         [((16, 24, units), bf16, VMEM)],
         [pltpu.VMEM((units, width), bf16), DMA],
     )
@@ -360,7 +363,7 @@
         [pltpu.VMEM((96, units), bf16), DMA((16,))],
     )
     parts = lax.all_to_all(spread.reshape(16, 48, units), (CORE,) + DP, 0, 0).reshape(768, units)
-    blocks_x, blocks_yx = swap(blocks, CORE), swap(blocks_y, CORE)
+    blocks_yx = swap(blocks_y, CORE)
     ggn_down, tangent_out, flag = call(
         functools.partial(ggn_down_kernel, scale),
         14,

time: 164 us -> 164 us (level)
  waiting for transfers between devices: 19.3 us -> 16.6 us
    ppermute x13, starting transfers between devices: 41.6 us -> 46.9 us  [swap(): return lax.ppermute(value, axis, [(0, 1), (1, 0)])]
    ppermute x13, waiting for transfers between devices: 8.02 us -> 3.22 us  [swap(): return lax.ppermute(value, axis, [(0, 1), (1, 0)])]
    all_to_all x1, starting transfers between devices: 11.8 us -> 8.12 us  [local(): lax.all_to_all(spread.reshape(16, 48, units), (CORE,) + DP, 0, 0)]
    all_to_all x1, waiting for transfers between devices: 1.3 us -> 3.4 us  [local(): lax.all_to_all(spread.reshape(16, 48, units), (CORE,) + DP, 0, 0)]
where the time goes in v13:
time: 164 us; the launch traced here: 163 us
  starting transfers between devices  80.4 us (49%)
  blocking collectives  48.1 us (29%)
  waiting for transfers between devices  16.6 us (10%)
  Pallas kernels  11.3 us (7%)
  local copies, waits for them, and re-layouts  5.21 us (3%)
    ppermute x13, starting transfers between devices, swap(): return lax.ppermute(value, axis, [(0, 1), (1, 0)])  46.9 us
    all_to_all x1, blocking collectives, local(): lax.all_to_all(spread.reshape(NZ, 48, 128), Z, 0, 0).reshape(768, 128)  19.9 us
    all_to_all x1, blocking collectives, local(): lax.all_to_all(blocks.reshape(NZ, 48, 128), Z, 0, 0).reshape(768, 128)  19.6 us
    all_to_all x1, starting transfers between devices, local(): rows = lax.all_to_all(rows.reshape(NZ, 48, 128), Z, 0, 0).reshape(768, 128)  15.8 us
    pallas_call x12, Pallas kernels, call(): pl.pallas_call(kernel, out_shape=[pltpu.HBM(s, t) if space is HBM else ja...  11.3 us
    all_to_all x1, blocking collectives, local(): lax.all_to_all(cot.reshape(NDP, 48, units), DP, 0, 0).reshape(384, units)  8.54 us
    all_to_all x1, starting transfers between devices, local(): lax.all_to_all(spread.reshape(16, 48, units), (CORE,) + DP, 0, 0)  8.12 us
    all_to_all x1, waiting for transfers between devices, local(): lax.all_to_all(spread.reshape(NDP, 48, 2 * units), DP, 0, 0)  6.54 us
  transfers between devices with their start and end apart: 17, of which 6 were waited for; matrix products, arithmetic and copies ran while one was open for 0% of the time, Pallas kernels for 2%

profile of v13, /device:TPU:1, one launch (start us, length us, event | category | flops | bytes accessed | tf_op | source)
XLA Modules:
  0.0 162.5 jit_solution(12097510977799231974)
XLA Ops:
  2.4 15.8 %all-to-all-start = ((bf16[16,48,128]{2,1,0:T(8,128)(2,1)}), bf16[16,48,128]{2,1,0:T(8,128)(2,1)S(1)}, u32[]{:S(2)}, u32[]{:S(2)}) async-start(bf16[16,48,128]{2,1,0:T(8,128)(2,1)} %bitcast.29), calls=%async_computation | async-start | bytes 393216 | tf_op jit(solution)/shard_map/all_to_all | solution.py:274
  18.2 2.9 %collective-permute-start.1 = (bf16[1024,256]{1,0:T(8,128)(2,1)S(1)}, bf16[1024,256]{1,0:T(8,128)(2,1)S(1)}, u32[]{:S(2)}, u32[]{:S(2)}) collective-permute-start(bf16[1024,256]{1,0:T(8,128)(2,1)S(1)} %copy-done.1), channel_id=1, source_target_pairs={{0,8},{8,0},{1,9},{9,1},{2,10},{10,2},{3,11},{11,3},{4,12},{12,4},... | collective-permute-start | bytes 1572872 | tf_op jit(solution)/shard_map/ppermute | solution.py:26
  21.1 1.9 %collective-permute-start.2 = (bf16[1024,256]{1,0:T(8,128)(2,1)}, bf16[1024,256]{1,0:T(8,128)(2,1)S(1)}, u32[]{:S(2)}, u32[]{:S(2)}) collective-permute-start(bf16[1024,256]{1,0:T(8,128)(2,1)} %rest_1_.1), channel_id=1, source_target_pairs={{0,8},{8,0},{1,9},{9,1},{2,10},{10,2},{3,11},{11,3},{4,12},{12,4},... | collective-permute-start | bytes 1572872 | tf_op jit(solution)/shard_map/ppermute | solution.py:26
  23.0 2.4 %collective-permute-start.3 = (bf16[1024,256]{1,0:T(8,128)(2,1)}, bf16[1024,256]{1,0:T(8,128)(2,1)S(1)}, u32[]{:S(2)}, u32[]{:S(2)}) collective-permute-start(bf16[1024,256]{1,0:T(8,128)(2,1)} %rest_2_.1), channel_id=1, source_target_pairs={{0,8},{8,0},{1,9},{9,1},{2,10},{10,2},{3,11},{11,3},{4,12},{12,4},... | collective-permute-start | bytes 1572872 | tf_op jit(solution)/shard_map/ppermute | solution.py:26
  25.4 1.9 %collective-permute-start.4 = (bf16[1024,256]{1,0:T(8,128)(2,1)}, bf16[1024,256]{1,0:T(8,128)(2,1)S(1)}, u32[]{:S(2)}, u32[]{:S(2)}) collective-permute-start(bf16[1024,256]{1,0:T(8,128)(2,1)} %rest_3_.1), channel_id=1, source_target_pairs={{0,8},{8,0},{1,9},{9,1},{2,10},{10,2},{3,11},{11,3},{4,12},{12,4},... | collective-permute-start | bytes 1572872 | tf_op jit(solution)/shard_map/ppermute | solution.py:26
  27.3 3.4 %all-to-all-done = bf16[16,48,128]{2,1,0:T(8,128)(2,1)S(1)} async-done(((bf16[16,48,128]{2,1,0:T(8,128)(2,1)}), bf16[16,48,128]{2,1,0:T(8,128)(2,1)S(1)}, u32[]{:S(2)}, u32[]{:S(2)}) %all-to-all-start) | async-done | bytes 196640 | tf_op jit(solution)/shard_map/all_to_all | solution.py:274
  30.8 4.8 %collective-permute-start = (bf16[96,1024]{1,0:T(8,128)(2,1)S(1)}, bf16[96,1024]{1,0:T(8,128)(2,1)S(1)}, u32[]{:S(2)}, u32[]{:S(2)}) collective-permute-start(bf16[96,1024]{1,0:T(8,128)(2,1)S(1)} %shard_map.112.rows), channel_id=1, source_target_pairs={{0,256},{256,0},{1,257},{257,1},{2,258},{258,2},{3,259},{259,3},{4... | collective-permute-start | bytes 589832 | tf_op jit(solution)/shard_map/ppermute | solution.py:26
  35.7 1.0 copy-done.2
  36.7 1.0 copy-done.4
  37.8 1.0 copy-done.6
  40.2 1.9 %shard_map.114 = (bf16[192,1024]{1,0:T(8,128)(2,1)}, bf16[16,24,1024]{2,1,0:T(8,128)(2,1)}) custom-call(bf16[96,1024]{1,0:T(8,128)(2,1)S(1)} %shard_map.112.rows, bf16[96,1024]{1,0:T(8,128)(2,1)S(1)} %collective-permute-done.rows_y, f32[8,128]{1,0:T(8,128)S(1)} %shard_map.113.after, bf16[1024,256]{1,0:T(8,128)(2,1)S(1)} %copy-done.1, ...), custom_call_target="tpu_custom_call" | custom-call | flops 805306368 | bytes 5767168 | tf_op jit(solution)/shard_map/pallas_call | solution.py:246
  42.0 4.3 %all-to-all-start.1 = ((bf16[8,48,1024]{2,1,0:T(8,128)(2,1)}), bf16[8,48,1024]{2,1,0:T(8,128)(2,1)S(1)}, u32[]{:S(2)}, u32[]{:S(2)}) async-start(bf16[8,48,1024]{2,1,0:T(8,128)(2,1)} %bitcast.28), calls=%async_computation.1 | async-start | bytes 1572864 | tf_op jit(solution)/shard_map/all_to_all | solution.py:300
  46.3 7.7 %collective-permute-start.5 = (bf16[192,1024]{1,0:T(8,128)(2,1)}, bf16[192,1024]{1,0:T(8,128)(2,1)S(1)}, u32[]{:S(2)}, u32[]{:S(2)}) collective-permute-start(bf16[192,1024]{1,0:T(8,128)(2,1)} %get-tuple-element.19.inputs), channel_id=1, source_target_pairs={{0,8},{8,0},{1,9},{9,1},{2,10},{10,2},{3,11},{11,3},{4,12},{12,4},... | collective-permute-start | bytes 1179656 | tf_op jit(solution)/shard_map/ppermute | solution.py:26
  54.0 1.9 %collective-permute-start.6 = (bf16[256,1024]{1,0:T(8,128)(2,1)S(1)}, bf16[256,1024]{1,0:T(8,128)(2,1)S(1)}, u32[]{:S(2)}, u32[]{:S(2)}) collective-permute-start(bf16[256,1024]{1,0:T(8,128)(2,1)S(1)} %copy-done), channel_id=1, source_target_pairs={{0,8},{8,0},{1,9},{9,1},{2,10},{10,2},{3,11},{11,3},{4,12},{12,4},... | collective-permute-start | bytes 1572872 | tf_op jit(solution)/shard_map/ppermute | solution.py:26
  56.0 2.4 %collective-permute-start.7 = (bf16[256,1024]{1,0:T(8,128)(2,1)S(1)}, bf16[256,1024]{1,0:T(8,128)(2,1)S(1)}, u32[]{:S(2)}, u32[]{:S(2)}) collective-permute-start(bf16[256,1024]{1,0:T(8,128)(2,1)S(1)} %copy-done.8), channel_id=1, source_target_pairs={{0,8},{8,0},{1,9},{9,1},{2,10},{10,2},{3,11},{11,3},{4,12},{12,4},... | collective-permute-start | bytes 1572872 | tf_op jit(solution)/shard_map/ppermute | solution.py:26
  59.3 5.4 %all-to-all-start.2 = ((bf16[8,48,512]{2,1,0:T(8,128)(2,1)}), bf16[8,48,512]{2,1,0:T(8,128)(2,1)S(1)}, u32[]{:S(2)}, u32[]{:S(2)}) async-start(bf16[8,48,512]{2,1,0:T(8,128)(2,1)} %bitcast.30), calls=%async_computation.2 | async-start | bytes 786432 | tf_op jit(solution)/shard_map/all_to_all | solution.py:310
  64.8 6.5 %all-to-all-done.2 = bf16[8,48,512]{2,1,0:T(8,128)(2,1)S(1)} async-done(((bf16[8,48,512]{2,1,0:T(8,128)(2,1)}), bf16[8,48,512]{2,1,0:T(8,128)(2,1)S(1)}, u32[]{:S(2)}, u32[]{:S(2)}) %all-to-all-start.2) | async-done | bytes 393248 | tf_op jit(solution)/shard_map/all_to_all | solution.py:310
  71.3 1.0 shard_map.116
  72.4 4.5 %collective-permute-start.9 = (bf16[96,1024]{1,0:T(8,128)(2,1)S(1)}, bf16[96,1024]{1,0:T(8,128)(2,1)S(1)}, u32[]{:S(2)}, u32[]{:S(2)}) collective-permute-start(bf16[96,1024]{1,0:T(8,128)(2,1)S(1)} %get-tuple-element.24), channel_id=1, source_target_pairs={{0,256},{256,0},{1,257},{257,1},{2,258},{258,2},{3,259},{259,3},{4... | collective-permute-start | bytes 589832 | tf_op jit(solution)/shard_map/ppermute | solution.py:26
  76.9 4.9 %collective-permute-start.8 = (bf16[192,256]{1,0:T(8,128)(2,1)S(1)}, bf16[192,256]{1,0:T(8,128)(2,1)S(1)}, u32[]{:S(2)}, u32[]{:S(2)}) collective-permute-start(bf16[192,256]{1,0:T(8,128)(2,1)S(1)} %get-tuple-element.22), channel_id=1, source_target_pairs={{0,8},{8,0},{1,9},{9,1},{2,10},{10,2},{3,11},{11,3},{4,12},{12,4},... | collective-permute-start | bytes 294920 | tf_op jit(solution)/shard_map/ppermute | solution.py:26
  82.8 19.6 %all_to_all.35 = bf16[16,48,128]{2,1,0:T(8,128)(2,1)S(1)} all-to-all(bf16[16,48,128]{2,1,0:T(8,128)(2,1)S(1)} %bitcast.20), channel_id=1, replica_groups=mesh['yh'=2,'z'=16,'core'=2,'x'=4,'yl'=2] {'z'}, dimensions={0} | all-to-all | bytes 393216 | tf_op jit(solution)/shard_map/all_to_all | solution.py:334
  102.4 19.9 %all_to_all.36 = bf16[16,48,128]{2,1,0:T(8,128)(2,1)S(1)} all-to-all(bf16[16,48,128]{2,1,0:T(8,128)(2,1)S(1)} %bitcast.24), channel_id=1, replica_groups=mesh['yh'=2,'z'=16,'core'=2,'x'=4,'yl'=2] {'z'}, dimensions={0} | all-to-all | bytes 393216 | tf_op jit(solution)/shard_map/all_to_all | solution.py:342
  122.4 1.9 %collective-permute-start.10 = (bf16[768,128]{1,0:T(8,128)(2,1)S(1)}, bf16[768,128]{1,0:T(8,128)(2,1)S(1)}, u32[]{:S(2)}, u32[]{:S(2)}) collective-permute-start(bf16[768,128]{1,0:T(8,128)(2,1)S(1)} %bitcast.15), channel_id=1, source_target_pairs={{0,256},{256,0},{1,257},{257,1},{2,258},{258,2},{3,259},{259,3},{4... | collective-permute-start | bytes 589832 | tf_op jit(solution)/shard_map/ppermute | solution.py:26
  124.3 7.5 %collective-permute-start.11 = (bf16[768,128]{1,0:T(8,128)(2,1)S(1)}, bf16[768,128]{1,0:T(8,128)(2,1)S(1)}, u32[]{:S(2)}, u32[]{:S(2)}) collective-permute-start(bf16[768,128]{1,0:T(8,128)(2,1)S(1)} %bitcast.16), channel_id=1, source_target_pairs={{0,8},{8,0},{1,9},{9,1},{2,10},{10,2},{3,11},{11,3},{4,12},{12,4},... | collective-permute-start | bytes 589832 | tf_op jit(solution)/shard_map/ppermute | solution.py:26
  131.8 1.0 collective-permute-done.11.rest_2_.after
  133.9 8.5 %all_to_all.37 = bf16[8,48,256]{2,1,0:T(8,128)(2,1)S(1)} all-to-all(bf16[8,48,256]{2,1,0:T(8,128)(2,1)S(1)} %bitcast.21), channel_id=1, replica_groups=mesh['yh'=2,'z'=16,'core'=2,'x'=4,'yl'=2] {'x','yl'}, dimensions={0} | all-to-all | bytes 393216 | tf_op jit(solution)/shard_map/all_to_all | solution.py:356
  143.3 8.1 %all-to-all-start.6 = ((bf16[16,48,256]{2,1,0:T(8,128)(2,1)}), bf16[16,48,256]{2,1,0:T(8,128)(2,1)S(1)}, u32[]{:S(2)}, u32[]{:S(2)}) async-start(bf16[16,48,256]{2,1,0:T(8,128)(2,1)} %bitcast.27), calls=%async_computation.6 | async-start | bytes 786432 | tf_op jit(solution)/shard_map/all_to_all | solution.py:365
  151.4 2.1 %collective-permute-start.12 = (bf16[768,128]{1,0:T(8,128)(2,1)S(1)}, bf16[768,128]{1,0:T(8,128)(2,1)S(1)}, u32[]{:S(2)}, u32[]{:S(2)}) collective-permute-start(bf16[768,128]{1,0:T(8,128)(2,1)S(1)} %collective-permute-done.10.rest_1_.blocks_y), channel_id=1, source_target_pairs={{0,8},{8,0},{1,9},{9,1},{2,10},{10,2},{3,11},{11,3},{4,12},{12,4},... | collective-permute-start | bytes 589832 | tf_op jit(solution)/shard_map/ppermute | solution.py:26
  153.5 1.2 collective-permute-done.12.rest_3_
  154.8 1.8 %shard_map.119 = (bf16[256,1024]{1,0:T(8,128)(2,1)}, bf16[6,1024]{1,0:T(8,128)(2,1)}, f32[8,128]{1,0:T(8,128)S(1)}) custom-call(s32[384]{0:T(512)S(1)} %copy-done.10, bf16[192,256]{1,0:T(8,128)(2,1)S(1)} %get-tuple-element.21.hidden, bf16[192,256]{1,0:T(8,128)(2,1)S(1)} %collective-permute-done.8.after.hidden_core, bf16[768,128]{1,0:T(8,128)(2,1)S(1)} %bitcast.18, ...), custom_call_target="tpu_custom_call" | custom-call | flops 201326592 | bytes 1525248 | tf_op jit(solution)/shard_map/pallas_call | solution.py:246
  156.6 3.4 %all-to-all-done.6 = bf16[16,48,256]{2,1,0:T(8,128)(2,1)S(1)} async-done(((bf16[16,48,256]{2,1,0:T(8,128)(2,1)}), bf16[16,48,256]{2,1,0:T(8,128)(2,1)S(1)}, u32[]{:S(2)}, u32[]{:S(2)}) %all-to-all-start.6) | async-done | bytes 393248 | tf_op jit(solution)/shard_map/all_to_all | solution.py:365
  160.0 2.5 %shard_map.122 = (bf16[1024,256]{1,0:T(8,128)(2,1)}, bf16[1024,256]{1,0:T(8,128)(2,1)}) custom-call(bf16[768,256]{1,0:T(8,128)(2,1)S(1)} %bitcast.26, bf16[192,1024]{1,0:T(8,128)(2,1)} %get-tuple-element.19.inputs, bf16[192,1024]{1,0:T(8,128)(2,1)S(1)} %collective-permute-done.5.after.inputs_x, f32[8,128]{1,0:T(8,128)S(1)} %get-tuple-element.28.after), custom_call_target="tpu_custom_call" | custom-call | flops 402653184 | bytes 2228224 | tf_op jit(solution)/shard_map/pallas_call | solution.py:246
  (39 shorter events, 7.1 us)
Async XLA Ops:
  0.6 17.5 %copy-start.1 = (bf16[1024,256]{1,0:T(8,128)(2,1)S(1)}, bf16[1024,256]{1,0:T(8,128)(2,1)}, u32[]{:S(2)}) copy-start(bf16[1024,256]{1,0:T(8,128)(2,1)} %rest_0_.1) | copy-start | bytes 1572868
  0.6 0.8 copy-start.9
  2.4 28.3 %all-to-all-start = ((bf16[16,48,128]{2,1,0:T(8,128)(2,1)}), bf16[16,48,128]{2,1,0:T(8,128)(2,1)S(1)}, u32[]{:S(2)}, u32[]{:S(2)}) async-start(bf16[16,48,128]{2,1,0:T(8,128)(2,1)} %bitcast.29), calls=%async_computation | async-start | bytes 393216 | tf_op jit(solution)/shard_map/all_to_all | solution.py:274
  18.2 20.6 %collective-permute-start.1 = (bf16[1024,256]{1,0:T(8,128)(2,1)S(1)}, bf16[1024,256]{1,0:T(8,128)(2,1)S(1)}, u32[]{:S(2)}, u32[]{:S(2)}) collective-permute-start(bf16[1024,256]{1,0:T(8,128)(2,1)S(1)} %copy-done.1), channel_id=1, source_target_pairs={{0,8},{8,0},{1,9},{9,1},{2,10},{10,2},{3,11},{11,3},{4,12},{12,4},... | collective-permute-start | bytes 1572872 | tf_op jit(solution)/shard_map/ppermute | solution.py:26
  21.1 17.8 %collective-permute-start.2 = (bf16[1024,256]{1,0:T(8,128)(2,1)}, bf16[1024,256]{1,0:T(8,128)(2,1)S(1)}, u32[]{:S(2)}, u32[]{:S(2)}) collective-permute-start(bf16[1024,256]{1,0:T(8,128)(2,1)} %rest_1_.1), channel_id=1, source_target_pairs={{0,8},{8,0},{1,9},{9,1},{2,10},{10,2},{3,11},{11,3},{4,12},{12,4},... | collective-permute-start | bytes 1572872 | tf_op jit(solution)/shard_map/ppermute | solution.py:26
  23.0 15.9 %collective-permute-start.3 = (bf16[1024,256]{1,0:T(8,128)(2,1)}, bf16[1024,256]{1,0:T(8,128)(2,1)S(1)}, u32[]{:S(2)}, u32[]{:S(2)}) collective-permute-start(bf16[1024,256]{1,0:T(8,128)(2,1)} %rest_2_.1), channel_id=1, source_target_pairs={{0,8},{8,0},{1,9},{9,1},{2,10},{10,2},{3,11},{11,3},{4,12},{12,4},... | collective-permute-start | bytes 1572872 | tf_op jit(solution)/shard_map/ppermute | solution.py:26
  25.4 13.4 %collective-permute-start.4 = (bf16[1024,256]{1,0:T(8,128)(2,1)}, bf16[1024,256]{1,0:T(8,128)(2,1)S(1)}, u32[]{:S(2)}, u32[]{:S(2)}) collective-permute-start(bf16[1024,256]{1,0:T(8,128)(2,1)} %rest_3_.1), channel_id=1, source_target_pairs={{0,8},{8,0},{1,9},{9,1},{2,10},{10,2},{3,11},{11,3},{4,12},{12,4},... | collective-permute-start | bytes 1572872 | tf_op jit(solution)/shard_map/ppermute | solution.py:26
  30.8 8.0 %collective-permute-start = (bf16[96,1024]{1,0:T(8,128)(2,1)S(1)}, bf16[96,1024]{1,0:T(8,128)(2,1)S(1)}, u32[]{:S(2)}, u32[]{:S(2)}) collective-permute-start(bf16[96,1024]{1,0:T(8,128)(2,1)S(1)} %shard_map.112.rows), channel_id=1, source_target_pairs={{0,256},{256,0},{1,257},{257,1},{2,258},{258,2},{3,259},{259,3},{4... | collective-permute-start | bytes 589832 | tf_op jit(solution)/shard_map/ppermute | solution.py:26
  35.7 1.0 copy-start.2
  36.7 1.0 copy-start.4
  37.8 1.0 copy-start.6
  38.8 1.0 copy-start.3
  38.8 1.2 copy-start.5
  38.8 1.4 copy-start.7
  42.0 12.0 %copy-start = (bf16[256,1024]{1,0:T(8,128)(2,1)S(1)}, bf16[256,1024]{1,0:T(8,128)(2,1)}, u32[]{:S(2)}) copy-start(bf16[256,1024]{1,0:T(8,128)(2,1)} %down.3) | copy-start | bytes 1572868
  42.0 13.9 %copy-start.8 = (bf16[256,1024]{1,0:T(8,128)(2,1)S(1)}, bf16[256,1024]{1,0:T(8,128)(2,1)}, u32[]{:S(2)}) copy-start(bf16[256,1024]{1,0:T(8,128)(2,1)} %probe.1) | copy-start | bytes 1572868
  42.0 16.3 %all-to-all-start.1 = ((bf16[8,48,1024]{2,1,0:T(8,128)(2,1)}), bf16[8,48,1024]{2,1,0:T(8,128)(2,1)S(1)}, u32[]{:S(2)}, u32[]{:S(2)}) async-start(bf16[8,48,1024]{2,1,0:T(8,128)(2,1)} %bitcast.28), calls=%async_computation.1 | async-start | bytes 1572864 | tf_op jit(solution)/shard_map/all_to_all | solution.py:300
  46.3 12.1 %collective-permute-start.5 = (bf16[192,1024]{1,0:T(8,128)(2,1)}, bf16[192,1024]{1,0:T(8,128)(2,1)S(1)}, u32[]{:S(2)}, u32[]{:S(2)}) collective-permute-start(bf16[192,1024]{1,0:T(8,128)(2,1)} %get-tuple-element.19.inputs), channel_id=1, source_target_pairs={{0,8},{8,0},{1,9},{9,1},{2,10},{10,2},{3,11},{11,3},{4,12},{12,4},... | collective-permute-start | bytes 1179656 | tf_op jit(solution)/shard_map/ppermute | solution.py:26
  54.0 10.8 %collective-permute-start.6 = (bf16[256,1024]{1,0:T(8,128)(2,1)S(1)}, bf16[256,1024]{1,0:T(8,128)(2,1)S(1)}, u32[]{:S(2)}, u32[]{:S(2)}) collective-permute-start(bf16[256,1024]{1,0:T(8,128)(2,1)S(1)} %copy-done), channel_id=1, source_target_pairs={{0,8},{8,0},{1,9},{9,1},{2,10},{10,2},{3,11},{11,3},{4,12},{12,4},... | collective-permute-start | bytes 1572872 | tf_op jit(solution)/shard_map/ppermute | solution.py:26
  56.0 8.8 %collective-permute-start.7 = (bf16[256,1024]{1,0:T(8,128)(2,1)S(1)}, bf16[256,1024]{1,0:T(8,128)(2,1)S(1)}, u32[]{:S(2)}, u32[]{:S(2)}) collective-permute-start(bf16[256,1024]{1,0:T(8,128)(2,1)S(1)} %copy-done.8), channel_id=1, source_target_pairs={{0,8},{8,0},{1,9},{9,1},{2,10},{10,2},{3,11},{11,3},{4,12},{12,4},... | collective-permute-start | bytes 1572872 | tf_op jit(solution)/shard_map/ppermute | solution.py:26
  59.3 12.0 %all-to-all-start.2 = ((bf16[8,48,512]{2,1,0:T(8,128)(2,1)}), bf16[8,48,512]{2,1,0:T(8,128)(2,1)S(1)}, u32[]{:S(2)}, u32[]{:S(2)}) async-start(bf16[8,48,512]{2,1,0:T(8,128)(2,1)} %bitcast.30), calls=%async_computation.2 | async-start | bytes 786432 | tf_op jit(solution)/shard_map/all_to_all | solution.py:310
  72.4 10.4 %collective-permute-start.9 = (bf16[96,1024]{1,0:T(8,128)(2,1)S(1)}, bf16[96,1024]{1,0:T(8,128)(2,1)S(1)}, u32[]{:S(2)}, u32[]{:S(2)}) collective-permute-start(bf16[96,1024]{1,0:T(8,128)(2,1)S(1)} %get-tuple-element.24), channel_id=1, source_target_pairs={{0,256},{256,0},{1,257},{257,1},{2,258},{258,2},{3,259},{259,3},{4... | collective-permute-start | bytes 589832 | tf_op jit(solution)/shard_map/ppermute | solution.py:26
  76.9 5.8 %collective-permute-start.8 = (bf16[192,256]{1,0:T(8,128)(2,1)S(1)}, bf16[192,256]{1,0:T(8,128)(2,1)S(1)}, u32[]{:S(2)}, u32[]{:S(2)}) collective-permute-start(bf16[192,256]{1,0:T(8,128)(2,1)S(1)} %get-tuple-element.22), channel_id=1, source_target_pairs={{0,8},{8,0},{1,9},{9,1},{2,10},{10,2},{3,11},{11,3},{4,12},{12,4},... | collective-permute-start | bytes 294920 | tf_op jit(solution)/shard_map/ppermute | solution.py:26
  122.4 9.4 %collective-permute-start.10 = (bf16[768,128]{1,0:T(8,128)(2,1)S(1)}, bf16[768,128]{1,0:T(8,128)(2,1)S(1)}, u32[]{:S(2)}, u32[]{:S(2)}) collective-permute-start(bf16[768,128]{1,0:T(8,128)(2,1)S(1)} %bitcast.15), channel_id=1, source_target_pairs={{0,256},{256,0},{1,257},{257,1},{2,258},{258,2},{3,259},{259,3},{4... | collective-permute-start | bytes 589832 | tf_op jit(solution)/shard_map/ppermute | solution.py:26
  124.3 8.6 %collective-permute-start.11 = (bf16[768,128]{1,0:T(8,128)(2,1)S(1)}, bf16[768,128]{1,0:T(8,128)(2,1)S(1)}, u32[]{:S(2)}, u32[]{:S(2)}) collective-permute-start(bf16[768,128]{1,0:T(8,128)(2,1)S(1)} %bitcast.16), channel_id=1, source_target_pairs={{0,8},{8,0},{1,9},{9,1},{2,10},{10,2},{3,11},{11,3},{4,12},{12,4},... | collective-permute-start | bytes 589832 | tf_op jit(solution)/shard_map/ppermute | solution.py:26
  143.3 11.5 %copy-start.10 = (s32[384]{0:T(512)S(1)}, s32[384]{0:T(512)}, u32[]{:S(2)}) copy-start(s32[384]{0:T(512)} %ids.1) | copy-start | bytes 4612
  143.3 16.7 %all-to-all-start.6 = ((bf16[16,48,256]{2,1,0:T(8,128)(2,1)}), bf16[16,48,256]{2,1,0:T(8,128)(2,1)S(1)}, u32[]{:S(2)}, u32[]{:S(2)}) async-start(bf16[16,48,256]{2,1,0:T(8,128)(2,1)} %bitcast.27), calls=%async_computation.6 | async-start | bytes 786432 | tf_op jit(solution)/shard_map/all_to_all | solution.py:365
  151.4 3.3 %collective-permute-start.12 = (bf16[768,128]{1,0:T(8,128)(2,1)S(1)}, bf16[768,128]{1,0:T(8,128)(2,1)S(1)}, u32[]{:S(2)}, u32[]{:S(2)}) collective-permute-start(bf16[768,128]{1,0:T(8,128)(2,1)S(1)} %collective-permute-done.10.rest_1_.blocks_y), channel_id=1, source_target_pairs={{0,8},{8,0},{1,9},{9,1},{2,10},{10,2},{3,11},{11,3},{4,12},{12,4},... | collective-permute-start | bytes 589832 | tf_op jit(solution)/shard_map/ppermute | solution.py:26
